TPU v7x, 32 devices: a whole 2x2x4 slice. The times are simulated.
32 devices in a mesh: ctx: 8 (over y, x, core), fsdp: 4 (over z).
Axes of the slice: x: 2, y: 2, z: 4, core: 2. Of those that a mesh axis runs over, the one named last changes fastest.
Arguments:
- queries: bfloat16 [4, 1024, 768], P('fsdp', 'ctx'), may hold values from -6 to 6
- key_rows: bfloat16 [4, 1024, 768], P('fsdp', 'ctx'), may hold values from -6 to 6
- value_rows: bfloat16 [4, 1024, 768], P('fsdp', 'ctx'), may hold values from -6 to 6
- lengths: int32 [4], P('fsdp'), may hold values from 512 to 1024, as said below
- out_weight: bfloat16 [768, 1536], P(None, 'fsdp'), may hold values from -0.21875 to 0.21875
Outputs:
- mixed: bfloat16 [4, 1024, 1536], P('fsdp', 'ctx')
Inputs may be any that keep to these rules, and one draw needn't show every extreme that they name: `lengths`: keys at frame positions at or beyond a recording's length are ignored.
All inputs are finite; a program needn't handle non-finite values.
Results may differ from a plain program's by a relative error of at most 0.011.
Values may be sent and summed in bfloat16 or wider, within the bound.
No kernel may reach another device: no remote copies, remote signals or barrier semaphores. Data moves between devices by JAX's collectives and lax.ppermute only.
A program may use at most 128 MiB of HBM per device.

v0:
```python
import math

import jax
import jax.numpy as jnp
from jax import lax
from jax.sharding import PartitionSpec as P

HEADS = 8


def per_device(queries, key_rows, value_rows, lengths, out_weight):
    frames = queries.shape[1]
    feature_width = queries.shape[2]
    head_size = feature_width // HEADS
    score_scale = 1.0 / math.sqrt(head_size)
    valid_frames = lengths[0]
    query_major = queries[0].reshape(frames, HEADS, head_size).transpose(1, 0, 2)
    block_kv = (
        lax.all_gather(key_rows, "ctx", axis=1, tiled=True),
        lax.all_gather(value_rows, "ctx", axis=1, tiled=True),
    )
    run_max = jnp.full((HEADS, frames), -1e30, jnp.float32)
    piece_len = block_kv[0].shape[1]
    key_major = block_kv[0][0].reshape(piece_len, HEADS, head_size).transpose(1, 0, 2)
    value_major = block_kv[1][0].reshape(piece_len, HEADS, head_size).transpose(1, 0, 2)
    inside = jnp.arange(piece_len, dtype=jnp.int32) < valid_frames
    bias = jnp.where(inside, jnp.float32(0.0), jnp.float32(-1e30))
    scores = (
        jnp.einsum("hqd,hkd->hqk", query_major, key_major, preferred_element_type=jnp.float32)
        * score_scale
        + bias[None, None, :]
    )
    new_max = jnp.maximum(run_max, jnp.max(scores, axis=-1))
    probs = jnp.exp(scores - new_max[..., None])
    run_sum = jnp.sum(probs, axis=-1)
    run_acc = jnp.einsum(
        "hqk,hkd->hqd", probs.astype(jnp.bfloat16), value_major, preferred_element_type=jnp.float32
    )
    run_max, run_sum, run_acc = (new_max, run_sum, run_acc)
    attention = (
        (run_acc / run_sum[..., None])
        .transpose(1, 0, 2)
        .reshape(frames, feature_width)
        .astype(jnp.bfloat16)
    )
    mixed = jnp.dot(
        attention,
        lax.all_gather(out_weight, "fsdp", axis=1, tiled=True),
        preferred_element_type=jnp.float32,
    ).astype(jnp.bfloat16)
    return mixed[None]


def solution(mesh):
    return jax.shard_map(
        per_device,
        mesh=mesh,
        in_specs=(
            P("fsdp", "ctx", None),
            P("fsdp", "ctx", None),
            P("fsdp", "ctx", None),
            P("fsdp"),
            P(None, "fsdp"),
        ),
        out_specs=P("fsdp", "ctx", None),
        check_vma=False,
    )
```

profile of v0, /device:TPU:0, one launch (start us, length us, event | category | flops | bytes accessed | tf_op | source)
XLA Modules:
  0.0 126.7 jit_solution(1252840006076723792)
XLA Ops:
  6.5 0.0 all-gather.4.cloned.1.call-start
  6.5 0.7 all-gather.4.cloned.1.call-update
  7.3 0.0 all-gather.6.cloned.1.call-start
  7.3 0.7 all-gather.6.cloned.1.call-update
  8.0 0.0 all-gather.8.cloned.1.call-start
  8.1 0.7 all-gather.8.cloned.1.call-update
  9.4 1.1 copy.9
  10.5 27.2 %all-gather.4.cloned.1.call-done = bf16[1,1024,768]{2,1,0:T(8,128)(2,1)} async-done(((bf16[1,128,768]{2,1,0:T(8,128)(2,1)}), bf16[1,1024,768]{2,1,0:T(8,128)(2,1)}) %all-gather.4.cloned.1.call-update) | async-done | bytes 1572880 | tf_op jit(solution)/shard_map/all_gather | solution.py:19
  37.7 1.7 %copy.10 = bf16[1,1024,768]{1,2,0:T(8,128)(2,1)S(1)} copy(bf16[1,1024,768]{2,1,0:T(8,128)(2,1)} %all-gather.4.cloned.1.call-done) | data formatting | bytes 3145728 | tf_op jit(solution)/shard_map/all_gather | solution.py:19
  39.4 25.9 %all-gather.6.cloned.1.call-done = bf16[1,1024,768]{2,1,0:T(8,128)(2,1)} async-done(((bf16[1,128,768]{2,1,0:T(8,128)(2,1)}), bf16[1,1024,768]{2,1,0:T(8,128)(2,1)}) %all-gather.6.cloned.1.call-update) | async-done | bytes 1572880 | tf_op jit(solution)/shard_map/all_gather | solution.py:20
  65.3 1.7 %copy.11 = bf16[1,1024,768]{1,2,0:T(8,128)(2,1)S(1)} copy(bf16[1,1024,768]{2,1,0:T(8,128)(2,1)} %all-gather.6.cloned.1.call-done) | data formatting | bytes 3145728 | tf_op jit(solution)/shard_map/all_gather | solution.py:20
  67.0 0.8 fusion
  67.8 1.0 fusion.1
  68.8 1.1 fusion.15
  69.9 47.3 %all-gather.8.cloned.1.call-done = bf16[768,1536]{1,0:T(8,128)(2,1)} async-done(((bf16[768,384]{1,0:T(8,128)(2,1)}), bf16[768,1536]{1,0:T(8,128)(2,1)}) %all-gather.8.cloned.1.call-update) | async-done | bytes 2359312 | tf_op jit(solution)/shard_map/all_gather | solution.py:48
  117.2 2.9 %fusion.3 = bf16[1,128,1536]{2,1,0:T(8,128)(2,1)} fusion(bf16[128,768]{0,1:T(8,128)(2,1)S(1)} %bitcast.29, bf16[768,1536]{1,0:T(8,128)(2,1)} %all-gather.8.cloned.1.call-done), kind=kOutput, calls=%fused_computation.6 | convolution fusion | flops 302186496 | bytes 2949120 | tf_op jit(solution)/shard_map/dot_general | solution.py:46
  (2 shorter events, 0.0 us)
Async XLA Ops:
  6.5 31.1 %all-gather.4.cloned.1.call-start = ((), (), s32[]{:S(2)}) async-start(), calls=%async_computation | async-start | bytes 1769472 | tf_op jit(solution)/shard_map/all_gather | solution.py:19
  7.3 58.0 %all-gather.6.cloned.1.call-start = ((), (), s32[]{:S(2)}) async-start(), calls=%async_computation.1 | async-start | bytes 1769472 | tf_op jit(solution)/shard_map/all_gather | solution.py:20
  8.0 109.2 %all-gather.8.cloned.1.call-start = ((), (), s32[]{:S(2)}) async-start(), calls=%async_computation.2 | async-start | bytes 2949120 | tf_op jit(solution)/shard_map/all_gather | solution.py:48
Sparse Core Ops, SparseCore 0:
  9.2 28.3 all-gather.3
  39.5 25.6 all-gather.5
  66.9 50.2 all-gather.7
where the time goes:
time: 127 us
  waiting for transfers between devices  102 us (80%)
  between operations  13.8 us (11%)
  matrix products  4.84 us (4%)
  local copies, waits for them, and re-layouts  4.5 us (4%)
    all_gather x1, waiting for transfers between devices, per_device(): lax.all_gather(out_weight, 'fsdp', axis=1, tiled=True)  47.3 us
    all_gather x1, waiting for transfers between devices, per_device(): lax.all_gather(key_rows, 'ctx', axis=1, tiled=True)  27.2 us
    all_gather x1, waiting for transfers between devices, per_device(): lax.all_gather(value_rows, 'ctx', axis=1, tiled=True)  25.9 us
    dot_general x1, matrix products, per_device(): jnp.dot(attention, lax.all_gather(out_weight, 'fsdp', axis=1, tiled=True)...  2.91 us
  transfers between devices with their start and end apart: 3, of which 3 were waited for; matrix products, arithmetic and copies ran while one was open for 6% of the time, Pallas kernels for 0%

commit v1 on v0

v1 whole, which is shorter than its diff:
```python
import functools
import math

import jax
import jax.numpy as jnp
from jax import lax
from jax.experimental import pallas as pl
from jax.experimental.pallas import tpu as pltpu
from jax.sharding import PartitionSpec as P

HEADS = 8
VMEM_LIMIT = 48 * 1024 * 1024
WHOLE = pl.BlockSpec(memory_space=pltpu.VMEM)
SCALARS = pl.BlockSpec(memory_space=pltpu.SMEM)


def params():
    return pltpu.CompilerParams(vmem_limit_bytes=VMEM_LIMIT)


def pack_kernel(query_ref, key_ref, value_ref, packed_ref):
    head_size = packed_ref.shape[2]
    for part, ref in enumerate((query_ref, key_ref, value_ref)):
        turned = ref[0].T
        for head in range(HEADS):
            packed_ref[head, part] = turned[head * head_size : (head + 1) * head_size, :]


def pack(queries, key_rows, value_rows):
    _, frames, features = queries.shape
    return pl.pallas_call(
        pack_kernel,
        out_shape=jax.ShapeDtypeStruct((HEADS, 3, features // HEADS, frames), queries.dtype),
        in_specs=[WHOLE] * 3,
        out_specs=WHOLE,
        compiler_params=params(),
        name="pack_heads",
    )(queries, key_rows, value_rows)


def attention_kernel(chunk_blocks, lengths_ref, query_ref, key_ref, value_ref, out_ref, key_scr, value_scr):
    key_blocks, _, head_size, block = key_ref.shape
    query_blocks = query_ref.shape[0]
    keys = key_blocks * block
    for at in range(key_blocks):
        key_scr[at * block : (at + 1) * block, :] = key_ref[at, 0].T
        value_scr[:, at * block : (at + 1) * block] = value_ref[at, 0]
    scale = jnp.float32(1.0 / math.sqrt(head_size))
    log2e = jnp.float32(math.log2(math.e))
    valid = lengths_ref[0]
    inside = lax.broadcasted_iota(jnp.int32, (keys, chunk_blocks * block), 0) < valid
    for first in range(0, query_blocks, chunk_blocks):
        query = jnp.concatenate([query_ref[first + at, 0] for at in range(chunk_blocks)], axis=1)
        scores = jnp.dot(key_scr[...], query, preferred_element_type=jnp.float32) * (scale * log2e)
        scores = jnp.where(inside, scores, jnp.float32(-1e30))
        row_max = jnp.max(scores, axis=0, keepdims=True)
        probs = jnp.exp2(scores - row_max)
        total = jnp.sum(probs, axis=0, keepdims=True)
        mixed = jnp.dot(value_scr[...], probs.astype(jnp.bfloat16), preferred_element_type=jnp.float32)
        mixed = (mixed / total).astype(jnp.bfloat16)
        for at in range(chunk_blocks):
            out_ref[first + at] = mixed[:, at * block : (at + 1) * block]


def attend(lengths, query, key, value, parts):
    query_blocks, _, head_size, block = query.shape
    key_blocks = key.shape[0]
    chunk_blocks = 2 if query_blocks % 2 == 0 else 1
    specs = [
        pl.BlockSpec((array.shape[0], 1, head_size, block), functools.partial(lambda part, i: (0, part, 0, 0), part))
        for array, part in zip((query, key, value), parts)
    ]
    return pl.pallas_call(
        functools.partial(attention_kernel, chunk_blocks),
        grid=(1,),
        out_shape=jax.ShapeDtypeStruct((query_blocks, head_size, block), jnp.bfloat16),
        in_specs=[SCALARS] + specs,
        out_specs=pl.BlockSpec((query_blocks, head_size, block), lambda i: (0, 0, 0)),
        scratch_shapes=[
            pltpu.VMEM((key_blocks * block, head_size), jnp.bfloat16),
            pltpu.VMEM((head_size, key_blocks * block), jnp.bfloat16),
        ],
        compiler_params=params(),
        cost_estimate=pl.CostEstimate(
            flops=4 * query_blocks * key_blocks * block * block * head_size,
            bytes_accessed=2 * (2 * query_blocks + 2 * key_blocks) * head_size * block,
            transcendentals=query_blocks * key_blocks * block * block,
        ),
        name="attend_one_head",
    )(lengths, query, key, value)


def project_kernel(places_ref, turned_ref, own_ref, *refs):
    out_ref = refs[-1]
    pieces = refs[:-1]
    features, columns = own_ref.shape
    shards = out_ref.shape[2] // columns
    per_shard = len(pieces) // (shards - 1)
    rows = features // per_shard
    own = jnp.dot(turned_ref[...].T, own_ref[...], preferred_element_type=jnp.float32)
    place = pl.multiple_of(places_ref[0] * columns, 128)
    out_ref[0, :, pl.ds(place, columns)] = own.astype(out_ref.dtype)
    turned = [
        turned_ref[pl.ds(pl.multiple_of((places_ref[1] ^ e) * rows, 64), rows), :].T for e in range(per_shard)
    ]
    for shard in range(1, shards):
        total = jnp.zeros((out_ref.shape[1], columns), jnp.float32)
        for e in range(per_shard):
            piece = pieces[(shard - 1) * per_shard + e]
            total = total + jnp.dot(turned[e], piece[...], preferred_element_type=jnp.float32)
        place = pl.multiple_of((places_ref[0] ^ shard) * columns, 128)
        out_ref[0, :, pl.ds(place, columns)] = total.astype(out_ref.dtype)


def project(places, turned, own, pieces, shards):
    features, frames = turned.shape
    return pl.pallas_call(
        project_kernel,
        out_shape=jax.ShapeDtypeStruct((1, frames, shards * own.shape[1]), jnp.bfloat16),
        in_specs=[SCALARS] + [WHOLE] * (2 + len(pieces)),
        out_specs=WHOLE,
        compiler_params=params(),
        cost_estimate=pl.CostEstimate(
            flops=2 * features * frames * shards * own.shape[1],
            bytes_accessed=2 * features * shards * own.shape[1],
            transcendentals=0,
        ),
        name="project_pieces",
    )(places, turned, own, *pieces)


def exchange(array, axis, size, flip):
    return lax.ppermute(array, axis, [(i, i ^ flip) for i in range(size)])


def weight_pieces(out_weight, ctx, fsdp):
    quarter = lax.axis_index("ctx") % 4
    rows = out_weight.shape[0] // 4
    mine = lax.dynamic_slice_in_dim(out_weight, quarter * rows, rows, 0)
    pieces = []
    for flip in range(1, fsdp):
        same = exchange(mine, "fsdp", fsdp, flip)
        other_chip = exchange(same, "ctx", ctx, 2)
        pieces += [same, exchange(same, "ctx", ctx, 1), other_chip, exchange(other_chip, "ctx", ctx, 1)]
    return pieces


def per_device(ctx, fsdp, queries, key_rows, value_rows, lengths, out_weight):
    _, frames, features = queries.shape
    groups = [[first + at for at in range(HEADS)] for first in range(0, ctx, HEADS)]
    swap = functools.partial(
        lax.all_to_all, axis_name="ctx", split_axis=0, concat_axis=0, axis_index_groups=groups, tiled=True
    )
    split_weight = fsdp in (2, 4) and ctx % 4 == 0
    if split_weight:
        pieces = weight_pieces(out_weight, ctx, fsdp)
    else:
        whole_weight = lax.all_gather(out_weight, "fsdp", axis=1, tiled=True)
    by_head = swap(pack(queries, key_rows, value_rows))
    if ctx == HEADS:
        mixed = attend(lengths, by_head, by_head, by_head, (0, 1, 2))
    else:
        across = [[head + first for first in range(0, ctx, HEADS)] for head in range(HEADS)]
        rest = lax.all_gather(by_head[:, 1:], "ctx", axis=0, axis_index_groups=across, tiled=True)
        mixed = attend(lengths, by_head[:, :1], rest, rest, (0, 0, 1))
    turned = swap(mixed).reshape(features, frames)
    if split_weight:
        places = jnp.stack([lax.axis_index("fsdp"), lax.axis_index("ctx") % 4]).astype(jnp.int32)
        return project(places, turned, out_weight, pieces, fsdp)
    return jnp.dot(turned.T, whole_weight, preferred_element_type=jnp.float32).astype(jnp.bfloat16)[None]


def solution(mesh):
    return jax.shard_map(
        functools.partial(per_device, mesh.shape["ctx"], mesh.shape["fsdp"]),
        mesh=mesh,
        in_specs=(
            P("fsdp", "ctx", None),
            P("fsdp", "ctx", None),
            P("fsdp", "ctx", None),
            P("fsdp"),
            P(None, "fsdp"),
        ),
        out_specs=P("fsdp", "ctx", None),
        check_vma=False,
    )
```

time: 127 us -> 43.8 us (0.34)
  waiting for transfers between devices: 102 us -> 14.4 us
  starting transfers between devices: 0.08 us -> 18.8 us
  between operations: 13.8 us -> 0.69 us
  Pallas kernels: 0 us -> 6.62 us
  matrix products: 4.84 us -> 0 us
  local copies, waits for them, and re-layouts: 4.5 us -> 2.81 us
    all_gather x3 -> x0, waiting for transfers between devices: 100 us -> none  [the longest x1 47.3 us: per_device(): lax.all_gather(out_weight, 'fsdp', axis=1, tiled=True)]
    ppermute x0 -> x12, waiting for transfers between devices: none -> 10.8 us  [exchange(): return lax.ppermute(array, axis, [(i, i ^ flip) for i in range(size)])]
    all_to_all x0 -> x2, starting transfers between devices: none -> 9.47 us  [the longest x1 5.3 us: per_device(): by_head = swap(pack(queries, key_rows, value_rows))]
    ppermute x0 -> x12, starting transfers between devices: none -> 9.37 us  [exchange(): return lax.ppermute(array, axis, [(i, i ^ flip) for i in range(size)])]
    pallas_call x0 -> x3, Pallas kernels: none -> 6.62 us  [the longest x1 3.59 us: attend(): pl.pallas_call(functools.partial(attention_kernel, chunk_blocks), grid=(1...]
    dot_general x3 -> x0, matrix products: 4.84 us -> none  [the longest x1 2.91 us: per_device(): jnp.dot(attention, lax.all_gather(out_weight, 'fsdp', axis=1, tiled=True)...]
    all_to_all x0 -> x2, waiting for transfers between devices: none -> 3.63 us  [the longest x1 3.62 us: per_device(): turned = swap(mixed).reshape(features, frames)]
    all_gather x2 -> x0, local copies, waits for them, and re-layouts: 3.42 us -> none  [the longest x1 1.71 us: per_device(): lax.all_gather(key_rows, 'ctx', axis=1, tiled=True)]
  transfers between devices with their start and end apart: 3 -> 14, of which waited for: 3 -> 7; matrix products, arithmetic and copies ran while one was open for 6% -> 0% of each run, Pallas kernels for 0% -> 8%
where the time goes in v1:
time: 43.8 us; the launch traced here: 43.5 us
  starting transfers between devices  18.8 us (43%)
  waiting for transfers between devices  14.4 us (33%)
  Pallas kernels  6.62 us (15%)
  local copies, waits for them, and re-layouts  2.81 us (6%)
  between operations  0.69 us (2%)
    ppermute x12, waiting for transfers between devices, exchange(): return lax.ppermute(array, axis, [(i, i ^ flip) for i in range(size)])  10.8 us
    ppermute x12, starting transfers between devices, exchange(): return lax.ppermute(array, axis, [(i, i ^ flip) for i in range(size)])  9.37 us
    all_to_all x1, starting transfers between devices, per_device(): by_head = swap(pack(queries, key_rows, value_rows))  5.3 us
    all_to_all x1, starting transfers between devices, per_device(): turned = swap(mixed).reshape(features, frames)  4.17 us
    all_to_all x1, waiting for transfers between devices, per_device(): turned = swap(mixed).reshape(features, frames)  3.62 us
    pallas_call x1, Pallas kernels, attend(): pl.pallas_call(functools.partial(attention_kernel, chunk_blocks), grid=(1...  3.59 us
    unnamed x8, local copies, waits for them, and re-layouts  2.78 us
    pallas_call x1, Pallas kernels, project(): pl.pallas_call(project_kernel, out_shape=jax.ShapeDtypeStruct((1, frames,...  2.01 us
  transfers between devices with their start and end apart: 14, of which 7 were waited for; matrix products, arithmetic and copies ran while one was open for 0% of the time, Pallas kernels for 8%

profile of v1, /device:TPU:0, one launch (start us, length us, event | category | flops | bytes accessed | tf_op | source)
XLA Modules:
  0.0 43.5 jit_solution(6030791850374416131)
XLA Ops:
  0.0 0.0 copy-start.1
  0.0 0.9 %copy-done.1 = bf16[1,128,768]{2,1,0:T(8,128)(2,1)S(1)} copy-done((bf16[1,128,768]{2,1,0:T(8,128)(2,1)S(1)}, bf16[1,128,768]{2,1,0:T(8,128)(2,1)}, u32[]{:S(2)}) %copy-start.1) | copy-done | bytes 196632
  0.9 0.0 copy-start.2
  0.9 0.9 %copy-done.2 = bf16[1,128,768]{2,1,0:T(8,128)(2,1)S(1)} copy-done((bf16[1,128,768]{2,1,0:T(8,128)(2,1)S(1)}, bf16[1,128,768]{2,1,0:T(8,128)(2,1)}, u32[]{:S(2)}) %copy-start.2) | copy-done | bytes 196632
  1.9 0.0 copy-start.3
  1.9 0.9 %copy-done.3 = bf16[1,128,768]{2,1,0:T(8,128)(2,1)S(1)} copy-done((bf16[1,128,768]{2,1,0:T(8,128)(2,1)S(1)}, bf16[1,128,768]{2,1,0:T(8,128)(2,1)}, u32[]{:S(2)}) %copy-start.3) | copy-done | bytes 196632
  2.8 1.0 %pack_heads.1 = bf16[8,3,96,128]{3,2,1,0:T(8,128)(2,1)} custom-call(bf16[1,128,768]{2,1,0:T(8,128)(2,1)S(1)} %copy-done.1, bf16[1,128,768]{2,1,0:T(8,128)(2,1)S(1)} %copy-done.2, bf16[1,128,768]{2,1,0:T(8,128)(2,1)S(1)} %copy-done.3), custom_call_target="tpu_custom_call" | custom-call | tf_op jit(solution)/shard_map/pack_heads/pallas_call | solution.py:31
  3.8 0.0 copy-start
  3.8 5.3 %all-to-all-start = ((bf16[8,3,96,128]{3,2,1,0:T(8,128)(2,1)}), bf16[8,3,96,128]{3,2,1,0:T(8,128)(2,1)S(1)}, u32[]{:S(2)}, u32[]{:S(2)}) async-start(bf16[8,3,96,128]{3,2,1,0:T(8,128)(2,1)} %pack_heads.1), calls=%async_computation | async-start | bytes 1179648 | tf_op jit(solution)/shard_map/all_to_all | solution.py:159
  9.1 0.0 copy-done
  9.2 1.6 %collective-permute-start = (bf16[192,384]{1,0:T(8,128)(2,1)S(1)}, bf16[192,384]{1,0:T(8,128)(2,1)S(1)}, u32[]{:S(2)}, u32[]{:S(2)}) collective-permute-start(bf16[192,384]{1,0:T(8,128)(2,1)S(1)} %constant_dynamic-slice_fusion), channel_id=1, source_target_pairs={{0,1},{1,0},{2,3},{3,2},{4,5},{5,4},{6,7},{7,6},{8,9},{9,8},{10,11... | collective-permute-start | bytes 442376 | tf_op jit(solution)/shard_map/ppermute | solution.py:133
  10.8 2.6 %collective-permute-start.4 = (bf16[192,384]{1,0:T(8,128)(2,1)S(1)}, bf16[192,384]{1,0:T(8,128)(2,1)S(1)}, u32[]{:S(2)}, u32[]{:S(2)}) collective-permute-start(bf16[192,384]{1,0:T(8,128)(2,1)S(1)} %constant_dynamic-slice_fusion), channel_id=1, source_target_pairs={{0,2},{1,3},{2,0},{3,1},{4,6},{5,7},{6,4},{7,5},{8,10},{9,11},{10,... | collective-permute-start | bytes 442376 | tf_op jit(solution)/shard_map/ppermute | solution.py:133
  13.4 0.2 collective-permute-start.8
  13.6 4.6 %collective-permute-done.refs_0_ = bf16[192,384]{1,0:T(8,128)(2,1)S(1)} collective-permute-done((bf16[192,384]{1,0:T(8,128)(2,1)S(1)}, bf16[192,384]{1,0:T(8,128)(2,1)S(1)}, u32[]{:S(2)}, u32[]{:S(2)}) %collective-permute-start) | collective-permute-done | bytes 147488 | tf_op jit(solution)/shard_map/ppermute | solution.py:133
  18.2 0.0 collective-permute-start.1
  18.2 1.3 %collective-permute-start.2 = (bf16[192,384]{1,0:T(8,128)(2,1)S(1)}, bf16[192,384]{1,0:T(8,128)(2,1)S(1)}, u32[]{:S(2)}, u32[]{:S(2)}) collective-permute-start(bf16[192,384]{1,0:T(8,128)(2,1)S(1)} %collective-permute-done.refs_0_), channel_id=1, source_target_pairs={{0,8},{4,12},{8,0},{12,4},{16,24},{20,28},{24,16},{28,20},{1,9},{5... | collective-permute-start | bytes 442376 | tf_op jit(solution)/shard_map/ppermute | solution.py:133
  19.6 5.2 %collective-permute-done.4.refs_4_ = bf16[192,384]{1,0:T(8,128)(2,1)S(1)} collective-permute-done((bf16[192,384]{1,0:T(8,128)(2,1)S(1)}, bf16[192,384]{1,0:T(8,128)(2,1)S(1)}, u32[]{:S(2)}, u32[]{:S(2)}) %collective-permute-start.4) | collective-permute-done | bytes 147488 | tf_op jit(solution)/shard_map/ppermute | solution.py:133
  24.7 2.0 %collective-permute-start.6 = (bf16[192,384]{1,0:T(8,128)(2,1)S(1)}, bf16[192,384]{1,0:T(8,128)(2,1)S(1)}, u32[]{:S(2)}, u32[]{:S(2)}) collective-permute-start(bf16[192,384]{1,0:T(8,128)(2,1)S(1)} %collective-permute-done.4.refs_4_), channel_id=1, source_target_pairs={{0,8},{4,12},{8,0},{12,4},{16,24},{20,28},{24,16},{28,20},{1,9},{5... | collective-permute-start | bytes 442376 | tf_op jit(solution)/shard_map/ppermute | solution.py:133
  26.8 0.0 collective-permute-done.8.refs_8_
  26.8 0.0 collective-permute-start.10
  27.4 0.0 all-to-all-done.query_ref.key_ref.value_ref
  27.4 3.6 %attend_one_head.1 = bf16[8,96,128]{2,1,0:T(8,128)(2,1)} custom-call(s32[1]{0:T(128)S(6)} %copy.6.lengths_ref, bf16[8,3,96,128]{3,2,1,0:T(8,128)(2,1)S(1)} %all-to-all-done.query_ref.key_ref.value_ref, bf16[8,3,96,128]{3,2,1,0:T(8,128)(2,1)S(1)} %all-to-all-done.query_ref.key_ref.value_ref, bf16[8,3,96,128]{3,2,1,0:T(8,128)(2,1)S(1)} %all-to-all-done.query_ref.key_ref.value_ref), custom_call_target="tpu_custom_call" | custom-call | flops 402653184 | bytes 786432 | tf_op jit(solution)/shard_map/attend_one_head/pallas_call | solution.py:73
  31.0 4.2 %all-to-all-start.1 = ((bf16[8,96,128]{2,1,0:T(8,128)(2,1)}), bf16[8,96,128]{2,1,0:T(8,128)(2,1)S(1)}, u32[]{:S(2)}, u32[]{:S(2)}) async-start(bf16[8,96,128]{2,1,0:T(8,128)(2,1)} %attend_one_head.1), calls=%async_computation.1 | async-start | bytes 393216 | tf_op jit(solution)/shard_map/all_to_all | solution.py:166
  35.2 0.5 %collective-permute-start.5 = (bf16[192,384]{1,0:T(8,128)(2,1)S(1)}, bf16[192,384]{1,0:T(8,128)(2,1)S(1)}, u32[]{:S(2)}, u32[]{:S(2)}) collective-permute-start(bf16[192,384]{1,0:T(8,128)(2,1)S(1)} %collective-permute-done.4.refs_4_), channel_id=1, source_target_pairs={{0,4},{4,0},{8,12},{12,8},{16,20},{20,16},{24,28},{28,24},{1,5},{5... | collective-permute-start | bytes 442376 | tf_op jit(solution)/shard_map/ppermute | solution.py:133
  35.7 0.0 collective-permute-done.1.refs_1_
  35.7 0.1 collective-permute-start.9
  35.8 0.0 collective-permute-done.2.refs_2_
  35.8 0.4 %collective-permute-start.3 = (bf16[192,384]{1,0:T(8,128)(2,1)S(1)}, bf16[192,384]{1,0:T(8,128)(2,1)S(1)}, u32[]{:S(2)}, u32[]{:S(2)}) collective-permute-start(bf16[192,384]{1,0:T(8,128)(2,1)S(1)} %collective-permute-done.2.refs_2_), channel_id=1, source_target_pairs={{0,4},{4,0},{8,12},{12,8},{16,20},{20,16},{24,28},{28,24},{1,5},{5... | collective-permute-start | bytes 442376 | tf_op jit(solution)/shard_map/ppermute | solution.py:133
  36.2 0.0 collective-permute-done.6.refs_6_
  36.2 0.1 collective-permute-start.7
  36.3 0.0 collective-permute-done.10.refs_10_
  36.3 0.4 %collective-permute-start.11 = (bf16[192,384]{1,0:T(8,128)(2,1)S(1)}, bf16[192,384]{1,0:T(8,128)(2,1)S(1)}, u32[]{:S(2)}, u32[]{:S(2)}) collective-permute-start(bf16[192,384]{1,0:T(8,128)(2,1)S(1)} %collective-permute-done.10.refs_10_), channel_id=1, source_target_pairs={{0,4},{4,0},{8,12},{12,8},{16,20},{20,16},{24,28},{28,24},{1,5},{5... | collective-permute-start | bytes 442376 | tf_op jit(solution)/shard_map/ppermute | solution.py:133
  36.8 0.1 pad_add_fusion.places_ref
  36.8 0.0 collective-permute-done.5.refs_5_
  36.8 0.3 collective-permute-done.9.refs_9_
  37.1 0.2 collective-permute-done.3.refs_3_
  37.3 0.3 collective-permute-done.7.refs_7_
  37.6 0.2 collective-permute-done.11.refs_11_
  37.8 3.6 %all-to-all-done.1 = bf16[8,96,128]{2,1,0:T(8,128)(2,1)S(1)} async-done(((bf16[8,96,128]{2,1,0:T(8,128)(2,1)}), bf16[8,96,128]{2,1,0:T(8,128)(2,1)S(1)}, u32[]{:S(2)}, u32[]{:S(2)}) %all-to-all-start.1) | async-done | bytes 196640 | tf_op jit(solution)/shard_map/all_to_all | solution.py:166
  41.4 2.0 %project_pieces.1 = bf16[1,128,1536]{2,1,0:T(8,128)(2,1)} custom-call(s32[2]{0:T(128)S(1)} %pad_add_fusion.places_ref, bf16[768,128]{1,0:T(8,128)(2,1)S(1)} %bitcast.3, bf16[768,384]{1,0:T(8,128)(2,1)S(1)} %copy-done, bf16[192,384]{1,0:T(8,128)(2,1)S(1)} %collective-permute-done.refs_0_, bf16[192,384]{1,0:T(8,128)(2,1)S(1)} %collective-permute-done.1.refs_1_, ...), custom_call_target="tpu_custom_call" | custom-call | flops 301989888 | bytes 2359296 | tf_op jit(solution)/shard_map/project_pieces/pallas_call | solution.py:117
  (1 shorter events, 0.0 us)
Async XLA Ops:
  0.0 0.9 %copy-start.1 = (bf16[1,128,768]{2,1,0:T(8,128)(2,1)S(1)}, bf16[1,128,768]{2,1,0:T(8,128)(2,1)}, u32[]{:S(2)}) copy-start(bf16[1,128,768]{2,1,0:T(8,128)(2,1)} %query_ref.1) | copy-start | bytes 589828
  0.9 0.9 %copy-start.2 = (bf16[1,128,768]{2,1,0:T(8,128)(2,1)S(1)}, bf16[1,128,768]{2,1,0:T(8,128)(2,1)}, u32[]{:S(2)}) copy-start(bf16[1,128,768]{2,1,0:T(8,128)(2,1)} %key_ref.1) | copy-start | bytes 589828
  1.9 0.9 %copy-start.3 = (bf16[1,128,768]{2,1,0:T(8,128)(2,1)S(1)}, bf16[1,128,768]{2,1,0:T(8,128)(2,1)}, u32[]{:S(2)}) copy-start(bf16[1,128,768]{2,1,0:T(8,128)(2,1)} %value_ref.1) | copy-start | bytes 589828
  3.8 5.3 %copy-start = (bf16[768,384]{1,0:T(8,128)(2,1)S(1)}, bf16[768,384]{1,0:T(8,128)(2,1)}, u32[]{:S(2)}) copy-start(bf16[768,384]{1,0:T(8,128)(2,1)} %own_ref.1) | copy-start | bytes 1769476
  3.8 23.6 %all-to-all-start = ((bf16[8,3,96,128]{3,2,1,0:T(8,128)(2,1)}), bf16[8,3,96,128]{3,2,1,0:T(8,128)(2,1)S(1)}, u32[]{:S(2)}, u32[]{:S(2)}) async-start(bf16[8,3,96,128]{3,2,1,0:T(8,128)(2,1)} %pack_heads.1), calls=%async_computation | async-start | bytes 1179648 | tf_op jit(solution)/shard_map/all_to_all | solution.py:159
  9.2 9.1 %collective-permute-start = (bf16[192,384]{1,0:T(8,128)(2,1)S(1)}, bf16[192,384]{1,0:T(8,128)(2,1)S(1)}, u32[]{:S(2)}, u32[]{:S(2)}) collective-permute-start(bf16[192,384]{1,0:T(8,128)(2,1)S(1)} %constant_dynamic-slice_fusion), channel_id=1, source_target_pairs={{0,1},{1,0},{2,3},{3,2},{4,5},{5,4},{6,7},{7,6},{8,9},{9,8},{10,11... | collective-permute-start | bytes 442376 | tf_op jit(solution)/shard_map/ppermute | solution.py:133
  10.8 13.9 %collective-permute-start.4 = (bf16[192,384]{1,0:T(8,128)(2,1)S(1)}, bf16[192,384]{1,0:T(8,128)(2,1)S(1)}, u32[]{:S(2)}, u32[]{:S(2)}) collective-permute-start(bf16[192,384]{1,0:T(8,128)(2,1)S(1)} %constant_dynamic-slice_fusion), channel_id=1, source_target_pairs={{0,2},{1,3},{2,0},{3,1},{4,6},{5,7},{6,4},{7,5},{8,10},{9,11},{10,... | collective-permute-start | bytes 442376 | tf_op jit(solution)/shard_map/ppermute | solution.py:133
  13.4 13.4 %collective-permute-start.8 = (bf16[192,384]{1,0:T(8,128)(2,1)S(1)}, bf16[192,384]{1,0:T(8,128)(2,1)S(1)}, u32[]{:S(2)}, u32[]{:S(2)}) collective-permute-start(bf16[192,384]{1,0:T(8,128)(2,1)S(1)} %constant_dynamic-slice_fusion), channel_id=1, source_target_pairs={{0,3},{1,2},{2,1},{3,0},{4,7},{5,6},{6,5},{7,4},{8,11},{9,10},{10,... | collective-permute-start | bytes 442376 | tf_op jit(solution)/shard_map/ppermute | solution.py:133
  18.2 17.5 %collective-permute-start.1 = (bf16[192,384]{1,0:T(8,128)(2,1)S(1)}, bf16[192,384]{1,0:T(8,128)(2,1)S(1)}, u32[]{:S(2)}, u32[]{:S(2)}) collective-permute-start(bf16[192,384]{1,0:T(8,128)(2,1)S(1)} %collective-permute-done.refs_0_), channel_id=1, source_target_pairs={{0,4},{4,0},{8,12},{12,8},{16,20},{20,16},{24,28},{28,24},{1,5},{5... | collective-permute-start | bytes 442376 | tf_op jit(solution)/shard_map/ppermute | solution.py:133
  18.2 17.6 %collective-permute-start.2 = (bf16[192,384]{1,0:T(8,128)(2,1)S(1)}, bf16[192,384]{1,0:T(8,128)(2,1)S(1)}, u32[]{:S(2)}, u32[]{:S(2)}) collective-permute-start(bf16[192,384]{1,0:T(8,128)(2,1)S(1)} %collective-permute-done.refs_0_), channel_id=1, source_target_pairs={{0,8},{4,12},{8,0},{12,4},{16,24},{20,28},{24,16},{28,20},{1,9},{5... | collective-permute-start | bytes 442376 | tf_op jit(solution)/shard_map/ppermute | solution.py:133
  24.7 11.5 %collective-permute-start.6 = (bf16[192,384]{1,0:T(8,128)(2,1)S(1)}, bf16[192,384]{1,0:T(8,128)(2,1)S(1)}, u32[]{:S(2)}, u32[]{:S(2)}) collective-permute-start(bf16[192,384]{1,0:T(8,128)(2,1)S(1)} %collective-permute-done.4.refs_4_), channel_id=1, source_target_pairs={{0,8},{4,12},{8,0},{12,4},{16,24},{20,28},{24,16},{28,20},{1,9},{5... | collective-permute-start | bytes 442376 | tf_op jit(solution)/shard_map/ppermute | solution.py:133
  26.8 9.6 %collective-permute-start.10 = (bf16[192,384]{1,0:T(8,128)(2,1)S(1)}, bf16[192,384]{1,0:T(8,128)(2,1)S(1)}, u32[]{:S(2)}, u32[]{:S(2)}) collective-permute-start(bf16[192,384]{1,0:T(8,128)(2,1)S(1)} %collective-permute-done.8.refs_8_), channel_id=1, source_target_pairs={{0,8},{4,12},{8,0},{12,4},{16,24},{20,28},{24,16},{28,20},{1,9},{5... | collective-permute-start | bytes 442376 | tf_op jit(solution)/shard_map/ppermute | solution.py:133
  31.0 10.4 %all-to-all-start.1 = ((bf16[8,96,128]{2,1,0:T(8,128)(2,1)}), bf16[8,96,128]{2,1,0:T(8,128)(2,1)S(1)}, u32[]{:S(2)}, u32[]{:S(2)}) async-start(bf16[8,96,128]{2,1,0:T(8,128)(2,1)} %attend_one_head.1), calls=%async_computation.1 | async-start | bytes 393216 | tf_op jit(solution)/shard_map/all_to_all | solution.py:166
  35.2 1.6 %collective-permute-start.5 = (bf16[192,384]{1,0:T(8,128)(2,1)S(1)}, bf16[192,384]{1,0:T(8,128)(2,1)S(1)}, u32[]{:S(2)}, u32[]{:S(2)}) collective-permute-start(bf16[192,384]{1,0:T(8,128)(2,1)S(1)} %collective-permute-done.4.refs_4_), channel_id=1, source_target_pairs={{0,4},{4,0},{8,12},{12,8},{16,20},{20,16},{24,28},{28,24},{1,5},{5... | collective-permute-start | bytes 442376 | tf_op jit(solution)/shard_map/ppermute | solution.py:133
  35.7 1.4 %collective-permute-start.9 = (bf16[192,384]{1,0:T(8,128)(2,1)S(1)}, bf16[192,384]{1,0:T(8,128)(2,1)S(1)}, u32[]{:S(2)}, u32[]{:S(2)}) collective-permute-start(bf16[192,384]{1,0:T(8,128)(2,1)S(1)} %collective-permute-done.8.refs_8_), channel_id=1, source_target_pairs={{0,4},{4,0},{8,12},{12,8},{16,20},{20,16},{24,28},{28,24},{1,5},{5... | collective-permute-start | bytes 442376 | tf_op jit(solution)/shard_map/ppermute | solution.py:133
  35.8 1.5 %collective-permute-start.3 = (bf16[192,384]{1,0:T(8,128)(2,1)S(1)}, bf16[192,384]{1,0:T(8,128)(2,1)S(1)}, u32[]{:S(2)}, u32[]{:S(2)}) collective-permute-start(bf16[192,384]{1,0:T(8,128)(2,1)S(1)} %collective-permute-done.2.refs_2_), channel_id=1, source_target_pairs={{0,4},{4,0},{8,12},{12,8},{16,20},{20,16},{24,28},{28,24},{1,5},{5... | collective-permute-start | bytes 442376 | tf_op jit(solution)/shard_map/ppermute | solution.py:133
  36.2 1.4 %collective-permute-start.7 = (bf16[192,384]{1,0:T(8,128)(2,1)S(1)}, bf16[192,384]{1,0:T(8,128)(2,1)S(1)}, u32[]{:S(2)}, u32[]{:S(2)}) collective-permute-start(bf16[192,384]{1,0:T(8,128)(2,1)S(1)} %collective-permute-done.6.refs_6_), channel_id=1, source_target_pairs={{0,4},{4,0},{8,12},{12,8},{16,20},{20,16},{24,28},{28,24},{1,5},{5... | collective-permute-start | bytes 442376 | tf_op jit(solution)/shard_map/ppermute | solution.py:133
  36.3 1.5 %collective-permute-start.11 = (bf16[192,384]{1,0:T(8,128)(2,1)S(1)}, bf16[192,384]{1,0:T(8,128)(2,1)S(1)}, u32[]{:S(2)}, u32[]{:S(2)}) collective-permute-start(bf16[192,384]{1,0:T(8,128)(2,1)S(1)} %collective-permute-done.10.refs_10_), channel_id=1, source_target_pairs={{0,4},{4,0},{8,12},{12,8},{16,20},{20,16},{24,28},{28,24},{1,5},{5... | collective-permute-start | bytes 442376 | tf_op jit(solution)/shard_map/ppermute | solution.py:133

commit v2 on v1

--- a/solution.py
+++ b/solution.py
@@ -18,22 +18,40 @@
     return pltpu.CompilerParams(vmem_limit_bytes=VMEM_LIMIT)
 
 
-def pack_kernel(query_ref, key_ref, value_ref, packed_ref):
+def pack_kernel(query_ref, key_ref, value_ref, packed_ref, rows, turned, in_sems, out_sems):
     head_size = packed_ref.shape[2]
-    for part, ref in enumerate((query_ref, key_ref, value_ref)):
-        turned = ref[0].T
-        for head in range(HEADS):
-            packed_ref[head, part] = turned[head * head_size : (head + 1) * head_size, :]
+    arrivals = [
+        pltpu.make_async_copy(ref.at[0], rows.at[part], in_sems.at[part])
+        for part, ref in enumerate((query_ref, key_ref, value_ref))
+    ]
+    for copy in arrivals:
+        copy.start()
+    departures = []
+    for part, copy in enumerate(arrivals):
+        copy.wait()
+        turned[:, part] = rows[part].T.reshape(HEADS, head_size, rows.shape[1])
+        copy = pltpu.make_async_copy(turned.at[:, part], packed_ref.at[:, part], out_sems.at[part])
+        copy.start()
+        departures.append(copy)
+    for copy in departures:
+        copy.wait()
 
 
 def pack(queries, key_rows, value_rows):
     _, frames, features = queries.shape
+    packed = (HEADS, 3, features // HEADS, frames)
     return pl.pallas_call(
         pack_kernel,
-        out_shape=jax.ShapeDtypeStruct((HEADS, 3, features // HEADS, frames), queries.dtype),
-        in_specs=[WHOLE] * 3,
-        out_specs=WHOLE,
-        compiler_params=params(),
+        out_shape=jax.ShapeDtypeStruct(packed, queries.dtype),
+        in_specs=[pl.BlockSpec(memory_space=pl.ANY)] * 3,
+        out_specs=pl.BlockSpec(memory_space=pl.ANY),
+        scratch_shapes=[
+            pltpu.VMEM((3, frames, features), queries.dtype),
+            pltpu.VMEM(packed, queries.dtype),
+            pltpu.SemaphoreType.DMA((3,)),
+            pltpu.SemaphoreType.DMA((3,)),
+        ],
+        compiler_params=pltpu.CompilerParams(vmem_limit_bytes=60 * 1024 * 1024),
         name="pack_heads",
     )(queries, key_rows, value_rows)
 
@@ -95,21 +113,18 @@
     pieces = refs[:-1]
     features, columns = own_ref.shape
     shards = out_ref.shape[2] // columns
-    per_shard = len(pieces) // (shards - 1)
-    rows = features // per_shard
+    rows = features // len(pieces)
     own = jnp.dot(turned_ref[...].T, own_ref[...], preferred_element_type=jnp.float32)
     place = pl.multiple_of(places_ref[0] * columns, 128)
     out_ref[0, :, pl.ds(place, columns)] = own.astype(out_ref.dtype)
-    turned = [
-        turned_ref[pl.ds(pl.multiple_of((places_ref[1] ^ e) * rows, 64), rows), :].T for e in range(per_shard)
-    ]
+    foreign = jnp.zeros((out_ref.shape[1], (shards - 1) * columns), jnp.float32)
+    for at, piece in enumerate(pieces):
+        turned = turned_ref[pl.ds(pl.multiple_of((places_ref[1] ^ at) * rows, 32), rows), :].T
+        foreign = foreign + jnp.dot(turned, piece[...], preferred_element_type=jnp.float32)
     for shard in range(1, shards):
-        total = jnp.zeros((out_ref.shape[1], columns), jnp.float32)
-        for e in range(per_shard):
-            piece = pieces[(shard - 1) * per_shard + e]
-            total = total + jnp.dot(turned[e], piece[...], preferred_element_type=jnp.float32)
         place = pl.multiple_of((places_ref[0] ^ shard) * columns, 128)
-        out_ref[0, :, pl.ds(place, columns)] = total.astype(out_ref.dtype)
+        part = foreign[:, (shard - 1) * columns : shard * columns]
+        out_ref[0, :, pl.ds(place, columns)] = part.astype(out_ref.dtype)
 
 
 def project(places, turned, own, pieces, shards):
@@ -133,16 +148,16 @@
     return lax.ppermute(array, axis, [(i, i ^ flip) for i in range(size)])
 
 
-def weight_pieces(out_weight, ctx, fsdp):
-    quarter = lax.axis_index("ctx") % 4
-    rows = out_weight.shape[0] // 4
-    mine = lax.dynamic_slice_in_dim(out_weight, quarter * rows, rows, 0)
-    pieces = []
-    for flip in range(1, fsdp):
-        same = exchange(mine, "fsdp", fsdp, flip)
-        other_chip = exchange(same, "ctx", ctx, 2)
-        pieces += [same, exchange(same, "ctx", ctx, 1), other_chip, exchange(other_chip, "ctx", ctx, 1)]
-    return pieces
+def weight_fetch(out_weight, ctx, fsdp, ways):
+    share = lax.axis_index("ctx") % ways
+    rows = out_weight.shape[0] // ways
+    mine = lax.dynamic_slice_in_dim(out_weight, share * rows, rows, 0)
+    fetched = jnp.concatenate([exchange(mine, "fsdp", fsdp, flip) for flip in range(1, fsdp)], axis=1)
+    return [fetched] + [exchange(fetched, "ctx", ctx, flip) for flip in range(2, ways, 2)]
+
+
+def weight_share(fetched, ctx):
+    return [piece for same in fetched for piece in (same, exchange(same, "ctx", ctx, 1))]
 
 
 def per_device(ctx, fsdp, queries, key_rows, value_rows, lengths, out_weight):
@@ -151,9 +166,9 @@
     swap = functools.partial(
         lax.all_to_all, axis_name="ctx", split_axis=0, concat_axis=0, axis_index_groups=groups, tiled=True
     )
-    split_weight = fsdp in (2, 4) and ctx % 4 == 0
+    split_weight = fsdp in (2, 4) and ctx % HEADS == 0
     if split_weight:
-        pieces = weight_pieces(out_weight, ctx, fsdp)
+        fetched = weight_fetch(out_weight, ctx, fsdp, HEADS)
     else:
         whole_weight = lax.all_gather(out_weight, "fsdp", axis=1, tiled=True)
     by_head = swap(pack(queries, key_rows, value_rows))
@@ -165,7 +180,9 @@
         mixed = attend(lengths, by_head[:, :1], rest, rest, (0, 0, 1))
     turned = swap(mixed).reshape(features, frames)
     if split_weight:
-        places = jnp.stack([lax.axis_index("fsdp"), lax.axis_index("ctx") % 4]).astype(jnp.int32)
+        fetched, _ = lax.optimization_barrier((fetched, mixed))
+        pieces = weight_share(fetched, ctx)
+        places = jnp.stack([lax.axis_index("fsdp"), lax.axis_index("ctx") % HEADS]).astype(jnp.int32)
         return project(places, turned, out_weight, pieces, fsdp)
     return jnp.dot(turned.T, whole_weight, preferred_element_type=jnp.float32).astype(jnp.bfloat16)[None]
 

time: 43.8 us -> 44.5 us (1.016)
  waiting for transfers between devices: 14.4 us -> 17.3 us
  local copies, waits for them, and re-layouts: 2.81 us -> 0.94 us
  starting transfers between devices: 18.8 us -> 17.3 us
  Pallas kernels: 6.62 us -> 7.77 us
    all_to_all x1, waiting for transfers between devices: 0.01 us -> 5.54 us  [per_device(): by_head = swap(pack(queries, key_rows, value_rows))]
    ppermute x12 -> x10, waiting for transfers between devices: 10.8 us -> 5.67 us  [exchange(): return lax.ppermute(array, axis, [(i, i ^ flip) for i in range(size)])]
    unnamed x8 -> x4, local copies, waits for them, and re-layouts: 2.78 us -> 0.03 us
    all_to_all x1, waiting for transfers between devices: 3.62 us -> 6.08 us  [per_device(): turned = swap(mixed).reshape(features, frames)]
    all_to_all x1, starting transfers between devices: 5.3 us -> 3.74 us  [per_device(): by_head = swap(pack(queries, key_rows, value_rows))]
    pallas_call x1, Pallas kernels: 1.03 us -> 1.97 us  [pack(): pl.pallas_call(pack_kernel, out_shape=jax.ShapeDtypeStruct(packed, querie...]
    dynamic_slice x1, local copies, waits for them, and re-layouts: 0.02 us -> 0.89 us  [weight_fetch(): mine = lax.dynamic_slice_in_dim(out_weight, share * rows, rows, 0)]
    ppermute x12 -> x10, starting transfers between devices: 9.37 us -> 10.2 us  [exchange(): return lax.ppermute(array, axis, [(i, i ^ flip) for i in range(size)])]
  transfers between devices with their start and end apart: 14 -> 12, of which waited for: 7 -> 5; matrix products, arithmetic and copies ran while one was open for 0% -> 0% of each run, Pallas kernels for 8% -> 13%
where the time goes in v2:
time: 44.5 us; the launch traced here: 44.1 us
  starting transfers between devices  17.3 us (39%)
  waiting for transfers between devices  17.3 us (39%)
  Pallas kernels  7.77 us (17%)
  local copies, waits for them, and re-layouts  0.94 us (2%)
  between operations  0.73 us (2%)
    ppermute x10, starting transfers between devices, exchange(): return lax.ppermute(array, axis, [(i, i ^ flip) for i in range(size)])  10.2 us
    all_to_all x1, waiting for transfers between devices, per_device(): turned = swap(mixed).reshape(features, frames)  6.08 us
    ppermute x10, waiting for transfers between devices, exchange(): return lax.ppermute(array, axis, [(i, i ^ flip) for i in range(size)])  5.67 us
    all_to_all x1, waiting for transfers between devices, per_device(): by_head = swap(pack(queries, key_rows, value_rows))  5.54 us
    all_to_all x1, starting transfers between devices, per_device(): by_head = swap(pack(queries, key_rows, value_rows))  3.74 us
    pallas_call x1, Pallas kernels, attend(): pl.pallas_call(functools.partial(attention_kernel, chunk_blocks), grid=(1...  3.59 us
    all_to_all x1, starting transfers between devices, per_device(): turned = swap(mixed).reshape(features, frames)  3.39 us
    pallas_call x1, Pallas kernels, project(): pl.pallas_call(project_kernel, out_shape=jax.ShapeDtypeStruct((1, frames,...  2.21 us
  transfers between devices with their start and end apart: 12, of which 5 were waited for; matrix products, arithmetic and copies ran while one was open for 0% of the time, Pallas kernels for 13%

profile of v2, /device:TPU:0, one launch (start us, length us, event | category | flops | bytes accessed | tf_op | source)
XLA Modules:
  0.0 44.1 jit_solution(4519845505350340685)
XLA Ops:
  0.0 0.9 %constant_dynamic-slice_fusion = bf16[96,384]{1,0:T(8,128)(2,1)S(1)} fusion(bf16[768,384]{1,0:T(8,128)(2,1)} %own_ref.1, s32[]{:T(128)S(6)} %select_n.13), kind=kLoop, calls=%fused_computation.4 | loop fusion | bytes 147460 | tf_op jit(solution)/shard_map/dynamic_slice | solution.py:154
  0.9 3.0 %collective-permute-start = (bf16[96,384]{1,0:T(8,128)(2,1)S(1)}, bf16[96,384]{1,0:T(8,128)(2,1)S(1)}, u32[]{:S(2)}, u32[]{:S(2)}) collective-permute-start(bf16[96,384]{1,0:T(8,128)(2,1)S(1)} %constant_dynamic-slice_fusion), channel_id=1, source_target_pairs={{0,1},{1,0},{2,3},{3,2},{4,5},{5,4},{6,7},{7,6},{8,9},{9,8},{10,11... | collective-permute-start | bytes 221192 | tf_op jit(solution)/shard_map/ppermute | solution.py:148
  3.9 2.5 %collective-permute-start.2 = (bf16[96,384]{1,0:T(8,128)(2,1)S(1)}, bf16[96,384]{1,0:T(8,128)(2,1)S(1)}, u32[]{:S(2)}, u32[]{:S(2)}) collective-permute-start(bf16[96,384]{1,0:T(8,128)(2,1)S(1)} %constant_dynamic-slice_fusion), channel_id=1, source_target_pairs={{0,3},{1,2},{2,1},{3,0},{4,7},{5,6},{6,5},{7,4},{8,11},{9,10},{10,... | collective-permute-start | bytes 221192 | tf_op jit(solution)/shard_map/ppermute | solution.py:148
  6.4 0.1 collective-permute-start.1
  6.5 2.0 %pack_heads.1 = bf16[8,3,96,128]{3,2,1,0:T(8,128)(2,1)} custom-call(bf16[1,128,768]{2,1,0:T(8,128)(2,1)} %query_ref.1, bf16[1,128,768]{2,1,0:T(8,128)(2,1)} %key_ref.1, bf16[1,128,768]{2,1,0:T(8,128)(2,1)} %value_ref.1), custom_call_target="tpu_custom_call" | custom-call | tf_op jit(solution)/shard_map/pack_heads/pallas_call | solution.py:43
  8.5 3.7 %all-to-all-start = ((bf16[8,3,96,128]{3,2,1,0:T(8,128)(2,1)}), bf16[8,3,96,128]{3,2,1,0:T(8,128)(2,1)S(1)}, u32[]{:S(2)}, u32[]{:S(2)}) async-start(bf16[8,3,96,128]{3,2,1,0:T(8,128)(2,1)} %pack_heads.1), calls=%async_computation | async-start | bytes 1179648 | tf_op jit(solution)/shard_map/all_to_all | solution.py:174
  12.2 0.0 collective-permute-done
  12.3 1.2 %collective-permute-done.1 = bf16[96,384]{1,0:T(8,128)(2,1)S(1)} collective-permute-done((bf16[96,384]{1,0:T(8,128)(2,1)S(1)}, bf16[96,384]{1,0:T(8,128)(2,1)S(1)}, u32[]{:S(2)}, u32[]{:S(2)}) %collective-permute-start.1) | collective-permute-done | bytes 73760 | tf_op jit(solution)/shard_map/ppermute | solution.py:148
  13.5 0.0 collective-permute-done.2
  13.5 2.5 %collective-permute-start.5 = (bf16[96,1152]{1,0:T(8,128)(2,1)S(1)}, bf16[96,1152]{1,0:T(8,128)(2,1)S(1)}, u32[]{:S(2)}, u32[]{:S(2)}) collective-permute-start(bf16[96,1152]{1,0:T(8,128)(2,1)S(1)} %constant_dynamic-update-slice_fusion.refs_0_), channel_id=1, source_target_pairs={{0,24},{4,28},{8,16},{12,20},{16,8},{20,12},{24,0},{28,4},{1,25},{... | collective-permute-start | bytes 663560 | tf_op jit(solution)/shard_map/ppermute | solution.py:148
  16.0 0.5 %collective-permute-start.4 = (bf16[96,1152]{1,0:T(8,128)(2,1)S(1)}, bf16[96,1152]{1,0:T(8,128)(2,1)S(1)}, u32[]{:S(2)}, u32[]{:S(2)}) collective-permute-start(bf16[96,1152]{1,0:T(8,128)(2,1)S(1)} %constant_dynamic-update-slice_fusion.refs_0_), channel_id=1, source_target_pairs={{0,16},{4,20},{8,24},{12,28},{16,0},{20,4},{24,8},{28,12},{1,17},{... | collective-permute-start | bytes 663560 | tf_op jit(solution)/shard_map/ppermute | solution.py:148
  16.5 0.5 %collective-permute-start.3 = (bf16[96,1152]{1,0:T(8,128)(2,1)S(1)}, bf16[96,1152]{1,0:T(8,128)(2,1)S(1)}, u32[]{:S(2)}, u32[]{:S(2)}) collective-permute-start(bf16[96,1152]{1,0:T(8,128)(2,1)S(1)} %constant_dynamic-update-slice_fusion.refs_0_), channel_id=1, source_target_pairs={{0,8},{4,12},{8,0},{12,4},{16,24},{20,28},{24,16},{28,20},{1,9},{5... | collective-permute-start | bytes 663560 | tf_op jit(solution)/shard_map/ppermute | solution.py:148
  17.7 5.5 %all-to-all-done.query_ref.key_ref.value_ref = bf16[8,3,96,128]{3,2,1,0:T(8,128)(2,1)S(1)} async-done(((bf16[8,3,96,128]{3,2,1,0:T(8,128)(2,1)}), bf16[8,3,96,128]{3,2,1,0:T(8,128)(2,1)S(1)}, u32[]{:S(2)}, u32[]{:S(2)}) %all-to-all-start) | async-done | bytes 589856 | tf_op jit(solution)/shard_map/all_to_all | solution.py:174
  23.3 0.0 copy-start
  23.3 3.6 %attend_one_head.1 = bf16[8,96,128]{2,1,0:T(8,128)(2,1)} custom-call(s32[1]{0:T(128)S(6)} %copy.8.lengths_ref, bf16[8,3,96,128]{3,2,1,0:T(8,128)(2,1)S(1)} %all-to-all-done.query_ref.key_ref.value_ref, bf16[8,3,96,128]{3,2,1,0:T(8,128)(2,1)S(1)} %all-to-all-done.query_ref.key_ref.value_ref, bf16[8,3,96,128]{3,2,1,0:T(8,128)(2,1)S(1)} %all-to-all-done.query_ref.key_ref.value_ref), custom_call_target="tpu_custom_call" | custom-call | flops 402653184 | bytes 786432 | tf_op jit(solution)/shard_map/attend_one_head/pallas_call | solution.py:91
  26.8 1.1 %collective-permute-done.5.refs_6_ = bf16[96,1152]{1,0:T(8,128)(2,1)S(1)} collective-permute-done((bf16[96,1152]{1,0:T(8,128)(2,1)S(1)}, bf16[96,1152]{1,0:T(8,128)(2,1)S(1)}, u32[]{:S(2)}, u32[]{:S(2)}) %collective-permute-start.5) | collective-permute-done | bytes 221216 | tf_op jit(solution)/shard_map/ppermute | solution.py:148
  27.9 3.3 %collective-permute-done.4.refs_4_ = bf16[96,1152]{1,0:T(8,128)(2,1)S(1)} collective-permute-done((bf16[96,1152]{1,0:T(8,128)(2,1)S(1)}, bf16[96,1152]{1,0:T(8,128)(2,1)S(1)}, u32[]{:S(2)}, u32[]{:S(2)}) %collective-permute-start.4) | collective-permute-done | bytes 221216 | tf_op jit(solution)/shard_map/ppermute | solution.py:148
  31.3 0.0 collective-permute-done.3.refs_2_
  31.3 0.0 collective-permute-start.6
  31.3 0.5 %collective-permute-start.7 = (bf16[96,1152]{1,0:T(8,128)(2,1)S(1)}, bf16[96,1152]{1,0:T(8,128)(2,1)S(1)}, u32[]{:S(2)}, u32[]{:S(2)}) collective-permute-start(bf16[96,1152]{1,0:T(8,128)(2,1)S(1)} %collective-permute-done.3.refs_2_), channel_id=1, source_target_pairs={{0,4},{4,0},{8,12},{12,8},{16,20},{20,16},{24,28},{28,24},{1,5},{5... | collective-permute-start | bytes 663560 | tf_op jit(solution)/shard_map/ppermute | solution.py:148
  31.8 0.0 collective-permute-start.8
  31.8 0.5 %collective-permute-start.9 = (bf16[96,1152]{1,0:T(8,128)(2,1)S(1)}, bf16[96,1152]{1,0:T(8,128)(2,1)S(1)}, u32[]{:S(2)}, u32[]{:S(2)}) collective-permute-start(bf16[96,1152]{1,0:T(8,128)(2,1)S(1)} %collective-permute-done.5.refs_6_), channel_id=1, source_target_pairs={{0,4},{4,0},{8,12},{12,8},{16,20},{20,16},{24,28},{28,24},{1,5},{5... | collective-permute-start | bytes 663560 | tf_op jit(solution)/shard_map/ppermute | solution.py:148
  32.3 3.4 %all-to-all-start.1 = ((bf16[8,96,128]{2,1,0:T(8,128)(2,1)}), bf16[8,96,128]{2,1,0:T(8,128)(2,1)S(1)}, u32[]{:S(2)}, u32[]{:S(2)}) async-start(bf16[8,96,128]{2,1,0:T(8,128)(2,1)} %attend_one_head.1), calls=%async_computation.1 | async-start | bytes 393216 | tf_op jit(solution)/shard_map/all_to_all | solution.py:181
  35.7 0.1 pad_add_fusion.places_ref
  35.8 6.1 %all-to-all-done.1 = bf16[8,96,128]{2,1,0:T(8,128)(2,1)S(1)} async-done(((bf16[8,96,128]{2,1,0:T(8,128)(2,1)}), bf16[8,96,128]{2,1,0:T(8,128)(2,1)S(1)}, u32[]{:S(2)}, u32[]{:S(2)}) %all-to-all-start.1) | async-done | bytes 196640 | tf_op jit(solution)/shard_map/all_to_all | solution.py:181
  41.9 0.0 collective-permute-done.6.refs_1_
  41.9 0.0 collective-permute-done.7.refs_3_
  41.9 0.0 collective-permute-done.8.refs_5_
  41.9 0.0 collective-permute-done.9.refs_7_
  41.9 0.0 copy-done
  41.9 2.2 %project_pieces.1 = bf16[1,128,1536]{2,1,0:T(8,128)(2,1)} custom-call(s32[2]{0:T(128)S(1)} %pad_add_fusion.places_ref, bf16[768,128]{1,0:T(8,128)(2,1)S(1)} %bitcast.3, bf16[768,384]{1,0:T(8,128)(2,1)S(1)} %copy-done, bf16[96,1152]{1,0:T(8,128)(2,1)S(1)} %constant_dynamic-update-slice_fusion.refs_0_, bf16[96,1152]{1,0:T(8,128)(2,1)S(1)} %collective-permute-done.6.refs_1_, ...), custom_call_target="tpu_custom_call" | custom-call | flops 301989888 | bytes 2359296 | tf_op jit(solution)/shard_map/project_pieces/pallas_call | solution.py:132
  (3 shorter events, 0.0 us)
Async XLA Ops:
  0.9 11.3 %collective-permute-start = (bf16[96,384]{1,0:T(8,128)(2,1)S(1)}, bf16[96,384]{1,0:T(8,128)(2,1)S(1)}, u32[]{:S(2)}, u32[]{:S(2)}) collective-permute-start(bf16[96,384]{1,0:T(8,128)(2,1)S(1)} %constant_dynamic-slice_fusion), channel_id=1, source_target_pairs={{0,1},{1,0},{2,3},{3,2},{4,5},{5,4},{6,7},{7,6},{8,9},{9,8},{10,11... | collective-permute-start | bytes 221192 | tf_op jit(solution)/shard_map/ppermute | solution.py:148
  3.9 9.6 %collective-permute-start.2 = (bf16[96,384]{1,0:T(8,128)(2,1)S(1)}, bf16[96,384]{1,0:T(8,128)(2,1)S(1)}, u32[]{:S(2)}, u32[]{:S(2)}) collective-permute-start(bf16[96,384]{1,0:T(8,128)(2,1)S(1)} %constant_dynamic-slice_fusion), channel_id=1, source_target_pairs={{0,3},{1,2},{2,1},{3,0},{4,7},{5,6},{6,5},{7,4},{8,11},{9,10},{10,... | collective-permute-start | bytes 221192 | tf_op jit(solution)/shard_map/ppermute | solution.py:148
  6.4 7.1 %collective-permute-start.1 = (bf16[96,384]{1,0:T(8,128)(2,1)S(1)}, bf16[96,384]{1,0:T(8,128)(2,1)S(1)}, u32[]{:S(2)}, u32[]{:S(2)}) collective-permute-start(bf16[96,384]{1,0:T(8,128)(2,1)S(1)} %constant_dynamic-slice_fusion), channel_id=1, source_target_pairs={{0,2},{1,3},{2,0},{3,1},{4,6},{5,7},{6,4},{7,5},{8,10},{9,11},{10,... | collective-permute-start | bytes 221192 | tf_op jit(solution)/shard_map/ppermute | solution.py:148
  8.5 14.8 %all-to-all-start = ((bf16[8,3,96,128]{3,2,1,0:T(8,128)(2,1)}), bf16[8,3,96,128]{3,2,1,0:T(8,128)(2,1)S(1)}, u32[]{:S(2)}, u32[]{:S(2)}) async-start(bf16[8,3,96,128]{3,2,1,0:T(8,128)(2,1)} %pack_heads.1), calls=%async_computation | async-start | bytes 1179648 | tf_op jit(solution)/shard_map/all_to_all | solution.py:174
  13.5 14.4 %collective-permute-start.5 = (bf16[96,1152]{1,0:T(8,128)(2,1)S(1)}, bf16[96,1152]{1,0:T(8,128)(2,1)S(1)}, u32[]{:S(2)}, u32[]{:S(2)}) collective-permute-start(bf16[96,1152]{1,0:T(8,128)(2,1)S(1)} %constant_dynamic-update-slice_fusion.refs_0_), channel_id=1, source_target_pairs={{0,24},{4,28},{8,16},{12,20},{16,8},{20,12},{24,0},{28,4},{1,25},{... | collective-permute-start | bytes 663560 | tf_op jit(solution)/shard_map/ppermute | solution.py:148
  16.0 15.2 %collective-permute-start.4 = (bf16[96,1152]{1,0:T(8,128)(2,1)S(1)}, bf16[96,1152]{1,0:T(8,128)(2,1)S(1)}, u32[]{:S(2)}, u32[]{:S(2)}) collective-permute-start(bf16[96,1152]{1,0:T(8,128)(2,1)S(1)} %constant_dynamic-update-slice_fusion.refs_0_), channel_id=1, source_target_pairs={{0,16},{4,20},{8,24},{12,28},{16,0},{20,4},{24,8},{28,12},{1,17},{... | collective-permute-start | bytes 663560 | tf_op jit(solution)/shard_map/ppermute | solution.py:148
  16.5 14.8 %collective-permute-start.3 = (bf16[96,1152]{1,0:T(8,128)(2,1)S(1)}, bf16[96,1152]{1,0:T(8,128)(2,1)S(1)}, u32[]{:S(2)}, u32[]{:S(2)}) collective-permute-start(bf16[96,1152]{1,0:T(8,128)(2,1)S(1)} %constant_dynamic-update-slice_fusion.refs_0_), channel_id=1, source_target_pairs={{0,8},{4,12},{8,0},{12,4},{16,24},{20,28},{24,16},{28,20},{1,9},{5... | collective-permute-start | bytes 663560 | tf_op jit(solution)/shard_map/ppermute | solution.py:148
  23.3 18.7 %copy-start = (bf16[768,384]{1,0:T(8,128)(2,1)S(1)}, bf16[768,384]{1,0:T(8,128)(2,1)}, u32[]{:S(2)}) copy-start(bf16[768,384]{1,0:T(8,128)(2,1)} %own_ref.1) | copy-start | bytes 1769476
  31.3 10.6 %collective-permute-start.6 = (bf16[96,1152]{1,0:T(8,128)(2,1)S(1)}, bf16[96,1152]{1,0:T(8,128)(2,1)S(1)}, u32[]{:S(2)}, u32[]{:S(2)}) collective-permute-start(bf16[96,1152]{1,0:T(8,128)(2,1)S(1)} %constant_dynamic-update-slice_fusion.refs_0_), channel_id=1, source_target_pairs={{0,4},{4,0},{8,12},{12,8},{16,20},{20,16},{24,28},{28,24},{1,5},{5... | collective-permute-start | bytes 663560 | tf_op jit(solution)/shard_map/ppermute | solution.py:148
  31.3 10.6 %collective-permute-start.7 = (bf16[96,1152]{1,0:T(8,128)(2,1)S(1)}, bf16[96,1152]{1,0:T(8,128)(2,1)S(1)}, u32[]{:S(2)}, u32[]{:S(2)}) collective-permute-start(bf16[96,1152]{1,0:T(8,128)(2,1)S(1)} %collective-permute-done.3.refs_2_), channel_id=1, source_target_pairs={{0,4},{4,0},{8,12},{12,8},{16,20},{20,16},{24,28},{28,24},{1,5},{5... | collective-permute-start | bytes 663560 | tf_op jit(solution)/shard_map/ppermute | solution.py:148
  31.8 10.1 %collective-permute-start.8 = (bf16[96,1152]{1,0:T(8,128)(2,1)S(1)}, bf16[96,1152]{1,0:T(8,128)(2,1)S(1)}, u32[]{:S(2)}, u32[]{:S(2)}) collective-permute-start(bf16[96,1152]{1,0:T(8,128)(2,1)S(1)} %collective-permute-done.4.refs_4_), channel_id=1, source_target_pairs={{0,4},{4,0},{8,12},{12,8},{16,20},{20,16},{24,28},{28,24},{1,5},{5... | collective-permute-start | bytes 663560 | tf_op jit(solution)/shard_map/ppermute | solution.py:148
  31.8 10.1 %collective-permute-start.9 = (bf16[96,1152]{1,0:T(8,128)(2,1)S(1)}, bf16[96,1152]{1,0:T(8,128)(2,1)S(1)}, u32[]{:S(2)}, u32[]{:S(2)}) collective-permute-start(bf16[96,1152]{1,0:T(8,128)(2,1)S(1)} %collective-permute-done.5.refs_6_), channel_id=1, source_target_pairs={{0,4},{4,0},{8,12},{12,8},{16,20},{20,16},{24,28},{28,24},{1,5},{5... | collective-permute-start | bytes 663560 | tf_op jit(solution)/shard_map/ppermute | solution.py:148
  32.3 9.6 %all-to-all-start.1 = ((bf16[8,96,128]{2,1,0:T(8,128)(2,1)}), bf16[8,96,128]{2,1,0:T(8,128)(2,1)S(1)}, u32[]{:S(2)}, u32[]{:S(2)}) async-start(bf16[8,96,128]{2,1,0:T(8,128)(2,1)} %attend_one_head.1), calls=%async_computation.1 | async-start | bytes 393216 | tf_op jit(solution)/shard_map/all_to_all | solution.py:181

commit v3 on v2

--- a/solution.py
+++ b/solution.py
@@ -108,69 +108,48 @@
     )(lengths, query, key, value)
 
 
-def project_kernel(places_ref, turned_ref, own_ref, *refs):
-    out_ref = refs[-1]
-    pieces = refs[:-1]
-    features, columns = own_ref.shape
-    shards = out_ref.shape[2] // columns
-    rows = features // len(pieces)
-    own = jnp.dot(turned_ref[...].T, own_ref[...], preferred_element_type=jnp.float32)
-    place = pl.multiple_of(places_ref[0] * columns, 128)
-    out_ref[0, :, pl.ds(place, columns)] = own.astype(out_ref.dtype)
-    foreign = jnp.zeros((out_ref.shape[1], (shards - 1) * columns), jnp.float32)
-    for at, piece in enumerate(pieces):
-        turned = turned_ref[pl.ds(pl.multiple_of((places_ref[1] ^ at) * rows, 32), rows), :].T
-        foreign = foreign + jnp.dot(turned, piece[...], preferred_element_type=jnp.float32)
-    for shard in range(1, shards):
-        place = pl.multiple_of((places_ref[0] ^ shard) * columns, 128)
-        part = foreign[:, (shard - 1) * columns : shard * columns]
-        out_ref[0, :, pl.ds(place, columns)] = part.astype(out_ref.dtype)
+def project_kernel(place_ref, turned_ref, near_ref, far_ref, out_ref):
+    rows = near_ref.shape[0]
+    total = jnp.zeros(out_ref.shape[1:], jnp.float32)
+    for flip, ref in enumerate((near_ref, far_ref)):
+        turned = turned_ref[pl.ds(pl.multiple_of((place_ref[0] ^ flip) * rows, rows), rows), :].T
+        total = total + jnp.dot(turned, ref[...], preferred_element_type=jnp.float32)
+    out_ref[0] = total.astype(out_ref.dtype)
 
 
-def project(places, turned, own, pieces, shards):
+def project(place, turned, near, far):
     features, frames = turned.shape
+    width = near.shape[1]
     return pl.pallas_call(
         project_kernel,
-        out_shape=jax.ShapeDtypeStruct((1, frames, shards * own.shape[1]), jnp.bfloat16),
-        in_specs=[SCALARS] + [WHOLE] * (2 + len(pieces)),
+        out_shape=jax.ShapeDtypeStruct((1, frames, width), jnp.bfloat16),
+        in_specs=[SCALARS] + [WHOLE] * 3,
         out_specs=WHOLE,
         compiler_params=params(),
         cost_estimate=pl.CostEstimate(
-            flops=2 * features * frames * shards * own.shape[1],
-            bytes_accessed=2 * features * shards * own.shape[1],
-            transcendentals=0,
+            flops=2 * features * frames * width, bytes_accessed=2 * features * width, transcendentals=0
         ),
-        name="project_pieces",
-    )(places, turned, own, *pieces)
+        name="project_halves",
+    )(place, turned, near, far)
 
 
 def exchange(array, axis, size, flip):
     return lax.ppermute(array, axis, [(i, i ^ flip) for i in range(size)])
 
 
-def weight_fetch(out_weight, ctx, fsdp, ways):
-    share = lax.axis_index("ctx") % ways
-    rows = out_weight.shape[0] // ways
-    mine = lax.dynamic_slice_in_dim(out_weight, share * rows, rows, 0)
-    fetched = jnp.concatenate([exchange(mine, "fsdp", fsdp, flip) for flip in range(1, fsdp)], axis=1)
-    return [fetched] + [exchange(fetched, "ctx", ctx, flip) for flip in range(2, ways, 2)]
+def weight_half(out_weight):
+    rows = out_weight.shape[0] // 2
+    mine = lax.dynamic_slice_in_dim(out_weight, lax.axis_index("ctx") % 2 * rows, rows, 0)
+    return lax.all_gather(mine, "fsdp", axis=1, tiled=True)
 
 
-def weight_share(fetched, ctx):
-    return [piece for same in fetched for piece in (same, exchange(same, "ctx", ctx, 1))]
-
-
-def per_device(ctx, fsdp, queries, key_rows, value_rows, lengths, out_weight):
+def per_device(ctx, queries, key_rows, value_rows, lengths, out_weight):
     _, frames, features = queries.shape
     groups = [[first + at for at in range(HEADS)] for first in range(0, ctx, HEADS)]
     swap = functools.partial(
         lax.all_to_all, axis_name="ctx", split_axis=0, concat_axis=0, axis_index_groups=groups, tiled=True
     )
-    split_weight = fsdp in (2, 4) and ctx % HEADS == 0
-    if split_weight:
-        fetched = weight_fetch(out_weight, ctx, fsdp, HEADS)
-    else:
-        whole_weight = lax.all_gather(out_weight, "fsdp", axis=1, tiled=True)
+    near = weight_half(out_weight)
     by_head = swap(pack(queries, key_rows, value_rows))
     if ctx == HEADS:
         mixed = attend(lengths, by_head, by_head, by_head, (0, 1, 2))
@@ -179,17 +158,15 @@
         rest = lax.all_gather(by_head[:, 1:], "ctx", axis=0, axis_index_groups=across, tiled=True)
         mixed = attend(lengths, by_head[:, :1], rest, rest, (0, 0, 1))
     turned = swap(mixed).reshape(features, frames)
-    if split_weight:
-        fetched, _ = lax.optimization_barrier((fetched, mixed))
-        pieces = weight_share(fetched, ctx)
-        places = jnp.stack([lax.axis_index("fsdp"), lax.axis_index("ctx") % HEADS]).astype(jnp.int32)
-        return project(places, turned, out_weight, pieces, fsdp)
-    return jnp.dot(turned.T, whole_weight, preferred_element_type=jnp.float32).astype(jnp.bfloat16)[None]
+    near, turned = lax.optimization_barrier((near, turned))
+    far = exchange(near, "ctx", ctx, 1)
+    place = (lax.axis_index("ctx") % 2).astype(jnp.int32).reshape(1)
+    return project(place, turned, near, far)
 
 
 def solution(mesh):
     return jax.shard_map(
-        functools.partial(per_device, mesh.shape["ctx"], mesh.shape["fsdp"]),
+        functools.partial(per_device, mesh.shape["ctx"]),
         mesh=mesh,
         in_specs=(
             P("fsdp", "ctx", None),

time: 44.5 us -> 54.7 us (1.23)
  between operations: 0.73 us -> 14.1 us
  starting transfers between devices: 17.3 us -> 5.19 us
  blocking collectives: 0 us -> 8.63 us
  local copies, waits for them, and re-layouts: 0.94 us -> 3.08 us
  Pallas kernels: 7.77 us -> 6.25 us
    ppermute x10 -> x1, starting transfers between devices: 10.2 us -> 0.01 us  [exchange(): return lax.ppermute(array, axis, [(i, i ^ flip) for i in range(size)])]
    all_to_all x0 -> x1, blocking collectives: none -> 8.63 us  [per_device(): turned = swap(mixed).reshape(features, frames)]
    all_to_all x1 -> x0, waiting for transfers between devices: 6.08 us -> none  [per_device(): turned = swap(mixed).reshape(features, frames)]
    all_gather x0 -> x1, waiting for transfers between devices: none -> 4.26 us  [weight_half(): return lax.all_gather(mine, 'fsdp', axis=1, tiled=True)]
    all_to_all x1, waiting for transfers between devices: 5.54 us -> 9.8 us  [per_device(): by_head = swap(pack(queries, key_rows, value_rows))]
    all_to_all x1 -> x0, starting transfers between devices: 3.39 us -> none  [per_device(): turned = swap(mixed).reshape(features, frames)]
    ppermute x10 -> x1, waiting for transfers between devices: 5.67 us -> 3.06 us  [exchange(): return lax.ppermute(array, axis, [(i, i ^ flip) for i in range(size)])]
    unnamed x4, local copies, waits for them, and re-layouts: 0.03 us -> 2.33 us
  transfers between devices with their start and end apart: 12 -> 3, of which waited for: 5 -> 3; matrix products, arithmetic and copies ran while one was open for 0% -> 0% of each run, Pallas kernels for 13% -> 9%
where the time goes in v3:
time: 54.7 us; the launch traced here: 54.3 us
  waiting for transfers between devices  17.1 us (31%)
  between operations  14.1 us (26%)
  blocking collectives  8.63 us (16%)
  Pallas kernels  6.25 us (11%)
  starting transfers between devices  5.19 us (9%)
  local copies, waits for them, and re-layouts  3.08 us (6%)
    all_to_all x1, waiting for transfers between devices, per_device(): by_head = swap(pack(queries, key_rows, value_rows))  9.8 us
    all_to_all x1, blocking collectives, per_device(): turned = swap(mixed).reshape(features, frames)  8.63 us
    all_to_all x1, starting transfers between devices, per_device(): by_head = swap(pack(queries, key_rows, value_rows))  5.18 us
    all_gather x1, waiting for transfers between devices, weight_half(): return lax.all_gather(mine, 'fsdp', axis=1, tiled=True)  4.26 us
    ppermute x1, waiting for transfers between devices, exchange(): return lax.ppermute(array, axis, [(i, i ^ flip) for i in range(size)])  3.06 us
    pallas_call x1, Pallas kernels, attend(): pl.pallas_call(functools.partial(attention_kernel, chunk_blocks), grid=(1...  2.91 us
    unnamed x4, local copies, waits for them, and re-layouts  2.33 us
    pallas_call x1, Pallas kernels, pack(): pl.pallas_call(pack_kernel, out_shape=jax.ShapeDtypeStruct(packed, querie...  1.99 us
  transfers between devices with their start and end apart: 3, of which 3 were waited for; matrix products, arithmetic and copies ran while one was open for 0% of the time, Pallas kernels for 9%

profile of v3, /device:TPU:0, one launch (start us, length us, event | category | flops | bytes accessed | tf_op | source)
XLA Modules:
  0.0 54.3 jit_solution(18031511466369470604)
XLA Ops:
  6.5 0.0 copy-start
  6.5 0.0 all-gather.2.cloned.1.call-start
  6.5 1.1 %copy-done = bf16[768,384]{1,0:T(8,128)(2,1)S(1)} copy-done((bf16[768,384]{1,0:T(8,128)(2,1)S(1)}, bf16[768,384]{1,0:T(8,128)(2,1)}, u32[]{:S(2)}) %copy-start) | copy-done | bytes 589848
  7.6 0.7 %constant_dynamic-slice_fusion = bf16[384,384]{1,0:T(8,128)(2,1)} fusion(bf16[768,384]{1,0:T(8,128)(2,1)S(1)} %copy-done, s32[]{:T(128)S(6)} %select_n.13), kind=kLoop, calls=%fused_computation | loop fusion | bytes 589828 | tf_op jit(solution)/shard_map/dynamic_slice | solution.py:142
  8.3 0.0 all-gather.2.cloned.1.call-update
  8.4 2.0 %pack_heads.1 = bf16[8,3,96,128]{3,2,1,0:T(8,128)(2,1)} custom-call(bf16[1,128,768]{2,1,0:T(8,128)(2,1)} %query_ref.1, bf16[1,128,768]{2,1,0:T(8,128)(2,1)} %key_ref.1, bf16[1,128,768]{2,1,0:T(8,128)(2,1)} %value_ref.1), custom_call_target="tpu_custom_call" | custom-call | tf_op jit(solution)/shard_map/pack_heads/pallas_call | solution.py:43
  10.4 5.2 %all-to-all-start = ((bf16[8,3,96,128]{3,2,1,0:T(8,128)(2,1)}), bf16[8,3,96,128]{3,2,1,0:T(8,128)(2,1)S(1)}, u32[]{:S(2)}, u32[]{:S(2)}) async-start(bf16[8,3,96,128]{3,2,1,0:T(8,128)(2,1)} %pack_heads.1), calls=%async_computation | async-start | bytes 1179648 | tf_op jit(solution)/shard_map/all_to_all | solution.py:153
  16.2 9.8 %all-to-all-done.query_ref.key_ref.value_ref = bf16[8,3,96,128]{3,2,1,0:T(8,128)(2,1)S(1)} async-done(((bf16[8,3,96,128]{3,2,1,0:T(8,128)(2,1)}), bf16[8,3,96,128]{3,2,1,0:T(8,128)(2,1)S(1)}, u32[]{:S(2)}, u32[]{:S(2)}) %all-to-all-start) | async-done | bytes 589856 | tf_op jit(solution)/shard_map/all_to_all | solution.py:153
  26.0 2.9 %attend_one_head.1 = bf16[8,96,128]{2,1,0:T(8,128)(2,1)S(1)} custom-call(s32[1]{0:T(128)S(6)} %copy.6.lengths_ref, bf16[8,3,96,128]{3,2,1,0:T(8,128)(2,1)S(1)} %all-to-all-done.query_ref.key_ref.value_ref, bf16[8,3,96,128]{3,2,1,0:T(8,128)(2,1)S(1)} %all-to-all-done.query_ref.key_ref.value_ref, ...), custom_call_target="tpu_custom_call" | custom-call | flops 402653184 | bytes 786432 | tf_op jit(solution)/shard_map/attend_one_head/pallas_call | solution.py:91
  28.9 8.6 %all_to_all.10 = bf16[8,96,128]{2,1,0:T(8,128)(2,1)S(1)} all-to-all(bf16[8,96,128]{2,1,0:T(8,128)(2,1)S(1)} %attend_one_head.1), channel_id=1, replica_groups={{0,4,8,12,16,20,24,28},{1,5,9,13,17,21,25,29},{2,6,10,14,18,22,26,30},{..., dimensions={0} | all-to-all | bytes 393216 | tf_op jit(solution)/shard_map/all_to_all | solution.py:160
  37.5 4.3 %all-gather.2.cloned.1.call-done.near_ref = bf16[384,1536]{1,0:T(8,128)(2,1)} async-done(((bf16[384,384]{1,0:T(8,128)(2,1)}), bf16[384,1536]{1,0:T(8,128)(2,1)}) %all-gather.2.cloned.1.call-update) | async-done | bytes 1179664 | tf_op jit(solution)/shard_map/all_gather | solution.py:143
  41.8 0.0 collective-permute-start
  41.8 3.1 %collective-permute-done.far_ref = bf16[384,1536]{1,0:T(8,128)(2,1)S(1)} collective-permute-done((bf16[384,1536]{1,0:T(8,128)(2,1)}, bf16[384,1536]{1,0:T(8,128)(2,1)S(1)}, u32[]{:S(2)}, u32[]{:S(2)}) %collective-permute-start) | collective-permute-done | bytes 1179680 | tf_op jit(solution)/shard_map/ppermute | solution.py:137
  44.9 0.0 copy-start.1
  44.9 1.3 %copy-done.1 = bf16[384,1536]{1,0:T(8,128)(2,1)S(1)} copy-done((bf16[384,1536]{1,0:T(8,128)(2,1)S(1)}, bf16[384,1536]{1,0:T(8,128)(2,1)}, u32[]{:S(2)}) %copy-start.1) | copy-done | bytes 1179672
  46.1 1.4 %project_halves.1 = bf16[1,128,1536]{2,1,0:T(8,128)(2,1)} custom-call(s32[1]{0:T(128)} %bitcast.place_ref, bf16[768,128]{1,0:T(8,128)(2,1)S(1)} %bitcast.2, bf16[384,1536]{1,0:T(8,128)(2,1)S(1)} %copy-done.1, bf16[384,1536]{1,0:T(8,128)(2,1)S(1)} %collective-permute-done.far_ref), custom_call_target="tpu_custom_call" | custom-call | flops 301989888 | bytes 2359296 | tf_op jit(solution)/shard_map/project_halves/pallas_call | solution.py:123
Async XLA Ops:
  6.5 1.1 %copy-start = (bf16[768,384]{1,0:T(8,128)(2,1)S(1)}, bf16[768,384]{1,0:T(8,128)(2,1)}, u32[]{:S(2)}) copy-start(bf16[768,384]{1,0:T(8,128)(2,1)} %param.9) | copy-start | bytes 1769476
  6.5 35.3 %all-gather.2.cloned.1.call-start = ((), (), s32[]{:S(2)}) async-start(), calls=%async_computation.2 | async-start | bytes 1474560 | tf_op jit(solution)/shard_map/all_gather | solution.py:143
  10.4 15.6 %all-to-all-start = ((bf16[8,3,96,128]{3,2,1,0:T(8,128)(2,1)}), bf16[8,3,96,128]{3,2,1,0:T(8,128)(2,1)S(1)}, u32[]{:S(2)}, u32[]{:S(2)}) async-start(bf16[8,3,96,128]{3,2,1,0:T(8,128)(2,1)} %pack_heads.1), calls=%async_computation | async-start | bytes 1179648 | tf_op jit(solution)/shard_map/all_to_all | solution.py:153
  41.8 3.1 %collective-permute-start = (bf16[384,1536]{1,0:T(8,128)(2,1)}, bf16[384,1536]{1,0:T(8,128)(2,1)S(1)}, u32[]{:S(2)}, u32[]{:S(2)}) collective-permute-start(bf16[384,1536]{1,0:T(8,128)(2,1)} %all-gather.2.cloned.1.call-done.near_ref), channel_id=1, source_target_pairs={{0,4},{4,0},{8,12},{12,8},{16,20},{20,16},{24,28},{28,24},{1,5},{5... | collective-permute-start | bytes 3538952 | tf_op jit(solution)/shard_map/ppermute | solution.py:137
  44.9 1.3 %copy-start.1 = (bf16[384,1536]{1,0:T(8,128)(2,1)S(1)}, bf16[384,1536]{1,0:T(8,128)(2,1)}, u32[]{:S(2)}) copy-start(bf16[384,1536]{1,0:T(8,128)(2,1)} %all-gather.2.cloned.1.call-done.near_ref) | copy-start | bytes 3538948
Sparse Core Ops, SparseCore 0:
  9.0 32.8 all-gather.1

commit v4 on v0

v4 whole, which is shorter than its diff:
```python
import functools
import math

import jax
import jax.numpy as jnp
from jax import lax
from jax.experimental import pallas as pl
from jax.experimental.pallas import tpu as pltpu
from jax.sharding import PartitionSpec as P

HEADS = 8
FLIPS = tuple(range(0, HEADS, 2))
WHOLE = pl.BlockSpec(memory_space=pltpu.VMEM)
SCALARS = pl.BlockSpec(memory_space=pltpu.SMEM)
ANYWHERE = pl.BlockSpec(memory_space=pl.ANY)


def params(mebibytes=48):
    return pltpu.CompilerParams(vmem_limit_bytes=mebibytes * 1024 * 1024)


def place_in_group():
    return lax.axis_index("ctx") % HEADS


def pack_kernel(query_ref, key_ref, value_ref, weight_ref, *refs):
    outs, share_ref = refs[: len(FLIPS)], refs[len(FLIPS)]
    rows, turned, sems = refs[len(FLIPS) + 1 :]
    head_size = outs[0].shape[2]
    place = place_in_group()
    first = pl.multiple_of(place * share_ref.shape[0], 32)
    cut = pltpu.make_async_copy(weight_ref.at[pl.ds(first, share_ref.shape[0])], share_ref, sems.at[3])
    arrivals = [
        pltpu.make_async_copy(ref.at[0], rows.at[part], sems.at[part])
        for part, ref in enumerate((query_ref, key_ref, value_ref))
    ]
    for copy in arrivals:
        copy.start()
    cut.start()
    for part, copy in enumerate(arrivals):
        copy.wait()
        turned[...] = rows[part].T
        for flip, out_ref in zip(FLIPS, outs):
            for other in range(2):
                head = pl.multiple_of((place ^ (flip + other)) * head_size, 32)
                out_ref[other, part] = turned[pl.ds(head, head_size), :]
    cut.wait()


def pack(queries, key_rows, value_rows, out_weight):
    _, frames, features = queries.shape
    blocks = jax.ShapeDtypeStruct((2, 3, features // HEADS, frames), queries.dtype)
    share = jax.ShapeDtypeStruct((out_weight.shape[0] // HEADS, out_weight.shape[1]), out_weight.dtype)
    outs = pl.pallas_call(
        pack_kernel,
        out_shape=[blocks] * len(FLIPS) + [share],
        in_specs=[ANYWHERE] * 4,
        out_specs=[WHOLE] * (len(FLIPS) + 1),
        scratch_shapes=[
            pltpu.VMEM((3, frames, features), queries.dtype),
            pltpu.VMEM((features, frames), queries.dtype),
            pltpu.SemaphoreType.DMA((4,)),
        ],
        compiler_params=params(60),
        name="pack_heads",
    )(queries, key_rows, value_rows, out_weight)
    return outs[: len(FLIPS)], outs[len(FLIPS)]


def attention_kernel(groups, lengths_ref, *refs):
    same, other = refs[: len(FLIPS)], refs[len(FLIPS) : 2 * len(FLIPS)]
    rest_ref = refs[2 * len(FLIPS)] if groups > 1 else None
    outs, (keys, values, query) = refs[-3 - len(FLIPS) : -3], refs[-3:]
    head_size, block = outs[0].shape[1:]
    place = place_in_group()
    scale = jnp.float32(math.log2(math.e) / math.sqrt(head_size))
    pad = keys.shape[1] - head_size
    at_row = lax.broadcasted_iota(jnp.int32, (pad, block), 0)
    at_frame = lax.broadcasted_iota(jnp.int32, (pad, block), 1)
    first_row = jnp.where(at_row == 0, 1.0, 0.0).astype(keys.dtype)

    def piece(flip, part):
        return same[flip // 2][0, part] if flip % 2 == 0 else other[flip // 2][part]

    for at in range(groups * HEADS):
        flip = at % HEADS
        key = piece(flip, 1) if groups == 1 else rest_ref[at, 0]
        value = piece(flip, 2) if groups == 1 else rest_ref[at, 1]
        frame = (at // HEADS * HEADS + (place ^ flip)) * block + at_frame
        bias = jnp.where((at_row == 0) & (frame >= lengths_ref[0]), -1e30, 0.0).astype(keys.dtype)
        keys[at * block : (at + 1) * block, :] = jnp.concatenate([key, bias], axis=0).T
        values[:head_size, at * block : (at + 1) * block] = value
        values[head_size:, at * block : (at + 1) * block] = first_row
    for half in range(2):
        query[head_size:, half * block : (half + 1) * block] = first_row
    for flip, out_ref in zip(FLIPS, outs):
        for half in range(2):
            query[:head_size, half * block : (half + 1) * block] = piece(flip + half, 0)
        scores = jnp.dot(keys[...], query[...], preferred_element_type=jnp.float32)
        row_max = jnp.max(scores, axis=0, keepdims=True) * scale
        probs = jnp.exp2(scores * scale - row_max).astype(jnp.bfloat16)
        mixed = jnp.dot(values[...], probs, preferred_element_type=jnp.float32)
        mixed = (mixed[:head_size] / mixed[head_size : head_size + 1]).astype(jnp.bfloat16)
        for half in range(2):
            out_ref[half] = mixed[:, half * block : (half + 1) * block]


def attend(lengths, same, other, rest, groups):
    _, head_size, block = other[0].shape
    keys = groups * HEADS * block
    padded = head_size + 32
    queries = HEADS * block
    rest = [] if rest is None else [rest]
    return pl.pallas_call(
        functools.partial(attention_kernel, groups),
        out_shape=[jax.ShapeDtypeStruct((2, head_size, block), jnp.bfloat16)] * len(FLIPS),
        in_specs=[SCALARS] + [WHOLE] * (2 * len(FLIPS) + len(rest)),
        out_specs=[WHOLE] * len(FLIPS),
        scratch_shapes=[
            pltpu.VMEM((keys, padded), jnp.bfloat16),
            pltpu.VMEM((padded, keys), jnp.bfloat16),
            pltpu.VMEM((padded, 2 * block), jnp.bfloat16),
        ],
        compiler_params=params(),
        cost_estimate=pl.CostEstimate(
            flops=4 * queries * keys * head_size,
            bytes_accessed=4 * (queries + keys) * head_size,
            transcendentals=queries * keys,
        ),
        name="attend_one_head",
    )(lengths, *same, *other, *rest)


def project_kernel(shards, *refs):
    each = len(FLIPS)
    heads_same, heads_other, weight_same, weight_other = (refs[at : at + each] for at in range(0, 4 * each, each))
    own_ref = refs[4 * len(FLIPS)] if shards > 1 else None
    out_ref, turned, weight = refs[-3:]
    place = place_in_group()
    rows = turned.shape[0] // HEADS
    for flip in range(HEADS):
        here = pl.ds(pl.multiple_of((place ^ flip) * rows, 32), rows)
        turned[here, :] = heads_other[flip // 2][...] if flip % 2 else heads_same[flip // 2][0]
        weight[here, :] = (weight_other if flip % 2 else weight_same)[flip // 2][...]
    attention = turned[...].T
    foreign = jnp.dot(attention, weight[...], preferred_element_type=jnp.float32).astype(out_ref.dtype)
    if shards == 1:
        out_ref[0] = foreign
        return
    columns = own_ref.shape[1]
    shard = lax.axis_index("fsdp")
    own = jnp.dot(attention, own_ref[...], preferred_element_type=jnp.float32).astype(out_ref.dtype)
    out_ref[0, :, pl.ds(pl.multiple_of(shard * columns, 128), columns)] = own
    for flip in range(1, shards):
        here = pl.ds(pl.multiple_of((shard ^ flip) * columns, 128), columns)
        out_ref[0, :, here] = foreign[:, (flip - 1) * columns : flip * columns]


def project(heads_same, heads_other, weight_same, weight_other, own, shards):
    rows, frames = heads_other[0].shape
    foreign = weight_same[0].shape[1]
    width = foreign + (own[0].shape[1] if own else 0)
    features = HEADS * rows
    pieces = [*heads_same, *heads_other, *weight_same, *weight_other, *own]
    return pl.pallas_call(
        functools.partial(project_kernel, shards),
        out_shape=jax.ShapeDtypeStruct((1, frames, width), jnp.bfloat16),
        in_specs=[WHOLE] * len(pieces),
        out_specs=WHOLE,
        scratch_shapes=[pltpu.VMEM((features, frames), jnp.bfloat16), pltpu.VMEM((features, foreign), jnp.bfloat16)],
        compiler_params=params(),
        cost_estimate=pl.CostEstimate(
            flops=2 * features * frames * width, bytes_accessed=2 * features * width, transcendentals=0
        ),
        name="project_heads",
    )(*pieces)


def per_device(ctx, fsdp, queries, key_rows, value_rows, lengths, out_weight):
    def exchange(array, axis, flip):
        size = ctx if axis == "ctx" else fsdp
        return lax.ppermute(array, axis, [(i, i ^ flip) for i in range(size)])

    by_chip, share = pack(queries, key_rows, value_rows, out_weight)
    split_columns = fsdp in (2, 4)
    if split_columns:
        share = jnp.concatenate([exchange(share, "fsdp", flip) for flip in range(1, fsdp)], axis=1)
    else:
        share = lax.all_gather(share, "fsdp", axis=1, tiled=True)

    same = [exchange(array, "ctx", flip) if flip else array for flip, array in zip(FLIPS, by_chip)]
    other = [exchange(array[1], "ctx", 1) for array in same]
    weight_same = [exchange(share, "ctx", flip) if flip else share for flip in FLIPS]

    groups = ctx // HEADS
    rest = None
    if groups > 1:
        pairs = [array for two in zip([a[0, 1:] for a in same], [a[1:] for a in other]) for array in two]
        across = [[head + first for first in range(0, ctx, HEADS)] for head in range(HEADS)]
        rest = lax.all_gather(jnp.stack(pairs), "ctx", axis=0, axis_index_groups=across, tiled=True)
    mixed = attend(lengths, same, other, rest, groups)

    heads_same = [exchange(array, "ctx", flip) if flip else array for flip, array in zip(FLIPS, mixed)]
    heads_other = [exchange(array[1], "ctx", 1) for array in heads_same]
    weight_same, _ = lax.optimization_barrier((weight_same, mixed))
    weight_other = [exchange(array, "ctx", 1) for array in weight_same]
    own = [out_weight] if split_columns else []
    return project(heads_same, heads_other, weight_same, weight_other, own, fsdp if split_columns else 1)


def solution(mesh):
    return jax.shard_map(
        functools.partial(per_device, mesh.shape["ctx"], mesh.shape["fsdp"]),
        mesh=mesh,
        in_specs=(
            P("fsdp", "ctx", None),
            P("fsdp", "ctx", None),
            P("fsdp", "ctx", None),
            P("fsdp"),
            P(None, "fsdp"),
        ),
        out_specs=P("fsdp", "ctx", None),
        check_vma=False,
    )
```

time: 127 us -> 48.1 us (0.38)
  waiting for transfers between devices: 102 us -> 18.7 us
  starting transfers between devices: 0.08 us -> 20.6 us
  between operations: 13.8 us -> 0.81 us
  Pallas kernels: 0 us -> 6.8 us
  matrix products: 4.84 us -> 0 us
  local copies, waits for them, and re-layouts: 4.5 us -> 1.01 us
    all_gather x3 -> x0, waiting for transfers between devices: 100 us -> none  [the longest x1 47.3 us: per_device(): lax.all_gather(out_weight, 'fsdp', axis=1, tiled=True)]
    ppermute x0 -> x24, starting transfers between devices: none -> 20.6 us  [exchange(): return lax.ppermute(array, axis, [(i, i ^ flip) for i in range(size)])]
    ppermute x0 -> x24, waiting for transfers between devices: none -> 18.7 us  [exchange(): return lax.ppermute(array, axis, [(i, i ^ flip) for i in range(size)])]
    pallas_call x0 -> x3, Pallas kernels: none -> 6.8 us  [the longest x1 3.18 us: attend(): pl.pallas_call(functools.partial(attention_kernel, groups), out_shape=[ja...]
    dot_general x3 -> x0, matrix products: 4.84 us -> none  [the longest x1 2.91 us: per_device(): jnp.dot(attention, lax.all_gather(out_weight, 'fsdp', axis=1, tiled=True)...]
    all_gather x2 -> x0, local copies, waits for them, and re-layouts: 3.42 us -> none  [the longest x1 1.71 us: per_device(): lax.all_gather(key_rows, 'ctx', axis=1, tiled=True)]
    unnamed x3 -> x0, waiting for transfers between devices: 2.09 us -> none
  transfers between devices with their start and end apart: 3 -> 24, of which waited for: 3 -> 6; matrix products, arithmetic and copies ran while one was open for 6% -> 2% of each run, Pallas kernels for 0% -> 7%
where the time goes in v4:
time: 48.1 us; the launch traced here: 48 us
  starting transfers between devices  20.6 us (43%)
  waiting for transfers between devices  18.7 us (39%)
  Pallas kernels  6.8 us (14%)
  local copies, waits for them, and re-layouts  1.01 us (2%)
  between operations  0.81 us (2%)
    ppermute x24, starting transfers between devices, exchange(): return lax.ppermute(array, axis, [(i, i ^ flip) for i in range(size)])  20.6 us
    ppermute x24, waiting for transfers between devices, exchange(): return lax.ppermute(array, axis, [(i, i ^ flip) for i in range(size)])  18.7 us
    pallas_call x1, Pallas kernels, attend(): pl.pallas_call(functools.partial(attention_kernel, groups), out_shape=[ja...  3.18 us
    pallas_call x1, Pallas kernels, pack(): pl.pallas_call(pack_kernel, out_shape=[blocks] * len(FLIPS) + [share], in...  2.15 us
    pallas_call x1, Pallas kernels, project(): pl.pallas_call(functools.partial(project_kernel, shards), out_shape=jax.S...  1.47 us
  transfers between devices with their start and end apart: 24, of which 6 were waited for; matrix products, arithmetic and copies ran while one was open for 2% of the time, Pallas kernels for 7%

profile of v4, /device:TPU:0, one launch (start us, length us, event | category | flops | bytes accessed | tf_op | source)
XLA Modules:
  0.0 48.0 jit_solution(1572786619216790887)
XLA Ops:
  0.0 2.1 %pack_heads.1 = (bf16[2,3,96,128]{3,2,1,0:T(8,128)(2,1)}, bf16[2,3,96,128]{3,2,1,0:T(8,128)(2,1)}, bf16[2,3,96,128]{3,2,1,0:T(8,128)(2,1)}, bf16[2,3,96,128]{3,2,1,0:T(8,128)(2,1)}, bf16[96,384]{1,0:T(8,128)(2,1)}) custom-call(bf16[1,128,768]{2,1,0:T(8,128)(2,1)} %query_ref.1, bf16[1,128,768]{2,1,0:T(8,128)(2,1)} %key_ref.1, bf16[1,128,768]{2,1,0:T(8,128)(2,1)} %value_ref.1, ...), custom_call_target="tpu_custom_call" | custom-call | tf_op jit(solution)/shard_map/pack_heads/pallas_call | solution.py:54
  2.2 5.1 %collective-permute-start.16 = (bf16[96,384]{1,0:T(8,128)(2,1)}, bf16[96,384]{1,0:T(8,128)(2,1)S(1)}, u32[]{:S(2)}, u32[]{:S(2)}) collective-permute-start(bf16[96,384]{1,0:T(8,128)(2,1)} %get-tuple-element.26), channel_id=1, source_target_pairs={{0,3},{1,2},{2,1},{3,0},{4,7},{5,6},{6,5},{7,4},{8,11},{9,10},{10,... | collective-permute-start | bytes 221192 | tf_op jit(solution)/shard_map/ppermute | solution.py:182
  7.3 0.0 collective-permute-start.15
  7.3 0.6 %collective-permute-start.14 = (bf16[96,384]{1,0:T(8,128)(2,1)}, bf16[96,384]{1,0:T(8,128)(2,1)S(1)}, u32[]{:S(2)}, u32[]{:S(2)}) collective-permute-start(bf16[96,384]{1,0:T(8,128)(2,1)} %get-tuple-element.26), channel_id=1, source_target_pairs={{0,1},{1,0},{2,3},{3,2},{4,5},{5,4},{6,7},{7,6},{8,9},{9,8},{10,11... | collective-permute-start | bytes 221192 | tf_op jit(solution)/shard_map/ppermute | solution.py:182
  7.9 0.9 %slice_bitcast_fusion.3 = bf16[3,96,128]{2,1,0:T(8,128)(2,1)S(1)} fusion(bf16[2,3,96,128]{3,2,1,0:T(8,128)(2,1)} %get-tuple-element.18.refs_0_), kind=kLoop, calls=%fused_computation.3 | loop fusion | bytes 147456 | tf_op jit(solution)/shard_map/squeeze | solution.py:192
  8.8 0.0 collective-permute-start.3
  8.9 1.7 %collective-permute-start = (bf16[2,3,96,128]{3,2,1,0:T(8,128)(2,1)}, bf16[2,3,96,128]{3,2,1,0:T(8,128)(2,1)S(1)}, u32[]{:S(2)}, u32[]{:S(2)}) collective-permute-start(bf16[2,3,96,128]{3,2,1,0:T(8,128)(2,1)} %get-tuple-element.19), channel_id=1, source_target_pairs={{0,8},{4,12},{8,0},{12,4},{16,24},{20,28},{24,16},{28,20},{1,9},{5... | collective-permute-start | bytes 442376 | tf_op jit(solution)/shard_map/ppermute | solution.py:182
  11.2 1.1 %collective-permute-done.14 = bf16[96,384]{1,0:T(8,128)(2,1)S(1)} collective-permute-done((bf16[96,384]{1,0:T(8,128)(2,1)}, bf16[96,384]{1,0:T(8,128)(2,1)S(1)}, u32[]{:S(2)}, u32[]{:S(2)}) %collective-permute-start.14) | collective-permute-done | bytes 73760 | tf_op jit(solution)/shard_map/ppermute | solution.py:182
  12.3 1.5 %collective-permute-start.1 = (bf16[2,3,96,128]{3,2,1,0:T(8,128)(2,1)S(1)}, bf16[2,3,96,128]{3,2,1,0:T(8,128)(2,1)S(1)}, u32[]{:S(2)}, u32[]{:S(2)}) collective-permute-start(bf16[2,3,96,128]{3,2,1,0:T(8,128)(2,1)S(1)} %copy-done.3), channel_id=1, source_target_pairs={{0,16},{4,20},{8,24},{12,28},{16,0},{20,4},{24,8},{28,12},{1,17},{... | collective-permute-start | bytes 442376 | tf_op jit(solution)/shard_map/ppermute | solution.py:182
  13.9 0.0 collective-permute-done.15
  13.9 2.3 %collective-permute-start.2 = (bf16[2,3,96,128]{3,2,1,0:T(8,128)(2,1)S(1)}, bf16[2,3,96,128]{3,2,1,0:T(8,128)(2,1)S(1)}, u32[]{:S(2)}, u32[]{:S(2)}) collective-permute-start(bf16[2,3,96,128]{3,2,1,0:T(8,128)(2,1)S(1)} %copy-done.2), channel_id=1, source_target_pairs={{0,24},{4,28},{8,16},{12,20},{16,8},{20,12},{24,0},{28,4},{1,25},{... | collective-permute-start | bytes 442376 | tf_op jit(solution)/shard_map/ppermute | solution.py:182
  16.2 0.0 collective-permute-done.refs_1_
  16.2 0.1 collective-permute-start.4
  16.3 4.3 %collective-permute-done.1.refs_2_ = bf16[2,3,96,128]{3,2,1,0:T(8,128)(2,1)S(1)} collective-permute-done((bf16[2,3,96,128]{3,2,1,0:T(8,128)(2,1)S(1)}, bf16[2,3,96,128]{3,2,1,0:T(8,128)(2,1)S(1)}, u32[]{:S(2)}, u32[]{:S(2)}) %collective-permute-start.1) | collective-permute-done | bytes 147488 | tf_op jit(solution)/shard_map/ppermute | solution.py:182
  20.6 0.1 collective-permute-start.5
  20.7 0.0 collective-permute-done.2.refs_3_
  20.7 0.5 %collective-permute-start.6 = (bf16[3,96,128]{2,1,0:T(8,128)(2,1)S(1)}, bf16[3,96,128]{2,1,0:T(8,128)(2,1)S(1)}, u32[]{:S(2)}, u32[]{:S(2)}) collective-permute-start(bf16[3,96,128]{2,1,0:T(8,128)(2,1)S(1)} %slice_bitcast_fusion), channel_id=1, source_target_pairs={{0,4},{4,0},{8,12},{12,8},{16,20},{20,16},{24,28},{28,24},{1,5},{5... | collective-permute-start | bytes 221192 | tf_op jit(solution)/shard_map/ppermute | solution.py:182
  21.3 0.0 collective-permute-done.16
  21.3 2.5 %collective-permute-start.19 = (bf16[96,1152]{1,0:T(8,128)(2,1)S(1)}, bf16[96,1152]{1,0:T(8,128)(2,1)S(1)}, u32[]{:S(2)}, u32[]{:S(2)}) collective-permute-start(bf16[96,1152]{1,0:T(8,128)(2,1)S(1)} %constant_dynamic-update-slice_fusion.refs_8_), channel_id=1, source_target_pairs={{0,24},{4,28},{8,16},{12,20},{16,8},{20,12},{24,0},{28,4},{1,25},{... | collective-permute-start | bytes 663560 | tf_op jit(solution)/shard_map/ppermute | solution.py:182
  23.8 0.0 collective-permute-done.3.refs_4_
  23.8 0.5 %collective-permute-start.18 = (bf16[96,1152]{1,0:T(8,128)(2,1)S(1)}, bf16[96,1152]{1,0:T(8,128)(2,1)S(1)}, u32[]{:S(2)}, u32[]{:S(2)}) collective-permute-start(bf16[96,1152]{1,0:T(8,128)(2,1)S(1)} %constant_dynamic-update-slice_fusion.refs_8_), channel_id=1, source_target_pairs={{0,16},{4,20},{8,24},{12,28},{16,0},{20,4},{24,8},{28,12},{1,17},{... | collective-permute-start | bytes 663560 | tf_op jit(solution)/shard_map/ppermute | solution.py:182
  24.3 0.0 collective-permute-done.4.refs_5_
  24.3 0.5 %collective-permute-start.17 = (bf16[96,1152]{1,0:T(8,128)(2,1)S(1)}, bf16[96,1152]{1,0:T(8,128)(2,1)S(1)}, u32[]{:S(2)}, u32[]{:S(2)}) collective-permute-start(bf16[96,1152]{1,0:T(8,128)(2,1)S(1)} %constant_dynamic-update-slice_fusion.refs_8_), channel_id=1, source_target_pairs={{0,8},{4,12},{8,0},{12,4},{16,24},{20,28},{24,16},{28,20},{1,9},{5... | collective-permute-start | bytes 663560 | tf_op jit(solution)/shard_map/ppermute | solution.py:182
  24.9 0.0 collective-permute-done.5.refs_6_
  24.9 0.0 collective-permute-done.6.refs_7_
  24.9 0.0 copy-start
  24.9 3.2 %attend_one_head.1 = (bf16[2,96,128]{2,1,0:T(8,128)(2,1)S(1)}, bf16[2,96,128]{2,1,0:T(8,128)(2,1)S(1)}, bf16[2,96,128]{2,1,0:T(8,128)(2,1)S(1)}, bf16[2,96,128]{2,1,0:T(8,128)(2,1)S(1)}) custom-call(s32[1]{0:T(128)S(6)} %copy.8.lengths_ref, bf16[2,3,96,128]{3,2,1,0:T(8,128)(2,1)S(1)} %copy-done.1, bf16[2,3,96,128]{3,2,1,0:T(8,128)(2,1)S(1)} %collective-permute-done.refs_1_, ...), custom_call_target="tpu_custom_call" | custom-call | flops 402653184 | bytes 786432 | tf_op jit(solution)/shard_map/attend_one_head/pallas_call | solution.py:114
  28.1 1.6 %collective-permute-start.7 = (bf16[2,96,128]{2,1,0:T(8,128)(2,1)S(1)}, bf16[2,96,128]{2,1,0:T(8,128)(2,1)S(1)}, u32[]{:S(2)}, u32[]{:S(2)}) collective-permute-start(bf16[2,96,128]{2,1,0:T(8,128)(2,1)S(1)} %get-tuple-element.23), channel_id=1, source_target_pairs={{0,8},{4,12},{8,0},{12,4},{16,24},{20,28},{24,16},{28,20},{1,9},{5... | collective-permute-start | bytes 147464 | tf_op jit(solution)/shard_map/ppermute | solution.py:182
  29.7 5.9 %collective-permute-done.7.refs_1_ = bf16[2,96,128]{2,1,0:T(8,128)(2,1)S(1)} collective-permute-done((bf16[2,96,128]{2,1,0:T(8,128)(2,1)S(1)}, bf16[2,96,128]{2,1,0:T(8,128)(2,1)S(1)}, u32[]{:S(2)}, u32[]{:S(2)}) %collective-permute-start.7) | collective-permute-done | bytes 49184 | tf_op jit(solution)/shard_map/ppermute | solution.py:182
  35.5 0.5 %collective-permute-start.8 = (bf16[2,96,128]{2,1,0:T(8,128)(2,1)S(1)}, bf16[2,96,128]{2,1,0:T(8,128)(2,1)S(1)}, u32[]{:S(2)}, u32[]{:S(2)}) collective-permute-start(bf16[2,96,128]{2,1,0:T(8,128)(2,1)S(1)} %get-tuple-element.24), channel_id=1, source_target_pairs={{0,16},{4,20},{8,24},{12,28},{16,0},{20,4},{24,8},{28,12},{1,17},{... | collective-permute-start | bytes 147464 | tf_op jit(solution)/shard_map/ppermute | solution.py:182
  36.0 3.6 %collective-permute-done.8.refs_2_ = bf16[2,96,128]{2,1,0:T(8,128)(2,1)S(1)} collective-permute-done((bf16[2,96,128]{2,1,0:T(8,128)(2,1)S(1)}, bf16[2,96,128]{2,1,0:T(8,128)(2,1)S(1)}, u32[]{:S(2)}, u32[]{:S(2)}) %collective-permute-start.8) | collective-permute-done | bytes 49184 | tf_op jit(solution)/shard_map/ppermute | solution.py:182
  39.6 1.4 %collective-permute-start.9 = (bf16[2,96,128]{2,1,0:T(8,128)(2,1)S(1)}, bf16[2,96,128]{2,1,0:T(8,128)(2,1)S(1)}, u32[]{:S(2)}, u32[]{:S(2)}) collective-permute-start(bf16[2,96,128]{2,1,0:T(8,128)(2,1)S(1)} %get-tuple-element.25), channel_id=1, source_target_pairs={{0,24},{4,28},{8,16},{12,20},{16,8},{20,12},{24,0},{28,4},{1,25},{... | collective-permute-start | bytes 147464 | tf_op jit(solution)/shard_map/ppermute | solution.py:182
  41.1 0.0 collective-permute-done.19.refs_11_
  41.1 0.0 collective-permute-done.18.refs_10_
  41.1 0.5 %collective-permute-start.12 = (bf16[96,128]{1,0:T(8,128)(2,1)S(1)}, bf16[96,128]{1,0:T(8,128)(2,1)S(1)}, u32[]{:S(2)}, u32[]{:S(2)}) collective-permute-start(bf16[96,128]{1,0:T(8,128)(2,1)S(1)} %slice_bitcast_fusion.5), channel_id=1, source_target_pairs={{0,4},{4,0},{8,12},{12,8},{16,20},{20,16},{24,28},{28,24},{1,5},{5... | collective-permute-start | bytes 73736 | tf_op jit(solution)/shard_map/ppermute | solution.py:182
  41.6 0.0 collective-permute-done.17.refs_9_
  41.6 0.1 collective-permute-start.20
  41.7 0.0 collective-permute-done.10.refs_4_
  41.7 0.4 collective-permute-start.21
  42.1 2.5 %collective-permute-done.9.refs_3_ = bf16[2,96,128]{2,1,0:T(8,128)(2,1)S(1)} collective-permute-done((bf16[2,96,128]{2,1,0:T(8,128)(2,1)S(1)}, bf16[2,96,128]{2,1,0:T(8,128)(2,1)S(1)}, u32[]{:S(2)}, u32[]{:S(2)}) %collective-permute-start.9) | collective-permute-done | bytes 49184 | tf_op jit(solution)/shard_map/ppermute | solution.py:182
  44.6 0.0 collective-permute-start.22
  44.6 0.0 collective-permute-done.11.refs_5_
  44.6 0.5 %collective-permute-start.23 = (bf16[96,1152]{1,0:T(8,128)(2,1)S(1)}, bf16[96,1152]{1,0:T(8,128)(2,1)S(1)}, u32[]{:S(2)}, u32[]{:S(2)}) collective-permute-start(bf16[96,1152]{1,0:T(8,128)(2,1)S(1)} %collective-permute-done.19.refs_11_), channel_id=1, source_target_pairs={{0,4},{4,0},{8,12},{12,8},{16,20},{20,16},{24,28},{28,24},{1,5},{5... | collective-permute-start | bytes 663560 | tf_op jit(solution)/shard_map/ppermute | solution.py:182
  45.1 0.0 collective-permute-done.12.refs_6_
  45.1 0.1 collective-permute-start.13
  45.2 1.2 %collective-permute-done.13.refs_7_ = bf16[96,128]{1,0:T(8,128)(2,1)S(1)} collective-permute-done((bf16[96,128]{1,0:T(8,128)(2,1)S(1)}, bf16[96,128]{1,0:T(8,128)(2,1)S(1)}, u32[]{:S(2)}, u32[]{:S(2)}) %collective-permute-start.13) | collective-permute-done | bytes 24608 | tf_op jit(solution)/shard_map/ppermute | solution.py:182
  46.5 0.0 collective-permute-done.23.refs_15_
  46.5 1.5 %project_heads.1 = bf16[1,128,1536]{2,1,0:T(8,128)(2,1)} custom-call(bf16[2,96,128]{2,1,0:T(8,128)(2,1)S(1)} %get-tuple-element.22.refs_0_, bf16[2,96,128]{2,1,0:T(8,128)(2,1)S(1)} %collective-permute-done.7.refs_1_, bf16[2,96,128]{2,1,0:T(8,128)(2,1)S(1)} %collective-permute-done.8.refs_2_, bf16[2,96,128]{2,1,0:T(8,128)(2,1)S(1)} %collective-permute-done.9.refs_3_, ...), custom_call_target="tpu_custom_call" | custom-call | flops 301989888 | bytes 2359296 | tf_op jit(solution)/shard_map/project_heads/pallas_call | solution.py:165
  (22 shorter events, 0.1 us)
Async XLA Ops:
  2.2 10.2 %copy-start.3 = (bf16[2,3,96,128]{3,2,1,0:T(8,128)(2,1)S(1)}, bf16[2,3,96,128]{3,2,1,0:T(8,128)(2,1)}, u32[]{:S(2)}) copy-start(bf16[2,3,96,128]{3,2,1,0:T(8,128)(2,1)} %get-tuple-element.20) | copy-start | bytes 442372
  2.2 19.1 %collective-permute-start.16 = (bf16[96,384]{1,0:T(8,128)(2,1)}, bf16[96,384]{1,0:T(8,128)(2,1)S(1)}, u32[]{:S(2)}, u32[]{:S(2)}) collective-permute-start(bf16[96,384]{1,0:T(8,128)(2,1)} %get-tuple-element.26), channel_id=1, source_target_pairs={{0,3},{1,2},{2,1},{3,0},{4,7},{5,6},{6,5},{7,4},{8,11},{9,10},{10,... | collective-permute-start | bytes 221192 | tf_op jit(solution)/shard_map/ppermute | solution.py:182
  7.3 6.6 %collective-permute-start.15 = (bf16[96,384]{1,0:T(8,128)(2,1)}, bf16[96,384]{1,0:T(8,128)(2,1)S(1)}, u32[]{:S(2)}, u32[]{:S(2)}) collective-permute-start(bf16[96,384]{1,0:T(8,128)(2,1)} %get-tuple-element.26), channel_id=1, source_target_pairs={{0,2},{1,3},{2,0},{3,1},{4,6},{5,7},{6,4},{7,5},{8,10},{9,11},{10,... | collective-permute-start | bytes 221192 | tf_op jit(solution)/shard_map/ppermute | solution.py:182
  7.3 5.0 %collective-permute-start.14 = (bf16[96,384]{1,0:T(8,128)(2,1)}, bf16[96,384]{1,0:T(8,128)(2,1)S(1)}, u32[]{:S(2)}, u32[]{:S(2)}) collective-permute-start(bf16[96,384]{1,0:T(8,128)(2,1)} %get-tuple-element.26), channel_id=1, source_target_pairs={{0,1},{1,0},{2,3},{3,2},{4,5},{5,4},{6,7},{7,6},{8,9},{9,8},{10,11... | collective-permute-start | bytes 221192 | tf_op jit(solution)/shard_map/ppermute | solution.py:182
  7.9 6.0 %copy-start.2 = (bf16[2,3,96,128]{3,2,1,0:T(8,128)(2,1)S(1)}, bf16[2,3,96,128]{3,2,1,0:T(8,128)(2,1)}, u32[]{:S(2)}) copy-start(bf16[2,3,96,128]{3,2,1,0:T(8,128)(2,1)} %get-tuple-element.21) | copy-start | bytes 442372
  8.8 15.0 %collective-permute-start.3 = (bf16[3,96,128]{2,1,0:T(8,128)(2,1)S(1)}, bf16[3,96,128]{2,1,0:T(8,128)(2,1)S(1)}, u32[]{:S(2)}, u32[]{:S(2)}) collective-permute-start(bf16[3,96,128]{2,1,0:T(8,128)(2,1)S(1)} %slice_bitcast_fusion.3), channel_id=1, source_target_pairs={{0,4},{4,0},{8,12},{12,8},{16,20},{20,16},{24,28},{28,24},{1,5},{5... | collective-permute-start | bytes 221192 | tf_op jit(solution)/shard_map/ppermute | solution.py:182
  8.9 7.3 %collective-permute-start = (bf16[2,3,96,128]{3,2,1,0:T(8,128)(2,1)}, bf16[2,3,96,128]{3,2,1,0:T(8,128)(2,1)S(1)}, u32[]{:S(2)}, u32[]{:S(2)}) collective-permute-start(bf16[2,3,96,128]{3,2,1,0:T(8,128)(2,1)} %get-tuple-element.19), channel_id=1, source_target_pairs={{0,8},{4,12},{8,0},{12,4},{16,24},{20,28},{24,16},{28,20},{1,9},{5... | collective-permute-start | bytes 442376 | tf_op jit(solution)/shard_map/ppermute | solution.py:182
  12.3 8.3 %collective-permute-start.1 = (bf16[2,3,96,128]{3,2,1,0:T(8,128)(2,1)S(1)}, bf16[2,3,96,128]{3,2,1,0:T(8,128)(2,1)S(1)}, u32[]{:S(2)}, u32[]{:S(2)}) collective-permute-start(bf16[2,3,96,128]{3,2,1,0:T(8,128)(2,1)S(1)} %copy-done.3), channel_id=1, source_target_pairs={{0,16},{4,20},{8,24},{12,28},{16,0},{20,4},{24,8},{28,12},{1,17},{... | collective-permute-start | bytes 442376 | tf_op jit(solution)/shard_map/ppermute | solution.py:182
  13.9 6.8 %collective-permute-start.2 = (bf16[2,3,96,128]{3,2,1,0:T(8,128)(2,1)S(1)}, bf16[2,3,96,128]{3,2,1,0:T(8,128)(2,1)S(1)}, u32[]{:S(2)}, u32[]{:S(2)}) collective-permute-start(bf16[2,3,96,128]{3,2,1,0:T(8,128)(2,1)S(1)} %copy-done.2), channel_id=1, source_target_pairs={{0,24},{4,28},{8,16},{12,20},{16,8},{20,12},{24,0},{28,4},{1,25},{... | collective-permute-start | bytes 442376 | tf_op jit(solution)/shard_map/ppermute | solution.py:182
  16.2 8.1 %collective-permute-start.4 = (bf16[3,96,128]{2,1,0:T(8,128)(2,1)S(1)}, bf16[3,96,128]{2,1,0:T(8,128)(2,1)S(1)}, u32[]{:S(2)}, u32[]{:S(2)}) collective-permute-start(bf16[3,96,128]{2,1,0:T(8,128)(2,1)S(1)} %slice_bitcast_fusion.2), channel_id=1, source_target_pairs={{0,4},{4,0},{8,12},{12,8},{16,20},{20,16},{24,28},{28,24},{1,5},{5... | collective-permute-start | bytes 221192 | tf_op jit(solution)/shard_map/ppermute | solution.py:182
  20.6 4.2 %copy-start.1 = (bf16[2,3,96,128]{3,2,1,0:T(8,128)(2,1)S(1)}, bf16[2,3,96,128]{3,2,1,0:T(8,128)(2,1)}, u32[]{:S(2)}) copy-start(bf16[2,3,96,128]{3,2,1,0:T(8,128)(2,1)} %get-tuple-element.18.refs_0_) | copy-start | bytes 442372
  20.6 4.2 %collective-permute-start.5 = (bf16[3,96,128]{2,1,0:T(8,128)(2,1)S(1)}, bf16[3,96,128]{2,1,0:T(8,128)(2,1)S(1)}, u32[]{:S(2)}, u32[]{:S(2)}) collective-permute-start(bf16[3,96,128]{2,1,0:T(8,128)(2,1)S(1)} %slice_bitcast_fusion.1), channel_id=1, source_target_pairs={{0,4},{4,0},{8,12},{12,8},{16,20},{20,16},{24,28},{28,24},{1,5},{5... | collective-permute-start | bytes 221192 | tf_op jit(solution)/shard_map/ppermute | solution.py:182
  20.7 4.1 %collective-permute-start.6 = (bf16[3,96,128]{2,1,0:T(8,128)(2,1)S(1)}, bf16[3,96,128]{2,1,0:T(8,128)(2,1)S(1)}, u32[]{:S(2)}, u32[]{:S(2)}) collective-permute-start(bf16[3,96,128]{2,1,0:T(8,128)(2,1)S(1)} %slice_bitcast_fusion), channel_id=1, source_target_pairs={{0,4},{4,0},{8,12},{12,8},{16,20},{20,16},{24,28},{28,24},{1,5},{5... | collective-permute-start | bytes 221192 | tf_op jit(solution)/shard_map/ppermute | solution.py:182
  21.3 19.7 %collective-permute-start.19 = (bf16[96,1152]{1,0:T(8,128)(2,1)S(1)}, bf16[96,1152]{1,0:T(8,128)(2,1)S(1)}, u32[]{:S(2)}, u32[]{:S(2)}) collective-permute-start(bf16[96,1152]{1,0:T(8,128)(2,1)S(1)} %constant_dynamic-update-slice_fusion.refs_8_), channel_id=1, source_target_pairs={{0,24},{4,28},{8,16},{12,20},{16,8},{20,12},{24,0},{28,4},{1,25},{... | collective-permute-start | bytes 663560 | tf_op jit(solution)/shard_map/ppermute | solution.py:182
  23.8 17.2 %collective-permute-start.18 = (bf16[96,1152]{1,0:T(8,128)(2,1)S(1)}, bf16[96,1152]{1,0:T(8,128)(2,1)S(1)}, u32[]{:S(2)}, u32[]{:S(2)}) collective-permute-start(bf16[96,1152]{1,0:T(8,128)(2,1)S(1)} %constant_dynamic-update-slice_fusion.refs_8_), channel_id=1, source_target_pairs={{0,16},{4,20},{8,24},{12,28},{16,0},{20,4},{24,8},{28,12},{1,17},{... | collective-permute-start | bytes 663560 | tf_op jit(solution)/shard_map/ppermute | solution.py:182
  24.3 17.2 %collective-permute-start.17 = (bf16[96,1152]{1,0:T(8,128)(2,1)S(1)}, bf16[96,1152]{1,0:T(8,128)(2,1)S(1)}, u32[]{:S(2)}, u32[]{:S(2)}) collective-permute-start(bf16[96,1152]{1,0:T(8,128)(2,1)S(1)} %constant_dynamic-update-slice_fusion.refs_8_), channel_id=1, source_target_pairs={{0,8},{4,12},{8,0},{12,4},{16,24},{20,28},{24,16},{28,20},{1,9},{5... | collective-permute-start | bytes 663560 | tf_op jit(solution)/shard_map/ppermute | solution.py:182
  24.9 21.6 %copy-start = (bf16[768,384]{1,0:T(8,128)(2,1)S(1)}, bf16[768,384]{1,0:T(8,128)(2,1)}, u32[]{:S(2)}) copy-start(bf16[768,384]{1,0:T(8,128)(2,1)} %refs_16_.1) | copy-start | bytes 1769476
  28.1 7.4 %collective-permute-start.7 = (bf16[2,96,128]{2,1,0:T(8,128)(2,1)S(1)}, bf16[2,96,128]{2,1,0:T(8,128)(2,1)S(1)}, u32[]{:S(2)}, u32[]{:S(2)}) collective-permute-start(bf16[2,96,128]{2,1,0:T(8,128)(2,1)S(1)} %get-tuple-element.23), channel_id=1, source_target_pairs={{0,8},{4,12},{8,0},{12,4},{16,24},{20,28},{24,16},{28,20},{1,9},{5... | collective-permute-start | bytes 147464 | tf_op jit(solution)/shard_map/ppermute | solution.py:182
  29.7 12.0 %collective-permute-start.10 = (bf16[96,128]{1,0:T(8,128)(2,1)S(1)}, bf16[96,128]{1,0:T(8,128)(2,1)S(1)}, u32[]{:S(2)}, u32[]{:S(2)}) collective-permute-start(bf16[96,128]{1,0:T(8,128)(2,1)S(1)} %slice_bitcast_fusion.7), channel_id=1, source_target_pairs={{0,4},{4,0},{8,12},{12,8},{16,20},{20,16},{24,28},{28,24},{1,5},{5... | collective-permute-start | bytes 73736 | tf_op jit(solution)/shard_map/ppermute | solution.py:182
  35.5 4.1 %collective-permute-start.8 = (bf16[2,96,128]{2,1,0:T(8,128)(2,1)S(1)}, bf16[2,96,128]{2,1,0:T(8,128)(2,1)S(1)}, u32[]{:S(2)}, u32[]{:S(2)}) collective-permute-start(bf16[2,96,128]{2,1,0:T(8,128)(2,1)S(1)} %get-tuple-element.24), channel_id=1, source_target_pairs={{0,16},{4,20},{8,24},{12,28},{16,0},{20,4},{24,8},{28,12},{1,17},{... | collective-permute-start | bytes 147464 | tf_op jit(solution)/shard_map/ppermute | solution.py:182
  39.6 5.0 %collective-permute-start.9 = (bf16[2,96,128]{2,1,0:T(8,128)(2,1)S(1)}, bf16[2,96,128]{2,1,0:T(8,128)(2,1)S(1)}, u32[]{:S(2)}, u32[]{:S(2)}) collective-permute-start(bf16[2,96,128]{2,1,0:T(8,128)(2,1)S(1)} %get-tuple-element.25), channel_id=1, source_target_pairs={{0,24},{4,28},{8,16},{12,20},{16,8},{20,12},{24,0},{28,4},{1,25},{... | collective-permute-start | bytes 147464 | tf_op jit(solution)/shard_map/ppermute | solution.py:182
  41.1 3.6 %collective-permute-start.11 = (bf16[96,128]{1,0:T(8,128)(2,1)S(1)}, bf16[96,128]{1,0:T(8,128)(2,1)S(1)}, u32[]{:S(2)}, u32[]{:S(2)}) collective-permute-start(bf16[96,128]{1,0:T(8,128)(2,1)S(1)} %slice_bitcast_fusion.6), channel_id=1, source_target_pairs={{0,4},{4,0},{8,12},{12,8},{16,20},{20,16},{24,28},{28,24},{1,5},{5... | collective-permute-start | bytes 73736 | tf_op jit(solution)/shard_map/ppermute | solution.py:182
  41.1 4.1 %collective-permute-start.12 = (bf16[96,128]{1,0:T(8,128)(2,1)S(1)}, bf16[96,128]{1,0:T(8,128)(2,1)S(1)}, u32[]{:S(2)}, u32[]{:S(2)}) collective-permute-start(bf16[96,128]{1,0:T(8,128)(2,1)S(1)} %slice_bitcast_fusion.5), channel_id=1, source_target_pairs={{0,4},{4,0},{8,12},{12,8},{16,20},{20,16},{24,28},{28,24},{1,5},{5... | collective-permute-start | bytes 73736 | tf_op jit(solution)/shard_map/ppermute | solution.py:182
  41.6 4.9 %collective-permute-start.20 = (bf16[96,1152]{1,0:T(8,128)(2,1)S(1)}, bf16[96,1152]{1,0:T(8,128)(2,1)S(1)}, u32[]{:S(2)}, u32[]{:S(2)}) collective-permute-start(bf16[96,1152]{1,0:T(8,128)(2,1)S(1)} %constant_dynamic-update-slice_fusion.refs_8_), channel_id=1, source_target_pairs={{0,4},{4,0},{8,12},{12,8},{16,20},{20,16},{24,28},{28,24},{1,5},{5... | collective-permute-start | bytes 663560 | tf_op jit(solution)/shard_map/ppermute | solution.py:182
  41.7 4.8 %collective-permute-start.21 = (bf16[96,1152]{1,0:T(8,128)(2,1)S(1)}, bf16[96,1152]{1,0:T(8,128)(2,1)S(1)}, u32[]{:S(2)}, u32[]{:S(2)}) collective-permute-start(bf16[96,1152]{1,0:T(8,128)(2,1)S(1)} %collective-permute-done.17.refs_9_), channel_id=1, source_target_pairs={{0,4},{4,0},{8,12},{12,8},{16,20},{20,16},{24,28},{28,24},{1,5},{5... | collective-permute-start | bytes 663560 | tf_op jit(solution)/shard_map/ppermute | solution.py:182
  44.6 1.8 %collective-permute-start.22 = (bf16[96,1152]{1,0:T(8,128)(2,1)S(1)}, bf16[96,1152]{1,0:T(8,128)(2,1)S(1)}, u32[]{:S(2)}, u32[]{:S(2)}) collective-permute-start(bf16[96,1152]{1,0:T(8,128)(2,1)S(1)} %collective-permute-done.18.refs_10_), channel_id=1, source_target_pairs={{0,4},{4,0},{8,12},{12,8},{16,20},{20,16},{24,28},{28,24},{1,5},{5... | collective-permute-start | bytes 663560 | tf_op jit(solution)/shard_map/ppermute | solution.py:182
  44.6 1.8 %collective-permute-start.23 = (bf16[96,1152]{1,0:T(8,128)(2,1)S(1)}, bf16[96,1152]{1,0:T(8,128)(2,1)S(1)}, u32[]{:S(2)}, u32[]{:S(2)}) collective-permute-start(bf16[96,1152]{1,0:T(8,128)(2,1)S(1)} %collective-permute-done.19.refs_11_), channel_id=1, source_target_pairs={{0,4},{4,0},{8,12},{12,8},{16,20},{20,16},{24,28},{28,24},{1,5},{5... | collective-permute-start | bytes 663560 | tf_op jit(solution)/shard_map/ppermute | solution.py:182
  45.1 1.3 %collective-permute-start.13 = (bf16[96,128]{1,0:T(8,128)(2,1)S(1)}, bf16[96,128]{1,0:T(8,128)(2,1)S(1)}, u32[]{:S(2)}, u32[]{:S(2)}) collective-permute-start(bf16[96,128]{1,0:T(8,128)(2,1)S(1)} %slice_bitcast_fusion.4), channel_id=1, source_target_pairs={{0,4},{4,0},{8,12},{12,8},{16,20},{20,16},{24,28},{28,24},{1,5},{5... | collective-permute-start | bytes 73736 | tf_op jit(solution)/shard_map/ppermute | solution.py:182

commit v5 on v4

--- a/solution.py
+++ b/solution.py
@@ -12,7 +12,7 @@
 FLIPS = tuple(range(0, HEADS, 2))
 WHOLE = pl.BlockSpec(memory_space=pltpu.VMEM)
 SCALARS = pl.BlockSpec(memory_space=pltpu.SMEM)
-ANYWHERE = pl.BlockSpec(memory_space=pl.ANY)
+IN_HBM = pl.BlockSpec(memory_space=pltpu.HBM)
 
 
 def params(mebibytes=48):
@@ -23,48 +23,44 @@
     return lax.axis_index("ctx") % HEADS
 
 
-def pack_kernel(query_ref, key_ref, value_ref, weight_ref, *refs):
-    outs, share_ref = refs[: len(FLIPS)], refs[len(FLIPS)]
-    rows, turned, sems = refs[len(FLIPS) + 1 :]
-    head_size = outs[0].shape[2]
-    place = place_in_group()
-    first = pl.multiple_of(place * share_ref.shape[0], 32)
-    cut = pltpu.make_async_copy(weight_ref.at[pl.ds(first, share_ref.shape[0])], share_ref, sems.at[3])
+def pack_kernel(query_ref, key_ref, value_ref, *refs):
+    outs = [refs[0:2], *([ref.at[0], ref.at[1]] for ref in refs[2 : 1 + len(FLIPS)])]
+    rows, turned, sems = refs[1 + len(FLIPS) :]
+    head_size = outs[0][0].shape[1]
+    place = place_in_group()
     arrivals = [
         pltpu.make_async_copy(ref.at[0], rows.at[part], sems.at[part])
         for part, ref in enumerate((query_ref, key_ref, value_ref))
     ]
     for copy in arrivals:
         copy.start()
-    cut.start()
     for part, copy in enumerate(arrivals):
         copy.wait()
-        turned[...] = rows[part].T
+        turned[part] = rows[part].T
         for flip, out_ref in zip(FLIPS, outs):
             for other in range(2):
                 head = pl.multiple_of((place ^ (flip + other)) * head_size, 32)
-                out_ref[other, part] = turned[pl.ds(head, head_size), :]
-    cut.wait()
-
-
-def pack(queries, key_rows, value_rows, out_weight):
+                out_ref[other][part] = turned[part, pl.ds(head, head_size), :]
+
+
+def pack(queries, key_rows, value_rows):
     _, frames, features = queries.shape
-    blocks = jax.ShapeDtypeStruct((2, 3, features // HEADS, frames), queries.dtype)
-    share = jax.ShapeDtypeStruct((out_weight.shape[0] // HEADS, out_weight.shape[1]), out_weight.dtype)
-    outs = pl.pallas_call(
+    block = (3, features // HEADS, frames)
+    own = jax.ShapeDtypeStruct(block, queries.dtype)
+    two = jax.ShapeDtypeStruct((2, *block), queries.dtype)
+    return pl.pallas_call(
         pack_kernel,
-        out_shape=[blocks] * len(FLIPS) + [share],
-        in_specs=[ANYWHERE] * 4,
-        out_specs=[WHOLE] * (len(FLIPS) + 1),
+        out_shape=[own] * 2 + [two] * (len(FLIPS) - 1),
+        in_specs=[IN_HBM] * 3,
+        out_specs=[WHOLE] * (1 + len(FLIPS)),
         scratch_shapes=[
             pltpu.VMEM((3, frames, features), queries.dtype),
-            pltpu.VMEM((features, frames), queries.dtype),
-            pltpu.SemaphoreType.DMA((4,)),
+            pltpu.VMEM((3, features, frames), queries.dtype),
+            pltpu.SemaphoreType.DMA((3,)),
         ],
         compiler_params=params(60),
         name="pack_heads",
-    )(queries, key_rows, value_rows, out_weight)
-    return outs[: len(FLIPS)], outs[len(FLIPS)]
+    )(queries, key_rows, value_rows)
 
 
 def attention_kernel(groups, lengths_ref, *refs):
@@ -80,7 +76,9 @@
     first_row = jnp.where(at_row == 0, 1.0, 0.0).astype(keys.dtype)
 
     def piece(flip, part):
-        return same[flip // 2][0, part] if flip % 2 == 0 else other[flip // 2][part]
+        if flip < 2:
+            return (same, other)[flip][0][part]
+        return other[flip // 2][1, part] if flip % 2 else same[flip // 2][0, part]
 
     for at in range(groups * HEADS):
         flip = at % HEADS
@@ -121,7 +119,7 @@
             pltpu.VMEM((padded, keys), jnp.bfloat16),
             pltpu.VMEM((padded, 2 * block), jnp.bfloat16),
         ],
-        compiler_params=params(),
+        compiler_params=params(24),
         cost_estimate=pl.CostEstimate(
             flops=4 * queries * keys * head_size,
             bytes_accessed=4 * (queries + keys) * head_size,
@@ -131,17 +129,25 @@
     )(lengths, *same, *other, *rest)
 
 
+def quarter_of(place, parity, core):
+    return (((place >> 2) ^ (place >> 1) ^ parity) & 1) * 2 + ((place ^ core) & 1)
+
+
 def project_kernel(shards, *refs):
     each = len(FLIPS)
-    heads_same, heads_other, weight_same, weight_other = (refs[at : at + each] for at in range(0, 4 * each, each))
-    own_ref = refs[4 * len(FLIPS)] if shards > 1 else None
+    heads_same, heads_other, halves = refs[:each], refs[each : 2 * each], refs[2 * each : 2 * each + 2]
+    own_ref = refs[2 * each + 2] if shards > 1 else None
     out_ref, turned, weight = refs[-3:]
     place = place_in_group()
     rows = turned.shape[0] // HEADS
     for flip in range(HEADS):
         here = pl.ds(pl.multiple_of((place ^ flip) * rows, 32), rows)
-        turned[here, :] = heads_other[flip // 2][...] if flip % 2 else heads_same[flip // 2][0]
-        weight[here, :] = (weight_other if flip % 2 else weight_same)[flip // 2][...]
+        turned[here, :] = heads_other[flip // 2][1] if flip % 2 else heads_same[flip // 2][0]
+    quarter = weight.shape[0] // 4
+    for core in range(2):
+        for parity in range(2):
+            here = pl.multiple_of(quarter_of(place, parity, core) * quarter, 32)
+            weight[pl.ds(here, quarter), :] = halves[core][parity * quarter : (parity + 1) * quarter, :]
     attention = turned[...].T
     foreign = jnp.dot(attention, weight[...], preferred_element_type=jnp.float32).astype(out_ref.dtype)
     if shards == 1:
@@ -156,19 +162,19 @@
         out_ref[0, :, here] = foreign[:, (flip - 1) * columns : flip * columns]
 
 
-def project(heads_same, heads_other, weight_same, weight_other, own, shards):
-    rows, frames = heads_other[0].shape
-    foreign = weight_same[0].shape[1]
+def project(heads_same, heads_other, near, far, own, shards):
+    _, rows, frames = heads_other[0].shape
+    foreign = near.shape[1]
     width = foreign + (own[0].shape[1] if own else 0)
     features = HEADS * rows
-    pieces = [*heads_same, *heads_other, *weight_same, *weight_other, *own]
+    pieces = [*heads_same, *heads_other, near, far, *own]
     return pl.pallas_call(
         functools.partial(project_kernel, shards),
         out_shape=jax.ShapeDtypeStruct((1, frames, width), jnp.bfloat16),
         in_specs=[WHOLE] * len(pieces),
         out_specs=WHOLE,
         scratch_shapes=[pltpu.VMEM((features, frames), jnp.bfloat16), pltpu.VMEM((features, foreign), jnp.bfloat16)],
-        compiler_params=params(),
+        compiler_params=params(24),
         cost_estimate=pl.CostEstimate(
             flops=2 * features * frames * width, bytes_accessed=2 * features * width, transcendentals=0
         ),
@@ -181,31 +187,44 @@
         size = ctx if axis == "ctx" else fsdp
         return lax.ppermute(array, axis, [(i, i ^ flip) for i in range(size)])
 
-    by_chip, share = pack(queries, key_rows, value_rows, out_weight)
-    split_columns = fsdp in (2, 4)
+    place = place_in_group()
+    rows = out_weight.shape[0] // 4
+    quarter = lax.dynamic_slice_in_dim(out_weight, quarter_of(place, 0, 0) * rows, rows, 0)
+    split_columns = fsdp == 4
     if split_columns:
-        share = jnp.concatenate([exchange(share, "fsdp", flip) for flip in range(1, fsdp)], axis=1)
+        far = exchange(quarter, "fsdp", 2)
+        near = exchange(quarter, "fsdp", 1)
+        quarter = jnp.concatenate([near, far, exchange(far, "fsdp", 1)], axis=1)
     else:
-        share = lax.all_gather(share, "fsdp", axis=1, tiled=True)
-
-    same = [exchange(array, "ctx", flip) if flip else array for flip, array in zip(FLIPS, by_chip)]
-    other = [exchange(array[1], "ctx", 1) for array in same]
-    weight_same = [exchange(share, "ctx", flip) if flip else share for flip in FLIPS]
+        quarter = lax.all_gather(quarter, "fsdp", axis=1, tiled=True)
+
+    own_same, own_other, *by_chip = pack(queries, key_rows, value_rows)
+    same = [exchange(array, "ctx", flip) for flip, array in zip(FLIPS[1:], by_chip)]
+    same = lax.optimization_barrier(same)
+    other = [exchange(array, "ctx", 1) for array in (own_other, *same)]
+    quarter, other = lax.optimization_barrier((quarter, other))
+    first = exchange(quarter[: rows // 2], "ctx", 2)
+    second = exchange(quarter[rows // 2 :], "ctx", 4)
 
     groups = ctx // HEADS
     rest = None
     if groups > 1:
-        pairs = [array for two in zip([a[0, 1:] for a in same], [a[1:] for a in other]) for array in two]
+        pairs = [own_same[1:], other[0][1:]]
+        for one, two in zip(same, other[1:]):
+            pairs += [one[0, 1:], two[1, 1:]]
         across = [[head + first for first in range(0, ctx, HEADS)] for head in range(HEADS)]
         rest = lax.all_gather(jnp.stack(pairs), "ctx", axis=0, axis_index_groups=across, tiled=True)
-    mixed = attend(lengths, same, other, rest, groups)
-
+    mixed = attend(lengths, [own_same, *same], other, rest, groups)
+
+    first, second, last = lax.optimization_barrier((first, second, mixed[-1]))
+    mixed = [*mixed[:-1], last]
     heads_same = [exchange(array, "ctx", flip) if flip else array for flip, array in zip(FLIPS, mixed)]
-    heads_other = [exchange(array[1], "ctx", 1) for array in heads_same]
-    weight_same, _ = lax.optimization_barrier((weight_same, mixed))
-    weight_other = [exchange(array, "ctx", 1) for array in weight_same]
+    near = jnp.concatenate([quarter, first, second], axis=0)
+    near, heads_same = lax.optimization_barrier((near, heads_same))
+    heads_other = [exchange(array, "ctx", 1) for array in heads_same]
+    far = exchange(near, "ctx", 1)
     own = [out_weight] if split_columns else []
-    return project(heads_same, heads_other, weight_same, weight_other, own, fsdp if split_columns else 1)
+    return project(heads_same, heads_other, near, far, own, fsdp if split_columns else 1)
 
 
 def solution(mesh):

time: 48.1 us -> 37.7 us (0.78)
  waiting for transfers between devices: 18.7 us -> 12.5 us
  starting transfers between devices: 20.6 us -> 16.4 us
    ppermute x24 -> x20, waiting for transfers between devices: 18.7 us -> 12.5 us  [exchange(): return lax.ppermute(array, axis, [(i, i ^ flip) for i in range(size)])]
    ppermute x24 -> x20, starting transfers between devices: 20.6 us -> 16.4 us  [exchange(): return lax.ppermute(array, axis, [(i, i ^ flip) for i in range(size)])]
    squeeze x8 -> x0, local copies, waits for them, and re-layouts: 0.96 us -> none  [the longest x4 0.95 us: per_device(): other = [exchange(array[1], 'ctx', 1) for array in same]]
    dynamic_slice x0 -> x1, local copies, waits for them, and re-layouts: none -> 0.92 us  [per_device(): lax.dynamic_slice_in_dim(out_weight, quarter_of(place, 0, 0) * rows, rows...]
  transfers between devices with their start and end apart: 24 -> 20, of which waited for: 6 -> 13; matrix products, arithmetic and copies ran while one was open for 2% -> 0% of each run, Pallas kernels for 7% -> 14%
where the time goes in v5:
time: 37.7 us; the launch traced here: 37.6 us
  starting transfers between devices  16.4 us (44%)
  waiting for transfers between devices  12.5 us (33%)
  Pallas kernels  6.89 us (18%)
  local copies, waits for them, and re-layouts  0.97 us (3%)
  between operations  0.73 us (2%)
    ppermute x20, starting transfers between devices, exchange(): return lax.ppermute(array, axis, [(i, i ^ flip) for i in range(size)])  16.4 us
    ppermute x20, waiting for transfers between devices, exchange(): return lax.ppermute(array, axis, [(i, i ^ flip) for i in range(size)])  12.5 us
    pallas_call x1, Pallas kernels, attend(): pl.pallas_call(functools.partial(attention_kernel, groups), out_shape=[ja...  3.19 us
    pallas_call x1, Pallas kernels, pack(): pl.pallas_call(pack_kernel, out_shape=[own] * 2 + [two] * (len(FLIPS) - 1...  2.1 us
    pallas_call x1, Pallas kernels, project(): pl.pallas_call(functools.partial(project_kernel, shards), out_shape=jax.S...  1.61 us
    dynamic_slice x1, local copies, waits for them, and re-layouts, per_device(): lax.dynamic_slice_in_dim(out_weight, quarter_of(place, 0, 0) * rows, rows...  0.92 us
  transfers between devices with their start and end apart: 20, of which 13 were waited for; matrix products, arithmetic and copies ran while one was open for 0% of the time, Pallas kernels for 14%

profile of v5, /device:TPU:0, one launch (start us, length us, event | category | flops | bytes accessed | tf_op | source)
XLA Modules:
  0.0 37.6 jit_solution(1407184369643855756)
XLA Ops:
  0.0 0.9 %constant_dynamic-slice_fusion = bf16[192,384]{1,0:T(8,128)(2,1)S(1)} fusion(bf16[768,384]{1,0:T(8,128)(2,1)} %refs_10_.1, s32[]{:T(128)S(6)} %select_n.11), kind=kLoop, calls=%fused_computation.2 | loop fusion | bytes 294916 | tf_op jit(solution)/shard_map/dynamic_slice | solution.py:192
  0.9 4.1 %collective-permute-start.1 = (bf16[192,384]{1,0:T(8,128)(2,1)S(1)}, bf16[192,384]{1,0:T(8,128)(2,1)S(1)}, u32[]{:S(2)}, u32[]{:S(2)}) collective-permute-start(bf16[192,384]{1,0:T(8,128)(2,1)S(1)} %constant_dynamic-slice_fusion), channel_id=1, source_target_pairs={{0,2},{1,3},{2,0},{3,1},{4,6},{5,7},{6,4},{7,5},{8,10},{9,11},{10,... | collective-permute-start | bytes 442376 | tf_op jit(solution)/shard_map/ppermute | solution.py:188
  5.0 2.1 %pack_heads.1 = (bf16[3,96,128]{2,1,0:T(8,128)(2,1)}, bf16[3,96,128]{2,1,0:T(8,128)(2,1)}, bf16[2,3,96,128]{3,2,1,0:T(8,128)(2,1)}, bf16[2,3,96,128]{3,2,1,0:T(8,128)(2,1)}, bf16[2,3,96,128]{3,2,1,0:T(8,128)(2,1)}) custom-call(bf16[1,128,768]{2,1,0:T(8,128)(2,1)} %query_ref.1, bf16[1,128,768]{2,1,0:T(8,128)(2,1)} %key_ref.1, bf16[1,128,768]{2,1,0:T(8,128)(2,1)} %value_ref.1), custom_call_target="tpu_custom_call" | custom-call | tf_op jit(solution)/shard_map/pack_heads/pallas_call | solution.py:51
  7.1 1.6 %collective-permute-start.4 = (bf16[2,3,96,128]{3,2,1,0:T(8,128)(2,1)}, bf16[2,3,96,128]{3,2,1,0:T(8,128)(2,1)S(1)}, u32[]{:S(2)}, u32[]{:S(2)}) collective-permute-start(bf16[2,3,96,128]{3,2,1,0:T(8,128)(2,1)} %get-tuple-element.31), channel_id=1, source_target_pairs={{0,8},{4,12},{8,0},{12,4},{16,24},{20,28},{24,16},{28,20},{1,9},{5... | collective-permute-start | bytes 442376 | tf_op jit(solution)/shard_map/ppermute | solution.py:188
  8.7 1.5 %collective-permute-start.5 = (bf16[2,3,96,128]{3,2,1,0:T(8,128)(2,1)}, bf16[2,3,96,128]{3,2,1,0:T(8,128)(2,1)S(1)}, u32[]{:S(2)}, u32[]{:S(2)}) collective-permute-start(bf16[2,3,96,128]{3,2,1,0:T(8,128)(2,1)} %get-tuple-element.32), channel_id=1, source_target_pairs={{0,16},{4,20},{8,24},{12,28},{16,0},{20,4},{24,8},{28,12},{1,17},{... | collective-permute-start | bytes 442376 | tf_op jit(solution)/shard_map/ppermute | solution.py:188
  10.2 0.5 %collective-permute-start.6 = (bf16[2,3,96,128]{3,2,1,0:T(8,128)(2,1)}, bf16[2,3,96,128]{3,2,1,0:T(8,128)(2,1)S(1)}, u32[]{:S(2)}, u32[]{:S(2)}) collective-permute-start(bf16[2,3,96,128]{3,2,1,0:T(8,128)(2,1)} %get-tuple-element.33), channel_id=1, source_target_pairs={{0,24},{4,28},{8,16},{12,20},{16,8},{20,12},{24,0},{28,4},{1,25},{... | collective-permute-start | bytes 442376 | tf_op jit(solution)/shard_map/ppermute | solution.py:188
  10.7 1.6 %collective-permute-start = (bf16[192,384]{1,0:T(8,128)(2,1)S(1)}, bf16[192,384]{1,0:T(8,128)(2,1)S(1)}, u32[]{:S(2)}, u32[]{:S(2)}) collective-permute-start(bf16[192,384]{1,0:T(8,128)(2,1)S(1)} %constant_dynamic-slice_fusion), channel_id=1, source_target_pairs={{0,1},{1,0},{2,3},{3,2},{4,5},{5,4},{6,7},{7,6},{8,9},{9,8},{10,11... | collective-permute-start | bytes 442376 | tf_op jit(solution)/shard_map/ppermute | solution.py:188
  12.3 0.0 collective-permute-done.1
  12.3 0.5 %collective-permute-start.2 = (bf16[192,384]{1,0:T(8,128)(2,1)S(1)}, bf16[192,384]{1,0:T(8,128)(2,1)S(1)}, u32[]{:S(2)}, u32[]{:S(2)}) collective-permute-start(bf16[192,384]{1,0:T(8,128)(2,1)S(1)} %collective-permute-done.1), channel_id=1, source_target_pairs={{0,1},{1,0},{2,3},{3,2},{4,5},{5,4},{6,7},{7,6},{8,9},{9,8},{10,11... | collective-permute-start | bytes 442376 | tf_op jit(solution)/shard_map/ppermute | solution.py:188
  12.8 0.7 %collective-permute-done.4.refs_1_ = bf16[2,3,96,128]{3,2,1,0:T(8,128)(2,1)S(1)} collective-permute-done((bf16[2,3,96,128]{3,2,1,0:T(8,128)(2,1)}, bf16[2,3,96,128]{3,2,1,0:T(8,128)(2,1)S(1)}, u32[]{:S(2)}, u32[]{:S(2)}) %collective-permute-start.4) | collective-permute-done | bytes 147488 | tf_op jit(solution)/shard_map/ppermute | solution.py:188
  13.5 0.0 copy-start.1
  13.5 0.0 collective-permute-start.3
  13.5 3.7 %collective-permute-done.5.refs_2_ = bf16[2,3,96,128]{3,2,1,0:T(8,128)(2,1)S(1)} collective-permute-done((bf16[2,3,96,128]{3,2,1,0:T(8,128)(2,1)}, bf16[2,3,96,128]{3,2,1,0:T(8,128)(2,1)S(1)}, u32[]{:S(2)}, u32[]{:S(2)}) %collective-permute-start.5) | collective-permute-done | bytes 147488 | tf_op jit(solution)/shard_map/ppermute | solution.py:188
  17.2 0.0 collective-permute-done.6.refs_3_
  17.2 0.0 collective-permute-start.7
  17.2 0.5 %collective-permute-start.8 = (bf16[2,3,96,128]{3,2,1,0:T(8,128)(2,1)S(1)}, bf16[2,3,96,128]{3,2,1,0:T(8,128)(2,1)S(1)}, u32[]{:S(2)}, u32[]{:S(2)}) collective-permute-start(bf16[2,3,96,128]{3,2,1,0:T(8,128)(2,1)S(1)} %collective-permute-done.5.refs_2_), channel_id=1, source_target_pairs={{0,4},{4,0},{8,12},{12,8},{16,20},{20,16},{24,28},{28,24},{1,5},{5... | collective-permute-start | bytes 442376 | tf_op jit(solution)/shard_map/ppermute | solution.py:188
  17.7 0.0 collective-permute-done
  17.7 0.0 collective-permute-start.9
  17.7 0.9 %collective-permute-done.2 = bf16[192,384]{1,0:T(8,128)(2,1)S(1)} collective-permute-done((bf16[192,384]{1,0:T(8,128)(2,1)S(1)}, bf16[192,384]{1,0:T(8,128)(2,1)S(1)}, u32[]{:S(2)}, u32[]{:S(2)}) %collective-permute-start.2) | collective-permute-done | bytes 147488 | tf_op jit(solution)/shard_map/ppermute | solution.py:188
  18.7 0.0 collective-permute-done.3.refs_4_
  18.7 0.0 collective-permute-done.7.refs_5_
  18.7 0.1 collective-permute-done.8.refs_6_
  18.8 0.3 collective-permute-done.9.refs_7_
  19.1 1.5 %collective-permute-start.11 = (bf16[96,1152]{1,0:T(8,128)(2,1)S(1)}, bf16[96,1152]{1,0:T(8,128)(2,1)S(1)}, u32[]{:S(2)}, u32[]{:S(2)}) collective-permute-start(bf16[96,1152]{1,0:T(8,128)(2,1)S(1)} %get-tuple-element.55), channel_id=1, source_target_pairs={{0,16},{4,20},{8,24},{12,28},{16,0},{20,4},{24,8},{28,12},{1,17},{... | collective-permute-start | bytes 663560 | tf_op jit(solution)/shard_map/ppermute | solution.py:188
  20.6 1.0 %collective-permute-start.10 = (bf16[96,1152]{1,0:T(8,128)(2,1)S(1)}, bf16[96,1152]{1,0:T(8,128)(2,1)S(1)}, u32[]{:S(2)}, u32[]{:S(2)}) collective-permute-start(bf16[96,1152]{1,0:T(8,128)(2,1)S(1)} %get-tuple-element.56), channel_id=1, source_target_pairs={{0,8},{4,12},{8,0},{12,4},{16,24},{20,28},{24,16},{28,20},{1,9},{5... | collective-permute-start | bytes 663560 | tf_op jit(solution)/shard_map/ppermute | solution.py:188
  22.3 0.0 copy-done.1
  22.3 3.2 %attend_one_head.1 = (bf16[2,96,128]{2,1,0:T(8,128)(2,1)S(1)}, bf16[2,96,128]{2,1,0:T(8,128)(2,1)S(1)}, bf16[2,96,128]{2,1,0:T(8,128)(2,1)S(1)}, bf16[2,96,128]{2,1,0:T(8,128)(2,1)S(1)}) custom-call(s32[1]{0:T(128)S(6)} %copy.6.lengths_ref, bf16[3,96,128]{2,1,0:T(8,128)(2,1)S(1)} %copy-done.1, bf16[2,3,96,128]{3,2,1,0:T(8,128)(2,1)S(1)} %collective-permute-done.4.refs_1_, ...), custom_call_target="tpu_custom_call" | custom-call | flops 402653184 | bytes 786432 | tf_op jit(solution)/shard_map/attend_one_head/pallas_call | solution.py:112
  25.5 1.1 %collective-permute-start.12 = (bf16[2,96,128]{2,1,0:T(8,128)(2,1)S(1)}, bf16[2,96,128]{2,1,0:T(8,128)(2,1)S(1)}, u32[]{:S(2)}, u32[]{:S(2)}) collective-permute-start(bf16[2,96,128]{2,1,0:T(8,128)(2,1)S(1)} %get-tuple-element.47), channel_id=1, source_target_pairs={{0,8},{4,12},{8,0},{12,4},{16,24},{20,28},{24,16},{28,20},{1,9},{5... | collective-permute-start | bytes 147464 | tf_op jit(solution)/shard_map/ppermute | solution.py:188
  26.6 0.6 %collective-permute-start.13 = (bf16[2,96,128]{2,1,0:T(8,128)(2,1)S(1)}, bf16[2,96,128]{2,1,0:T(8,128)(2,1)S(1)}, u32[]{:S(2)}, u32[]{:S(2)}) collective-permute-start(bf16[2,96,128]{2,1,0:T(8,128)(2,1)S(1)} %get-tuple-element.48), channel_id=1, source_target_pairs={{0,16},{4,20},{8,24},{12,28},{16,0},{20,4},{24,8},{28,12},{1,17},{... | collective-permute-start | bytes 147464 | tf_op jit(solution)/shard_map/ppermute | solution.py:188
  27.2 0.0 collective-permute-done.11
  27.2 1.1 %collective-permute-done.10 = bf16[96,1152]{1,0:T(8,128)(2,1)S(1)} collective-permute-done((bf16[96,1152]{1,0:T(8,128)(2,1)S(1)}, bf16[96,1152]{1,0:T(8,128)(2,1)S(1)}, u32[]{:S(2)}, u32[]{:S(2)}) %collective-permute-start.10) | collective-permute-done | bytes 221216 | tf_op jit(solution)/shard_map/ppermute | solution.py:188
  28.3 0.9 %collective-permute-start.14 = (bf16[2,96,128]{2,1,0:T(8,128)(2,1)S(1)}, bf16[2,96,128]{2,1,0:T(8,128)(2,1)S(1)}, u32[]{:S(2)}, u32[]{:S(2)}) collective-permute-start(bf16[2,96,128]{2,1,0:T(8,128)(2,1)S(1)} %get-tuple-element.49), channel_id=1, source_target_pairs={{0,24},{4,28},{8,16},{12,20},{16,8},{20,12},{24,0},{28,4},{1,25},{... | collective-permute-start | bytes 147464 | tf_op jit(solution)/shard_map/ppermute | solution.py:188
  29.2 0.1 pad_maximum_fusion.refs_8_
  29.3 0.4 collective-permute-done.12.refs_1_
  29.6 1.6 %collective-permute-done.13.refs_2_ = bf16[2,96,128]{2,1,0:T(8,128)(2,1)S(1)} collective-permute-done((bf16[2,96,128]{2,1,0:T(8,128)(2,1)S(1)}, bf16[2,96,128]{2,1,0:T(8,128)(2,1)S(1)}, u32[]{:S(2)}, u32[]{:S(2)}) %collective-permute-start.13) | collective-permute-done | bytes 49184 | tf_op jit(solution)/shard_map/ppermute | solution.py:188
  31.2 2.1 %collective-permute-done.14.refs_3_ = bf16[2,96,128]{2,1,0:T(8,128)(2,1)S(1)} collective-permute-done((bf16[2,96,128]{2,1,0:T(8,128)(2,1)S(1)}, bf16[2,96,128]{2,1,0:T(8,128)(2,1)S(1)}, u32[]{:S(2)}, u32[]{:S(2)}) %collective-permute-start.14) | collective-permute-done | bytes 49184 | tf_op jit(solution)/shard_map/ppermute | solution.py:188
  33.3 0.0 collective-permute-start.19
  33.3 0.5 %collective-permute-start.15 = (bf16[2,96,128]{2,1,0:T(8,128)(2,1)S(1)}, bf16[2,96,128]{2,1,0:T(8,128)(2,1)S(1)}, u32[]{:S(2)}, u32[]{:S(2)}) collective-permute-start(bf16[2,96,128]{2,1,0:T(8,128)(2,1)S(1)} %get-tuple-element.50.refs_0_), channel_id=1, source_target_pairs={{0,4},{4,0},{8,12},{12,8},{16,20},{20,16},{24,28},{28,24},{1,5},{5... | collective-permute-start | bytes 147464 | tf_op jit(solution)/shard_map/ppermute | solution.py:188
  33.8 0.0 collective-permute-start.16
  33.8 0.5 %collective-permute-start.17 = (bf16[2,96,128]{2,1,0:T(8,128)(2,1)S(1)}, bf16[2,96,128]{2,1,0:T(8,128)(2,1)S(1)}, u32[]{:S(2)}, u32[]{:S(2)}) collective-permute-start(bf16[2,96,128]{2,1,0:T(8,128)(2,1)S(1)} %collective-permute-done.13.refs_2_), channel_id=1, source_target_pairs={{0,4},{4,0},{8,12},{12,8},{16,20},{20,16},{24,28},{28,24},{1,5},{5... | collective-permute-start | bytes 147464 | tf_op jit(solution)/shard_map/ppermute | solution.py:188
  34.3 0.0 collective-permute-start.18
  34.3 1.5 %collective-permute-done.15.refs_4_ = bf16[2,96,128]{2,1,0:T(8,128)(2,1)S(1)} collective-permute-done((bf16[2,96,128]{2,1,0:T(8,128)(2,1)S(1)}, bf16[2,96,128]{2,1,0:T(8,128)(2,1)S(1)}, u32[]{:S(2)}, u32[]{:S(2)}) %collective-permute-start.15) | collective-permute-done | bytes 49184 | tf_op jit(solution)/shard_map/ppermute | solution.py:188
  35.8 0.1 collective-permute-done.16.refs_5_
  35.8 0.1 collective-permute-done.17.refs_6_
  35.9 0.1 collective-permute-done.18.refs_7_
  36.0 0.0 collective-permute-done.19.refs_9_
  36.0 0.0 copy-done
  36.0 1.6 %project_heads.1 = bf16[1,128,1536]{2,1,0:T(8,128)(2,1)} custom-call(bf16[2,96,128]{2,1,0:T(8,128)(2,1)S(1)} %get-tuple-element.50.refs_0_, bf16[2,96,128]{2,1,0:T(8,128)(2,1)S(1)} %collective-permute-done.12.refs_1_, bf16[2,96,128]{2,1,0:T(8,128)(2,1)S(1)} %collective-permute-done.13.refs_2_, bf16[2,96,128]{2,1,0:T(8,128)(2,1)S(1)} %collective-permute-done.14.refs_3_, ...), custom_call_target="tpu_custom_call" | custom-call | flops 301989888 | bytes 2359296 | tf_op jit(solution)/shard_map/project_heads/pallas_call | solution.py:171
  (3 shorter events, 0.1 us)
Async XLA Ops:
  0.9 11.3 %collective-permute-start.1 = (bf16[192,384]{1,0:T(8,128)(2,1)S(1)}, bf16[192,384]{1,0:T(8,128)(2,1)S(1)}, u32[]{:S(2)}, u32[]{:S(2)}) collective-permute-start(bf16[192,384]{1,0:T(8,128)(2,1)S(1)} %constant_dynamic-slice_fusion), channel_id=1, source_target_pairs={{0,2},{1,3},{2,0},{3,1},{4,6},{5,7},{6,4},{7,5},{8,10},{9,11},{10,... | collective-permute-start | bytes 442376 | tf_op jit(solution)/shard_map/ppermute | solution.py:188
  7.1 6.4 %collective-permute-start.4 = (bf16[2,3,96,128]{3,2,1,0:T(8,128)(2,1)}, bf16[2,3,96,128]{3,2,1,0:T(8,128)(2,1)S(1)}, u32[]{:S(2)}, u32[]{:S(2)}) collective-permute-start(bf16[2,3,96,128]{3,2,1,0:T(8,128)(2,1)} %get-tuple-element.31), channel_id=1, source_target_pairs={{0,8},{4,12},{8,0},{12,4},{16,24},{20,28},{24,16},{28,20},{1,9},{5... | collective-permute-start | bytes 442376 | tf_op jit(solution)/shard_map/ppermute | solution.py:188
  8.7 8.5 %collective-permute-start.5 = (bf16[2,3,96,128]{3,2,1,0:T(8,128)(2,1)}, bf16[2,3,96,128]{3,2,1,0:T(8,128)(2,1)S(1)}, u32[]{:S(2)}, u32[]{:S(2)}) collective-permute-start(bf16[2,3,96,128]{3,2,1,0:T(8,128)(2,1)} %get-tuple-element.32), channel_id=1, source_target_pairs={{0,16},{4,20},{8,24},{12,28},{16,0},{20,4},{24,8},{28,12},{1,17},{... | collective-permute-start | bytes 442376 | tf_op jit(solution)/shard_map/ppermute | solution.py:188
  10.2 7.0 %collective-permute-start.6 = (bf16[2,3,96,128]{3,2,1,0:T(8,128)(2,1)}, bf16[2,3,96,128]{3,2,1,0:T(8,128)(2,1)S(1)}, u32[]{:S(2)}, u32[]{:S(2)}) collective-permute-start(bf16[2,3,96,128]{3,2,1,0:T(8,128)(2,1)} %get-tuple-element.33), channel_id=1, source_target_pairs={{0,24},{4,28},{8,16},{12,20},{16,8},{20,12},{24,0},{28,4},{1,25},{... | collective-permute-start | bytes 442376 | tf_op jit(solution)/shard_map/ppermute | solution.py:188
  10.7 7.0 %collective-permute-start = (bf16[192,384]{1,0:T(8,128)(2,1)S(1)}, bf16[192,384]{1,0:T(8,128)(2,1)S(1)}, u32[]{:S(2)}, u32[]{:S(2)}) collective-permute-start(bf16[192,384]{1,0:T(8,128)(2,1)S(1)} %constant_dynamic-slice_fusion), channel_id=1, source_target_pairs={{0,1},{1,0},{2,3},{3,2},{4,5},{5,4},{6,7},{7,6},{8,9},{9,8},{10,11... | collective-permute-start | bytes 442376 | tf_op jit(solution)/shard_map/ppermute | solution.py:188
  12.3 6.4 %collective-permute-start.2 = (bf16[192,384]{1,0:T(8,128)(2,1)S(1)}, bf16[192,384]{1,0:T(8,128)(2,1)S(1)}, u32[]{:S(2)}, u32[]{:S(2)}) collective-permute-start(bf16[192,384]{1,0:T(8,128)(2,1)S(1)} %collective-permute-done.1), channel_id=1, source_target_pairs={{0,1},{1,0},{2,3},{3,2},{4,5},{5,4},{6,7},{7,6},{8,9},{9,8},{10,11... | collective-permute-start | bytes 442376 | tf_op jit(solution)/shard_map/ppermute | solution.py:188
  13.5 8.8 %copy-start.1 = (bf16[3,96,128]{2,1,0:T(8,128)(2,1)S(1)}, bf16[3,96,128]{2,1,0:T(8,128)(2,1)}, u32[]{:S(2)}) copy-start(bf16[3,96,128]{2,1,0:T(8,128)(2,1)} %get-tuple-element.38.refs_0_) | copy-start | bytes 221188
  13.5 5.2 %collective-permute-start.3 = (bf16[3,96,128]{2,1,0:T(8,128)(2,1)}, bf16[3,96,128]{2,1,0:T(8,128)(2,1)S(1)}, u32[]{:S(2)}, u32[]{:S(2)}) collective-permute-start(bf16[3,96,128]{2,1,0:T(8,128)(2,1)} %get-tuple-element.30), channel_id=1, source_target_pairs={{0,4},{4,0},{8,12},{12,8},{16,20},{20,16},{24,28},{28,24},{1,5},{5... | collective-permute-start | bytes 221192 | tf_op jit(solution)/shard_map/ppermute | solution.py:188
  17.2 1.5 %collective-permute-start.7 = (bf16[2,3,96,128]{3,2,1,0:T(8,128)(2,1)S(1)}, bf16[2,3,96,128]{3,2,1,0:T(8,128)(2,1)S(1)}, u32[]{:S(2)}, u32[]{:S(2)}) collective-permute-start(bf16[2,3,96,128]{3,2,1,0:T(8,128)(2,1)S(1)} %collective-permute-done.4.refs_1_), channel_id=1, source_target_pairs={{0,4},{4,0},{8,12},{12,8},{16,20},{20,16},{24,28},{28,24},{1,5},{5... | collective-permute-start | bytes 442376 | tf_op jit(solution)/shard_map/ppermute | solution.py:188
  17.2 1.6 %collective-permute-start.8 = (bf16[2,3,96,128]{3,2,1,0:T(8,128)(2,1)S(1)}, bf16[2,3,96,128]{3,2,1,0:T(8,128)(2,1)S(1)}, u32[]{:S(2)}, u32[]{:S(2)}) collective-permute-start(bf16[2,3,96,128]{3,2,1,0:T(8,128)(2,1)S(1)} %collective-permute-done.5.refs_2_), channel_id=1, source_target_pairs={{0,4},{4,0},{8,12},{12,8},{16,20},{20,16},{24,28},{28,24},{1,5},{5... | collective-permute-start | bytes 442376 | tf_op jit(solution)/shard_map/ppermute | solution.py:188
  17.7 1.4 %collective-permute-start.9 = (bf16[2,3,96,128]{3,2,1,0:T(8,128)(2,1)S(1)}, bf16[2,3,96,128]{3,2,1,0:T(8,128)(2,1)S(1)}, u32[]{:S(2)}, u32[]{:S(2)}) collective-permute-start(bf16[2,3,96,128]{3,2,1,0:T(8,128)(2,1)S(1)} %collective-permute-done.6.refs_3_), channel_id=1, source_target_pairs={{0,4},{4,0},{8,12},{12,8},{16,20},{20,16},{24,28},{28,24},{1,5},{5... | collective-permute-start | bytes 442376 | tf_op jit(solution)/shard_map/ppermute | solution.py:188
  19.1 8.0 %collective-permute-start.11 = (bf16[96,1152]{1,0:T(8,128)(2,1)S(1)}, bf16[96,1152]{1,0:T(8,128)(2,1)S(1)}, u32[]{:S(2)}, u32[]{:S(2)}) collective-permute-start(bf16[96,1152]{1,0:T(8,128)(2,1)S(1)} %get-tuple-element.55), channel_id=1, source_target_pairs={{0,16},{4,20},{8,24},{12,28},{16,0},{20,4},{24,8},{28,12},{1,17},{... | collective-permute-start | bytes 663560 | tf_op jit(solution)/shard_map/ppermute | solution.py:188
  20.6 7.6 %collective-permute-start.10 = (bf16[96,1152]{1,0:T(8,128)(2,1)S(1)}, bf16[96,1152]{1,0:T(8,128)(2,1)S(1)}, u32[]{:S(2)}, u32[]{:S(2)}) collective-permute-start(bf16[96,1152]{1,0:T(8,128)(2,1)S(1)} %get-tuple-element.56), channel_id=1, source_target_pairs={{0,8},{4,12},{8,0},{12,4},{16,24},{20,28},{24,16},{28,20},{1,9},{5... | collective-permute-start | bytes 663560 | tf_op jit(solution)/shard_map/ppermute | solution.py:188
  25.5 4.2 %collective-permute-start.12 = (bf16[2,96,128]{2,1,0:T(8,128)(2,1)S(1)}, bf16[2,96,128]{2,1,0:T(8,128)(2,1)S(1)}, u32[]{:S(2)}, u32[]{:S(2)}) collective-permute-start(bf16[2,96,128]{2,1,0:T(8,128)(2,1)S(1)} %get-tuple-element.47), channel_id=1, source_target_pairs={{0,8},{4,12},{8,0},{12,4},{16,24},{20,28},{24,16},{28,20},{1,9},{5... | collective-permute-start | bytes 147464 | tf_op jit(solution)/shard_map/ppermute | solution.py:188
  26.6 4.6 %collective-permute-start.13 = (bf16[2,96,128]{2,1,0:T(8,128)(2,1)S(1)}, bf16[2,96,128]{2,1,0:T(8,128)(2,1)S(1)}, u32[]{:S(2)}, u32[]{:S(2)}) collective-permute-start(bf16[2,96,128]{2,1,0:T(8,128)(2,1)S(1)} %get-tuple-element.48), channel_id=1, source_target_pairs={{0,16},{4,20},{8,24},{12,28},{16,0},{20,4},{24,8},{28,12},{1,17},{... | collective-permute-start | bytes 147464 | tf_op jit(solution)/shard_map/ppermute | solution.py:188
  28.3 7.7 %copy-start = (bf16[768,384]{1,0:T(8,128)(2,1)S(1)}, bf16[768,384]{1,0:T(8,128)(2,1)}, u32[]{:S(2)}) copy-start(bf16[768,384]{1,0:T(8,128)(2,1)} %refs_10_.1) | copy-start | bytes 1769476
  28.3 5.0 %collective-permute-start.14 = (bf16[2,96,128]{2,1,0:T(8,128)(2,1)S(1)}, bf16[2,96,128]{2,1,0:T(8,128)(2,1)S(1)}, u32[]{:S(2)}, u32[]{:S(2)}) collective-permute-start(bf16[2,96,128]{2,1,0:T(8,128)(2,1)S(1)} %get-tuple-element.49), channel_id=1, source_target_pairs={{0,24},{4,28},{8,16},{12,20},{16,8},{20,12},{24,0},{28,4},{1,25},{... | collective-permute-start | bytes 147464 | tf_op jit(solution)/shard_map/ppermute | solution.py:188
  33.3 2.7 %collective-permute-start.19 = (bf16[384,1152]{1,0:T(8,128)(2,1)S(1)}, bf16[384,1152]{1,0:T(8,128)(2,1)S(1)}, u32[]{:S(2)}, u32[]{:S(2)}) collective-permute-start(bf16[384,1152]{1,0:T(8,128)(2,1)S(1)} %pad_maximum_fusion.refs_8_), channel_id=1, source_target_pairs={{0,4},{4,0},{8,12},{12,8},{16,20},{20,16},{24,28},{28,24},{1,5},{5... | collective-permute-start | bytes 2654216 | tf_op jit(solution)/shard_map/ppermute | solution.py:188
  33.3 2.5 %collective-permute-start.15 = (bf16[2,96,128]{2,1,0:T(8,128)(2,1)S(1)}, bf16[2,96,128]{2,1,0:T(8,128)(2,1)S(1)}, u32[]{:S(2)}, u32[]{:S(2)}) collective-permute-start(bf16[2,96,128]{2,1,0:T(8,128)(2,1)S(1)} %get-tuple-element.50.refs_0_), channel_id=1, source_target_pairs={{0,4},{4,0},{8,12},{12,8},{16,20},{20,16},{24,28},{28,24},{1,5},{5... | collective-permute-start | bytes 147464 | tf_op jit(solution)/shard_map/ppermute | solution.py:188
  33.8 2.1 %collective-permute-start.16 = (bf16[2,96,128]{2,1,0:T(8,128)(2,1)S(1)}, bf16[2,96,128]{2,1,0:T(8,128)(2,1)S(1)}, u32[]{:S(2)}, u32[]{:S(2)}) collective-permute-start(bf16[2,96,128]{2,1,0:T(8,128)(2,1)S(1)} %collective-permute-done.12.refs_1_), channel_id=1, source_target_pairs={{0,4},{4,0},{8,12},{12,8},{16,20},{20,16},{24,28},{28,24},{1,5},{5... | collective-permute-start | bytes 147464 | tf_op jit(solution)/shard_map/ppermute | solution.py:188
  33.8 2.1 %collective-permute-start.17 = (bf16[2,96,128]{2,1,0:T(8,128)(2,1)S(1)}, bf16[2,96,128]{2,1,0:T(8,128)(2,1)S(1)}, u32[]{:S(2)}, u32[]{:S(2)}) collective-permute-start(bf16[2,96,128]{2,1,0:T(8,128)(2,1)S(1)} %collective-permute-done.13.refs_2_), channel_id=1, source_target_pairs={{0,4},{4,0},{8,12},{12,8},{16,20},{20,16},{24,28},{28,24},{1,5},{5... | collective-permute-start | bytes 147464 | tf_op jit(solution)/shard_map/ppermute | solution.py:188
  34.3 1.7 %collective-permute-start.18 = (bf16[2,96,128]{2,1,0:T(8,128)(2,1)S(1)}, bf16[2,96,128]{2,1,0:T(8,128)(2,1)S(1)}, u32[]{:S(2)}, u32[]{:S(2)}) collective-permute-start(bf16[2,96,128]{2,1,0:T(8,128)(2,1)S(1)} %collective-permute-done.14.refs_3_), channel_id=1, source_target_pairs={{0,4},{4,0},{8,12},{12,8},{16,20},{20,16},{24,28},{28,24},{1,5},{5... | collective-permute-start | bytes 147464 | tf_op jit(solution)/shard_map/ppermute | solution.py:188

commit v6 on v5

--- a/solution.py
+++ b/solution.py
@@ -11,7 +11,6 @@
 HEADS = 8
 FLIPS = tuple(range(0, HEADS, 2))
 WHOLE = pl.BlockSpec(memory_space=pltpu.VMEM)
-SCALARS = pl.BlockSpec(memory_space=pltpu.SMEM)
 IN_HBM = pl.BlockSpec(memory_space=pltpu.HBM)
 
 
@@ -46,8 +45,8 @@
 def pack(queries, key_rows, value_rows):
     _, frames, features = queries.shape
     block = (3, features // HEADS, frames)
-    own = jax.ShapeDtypeStruct(block, queries.dtype)
-    two = jax.ShapeDtypeStruct((2, *block), queries.dtype)
+    own = pltpu.VMEM(block, queries.dtype)
+    two = pltpu.VMEM((2, *block), queries.dtype)
     return pl.pallas_call(
         pack_kernel,
         out_shape=[own] * 2 + [two] * (len(FLIPS) - 1),
@@ -58,43 +57,47 @@
             pltpu.VMEM((3, features, frames), queries.dtype),
             pltpu.SemaphoreType.DMA((3,)),
         ],
-        compiler_params=params(60),
+        compiler_params=params(24),
         name="pack_heads",
-    )(queries, key_rows, value_rows)
+    )(*(pltpu.with_memory_space_constraint(array, pltpu.HBM) for array in (queries, key_rows, value_rows)))
 
 
 def attention_kernel(groups, lengths_ref, *refs):
     same, other = refs[: len(FLIPS)], refs[len(FLIPS) : 2 * len(FLIPS)]
     rest_ref = refs[2 * len(FLIPS)] if groups > 1 else None
-    outs, (keys, values, query) = refs[-3 - len(FLIPS) : -3], refs[-3:]
+    outs, (keys, values) = refs[-2 - len(FLIPS) : -2], refs[-2:]
     head_size, block = outs[0].shape[1:]
     place = place_in_group()
     scale = jnp.float32(math.log2(math.e) / math.sqrt(head_size))
     pad = keys.shape[1] - head_size
-    at_row = lax.broadcasted_iota(jnp.int32, (pad, block), 0)
-    at_frame = lax.broadcasted_iota(jnp.int32, (pad, block), 1)
-    first_row = jnp.where(at_row == 0, 1.0, 0.0).astype(keys.dtype)
 
     def piece(flip, part):
         if flip < 2:
             return (same, other)[flip][0][part]
         return other[flip // 2][1, part] if flip % 2 else same[flip // 2][0, part]
 
+    ones = jnp.where(lax.broadcasted_iota(jnp.int32, (pad, block), 0) == 0, 1.0, 0.0).astype(keys.dtype)
     for at in range(groups * HEADS):
-        flip = at % HEADS
-        key = piece(flip, 1) if groups == 1 else rest_ref[at, 0]
-        value = piece(flip, 2) if groups == 1 else rest_ref[at, 1]
-        frame = (at // HEADS * HEADS + (place ^ flip)) * block + at_frame
-        bias = jnp.where((at_row == 0) & (frame >= lengths_ref[0]), -1e30, 0.0).astype(keys.dtype)
-        keys[at * block : (at + 1) * block, :] = jnp.concatenate([key, bias], axis=0).T
-        values[:head_size, at * block : (at + 1) * block] = value
-        values[head_size:, at * block : (at + 1) * block] = first_row
-    for half in range(2):
-        query[head_size:, half * block : (half + 1) * block] = first_row
+        here = slice(at * block, (at + 1) * block)
+        keys[here, :head_size] = (piece(at, 1) if groups == 1 else rest_ref[at, 0]).T
+        values[:head_size, here] = piece(at, 2) if groups == 1 else rest_ref[at, 1]
+        values[head_size:, here] = ones
+    at_frame = lax.broadcasted_iota(jnp.int32, (block, pad), 0)
+    at_feature = lax.broadcasted_iota(jnp.int32, (block, pad), 1)
+    for at in range(groups * HEADS):
+        frame = (at // HEADS * HEADS + (place ^ (at % HEADS))) * block + at_frame
+        bias = jnp.where((at_feature == 0) & (frame >= lengths_ref[:1, :pad]), -1e30, 0.0)
+        keys[at * block : (at + 1) * block, head_size:] = bias.astype(keys.dtype)
+
+    def score(flip):
+        query = [jnp.concatenate([piece(flip + half, 0), ones], axis=0) for half in range(2)]
+        return jnp.dot(keys[...], jnp.concatenate(query, axis=1), preferred_element_type=jnp.float32)
+
+    later = score(0)
     for flip, out_ref in zip(FLIPS, outs):
-        for half in range(2):
-            query[:head_size, half * block : (half + 1) * block] = piece(flip + half, 0)
-        scores = jnp.dot(keys[...], query[...], preferred_element_type=jnp.float32)
+        scores = later
+        if flip + 2 < HEADS:
+            later = score(flip + 2)
         row_max = jnp.max(scores, axis=0, keepdims=True) * scale
         probs = jnp.exp2(scores * scale - row_max).astype(jnp.bfloat16)
         mixed = jnp.dot(values[...], probs, preferred_element_type=jnp.float32)
@@ -112,12 +115,11 @@
     return pl.pallas_call(
         functools.partial(attention_kernel, groups),
         out_shape=[jax.ShapeDtypeStruct((2, head_size, block), jnp.bfloat16)] * len(FLIPS),
-        in_specs=[SCALARS] + [WHOLE] * (2 * len(FLIPS) + len(rest)),
+        in_specs=[WHOLE] * (1 + 2 * len(FLIPS) + len(rest)),
         out_specs=[WHOLE] * len(FLIPS),
         scratch_shapes=[
             pltpu.VMEM((keys, padded), jnp.bfloat16),
             pltpu.VMEM((padded, keys), jnp.bfloat16),
-            pltpu.VMEM((padded, 2 * block), jnp.bfloat16),
         ],
         compiler_params=params(24),
         cost_estimate=pl.CostEstimate(
@@ -135,19 +137,22 @@
 
 def project_kernel(shards, *refs):
     each = len(FLIPS)
-    heads_same, heads_other, halves = refs[:each], refs[each : 2 * each], refs[2 * each : 2 * each + 2]
-    own_ref = refs[2 * each + 2] if shards > 1 else None
+    heads_same, heads_other, pieces = refs[:each], refs[each : 2 * each], refs[2 * each : 2 * each + 6]
+    own_ref = refs[2 * each + 6] if shards > 1 else None
     out_ref, turned, weight = refs[-3:]
     place = place_in_group()
     rows = turned.shape[0] // HEADS
     for flip in range(HEADS):
         here = pl.ds(pl.multiple_of((place ^ flip) * rows, 32), rows)
         turned[here, :] = heads_other[flip // 2][1] if flip % 2 else heads_same[flip // 2][0]
-    quarter = weight.shape[0] // 4
+    rows = weight.shape[0] // 4
     for core in range(2):
-        for parity in range(2):
-            here = pl.multiple_of(quarter_of(place, parity, core) * quarter, 32)
-            weight[pl.ds(here, quarter), :] = halves[core][parity * quarter : (parity + 1) * quarter, :]
+        quarter, first, second = pieces[3 * core : 3 * core + 3]
+        here = pl.multiple_of(quarter_of(place, 0, core) * rows, 32)
+        weight[pl.ds(here, rows), :] = quarter[...]
+        here = pl.multiple_of(quarter_of(place, 1, core) * rows, 32)
+        weight[pl.ds(here, rows // 2), :] = first[...]
+        weight[pl.ds(here + rows // 2, rows // 2), :] = second[...]
     attention = turned[...].T
     foreign = jnp.dot(attention, weight[...], preferred_element_type=jnp.float32).astype(out_ref.dtype)
     if shards == 1:
@@ -164,10 +169,10 @@
 
 def project(heads_same, heads_other, near, far, own, shards):
     _, rows, frames = heads_other[0].shape
-    foreign = near.shape[1]
+    foreign = near[0].shape[1]
     width = foreign + (own[0].shape[1] if own else 0)
     features = HEADS * rows
-    pieces = [*heads_same, *heads_other, near, far, *own]
+    pieces = [*heads_same, *heads_other, *near, *far, *own]
     return pl.pallas_call(
         functools.partial(project_kernel, shards),
         out_shape=jax.ShapeDtypeStruct((1, frames, width), jnp.bfloat16),
@@ -191,10 +196,11 @@
     rows = out_weight.shape[0] // 4
     quarter = lax.dynamic_slice_in_dim(out_weight, quarter_of(place, 0, 0) * rows, rows, 0)
     split_columns = fsdp == 4
+    lengths = jnp.broadcast_to(lengths, (8, 128))
     if split_columns:
-        far = exchange(quarter, "fsdp", 2)
-        near = exchange(quarter, "fsdp", 1)
-        quarter = jnp.concatenate([near, far, exchange(far, "fsdp", 1)], axis=1)
+        one, two = exchange(quarter, "fsdp", 1), exchange(quarter, "fsdp", 2)
+        two, lengths = lax.optimization_barrier((two, lengths))
+        quarter = jnp.concatenate([one, two, exchange(two, "fsdp", 1)], axis=1)
     else:
         quarter = lax.all_gather(quarter, "fsdp", axis=1, tiled=True)
 
@@ -216,13 +222,14 @@
         rest = lax.all_gather(jnp.stack(pairs), "ctx", axis=0, axis_index_groups=across, tiled=True)
     mixed = attend(lengths, [own_same, *same], other, rest, groups)
 
-    first, second, last = lax.optimization_barrier((first, second, mixed[-1]))
-    mixed = [*mixed[:-1], last]
-    heads_same = [exchange(array, "ctx", flip) if flip else array for flip, array in zip(FLIPS, mixed)]
-    near = jnp.concatenate([quarter, first, second], axis=0)
-    near, heads_same = lax.optimization_barrier((near, heads_same))
+    far = exchange(quarter, "ctx", 1)
+    first, second, far, last = lax.optimization_barrier((first, second, far, mixed[2]))
+    heads = [exchange(array, "ctx", flip) for flip, array in zip(FLIPS[1:], (mixed[1], last, mixed[3]))]
+    heads, first, second = lax.optimization_barrier((heads, first, second))
+    near = [quarter, first, second]
+    far = [far, exchange(first, "ctx", 1), exchange(second, "ctx", 1)]
+    heads_same = [mixed[0], *heads]
     heads_other = [exchange(array, "ctx", 1) for array in heads_same]
-    far = exchange(near, "ctx", 1)
     own = [out_weight] if split_columns else []
     return project(heads_same, heads_other, near, far, own, fsdp if split_columns else 1)
 

time: 37.7 us -> 37.4 us (level)
  Pallas kernels: 6.89 us -> 5.11 us
  starting transfers between devices: 16.4 us -> 17.3 us
  waiting for transfers between devices: 12.5 us -> 13.1 us
    pallas_call x1, Pallas kernels: 3.19 us -> 2.21 us  [attend(): pl.pallas_call(functools.partial(attention_kernel, groups), out_shape=[ja...]
    ppermute x20 -> x22, starting transfers between devices: 16.4 us -> 17.3 us  [exchange(): return lax.ppermute(array, axis, [(i, i ^ flip) for i in range(size)])]
    pallas_call x1, Pallas kernels: 2.1 us -> 1.31 us  [pack(): pl.pallas_call(pack_kernel, out_shape=[own] * 2 + [two] * (len(FLIPS) - 1...]
    ppermute x20 -> x22, waiting for transfers between devices: 12.5 us -> 13.1 us  [exchange(): return lax.ppermute(array, axis, [(i, i ^ flip) for i in range(size)])]
  transfers between devices with their start and end apart: 20 -> 22, of which waited for: 13 -> 10; matrix products, arithmetic and copies ran while one was open for 0% -> 0% of each run, Pallas kernels for 14% -> 9%
where the time goes in v6:
time: 37.4 us; the launch traced here: 37.3 us
  starting transfers between devices  17.3 us (46%)
  waiting for transfers between devices  13.1 us (35%)
  Pallas kernels  5.11 us (14%)
  local copies, waits for them, and re-layouts  0.97 us (3%)
  between operations  0.76 us (2%)
    ppermute x22, starting transfers between devices, exchange(): return lax.ppermute(array, axis, [(i, i ^ flip) for i in range(size)])  17.3 us
    ppermute x22, waiting for transfers between devices, exchange(): return lax.ppermute(array, axis, [(i, i ^ flip) for i in range(size)])  13.1 us
    pallas_call x1, Pallas kernels, attend(): pl.pallas_call(functools.partial(attention_kernel, groups), out_shape=[ja...  2.21 us
    pallas_call x1, Pallas kernels, project(): pl.pallas_call(functools.partial(project_kernel, shards), out_shape=jax.S...  1.59 us
    pallas_call x1, Pallas kernels, pack(): pl.pallas_call(pack_kernel, out_shape=[own] * 2 + [two] * (len(FLIPS) - 1...  1.31 us
    dynamic_slice x1, local copies, waits for them, and re-layouts, per_device(): lax.dynamic_slice_in_dim(out_weight, quarter_of(place, 0, 0) * rows, rows...  0.92 us
  transfers between devices with their start and end apart: 22, of which 10 were waited for; matrix products, arithmetic and copies ran while one was open for 0% of the time, Pallas kernels for 9%

profile of v6, /device:TPU:0, one launch (start us, length us, event | category | flops | bytes accessed | tf_op | source)
XLA Modules:
  0.0 37.3 jit_solution(13721317524791675495)
XLA Ops:
  0.0 0.9 %constant_dynamic-slice_fusion = bf16[192,384]{1,0:T(8,128)(2,1)S(1)} fusion(bf16[768,384]{1,0:T(8,128)(2,1)} %refs_14_.1, s32[]{:T(128)S(6)} %select_n.11), kind=kLoop, calls=%fused_computation.1 | loop fusion | bytes 294916 | tf_op jit(solution)/shard_map/dynamic_slice | solution.py:197
  0.9 4.1 %collective-permute-start = (bf16[192,384]{1,0:T(8,128)(2,1)S(1)}, bf16[192,384]{1,0:T(8,128)(2,1)S(1)}, u32[]{:S(2)}, u32[]{:S(2)}) collective-permute-start(bf16[192,384]{1,0:T(8,128)(2,1)S(1)} %constant_dynamic-slice_fusion), channel_id=1, source_target_pairs={{0,2},{1,3},{2,0},{3,1},{4,6},{5,7},{6,4},{7,5},{8,10},{9,11},{10,... | collective-permute-start | bytes 442376 | tf_op jit(solution)/shard_map/ppermute | solution.py:193
  5.0 1.3 %pack_heads.1 = (bf16[3,96,128]{2,1,0:T(8,128)(2,1)S(1)}, bf16[3,96,128]{2,1,0:T(8,128)(2,1)S(1)}, bf16[2,3,96,128]{3,2,1,0:T(8,128)(2,1)S(1)}, bf16[2,3,96,128]...) custom-call(bf16[1,128,768]{2,1,0:T(8,128)(2,1)} %query_ref.1, bf16[1,128,768]{2,1,0:T(8,128)(2,1)} %key_ref.1, ...), custom_call_target="tpu_custom_call" | custom-call | tf_op jit(solution)/shard_map/pack_heads/pallas_call | solution.py:50
  6.3 1.6 %collective-permute-start.1 = (bf16[2,3,96,128]{3,2,1,0:T(8,128)(2,1)S(1)}, bf16[2,3,96,128]{3,2,1,0:T(8,128)(2,1)S(1)}, u32[]{:S(2)}, u32[]{:S(2)}) collective-permute-start(bf16[2,3,96,128]{3,2,1,0:T(8,128)(2,1)S(1)} %get-tuple-element.35), channel_id=1, source_target_pairs={{0,8},{4,12},{8,0},{12,4},{16,24},{20,28},{24,16},{28,20},{1,9},{5... | collective-permute-start | bytes 442376 | tf_op jit(solution)/shard_map/ppermute | solution.py:193
  7.9 1.5 %collective-permute-start.2 = (bf16[2,3,96,128]{3,2,1,0:T(8,128)(2,1)S(1)}, bf16[2,3,96,128]{3,2,1,0:T(8,128)(2,1)S(1)}, u32[]{:S(2)}, u32[]{:S(2)}) collective-permute-start(bf16[2,3,96,128]{3,2,1,0:T(8,128)(2,1)S(1)} %get-tuple-element.36), channel_id=1, source_target_pairs={{0,16},{4,20},{8,24},{12,28},{16,0},{20,4},{24,8},{28,12},{1,17},{... | collective-permute-start | bytes 442376 | tf_op jit(solution)/shard_map/ppermute | solution.py:193
  9.4 0.5 %collective-permute-start.3 = (bf16[2,3,96,128]{3,2,1,0:T(8,128)(2,1)S(1)}, bf16[2,3,96,128]{3,2,1,0:T(8,128)(2,1)S(1)}, u32[]{:S(2)}, u32[]{:S(2)}) collective-permute-start(bf16[2,3,96,128]{3,2,1,0:T(8,128)(2,1)S(1)} %get-tuple-element.37), channel_id=1, source_target_pairs={{0,24},{4,28},{8,16},{12,20},{16,8},{20,12},{24,0},{28,4},{1,25},{... | collective-permute-start | bytes 442376 | tf_op jit(solution)/shard_map/ppermute | solution.py:193
  9.9 1.6 %collective-permute-start.4 = (bf16[192,384]{1,0:T(8,128)(2,1)S(1)}, bf16[192,384]{1,0:T(8,128)(2,1)S(1)}, u32[]{:S(2)}, u32[]{:S(2)}) collective-permute-start(bf16[192,384]{1,0:T(8,128)(2,1)S(1)} %constant_dynamic-slice_fusion), channel_id=1, source_target_pairs={{0,1},{1,0},{2,3},{3,2},{4,5},{5,4},{6,7},{7,6},{8,9},{9,8},{10,11... | collective-permute-start | bytes 442376 | tf_op jit(solution)/shard_map/ppermute | solution.py:193
  12.1 0.0 collective-permute-done
  12.2 0.7 %collective-permute-start.5 = (bf16[192,384]{1,0:T(8,128)(2,1)S(1)}, bf16[192,384]{1,0:T(8,128)(2,1)S(1)}, u32[]{:S(2)}, u32[]{:S(2)}) collective-permute-start(bf16[192,384]{1,0:T(8,128)(2,1)S(1)} %collective-permute-done), channel_id=1, source_target_pairs={{0,1},{1,0},{2,3},{3,2},{4,5},{5,4},{6,7},{7,6},{8,9},{9,8},{10,11... | collective-permute-start | bytes 442376 | tf_op jit(solution)/shard_map/ppermute | solution.py:193
  12.8 0.0 collective-permute-done.1.refs_1_
  12.8 0.0 collective-permute-start.6
  12.8 3.4 %collective-permute-done.2.refs_2_ = bf16[2,3,96,128]{3,2,1,0:T(8,128)(2,1)S(1)} collective-permute-done((bf16[2,3,96,128]{3,2,1,0:T(8,128)(2,1)S(1)}, bf16[2,3,96,128]{3,2,1,0:T(8,128)(2,1)S(1)}, u32[]{:S(2)}, u32[]{:S(2)}) %collective-permute-start.2) | collective-permute-done | bytes 147488 | tf_op jit(solution)/shard_map/ppermute | solution.py:193
  16.2 0.0 collective-permute-done.3.refs_3_
  16.2 0.0 collective-permute-start.7
  16.2 0.5 %collective-permute-start.8 = (bf16[2,3,96,128]{3,2,1,0:T(8,128)(2,1)S(1)}, bf16[2,3,96,128]{3,2,1,0:T(8,128)(2,1)S(1)}, u32[]{:S(2)}, u32[]{:S(2)}) collective-permute-start(bf16[2,3,96,128]{3,2,1,0:T(8,128)(2,1)S(1)} %collective-permute-done.2.refs_2_), channel_id=1, source_target_pairs={{0,4},{4,0},{8,12},{12,8},{16,20},{20,16},{24,28},{28,24},{1,5},{5... | collective-permute-start | bytes 442376 | tf_op jit(solution)/shard_map/ppermute | solution.py:193
  16.7 0.0 collective-permute-done.4
  16.7 0.0 collective-permute-start.9
  16.7 1.6 %collective-permute-done.5 = bf16[192,384]{1,0:T(8,128)(2,1)S(1)} collective-permute-done((bf16[192,384]{1,0:T(8,128)(2,1)S(1)}, bf16[192,384]{1,0:T(8,128)(2,1)S(1)}, u32[]{:S(2)}, u32[]{:S(2)}) %collective-permute-start.5) | collective-permute-done | bytes 147488 | tf_op jit(solution)/shard_map/ppermute | solution.py:193
  18.4 0.0 collective-permute-done.6.refs_4_
  18.4 0.0 collective-permute-done.7.refs_5_
  18.4 0.0 collective-permute-done.8.refs_6_
  18.4 0.0 collective-permute-done.9.refs_7_
  18.4 0.1 collective-permute-start.13
  18.6 1.6 %collective-permute-start.12 = (bf16[96,1152]{1,0:T(8,128)(2,1)S(1)}, bf16[96,1152]{1,0:T(8,128)(2,1)S(1)}, u32[]{:S(2)}, u32[]{:S(2)}) collective-permute-start(bf16[96,1152]{1,0:T(8,128)(2,1)S(1)} %get-tuple-element.61), channel_id=1, source_target_pairs={{0,16},{4,20},{8,24},{12,28},{16,0},{20,4},{24,8},{28,12},{1,17},{... | collective-permute-start | bytes 663560 | tf_op jit(solution)/shard_map/ppermute | solution.py:193
  20.2 1.5 %collective-permute-start.11 = (bf16[96,1152]{1,0:T(8,128)(2,1)S(1)}, bf16[96,1152]{1,0:T(8,128)(2,1)S(1)}, u32[]{:S(2)}, u32[]{:S(2)}) collective-permute-start(bf16[96,1152]{1,0:T(8,128)(2,1)S(1)} %get-tuple-element.62), channel_id=1, source_target_pairs={{0,8},{4,12},{8,0},{12,4},{16,24},{20,28},{24,16},{28,20},{1,9},{5... | collective-permute-start | bytes 663560 | tf_op jit(solution)/shard_map/ppermute | solution.py:193
  21.7 2.2 %attend_one_head.1 = (bf16[2,96,128]{2,1,0:T(8,128)(2,1)S(1)}, bf16[2,96,128]{2,1,0:T(8,128)(2,1)S(1)}, bf16[2,96,128]{2,1,0:T(8,128)(2,1)S(1)}, bf16[2,96,128]{2,1,0:T(8,128)(2,1)S(1)}) custom-call(s32[8,128]{1,0:T(8,128)S(1)} %broadcast_in_dim.2.lengths_ref, bf16[3,96,128]{2,1,0:T(8,128)(2,1)S(1)} %get-tuple-element.34.refs_0_, ...), custom_call_target="tpu_custom_call" | custom-call | flops 402653184 | bytes 786432 | tf_op jit(solution)/shard_map/attend_one_head/pallas_call | solution.py:115
  23.9 0.6 %collective-permute-start.10 = (bf16[2,96,128]{2,1,0:T(8,128)(2,1)S(1)}, bf16[2,96,128]{2,1,0:T(8,128)(2,1)S(1)}, u32[]{:S(2)}, u32[]{:S(2)}) collective-permute-start(bf16[2,96,128]{2,1,0:T(8,128)(2,1)S(1)} %get-tuple-element.48), channel_id=1, source_target_pairs={{0,8},{4,12},{8,0},{12,4},{16,24},{20,28},{24,16},{28,20},{1,9},{5... | collective-permute-start | bytes 147464 | tf_op jit(solution)/shard_map/ppermute | solution.py:193
  24.5 1.4 %collective-permute-start.15 = (bf16[2,96,128]{2,1,0:T(8,128)(2,1)S(1)}, bf16[2,96,128]{2,1,0:T(8,128)(2,1)S(1)}, u32[]{:S(2)}, u32[]{:S(2)}) collective-permute-start(bf16[2,96,128]{2,1,0:T(8,128)(2,1)S(1)} %get-tuple-element.52), channel_id=1, source_target_pairs={{0,24},{4,28},{8,16},{12,20},{16,8},{20,12},{24,0},{28,4},{1,25},{... | collective-permute-start | bytes 147464 | tf_op jit(solution)/shard_map/ppermute | solution.py:193
  25.9 0.5 %collective-permute-done.12.refs_10_ = bf16[96,1152]{1,0:T(8,128)(2,1)S(1)} collective-permute-done((bf16[96,1152]{1,0:T(8,128)(2,1)S(1)}, bf16[96,1152]{1,0:T(8,128)(2,1)S(1)}, u32[]{:S(2)}, u32[]{:S(2)}) %collective-permute-start.12) | collective-permute-done | bytes 221216 | tf_op jit(solution)/shard_map/ppermute | solution.py:193
  26.5 2.0 %collective-permute-done.11.refs_9_ = bf16[96,1152]{1,0:T(8,128)(2,1)S(1)} collective-permute-done((bf16[96,1152]{1,0:T(8,128)(2,1)S(1)}, bf16[96,1152]{1,0:T(8,128)(2,1)S(1)}, u32[]{:S(2)}, u32[]{:S(2)}) %collective-permute-start.11) | collective-permute-done | bytes 221216 | tf_op jit(solution)/shard_map/ppermute | solution.py:193
  28.5 0.0 collective-permute-done.13.refs_11_
  28.5 0.5 %collective-permute-start.14 = (bf16[2,96,128]{2,1,0:T(8,128)(2,1)S(1)}, bf16[2,96,128]{2,1,0:T(8,128)(2,1)S(1)}, u32[]{:S(2)}, u32[]{:S(2)}) collective-permute-start(bf16[2,96,128]{2,1,0:T(8,128)(2,1)S(1)} %get-tuple-element.51), channel_id=1, source_target_pairs={{0,16},{4,20},{8,24},{12,28},{16,0},{20,4},{24,8},{28,12},{1,17},{... | collective-permute-start | bytes 147464 | tf_op jit(solution)/shard_map/ppermute | solution.py:193
  28.9 0.4 %collective-permute-done.10.refs_1_ = bf16[2,96,128]{2,1,0:T(8,128)(2,1)S(1)} collective-permute-done((bf16[2,96,128]{2,1,0:T(8,128)(2,1)S(1)}, bf16[2,96,128]{2,1,0:T(8,128)(2,1)S(1)}, u32[]{:S(2)}, u32[]{:S(2)}) %collective-permute-start.10) | collective-permute-done | bytes 49184 | tf_op jit(solution)/shard_map/ppermute | solution.py:193
  29.3 0.4 %collective-permute-done.15.refs_3_ = bf16[2,96,128]{2,1,0:T(8,128)(2,1)S(1)} collective-permute-done((bf16[2,96,128]{2,1,0:T(8,128)(2,1)S(1)}, bf16[2,96,128]{2,1,0:T(8,128)(2,1)S(1)}, u32[]{:S(2)}, u32[]{:S(2)}) %collective-permute-start.15) | collective-permute-done | bytes 49184 | tf_op jit(solution)/shard_map/ppermute | solution.py:193
  29.7 2.8 %collective-permute-done.14.refs_2_ = bf16[2,96,128]{2,1,0:T(8,128)(2,1)S(1)} collective-permute-done((bf16[2,96,128]{2,1,0:T(8,128)(2,1)S(1)}, bf16[2,96,128]{2,1,0:T(8,128)(2,1)S(1)}, u32[]{:S(2)}, u32[]{:S(2)}) %collective-permute-start.14) | collective-permute-done | bytes 49184 | tf_op jit(solution)/shard_map/ppermute | solution.py:193
  32.6 0.0 collective-permute-start.20
  32.6 0.5 %collective-permute-start.21 = (bf16[96,1152]{1,0:T(8,128)(2,1)S(1)}, bf16[96,1152]{1,0:T(8,128)(2,1)S(1)}, u32[]{:S(2)}, u32[]{:S(2)}) collective-permute-start(bf16[96,1152]{1,0:T(8,128)(2,1)S(1)} %collective-permute-done.12.refs_10_), channel_id=1, source_target_pairs={{0,4},{4,0},{8,12},{12,8},{16,20},{20,16},{24,28},{28,24},{1,5},{5... | collective-permute-start | bytes 663560 | tf_op jit(solution)/shard_map/ppermute | solution.py:193
  33.1 0.0 collective-permute-start.16
  33.1 0.5 %collective-permute-start.17 = (bf16[2,96,128]{2,1,0:T(8,128)(2,1)S(1)}, bf16[2,96,128]{2,1,0:T(8,128)(2,1)S(1)}, u32[]{:S(2)}, u32[]{:S(2)}) collective-permute-start(bf16[2,96,128]{2,1,0:T(8,128)(2,1)S(1)} %collective-permute-done.10.refs_1_), channel_id=1, source_target_pairs={{0,4},{4,0},{8,12},{12,8},{16,20},{20,16},{24,28},{28,24},{1,5},{5... | collective-permute-start | bytes 147464 | tf_op jit(solution)/shard_map/ppermute | solution.py:193
  33.6 0.0 collective-permute-start.18
  33.6 0.8 %collective-permute-done.16.refs_4_ = bf16[2,96,128]{2,1,0:T(8,128)(2,1)S(1)} collective-permute-done((bf16[2,96,128]{2,1,0:T(8,128)(2,1)S(1)}, bf16[2,96,128]{2,1,0:T(8,128)(2,1)S(1)}, u32[]{:S(2)}, u32[]{:S(2)}) %collective-permute-start.16) | collective-permute-done | bytes 49184 | tf_op jit(solution)/shard_map/ppermute | solution.py:193
  34.4 0.2 collective-permute-start.19
  34.6 0.0 collective-permute-done.17.refs_5_
  34.6 0.2 collective-permute-done.18.refs_6_
  34.8 0.8 %collective-permute-done.19.refs_7_ = bf16[2,96,128]{2,1,0:T(8,128)(2,1)S(1)} collective-permute-done((bf16[2,96,128]{2,1,0:T(8,128)(2,1)S(1)}, bf16[2,96,128]{2,1,0:T(8,128)(2,1)S(1)}, u32[]{:S(2)}, u32[]{:S(2)}) %collective-permute-start.19) | collective-permute-done | bytes 49184 | tf_op jit(solution)/shard_map/ppermute | solution.py:193
  35.7 0.0 collective-permute-done.20.refs_12_
  35.7 0.0 collective-permute-done.21.refs_13_
  35.7 1.6 %project_heads.1 = bf16[1,128,1536]{2,1,0:T(8,128)(2,1)} custom-call(bf16[2,96,128]{2,1,0:T(8,128)(2,1)S(1)} %get-tuple-element.47.refs_0_, bf16[2,96,128]{2,1,0:T(8,128)(2,1)S(1)} %collective-permute-done.10.refs_1_, bf16[2,96,128]{2,1,0:T(8,128)(2,1)S(1)} %collective-permute-done.14.refs_2_, bf16[2,96,128]{2,1,0:T(8,128)(2,1)S(1)} %collective-permute-done.15.refs_3_, ...), custom_call_target="tpu_custom_call" | custom-call | flops 301989888 | bytes 2359296 | tf_op jit(solution)/shard_map/project_heads/pallas_call | solution.py:176
  (5 shorter events, 0.1 us)
Async XLA Ops:
  0.9 11.2 %collective-permute-start = (bf16[192,384]{1,0:T(8,128)(2,1)S(1)}, bf16[192,384]{1,0:T(8,128)(2,1)S(1)}, u32[]{:S(2)}, u32[]{:S(2)}) collective-permute-start(bf16[192,384]{1,0:T(8,128)(2,1)S(1)} %constant_dynamic-slice_fusion), channel_id=1, source_target_pairs={{0,2},{1,3},{2,0},{3,1},{4,6},{5,7},{6,4},{7,5},{8,10},{9,11},{10,... | collective-permute-start | bytes 442376 | tf_op jit(solution)/shard_map/ppermute | solution.py:193
  6.3 6.5 %collective-permute-start.1 = (bf16[2,3,96,128]{3,2,1,0:T(8,128)(2,1)S(1)}, bf16[2,3,96,128]{3,2,1,0:T(8,128)(2,1)S(1)}, u32[]{:S(2)}, u32[]{:S(2)}) collective-permute-start(bf16[2,3,96,128]{3,2,1,0:T(8,128)(2,1)S(1)} %get-tuple-element.35), channel_id=1, source_target_pairs={{0,8},{4,12},{8,0},{12,4},{16,24},{20,28},{24,16},{28,20},{1,9},{5... | collective-permute-start | bytes 442376 | tf_op jit(solution)/shard_map/ppermute | solution.py:193
  7.9 8.3 %collective-permute-start.2 = (bf16[2,3,96,128]{3,2,1,0:T(8,128)(2,1)S(1)}, bf16[2,3,96,128]{3,2,1,0:T(8,128)(2,1)S(1)}, u32[]{:S(2)}, u32[]{:S(2)}) collective-permute-start(bf16[2,3,96,128]{3,2,1,0:T(8,128)(2,1)S(1)} %get-tuple-element.36), channel_id=1, source_target_pairs={{0,16},{4,20},{8,24},{12,28},{16,0},{20,4},{24,8},{28,12},{1,17},{... | collective-permute-start | bytes 442376 | tf_op jit(solution)/shard_map/ppermute | solution.py:193
  9.4 6.8 %collective-permute-start.3 = (bf16[2,3,96,128]{3,2,1,0:T(8,128)(2,1)S(1)}, bf16[2,3,96,128]{3,2,1,0:T(8,128)(2,1)S(1)}, u32[]{:S(2)}, u32[]{:S(2)}) collective-permute-start(bf16[2,3,96,128]{3,2,1,0:T(8,128)(2,1)S(1)} %get-tuple-element.37), channel_id=1, source_target_pairs={{0,24},{4,28},{8,16},{12,20},{16,8},{20,12},{24,0},{28,4},{1,25},{... | collective-permute-start | bytes 442376 | tf_op jit(solution)/shard_map/ppermute | solution.py:193
  9.9 6.8 %collective-permute-start.4 = (bf16[192,384]{1,0:T(8,128)(2,1)S(1)}, bf16[192,384]{1,0:T(8,128)(2,1)S(1)}, u32[]{:S(2)}, u32[]{:S(2)}) collective-permute-start(bf16[192,384]{1,0:T(8,128)(2,1)S(1)} %constant_dynamic-slice_fusion), channel_id=1, source_target_pairs={{0,1},{1,0},{2,3},{3,2},{4,5},{5,4},{6,7},{7,6},{8,9},{9,8},{10,11... | collective-permute-start | bytes 442376 | tf_op jit(solution)/shard_map/ppermute | solution.py:193
  12.2 6.2 %collective-permute-start.5 = (bf16[192,384]{1,0:T(8,128)(2,1)S(1)}, bf16[192,384]{1,0:T(8,128)(2,1)S(1)}, u32[]{:S(2)}, u32[]{:S(2)}) collective-permute-start(bf16[192,384]{1,0:T(8,128)(2,1)S(1)} %collective-permute-done), channel_id=1, source_target_pairs={{0,1},{1,0},{2,3},{3,2},{4,5},{5,4},{6,7},{7,6},{8,9},{9,8},{10,11... | collective-permute-start | bytes 442376 | tf_op jit(solution)/shard_map/ppermute | solution.py:193
  12.8 5.6 %collective-permute-start.6 = (bf16[3,96,128]{2,1,0:T(8,128)(2,1)S(1)}, bf16[3,96,128]{2,1,0:T(8,128)(2,1)S(1)}, u32[]{:S(2)}, u32[]{:S(2)}) collective-permute-start(bf16[3,96,128]{2,1,0:T(8,128)(2,1)S(1)} %get-tuple-element.42), channel_id=1, source_target_pairs={{0,4},{4,0},{8,12},{12,8},{16,20},{20,16},{24,28},{28,24},{1,5},{5... | collective-permute-start | bytes 221192 | tf_op jit(solution)/shard_map/ppermute | solution.py:193
  16.2 2.2 %collective-permute-start.7 = (bf16[2,3,96,128]{3,2,1,0:T(8,128)(2,1)S(1)}, bf16[2,3,96,128]{3,2,1,0:T(8,128)(2,1)S(1)}, u32[]{:S(2)}, u32[]{:S(2)}) collective-permute-start(bf16[2,3,96,128]{3,2,1,0:T(8,128)(2,1)S(1)} %collective-permute-done.1.refs_1_), channel_id=1, source_target_pairs={{0,4},{4,0},{8,12},{12,8},{16,20},{20,16},{24,28},{28,24},{1,5},{5... | collective-permute-start | bytes 442376 | tf_op jit(solution)/shard_map/ppermute | solution.py:193
  16.2 2.2 %collective-permute-start.8 = (bf16[2,3,96,128]{3,2,1,0:T(8,128)(2,1)S(1)}, bf16[2,3,96,128]{3,2,1,0:T(8,128)(2,1)S(1)}, u32[]{:S(2)}, u32[]{:S(2)}) collective-permute-start(bf16[2,3,96,128]{3,2,1,0:T(8,128)(2,1)S(1)} %collective-permute-done.2.refs_2_), channel_id=1, source_target_pairs={{0,4},{4,0},{8,12},{12,8},{16,20},{20,16},{24,28},{28,24},{1,5},{5... | collective-permute-start | bytes 442376 | tf_op jit(solution)/shard_map/ppermute | solution.py:193
  16.7 1.7 %collective-permute-start.9 = (bf16[2,3,96,128]{3,2,1,0:T(8,128)(2,1)S(1)}, bf16[2,3,96,128]{3,2,1,0:T(8,128)(2,1)S(1)}, u32[]{:S(2)}, u32[]{:S(2)}) collective-permute-start(bf16[2,3,96,128]{3,2,1,0:T(8,128)(2,1)S(1)} %collective-permute-done.3.refs_3_), channel_id=1, source_target_pairs={{0,4},{4,0},{8,12},{12,8},{16,20},{20,16},{24,28},{28,24},{1,5},{5... | collective-permute-start | bytes 442376 | tf_op jit(solution)/shard_map/ppermute | solution.py:193
  18.4 10.0 %collective-permute-start.13 = (bf16[192,1152]{1,0:T(8,128)(2,1)S(1)}, bf16[192,1152]{1,0:T(8,128)(2,1)S(1)}, u32[]{:S(2)}, u32[]{:S(2)}) collective-permute-start(bf16[192,1152]{1,0:T(8,128)(2,1)S(1)} %pad_maximum_fusion.refs_8_), channel_id=1, source_target_pairs={{0,4},{4,0},{8,12},{12,8},{16,20},{20,16},{24,28},{28,24},{1,5},{5... | collective-permute-start | bytes 1327112 | tf_op jit(solution)/shard_map/ppermute | solution.py:193
  18.6 7.9 %collective-permute-start.12 = (bf16[96,1152]{1,0:T(8,128)(2,1)S(1)}, bf16[96,1152]{1,0:T(8,128)(2,1)S(1)}, u32[]{:S(2)}, u32[]{:S(2)}) collective-permute-start(bf16[96,1152]{1,0:T(8,128)(2,1)S(1)} %get-tuple-element.61), channel_id=1, source_target_pairs={{0,16},{4,20},{8,24},{12,28},{16,0},{20,4},{24,8},{28,12},{1,17},{... | collective-permute-start | bytes 663560 | tf_op jit(solution)/shard_map/ppermute | solution.py:193
  20.2 8.3 %collective-permute-start.11 = (bf16[96,1152]{1,0:T(8,128)(2,1)S(1)}, bf16[96,1152]{1,0:T(8,128)(2,1)S(1)}, u32[]{:S(2)}, u32[]{:S(2)}) collective-permute-start(bf16[96,1152]{1,0:T(8,128)(2,1)S(1)} %get-tuple-element.62), channel_id=1, source_target_pairs={{0,8},{4,12},{8,0},{12,4},{16,24},{20,28},{24,16},{28,20},{1,9},{5... | collective-permute-start | bytes 663560 | tf_op jit(solution)/shard_map/ppermute | solution.py:193
  21.7 14.0 %copy-start = (bf16[768,384]{1,0:T(8,128)(2,1)S(1)}, bf16[768,384]{1,0:T(8,128)(2,1)}, u32[]{:S(2)}) copy-start(bf16[768,384]{1,0:T(8,128)(2,1)} %refs_14_.1) | copy-start | bytes 1769476
  23.9 5.4 %collective-permute-start.10 = (bf16[2,96,128]{2,1,0:T(8,128)(2,1)S(1)}, bf16[2,96,128]{2,1,0:T(8,128)(2,1)S(1)}, u32[]{:S(2)}, u32[]{:S(2)}) collective-permute-start(bf16[2,96,128]{2,1,0:T(8,128)(2,1)S(1)} %get-tuple-element.48), channel_id=1, source_target_pairs={{0,8},{4,12},{8,0},{12,4},{16,24},{20,28},{24,16},{28,20},{1,9},{5... | collective-permute-start | bytes 147464 | tf_op jit(solution)/shard_map/ppermute | solution.py:193
  24.5 5.2 %collective-permute-start.15 = (bf16[2,96,128]{2,1,0:T(8,128)(2,1)S(1)}, bf16[2,96,128]{2,1,0:T(8,128)(2,1)S(1)}, u32[]{:S(2)}, u32[]{:S(2)}) collective-permute-start(bf16[2,96,128]{2,1,0:T(8,128)(2,1)S(1)} %get-tuple-element.52), channel_id=1, source_target_pairs={{0,24},{4,28},{8,16},{12,20},{16,8},{20,12},{24,0},{28,4},{1,25},{... | collective-permute-start | bytes 147464 | tf_op jit(solution)/shard_map/ppermute | solution.py:193
  28.5 4.1 %collective-permute-start.14 = (bf16[2,96,128]{2,1,0:T(8,128)(2,1)S(1)}, bf16[2,96,128]{2,1,0:T(8,128)(2,1)S(1)}, u32[]{:S(2)}, u32[]{:S(2)}) collective-permute-start(bf16[2,96,128]{2,1,0:T(8,128)(2,1)S(1)} %get-tuple-element.51), channel_id=1, source_target_pairs={{0,16},{4,20},{8,24},{12,28},{16,0},{20,4},{24,8},{28,12},{1,17},{... | collective-permute-start | bytes 147464 | tf_op jit(solution)/shard_map/ppermute | solution.py:193
  32.6 3.1 %collective-permute-start.20 = (bf16[96,1152]{1,0:T(8,128)(2,1)S(1)}, bf16[96,1152]{1,0:T(8,128)(2,1)S(1)}, u32[]{:S(2)}, u32[]{:S(2)}) collective-permute-start(bf16[96,1152]{1,0:T(8,128)(2,1)S(1)} %collective-permute-done.11.refs_9_), channel_id=1, source_target_pairs={{0,4},{4,0},{8,12},{12,8},{16,20},{20,16},{24,28},{28,24},{1,5},{5... | collective-permute-start | bytes 663560 | tf_op jit(solution)/shard_map/ppermute | solution.py:193
  32.6 3.1 %collective-permute-start.21 = (bf16[96,1152]{1,0:T(8,128)(2,1)S(1)}, bf16[96,1152]{1,0:T(8,128)(2,1)S(1)}, u32[]{:S(2)}, u32[]{:S(2)}) collective-permute-start(bf16[96,1152]{1,0:T(8,128)(2,1)S(1)} %collective-permute-done.12.refs_10_), channel_id=1, source_target_pairs={{0,4},{4,0},{8,12},{12,8},{16,20},{20,16},{24,28},{28,24},{1,5},{5... | collective-permute-start | bytes 663560 | tf_op jit(solution)/shard_map/ppermute | solution.py:193
  33.1 1.4 %collective-permute-start.16 = (bf16[2,96,128]{2,1,0:T(8,128)(2,1)S(1)}, bf16[2,96,128]{2,1,0:T(8,128)(2,1)S(1)}, u32[]{:S(2)}, u32[]{:S(2)}) collective-permute-start(bf16[2,96,128]{2,1,0:T(8,128)(2,1)S(1)} %get-tuple-element.47.refs_0_), channel_id=1, source_target_pairs={{0,4},{4,0},{8,12},{12,8},{16,20},{20,16},{24,28},{28,24},{1,5},{5... | collective-permute-start | bytes 147464 | tf_op jit(solution)/shard_map/ppermute | solution.py:193
  33.1 1.5 %collective-permute-start.17 = (bf16[2,96,128]{2,1,0:T(8,128)(2,1)S(1)}, bf16[2,96,128]{2,1,0:T(8,128)(2,1)S(1)}, u32[]{:S(2)}, u32[]{:S(2)}) collective-permute-start(bf16[2,96,128]{2,1,0:T(8,128)(2,1)S(1)} %collective-permute-done.10.refs_1_), channel_id=1, source_target_pairs={{0,4},{4,0},{8,12},{12,8},{16,20},{20,16},{24,28},{28,24},{1,5},{5... | collective-permute-start | bytes 147464 | tf_op jit(solution)/shard_map/ppermute | solution.py:193
  33.6 1.2 %collective-permute-start.18 = (bf16[2,96,128]{2,1,0:T(8,128)(2,1)S(1)}, bf16[2,96,128]{2,1,0:T(8,128)(2,1)S(1)}, u32[]{:S(2)}, u32[]{:S(2)}) collective-permute-start(bf16[2,96,128]{2,1,0:T(8,128)(2,1)S(1)} %collective-permute-done.14.refs_2_), channel_id=1, source_target_pairs={{0,4},{4,0},{8,12},{12,8},{16,20},{20,16},{24,28},{28,24},{1,5},{5... | collective-permute-start | bytes 147464 | tf_op jit(solution)/shard_map/ppermute | solution.py:193
  34.4 1.2 %collective-permute-start.19 = (bf16[2,96,128]{2,1,0:T(8,128)(2,1)S(1)}, bf16[2,96,128]{2,1,0:T(8,128)(2,1)S(1)}, u32[]{:S(2)}, u32[]{:S(2)}) collective-permute-start(bf16[2,96,128]{2,1,0:T(8,128)(2,1)S(1)} %collective-permute-done.15.refs_3_), channel_id=1, source_target_pairs={{0,4},{4,0},{8,12},{12,8},{16,20},{20,16},{24,28},{28,24},{1,5},{5... | collective-permute-start | bytes 147464 | tf_op jit(solution)/shard_map/ppermute | solution.py:193

commit v7 on v6

--- a/solution.py
+++ b/solution.py
@@ -72,9 +72,9 @@
     pad = keys.shape[1] - head_size
 
     def piece(flip, part):
-        if flip < 2:
-            return (same, other)[flip][0][part]
-        return other[flip // 2][1, part] if flip % 2 else same[flip // 2][0, part]
+        if flip % 2:
+            return other[flip // 2][1, part] if flip > 1 else other[0][part]
+        return same[flip // 2][0, part] if flip else same[0][part]
 
     ones = jnp.where(lax.broadcasted_iota(jnp.int32, (pad, block), 0) == 0, 1.0, 0.0).astype(keys.dtype)
     for at in range(groups * HEADS):
@@ -110,7 +110,6 @@
     _, head_size, block = other[0].shape
     keys = groups * HEADS * block
     padded = head_size + 32
-    queries = HEADS * block
     rest = [] if rest is None else [rest]
     return pl.pallas_call(
         functools.partial(attention_kernel, groups),
@@ -122,43 +121,63 @@
             pltpu.VMEM((padded, keys), jnp.bfloat16),
         ],
         compiler_params=params(24),
-        cost_estimate=pl.CostEstimate(
-            flops=4 * queries * keys * head_size,
-            bytes_accessed=4 * (queries + keys) * head_size,
-            transcendentals=queries * keys,
-        ),
+        cost_estimate=pl.CostEstimate(flops=0, bytes_accessed=0, transcendentals=0),
         name="attend_one_head",
     )(lengths, *same, *other, *rest)
 
 
-def quarter_of(place, parity, core):
-    return (((place >> 2) ^ (place >> 1) ^ parity) & 1) * 2 + ((place ^ core) & 1)
+def second_entries_kernel(*refs):
+    for at, ref in enumerate(refs[:-1]):
+        refs[-1][at] = ref[1]
+
+
+def second_entries(arrays):
+    return pl.pallas_call(
+        second_entries_kernel,
+        out_shape=jax.ShapeDtypeStruct((len(arrays), *arrays[0].shape[1:]), arrays[0].dtype),
+        in_specs=[WHOLE] * len(arrays),
+        out_specs=WHOLE,
+        compiler_params=params(16),
+        name="second_entries",
+    )(*arrays)
+
+
+def parity_of(place):
+    return ((place >> 2) ^ (place >> 1)) & 1
 
 
 def project_kernel(shards, *refs):
     each = len(FLIPS)
-    heads_same, heads_other, pieces = refs[:each], refs[each : 2 * each], refs[2 * each : 2 * each + 6]
-    own_ref = refs[2 * each + 6] if shards > 1 else None
+    heads_same, heads_other, pieces = refs[:each], refs[each], refs[each + 1 : -3]
     out_ref, turned, weight = refs[-3:]
     place = place_in_group()
+    core, parity = place & 1, parity_of(place)
     rows = turned.shape[0] // HEADS
     for flip in range(HEADS):
         here = pl.ds(pl.multiple_of((place ^ flip) * rows, 32), rows)
-        turned[here, :] = heads_other[flip // 2][1] if flip % 2 else heads_same[flip // 2][0]
-    rows = weight.shape[0] // 4
-    for core in range(2):
-        quarter, first, second = pieces[3 * core : 3 * core + 3]
-        here = pl.multiple_of(quarter_of(place, 0, core) * rows, 32)
-        weight[pl.ds(here, rows), :] = quarter[...]
-        here = pl.multiple_of(quarter_of(place, 1, core) * rows, 32)
-        weight[pl.ds(here, rows // 2), :] = first[...]
-        weight[pl.ds(here + rows // 2, rows // 2), :] = second[...]
+        turned[here, :] = heads_other[flip // 2] if flip % 2 else heads_same[flip // 2][0]
+    half = weight.shape[0] // 2
+    if shards == 1:
+        for other, ref in enumerate(pieces):
+            weight[pl.ds(pl.multiple_of((core ^ other) * half, 32), half), :] = ref[...]
+    else:
+        *pieces, own_ref = pieces
+        columns = own_ref.shape[1]
+        part = pieces[2].shape[0]
+        for other in range(2):
+            fetched, passed, third, third_passed = pieces[4 * other : 4 * other + 4]
+            near = pl.ds(pl.multiple_of((1 - (core ^ other)) * columns, 128), columns)
+            last = slice(2 * columns, 3 * columns)
+            for flip, whole_ref, part_ref in ((0, fetched, third), (1, passed, third_passed)):
+                first = (parity ^ flip) * half
+                weight[pl.ds(pl.multiple_of(first, 32), half), near] = whole_ref[...]
+                first = first + (core ^ other) * (half - part)
+                weight[pl.ds(pl.multiple_of(first, 16), part), last] = part_ref[...]
     attention = turned[...].T
     foreign = jnp.dot(attention, weight[...], preferred_element_type=jnp.float32).astype(out_ref.dtype)
     if shards == 1:
         out_ref[0] = foreign
         return
-    columns = own_ref.shape[1]
     shard = lax.axis_index("fsdp")
     own = jnp.dot(attention, own_ref[...], preferred_element_type=jnp.float32).astype(out_ref.dtype)
     out_ref[0, :, pl.ds(pl.multiple_of(shard * columns, 128), columns)] = own
@@ -167,12 +186,12 @@
         out_ref[0, :, here] = foreign[:, (flip - 1) * columns : flip * columns]
 
 
-def project(heads_same, heads_other, near, far, own, shards):
-    _, rows, frames = heads_other[0].shape
-    foreign = near[0].shape[1]
+def project(heads_same, heads_other, pieces, own, shards):
+    _, rows, frames = heads_other.shape
+    foreign = (shards - 1) * own[0].shape[1] if own else pieces[0].shape[1]
     width = foreign + (own[0].shape[1] if own else 0)
     features = HEADS * rows
-    pieces = [*heads_same, *heads_other, *near, *far, *own]
+    pieces = [*heads_same, heads_other, *pieces, *own]
     return pl.pallas_call(
         functools.partial(project_kernel, shards),
         out_shape=jax.ShapeDtypeStruct((1, frames, width), jnp.bfloat16),
@@ -192,46 +211,61 @@
         size = ctx if axis == "ctx" else fsdp
         return lax.ppermute(array, axis, [(i, i ^ flip) for i in range(size)])
 
-    place = place_in_group()
-    rows = out_weight.shape[0] // 4
-    quarter = lax.dynamic_slice_in_dim(out_weight, quarter_of(place, 0, 0) * rows, rows, 0)
+    def exchange_in_plane(array):
+        return lax.ppermute(array, "ctx", [(i, i ^ (4 if i % 2 else 2)) for i in range(ctx)])
+
+    def exchange_along(array, *flips):
+        pairs = [(i * fsdp + z, i * fsdp + (z ^ flips[i % 2])) for i in range(ctx) for z in range(fsdp)]
+        return lax.ppermute(array, ("ctx", "fsdp"), pairs)
+
+    place = place_in_group()
+    core = place & 1
+    rows = out_weight.shape[0] // 2
     split_columns = fsdp == 4
     lengths = jnp.broadcast_to(lengths, (8, 128))
     if split_columns:
-        one, two = exchange(quarter, "fsdp", 1), exchange(quarter, "fsdp", 2)
-        two, lengths = lax.optimization_barrier((two, lengths))
-        quarter = jnp.concatenate([one, two, exchange(two, "fsdp", 1)], axis=1)
+        half = lax.dynamic_slice_in_dim(out_weight, parity_of(place) * rows, rows, 0)
+        fetched = exchange_along(half, 2, 1)
+        part = rows // 2 + 16
+        third = lax.dynamic_slice_in_dim(fetched, core * (rows - part), part, 0)
+        third = exchange_along(third, 1, 2)
+        passed = exchange_in_plane(fetched)
+        fetched_other = exchange(fetched, "ctx", 1)
     else:
-        quarter = lax.all_gather(quarter, "fsdp", axis=1, tiled=True)
+        half = lax.dynamic_slice_in_dim(out_weight, core * rows, rows, 0)
+        half = lax.all_gather(half, "fsdp", axis=1, tiled=True)
 
     own_same, own_other, *by_chip = pack(queries, key_rows, value_rows)
     same = [exchange(array, "ctx", flip) for flip, array in zip(FLIPS[1:], by_chip)]
-    same = lax.optimization_barrier(same)
-    other = [exchange(array, "ctx", 1) for array in (own_other, *same)]
-    quarter, other = lax.optimization_barrier((quarter, other))
-    first = exchange(quarter[: rows // 2], "ctx", 2)
-    second = exchange(quarter[rows // 2 :], "ctx", 4)
+    same, own_other = lax.optimization_barrier((same, exchange(own_other, "ctx", 1)))
+    other = [own_other, *(exchange(array, "ctx", 1) for array in same)]
 
     groups = ctx // HEADS
     rest = None
     if groups > 1:
-        pairs = [own_same[1:], other[0][1:]]
+        pairs = [own_same[1:], own_other[1:]]
         for one, two in zip(same, other[1:]):
             pairs += [one[0, 1:], two[1, 1:]]
         across = [[head + first for first in range(0, ctx, HEADS)] for head in range(HEADS)]
         rest = lax.all_gather(jnp.stack(pairs), "ctx", axis=0, axis_index_groups=across, tiled=True)
     mixed = attend(lengths, [own_same, *same], other, rest, groups)
 
-    far = exchange(quarter, "ctx", 1)
-    first, second, far, last = lax.optimization_barrier((first, second, far, mixed[2]))
-    heads = [exchange(array, "ctx", flip) for flip, array in zip(FLIPS[1:], (mixed[1], last, mixed[3]))]
-    heads, first, second = lax.optimization_barrier((heads, first, second))
-    near = [quarter, first, second]
-    far = [far, exchange(first, "ctx", 1), exchange(second, "ctx", 1)]
+    own = []
+    if split_columns:
+        third, passed, last = lax.optimization_barrier((third, passed, mixed[2]))
+        mixed = [*mixed[:2], last, mixed[3]]
+        third_passed = exchange_in_plane(third)
+    heads = [exchange(array, "ctx", flip) for flip, array in zip(FLIPS[1:], mixed[1:])]
+    if split_columns:
+        heads, third_passed = lax.optimization_barrier((heads, third_passed))
+        pieces = [fetched, passed, third, third_passed]
+        pieces += [fetched_other, *(exchange(array, "ctx", 1) for array in pieces[1:])]
+        own = [out_weight]
+    else:
+        pieces = [half, exchange(half, "ctx", 1)]
     heads_same = [mixed[0], *heads]
-    heads_other = [exchange(array, "ctx", 1) for array in heads_same]
-    own = [out_weight] if split_columns else []
-    return project(heads_same, heads_other, near, far, own, fsdp if split_columns else 1)
+    heads_other = exchange(second_entries(heads_same), "ctx", 1)
+    return project(heads_same, heads_other, pieces, own, fsdp if split_columns else 1)
 
 
 def solution(mesh):

time: 37.4 us -> 36.3 us (0.971)
  waiting for transfers between devices: 13.1 us -> 10.9 us
  starting transfers between devices: 17.3 us -> 18.3 us
    ppermute x0 -> x4, starting transfers between devices: none -> 8.03 us  [the longest x2 5.83 us: exchange_along(): return lax.ppermute(array, ('ctx', 'fsdp'), pairs)]
    ppermute x22 -> x15, starting transfers between devices: 17.3 us -> 10.3 us  [exchange(): return lax.ppermute(array, axis, [(i, i ^ flip) for i in range(size)])]
    ppermute x22 -> x15, waiting for transfers between devices: 13.1 us -> 8.07 us  [exchange(): return lax.ppermute(array, axis, [(i, i ^ flip) for i in range(size)])]
    ppermute x0 -> x4, waiting for transfers between devices: none -> 2.82 us  [the longest x2 2.81 us: exchange_along(): return lax.ppermute(array, ('ctx', 'fsdp'), pairs)]
    dynamic_slice x1 -> x2, local copies, waits for them, and re-layouts: 0.92 us -> 1.01 us  [the longest x1 0.99 us: per_device(): lax.dynamic_slice_in_dim(out_weight, parity_of(place) * rows, rows, 0)]
  transfers between devices with their start and end apart: 22 -> 19, of which waited for: 10 -> 9; matrix products, arithmetic and copies ran while one was open for 0% -> 0% of each run, Pallas kernels for 9% -> 10%
where the time goes in v7:
time: 36.3 us; the launch traced here: 36 us
  starting transfers between devices  18.3 us (50%)
  waiting for transfers between devices  10.9 us (30%)
  Pallas kernels  5.03 us (14%)
  local copies, waits for them, and re-layouts  1.01 us (3%)
  between operations  0.71 us (2%)
    ppermute x15, starting transfers between devices, exchange(): return lax.ppermute(array, axis, [(i, i ^ flip) for i in range(size)])  10.3 us
    ppermute x15, waiting for transfers between devices, exchange(): return lax.ppermute(array, axis, [(i, i ^ flip) for i in range(size)])  8.07 us
    ppermute x2, starting transfers between devices, exchange_along(): return lax.ppermute(array, ('ctx', 'fsdp'), pairs)  5.83 us
    ppermute x2, waiting for transfers between devices, exchange_along(): return lax.ppermute(array, ('ctx', 'fsdp'), pairs)  2.81 us
    pallas_call x1, Pallas kernels, attend(): pl.pallas_call(functools.partial(attention_kernel, groups), out_shape=[ja...  2.2 us
    ppermute x2, starting transfers between devices, exchange_in_plane(): lax.ppermute(array, 'ctx', [(i, i ^ (4 if i % 2 else 2)) for i in range(c...  2.2 us
    pallas_call x1, Pallas kernels, project(): pl.pallas_call(functools.partial(project_kernel, shards), out_shape=jax.S...  1.52 us
    pallas_call x1, Pallas kernels, pack(): pl.pallas_call(pack_kernel, out_shape=[own] * 2 + [two] * (len(FLIPS) - 1...  1.31 us
  transfers between devices with their start and end apart: 19, of which 9 were waited for; matrix products, arithmetic and copies ran while one was open for 0% of the time, Pallas kernels for 10%

profile of v7, /device:TPU:0, one launch (start us, length us, event | category | flops | bytes accessed | tf_op | source)
XLA Modules:
  0.0 36.0 jit_solution(8027021998242173570)
XLA Ops:
  0.0 1.0 %constant_dynamic-slice_fusion.1 = bf16[384,384]{1,0:T(8,128)(2,1)S(1)} fusion(bf16[768,384]{1,0:T(8,128)(2,1)} %refs_13_.1, s32[]{:T(128)S(6)} %select_n.14), kind=kLoop, calls=%fused_computation.1 | loop fusion | bytes 589828 | tf_op jit(solution)/shard_map/dynamic_slice | solution.py:227
  1.0 4.1 %collective-permute-start.8 = (bf16[384,384]{1,0:T(8,128)(2,1)S(1)}, bf16[384,384]{1,0:T(8,128)(2,1)S(1)}, u32[]{:S(2)}, u32[]{:S(2)}) collective-permute-start(bf16[384,384]{1,0:T(8,128)(2,1)S(1)} %constant_dynamic-slice_fusion.1), channel_id=1, source_target_pairs={{0,2},{1,3},{2,0},{3,1},{4,5},{5,4},{6,7},{7,6},{8,10},{9,11},{10,... | collective-permute-start | bytes 884744 | tf_op jit(solution)/shard_map/ppermute | solution.py:219
  5.1 1.3 %pack_heads.1 = (bf16[3,96,128]{2,1,0:T(8,128)(2,1)S(1)}, bf16[3,96,128]{2,1,0:T(8,128)(2,1)S(1)}, bf16[2,3,96,128]{3,2,1,0:T(8,128)(2,1)S(1)}, bf16[2,3,96,128]...) custom-call(bf16[1,128,768]{2,1,0:T(8,128)(2,1)} %query_ref.1, bf16[1,128,768]{2,1,0:T(8,128)(2,1)} %key_ref.1, ...), custom_call_target="tpu_custom_call" | custom-call | tf_op jit(solution)/shard_map/pack_heads/pallas_call | solution.py:50
  6.4 1.6 %collective-permute-start = (bf16[2,3,96,128]{3,2,1,0:T(8,128)(2,1)S(1)}, bf16[2,3,96,128]{3,2,1,0:T(8,128)(2,1)S(1)}, u32[]{:S(2)}, u32[]{:S(2)}) collective-permute-start(bf16[2,3,96,128]{3,2,1,0:T(8,128)(2,1)S(1)} %get-tuple-element.26), channel_id=1, source_target_pairs={{0,8},{4,12},{8,0},{12,4},{16,24},{20,28},{24,16},{28,20},{1,9},{5... | collective-permute-start | bytes 442376 | tf_op jit(solution)/shard_map/ppermute | solution.py:212
  8.0 1.5 %collective-permute-start.1 = (bf16[2,3,96,128]{3,2,1,0:T(8,128)(2,1)S(1)}, bf16[2,3,96,128]{3,2,1,0:T(8,128)(2,1)S(1)}, u32[]{:S(2)}, u32[]{:S(2)}) collective-permute-start(bf16[2,3,96,128]{3,2,1,0:T(8,128)(2,1)S(1)} %get-tuple-element.27), channel_id=1, source_target_pairs={{0,16},{4,20},{8,24},{12,28},{16,0},{20,4},{24,8},{28,12},{1,17},{... | collective-permute-start | bytes 442376 | tf_op jit(solution)/shard_map/ppermute | solution.py:212
  9.5 0.5 %collective-permute-start.2 = (bf16[2,3,96,128]{3,2,1,0:T(8,128)(2,1)S(1)}, bf16[2,3,96,128]{3,2,1,0:T(8,128)(2,1)S(1)}, u32[]{:S(2)}, u32[]{:S(2)}) collective-permute-start(bf16[2,3,96,128]{3,2,1,0:T(8,128)(2,1)S(1)} %get-tuple-element.28), channel_id=1, source_target_pairs={{0,24},{4,28},{8,16},{12,20},{16,8},{20,12},{24,0},{28,4},{1,25},{... | collective-permute-start | bytes 442376 | tf_op jit(solution)/shard_map/ppermute | solution.py:212
  10.0 1.7 %collective-permute-done.8.refs_5_ = bf16[384,384]{1,0:T(8,128)(2,1)S(1)} collective-permute-done((bf16[384,384]{1,0:T(8,128)(2,1)S(1)}, bf16[384,384]{1,0:T(8,128)(2,1)S(1)}, u32[]{:S(2)}, u32[]{:S(2)}) %collective-permute-start.8) | collective-permute-done | bytes 294944 | tf_op jit(solution)/shard_map/ppermute | solution.py:219
  11.7 2.1 %collective-permute-start.10 = (bf16[384,384]{1,0:T(8,128)(2,1)S(1)}, bf16[384,384]{1,0:T(8,128)(2,1)S(1)}, u32[]{:S(2)}, u32[]{:S(2)}) collective-permute-start(bf16[384,384]{1,0:T(8,128)(2,1)S(1)} %collective-permute-done.8.refs_5_), channel_id=1, source_target_pairs={{0,8},{4,20},{8,0},{12,28},{16,24},{20,4},{24,16},{28,12},{1,9},{5... | collective-permute-start | bytes 884744 | tf_op jit(solution)/shard_map/ppermute | solution.py:215
  13.8 0.0 collective-permute-start.3
  13.8 1.2 %collective-permute-done.3.refs_4_ = bf16[3,96,128]{2,1,0:T(8,128)(2,1)S(1)} collective-permute-done((bf16[3,96,128]{2,1,0:T(8,128)(2,1)S(1)}, bf16[3,96,128]{2,1,0:T(8,128)(2,1)S(1)}, u32[]{:S(2)}, u32[]{:S(2)}) %collective-permute-start.3) | collective-permute-done | bytes 73760 | tf_op jit(solution)/shard_map/ppermute | solution.py:212
  15.1 1.7 %collective-permute-start.9 = (bf16[208,384]{1,0:T(8,128)(2,1)S(1)}, bf16[208,384]{1,0:T(8,128)(2,1)S(1)}, u32[]{:S(2)}, u32[]{:S(2)}) collective-permute-start(bf16[208,384]{1,0:T(8,128)(2,1)S(1)} %constant_dynamic-slice_fusion), channel_id=1, source_target_pairs={{0,1},{1,0},{2,3},{3,2},{4,6},{5,7},{6,4},{7,5},{8,9},{9,8},{10,11... | collective-permute-start | bytes 479240 | tf_op jit(solution)/shard_map/ppermute | solution.py:219
  16.8 0.0 collective-permute-done.refs_1_
  16.8 0.0 collective-permute-done.1.refs_2_
  16.8 0.0 collective-permute-done.2.refs_3_
  16.8 0.1 collective-permute-start.4
  16.9 0.5 %collective-permute-start.5 = (bf16[2,3,96,128]{3,2,1,0:T(8,128)(2,1)S(1)}, bf16[2,3,96,128]{3,2,1,0:T(8,128)(2,1)S(1)}, u32[]{:S(2)}, u32[]{:S(2)}) collective-permute-start(bf16[2,3,96,128]{3,2,1,0:T(8,128)(2,1)S(1)} %collective-permute-done.1.refs_2_), channel_id=1, source_target_pairs={{0,4},{4,0},{8,12},{12,8},{16,20},{20,16},{24,28},{28,24},{1,5},{5... | collective-permute-start | bytes 442376 | tf_op jit(solution)/shard_map/ppermute | solution.py:212
  17.4 0.1 collective-permute-start.6
  18.1 0.1 collective-permute-done.4.refs_5_
  18.3 0.2 collective-permute-done.5.refs_6_
  18.5 0.3 collective-permute-done.6.refs_7_
  18.8 0.0 copy-start
  18.8 2.2 %attend_one_head.1 = (bf16[2,96,128]{2,1,0:T(8,128)(2,1)S(1)}, bf16[2,96,128]{2,1,0:T(8,128)(2,1)S(1)}, bf16[2,96,128]{2,1,0:T(8,128)(2,1)S(1)}, bf16[2,96,128]{2,1,0:T(8,128)(2,1)S(1)}) custom-call(s32[8,128]{1,0:T(8,128)S(1)} %broadcast_in_dim.2.lengths_ref, bf16[3,96,128]{2,1,0:T(8,128)(2,1)S(1)} %get-tuple-element.25.refs_0_, ...), custom_call_target="tpu_custom_call" | custom-call | tf_op jit(solution)/shard_map/attend_one_head/pallas_call | solution.py:114
  21.0 1.1 %collective-permute-done.9.refs_7_ = bf16[208,384]{1,0:T(8,128)(2,1)S(1)} collective-permute-done((bf16[208,384]{1,0:T(8,128)(2,1)S(1)}, bf16[208,384]{1,0:T(8,128)(2,1)S(1)}, u32[]{:S(2)}, u32[]{:S(2)}) %collective-permute-start.9) | collective-permute-done | bytes 159776 | tf_op jit(solution)/shard_map/ppermute | solution.py:219
  22.1 0.0 collective-permute-done.10.refs_6_
  22.1 0.1 collective-permute-start.13
  22.2 0.4 %collective-permute-start.15 = (bf16[384,384]{1,0:T(8,128)(2,1)S(1)}, bf16[384,384]{1,0:T(8,128)(2,1)S(1)}, u32[]{:S(2)}, u32[]{:S(2)}) collective-permute-start(bf16[384,384]{1,0:T(8,128)(2,1)S(1)} %collective-permute-done.8.refs_5_), channel_id=1, source_target_pairs={{0,4},{4,0},{8,12},{12,8},{16,20},{20,16},{24,28},{28,24},{1,5},{5... | collective-permute-start | bytes 884744 | tf_op jit(solution)/shard_map/ppermute | solution.py:212
  22.5 0.1 collective-permute-start.16
  22.7 1.9 %collective-permute-start.7 = (bf16[2,96,128]{2,1,0:T(8,128)(2,1)S(1)}, bf16[2,96,128]{2,1,0:T(8,128)(2,1)S(1)}, u32[]{:S(2)}, u32[]{:S(2)}) collective-permute-start(bf16[2,96,128]{2,1,0:T(8,128)(2,1)S(1)} %get-tuple-element.35), channel_id=1, source_target_pairs={{0,8},{4,12},{8,0},{12,4},{16,24},{20,28},{24,16},{28,20},{1,9},{5... | collective-permute-start | bytes 147464 | tf_op jit(solution)/shard_map/ppermute | solution.py:212
  24.6 1.5 %collective-permute-start.12 = (bf16[2,96,128]{2,1,0:T(8,128)(2,1)S(1)}, bf16[2,96,128]{2,1,0:T(8,128)(2,1)S(1)}, u32[]{:S(2)}, u32[]{:S(2)}) collective-permute-start(bf16[2,96,128]{2,1,0:T(8,128)(2,1)S(1)} %get-tuple-element.38), channel_id=1, source_target_pairs={{0,24},{4,28},{8,16},{12,20},{16,8},{20,12},{24,0},{28,4},{1,25},{... | collective-permute-start | bytes 147464 | tf_op jit(solution)/shard_map/ppermute | solution.py:212
  26.1 2.7 %collective-permute-done.7.refs_1_ = bf16[2,96,128]{2,1,0:T(8,128)(2,1)S(1)} collective-permute-done((bf16[2,96,128]{2,1,0:T(8,128)(2,1)S(1)}, bf16[2,96,128]{2,1,0:T(8,128)(2,1)S(1)}, u32[]{:S(2)}, u32[]{:S(2)}) %collective-permute-start.7) | collective-permute-done | bytes 49184 | tf_op jit(solution)/shard_map/ppermute | solution.py:212
  28.8 1.6 %collective-permute-start.11 = (bf16[2,96,128]{2,1,0:T(8,128)(2,1)S(1)}, bf16[2,96,128]{2,1,0:T(8,128)(2,1)S(1)}, u32[]{:S(2)}, u32[]{:S(2)}) collective-permute-start(bf16[2,96,128]{2,1,0:T(8,128)(2,1)S(1)} %get-tuple-element.37), channel_id=1, source_target_pairs={{0,16},{4,20},{8,24},{12,28},{16,0},{20,4},{24,8},{28,12},{1,17},{... | collective-permute-start | bytes 147464 | tf_op jit(solution)/shard_map/ppermute | solution.py:212
  30.4 0.0 collective-permute-done.12.refs_3_
  30.4 0.0 collective-permute-start.17
  30.5 2.5 %collective-permute-done.11.refs_2_ = bf16[2,96,128]{2,1,0:T(8,128)(2,1)S(1)} collective-permute-done((bf16[2,96,128]{2,1,0:T(8,128)(2,1)S(1)}, bf16[2,96,128]{2,1,0:T(8,128)(2,1)S(1)}, u32[]{:S(2)}, u32[]{:S(2)}) %collective-permute-start.11) | collective-permute-done | bytes 49184 | tf_op jit(solution)/shard_map/ppermute | solution.py:212
  32.9 0.0 collective-permute-done.13.refs_8_
  32.9 0.0 collective-permute-start.18
  32.9 0.6 %collective-permute-start.14 = (bf16[4,96,128]{2,1,0:T(8,128)(2,1)S(1)}, bf16[4,96,128]{2,1,0:T(8,128)(2,1)S(1)}, u32[]{:S(2)}, u32[]{:S(2)}) collective-permute-start(bf16[4,96,128]{2,1,0:T(8,128)(2,1)S(1)} %second_entries.1), channel_id=1, source_target_pairs={{0,4},{4,0},{8,12},{12,8},{16,20},{20,16},{24,28},{28,24},{1,5},{5... | collective-permute-start | bytes 294920 | tf_op jit(solution)/shard_map/ppermute | solution.py:212
  33.5 0.0 collective-permute-done.15.refs_9_
  33.5 0.0 collective-permute-done.17.refs_11_
  33.5 0.9 %collective-permute-done.14.refs_4_ = bf16[4,96,128]{2,1,0:T(8,128)(2,1)S(1)} collective-permute-done((bf16[4,96,128]{2,1,0:T(8,128)(2,1)S(1)}, bf16[4,96,128]{2,1,0:T(8,128)(2,1)S(1)}, u32[]{:S(2)}, u32[]{:S(2)}) %collective-permute-start.14) | collective-permute-done | bytes 98336 | tf_op jit(solution)/shard_map/ppermute | solution.py:212
  34.5 0.0 collective-permute-done.16.refs_10_
  34.5 0.0 collective-permute-done.18.refs_12_
  34.5 0.0 copy-done
  34.5 1.5 %project_heads.1 = bf16[1,128,1536]{2,1,0:T(8,128)(2,1)} custom-call(bf16[2,96,128]{2,1,0:T(8,128)(2,1)S(1)} %get-tuple-element.34.refs_0_, bf16[2,96,128]{2,1,0:T(8,128)(2,1)S(1)} %collective-permute-done.7.refs_1_, bf16[2,96,128]{2,1,0:T(8,128)(2,1)S(1)} %collective-permute-done.11.refs_2_, bf16[2,96,128]{2,1,0:T(8,128)(2,1)S(1)} %collective-permute-done.12.refs_3_, ...), custom_call_target="tpu_custom_call" | custom-call | flops 301989888 | bytes 2359296 | tf_op jit(solution)/shard_map/project_heads/pallas_call | solution.py:195
  (3 shorter events, 0.0 us)
Async XLA Ops:
  1.0 10.7 %collective-permute-start.8 = (bf16[384,384]{1,0:T(8,128)(2,1)S(1)}, bf16[384,384]{1,0:T(8,128)(2,1)S(1)}, u32[]{:S(2)}, u32[]{:S(2)}) collective-permute-start(bf16[384,384]{1,0:T(8,128)(2,1)S(1)} %constant_dynamic-slice_fusion.1), channel_id=1, source_target_pairs={{0,2},{1,3},{2,0},{3,1},{4,5},{5,4},{6,7},{7,6},{8,10},{9,11},{10,... | collective-permute-start | bytes 884744 | tf_op jit(solution)/shard_map/ppermute | solution.py:219
  6.4 10.4 %collective-permute-start = (bf16[2,3,96,128]{3,2,1,0:T(8,128)(2,1)S(1)}, bf16[2,3,96,128]{3,2,1,0:T(8,128)(2,1)S(1)}, u32[]{:S(2)}, u32[]{:S(2)}) collective-permute-start(bf16[2,3,96,128]{3,2,1,0:T(8,128)(2,1)S(1)} %get-tuple-element.26), channel_id=1, source_target_pairs={{0,8},{4,12},{8,0},{12,4},{16,24},{20,28},{24,16},{28,20},{1,9},{5... | collective-permute-start | bytes 442376 | tf_op jit(solution)/shard_map/ppermute | solution.py:212
  8.0 8.8 %collective-permute-start.1 = (bf16[2,3,96,128]{3,2,1,0:T(8,128)(2,1)S(1)}, bf16[2,3,96,128]{3,2,1,0:T(8,128)(2,1)S(1)}, u32[]{:S(2)}, u32[]{:S(2)}) collective-permute-start(bf16[2,3,96,128]{3,2,1,0:T(8,128)(2,1)S(1)} %get-tuple-element.27), channel_id=1, source_target_pairs={{0,16},{4,20},{8,24},{12,28},{16,0},{20,4},{24,8},{28,12},{1,17},{... | collective-permute-start | bytes 442376 | tf_op jit(solution)/shard_map/ppermute | solution.py:212
  9.5 7.3 %collective-permute-start.2 = (bf16[2,3,96,128]{3,2,1,0:T(8,128)(2,1)S(1)}, bf16[2,3,96,128]{3,2,1,0:T(8,128)(2,1)S(1)}, u32[]{:S(2)}, u32[]{:S(2)}) collective-permute-start(bf16[2,3,96,128]{3,2,1,0:T(8,128)(2,1)S(1)} %get-tuple-element.28), channel_id=1, source_target_pairs={{0,24},{4,28},{8,16},{12,20},{16,8},{20,12},{24,0},{28,4},{1,25},{... | collective-permute-start | bytes 442376 | tf_op jit(solution)/shard_map/ppermute | solution.py:212
  11.7 10.4 %collective-permute-start.10 = (bf16[384,384]{1,0:T(8,128)(2,1)S(1)}, bf16[384,384]{1,0:T(8,128)(2,1)S(1)}, u32[]{:S(2)}, u32[]{:S(2)}) collective-permute-start(bf16[384,384]{1,0:T(8,128)(2,1)S(1)} %collective-permute-done.8.refs_5_), channel_id=1, source_target_pairs={{0,8},{4,20},{8,0},{12,28},{16,24},{20,4},{24,16},{28,12},{1,9},{5... | collective-permute-start | bytes 884744 | tf_op jit(solution)/shard_map/ppermute | solution.py:215
  13.8 1.3 %collective-permute-start.3 = (bf16[3,96,128]{2,1,0:T(8,128)(2,1)S(1)}, bf16[3,96,128]{2,1,0:T(8,128)(2,1)S(1)}, u32[]{:S(2)}, u32[]{:S(2)}) collective-permute-start(bf16[3,96,128]{2,1,0:T(8,128)(2,1)S(1)} %get-tuple-element.29), channel_id=1, source_target_pairs={{0,4},{4,0},{8,12},{12,8},{16,20},{20,16},{24,28},{28,24},{1,5},{5... | collective-permute-start | bytes 221192 | tf_op jit(solution)/shard_map/ppermute | solution.py:212
  15.1 7.0 %collective-permute-start.9 = (bf16[208,384]{1,0:T(8,128)(2,1)S(1)}, bf16[208,384]{1,0:T(8,128)(2,1)S(1)}, u32[]{:S(2)}, u32[]{:S(2)}) collective-permute-start(bf16[208,384]{1,0:T(8,128)(2,1)S(1)} %constant_dynamic-slice_fusion), channel_id=1, source_target_pairs={{0,1},{1,0},{2,3},{3,2},{4,6},{5,7},{6,4},{7,5},{8,9},{9,8},{10,11... | collective-permute-start | bytes 479240 | tf_op jit(solution)/shard_map/ppermute | solution.py:219
  16.8 1.4 %collective-permute-start.4 = (bf16[2,3,96,128]{3,2,1,0:T(8,128)(2,1)S(1)}, bf16[2,3,96,128]{3,2,1,0:T(8,128)(2,1)S(1)}, u32[]{:S(2)}, u32[]{:S(2)}) collective-permute-start(bf16[2,3,96,128]{3,2,1,0:T(8,128)(2,1)S(1)} %collective-permute-done.refs_1_), channel_id=1, source_target_pairs={{0,4},{4,0},{8,12},{12,8},{16,20},{20,16},{24,28},{28,24},{1,5},{5... | collective-permute-start | bytes 442376 | tf_op jit(solution)/shard_map/ppermute | solution.py:212
  16.9 1.6 %collective-permute-start.5 = (bf16[2,3,96,128]{3,2,1,0:T(8,128)(2,1)S(1)}, bf16[2,3,96,128]{3,2,1,0:T(8,128)(2,1)S(1)}, u32[]{:S(2)}, u32[]{:S(2)}) collective-permute-start(bf16[2,3,96,128]{3,2,1,0:T(8,128)(2,1)S(1)} %collective-permute-done.1.refs_2_), channel_id=1, source_target_pairs={{0,4},{4,0},{8,12},{12,8},{16,20},{20,16},{24,28},{28,24},{1,5},{5... | collective-permute-start | bytes 442376 | tf_op jit(solution)/shard_map/ppermute | solution.py:212
  17.4 1.4 %collective-permute-start.6 = (bf16[2,3,96,128]{3,2,1,0:T(8,128)(2,1)S(1)}, bf16[2,3,96,128]{3,2,1,0:T(8,128)(2,1)S(1)}, u32[]{:S(2)}, u32[]{:S(2)}) collective-permute-start(bf16[2,3,96,128]{3,2,1,0:T(8,128)(2,1)S(1)} %collective-permute-done.2.refs_3_), channel_id=1, source_target_pairs={{0,4},{4,0},{8,12},{12,8},{16,20},{20,16},{24,28},{28,24},{1,5},{5... | collective-permute-start | bytes 442376 | tf_op jit(solution)/shard_map/ppermute | solution.py:212
  18.8 15.7 %copy-start = (bf16[768,384]{1,0:T(8,128)(2,1)S(1)}, bf16[768,384]{1,0:T(8,128)(2,1)}, u32[]{:S(2)}) copy-start(bf16[768,384]{1,0:T(8,128)(2,1)} %refs_13_.1) | copy-start | bytes 1769476
  22.1 10.9 %collective-permute-start.13 = (bf16[208,384]{1,0:T(8,128)(2,1)S(1)}, bf16[208,384]{1,0:T(8,128)(2,1)S(1)}, u32[]{:S(2)}, u32[]{:S(2)}) collective-permute-start(bf16[208,384]{1,0:T(8,128)(2,1)S(1)} %collective-permute-done.9.refs_7_), channel_id=1, source_target_pairs={{0,8},{4,20},{8,0},{12,28},{16,24},{20,4},{24,16},{28,12},{1,9},{5... | collective-permute-start | bytes 479240 | tf_op jit(solution)/shard_map/ppermute | solution.py:215
  22.2 11.4 %collective-permute-start.15 = (bf16[384,384]{1,0:T(8,128)(2,1)S(1)}, bf16[384,384]{1,0:T(8,128)(2,1)S(1)}, u32[]{:S(2)}, u32[]{:S(2)}) collective-permute-start(bf16[384,384]{1,0:T(8,128)(2,1)S(1)} %collective-permute-done.8.refs_5_), channel_id=1, source_target_pairs={{0,4},{4,0},{8,12},{12,8},{16,20},{20,16},{24,28},{28,24},{1,5},{5... | collective-permute-start | bytes 884744 | tf_op jit(solution)/shard_map/ppermute | solution.py:212
  22.5 11.9 %collective-permute-start.16 = (bf16[384,384]{1,0:T(8,128)(2,1)S(1)}, bf16[384,384]{1,0:T(8,128)(2,1)S(1)}, u32[]{:S(2)}, u32[]{:S(2)}) collective-permute-start(bf16[384,384]{1,0:T(8,128)(2,1)S(1)} %collective-permute-done.10.refs_6_), channel_id=1, source_target_pairs={{0,4},{4,0},{8,12},{12,8},{16,20},{20,16},{24,28},{28,24},{1,5},{5... | collective-permute-start | bytes 884744 | tf_op jit(solution)/shard_map/ppermute | solution.py:212
  22.7 6.2 %collective-permute-start.7 = (bf16[2,96,128]{2,1,0:T(8,128)(2,1)S(1)}, bf16[2,96,128]{2,1,0:T(8,128)(2,1)S(1)}, u32[]{:S(2)}, u32[]{:S(2)}) collective-permute-start(bf16[2,96,128]{2,1,0:T(8,128)(2,1)S(1)} %get-tuple-element.35), channel_id=1, source_target_pairs={{0,8},{4,12},{8,0},{12,4},{16,24},{20,28},{24,16},{28,20},{1,9},{5... | collective-permute-start | bytes 147464 | tf_op jit(solution)/shard_map/ppermute | solution.py:212
  24.6 5.8 %collective-permute-start.12 = (bf16[2,96,128]{2,1,0:T(8,128)(2,1)S(1)}, bf16[2,96,128]{2,1,0:T(8,128)(2,1)S(1)}, u32[]{:S(2)}, u32[]{:S(2)}) collective-permute-start(bf16[2,96,128]{2,1,0:T(8,128)(2,1)S(1)} %get-tuple-element.38), channel_id=1, source_target_pairs={{0,24},{4,28},{8,16},{12,20},{16,8},{20,12},{24,0},{28,4},{1,25},{... | collective-permute-start | bytes 147464 | tf_op jit(solution)/shard_map/ppermute | solution.py:212
  28.8 4.1 %collective-permute-start.11 = (bf16[2,96,128]{2,1,0:T(8,128)(2,1)S(1)}, bf16[2,96,128]{2,1,0:T(8,128)(2,1)S(1)}, u32[]{:S(2)}, u32[]{:S(2)}) collective-permute-start(bf16[2,96,128]{2,1,0:T(8,128)(2,1)S(1)} %get-tuple-element.37), channel_id=1, source_target_pairs={{0,16},{4,20},{8,24},{12,28},{16,0},{20,4},{24,8},{28,12},{1,17},{... | collective-permute-start | bytes 147464 | tf_op jit(solution)/shard_map/ppermute | solution.py:212
  30.4 3.1 %collective-permute-start.17 = (bf16[208,384]{1,0:T(8,128)(2,1)S(1)}, bf16[208,384]{1,0:T(8,128)(2,1)S(1)}, u32[]{:S(2)}, u32[]{:S(2)}) collective-permute-start(bf16[208,384]{1,0:T(8,128)(2,1)S(1)} %collective-permute-done.9.refs_7_), channel_id=1, source_target_pairs={{0,4},{4,0},{8,12},{12,8},{16,20},{20,16},{24,28},{28,24},{1,5},{5... | collective-permute-start | bytes 479240 | tf_op jit(solution)/shard_map/ppermute | solution.py:212
  32.9 1.5 %collective-permute-start.18 = (bf16[208,384]{1,0:T(8,128)(2,1)S(1)}, bf16[208,384]{1,0:T(8,128)(2,1)S(1)}, u32[]{:S(2)}, u32[]{:S(2)}) collective-permute-start(bf16[208,384]{1,0:T(8,128)(2,1)S(1)} %collective-permute-done.13.refs_8_), channel_id=1, source_target_pairs={{0,4},{4,0},{8,12},{12,8},{16,20},{20,16},{24,28},{28,24},{1,5},{5... | collective-permute-start | bytes 479240 | tf_op jit(solution)/shard_map/ppermute | solution.py:212
  32.9 1.5 %collective-permute-start.14 = (bf16[4,96,128]{2,1,0:T(8,128)(2,1)S(1)}, bf16[4,96,128]{2,1,0:T(8,128)(2,1)S(1)}, u32[]{:S(2)}, u32[]{:S(2)}) collective-permute-start(bf16[4,96,128]{2,1,0:T(8,128)(2,1)S(1)} %second_entries.1), channel_id=1, source_target_pairs={{0,4},{4,0},{8,12},{12,8},{16,20},{20,16},{24,28},{28,24},{1,5},{5... | collective-permute-start | bytes 294920 | tf_op jit(solution)/shard_map/ppermute | solution.py:212

commit v8 on v7

--- a/solution.py
+++ b/solution.py
@@ -226,18 +226,21 @@
     if split_columns:
         half = lax.dynamic_slice_in_dim(out_weight, parity_of(place) * rows, rows, 0)
         fetched = exchange_along(half, 2, 1)
+    else:
+        half = lax.dynamic_slice_in_dim(out_weight, core * rows, rows, 0)
+        half = lax.all_gather(half, "fsdp", axis=1, tiled=True)
+
+    own_same, own_other, *by_chip = pack(queries, key_rows, value_rows)
+    same = [exchange(array, "ctx", flip) for flip, array in zip(FLIPS[1:], by_chip)]
+    own_other = exchange(own_other, "ctx", 1)
+    if split_columns:
+        fetched, own_other = lax.optimization_barrier((fetched, own_other))
+        passed = exchange_in_plane(fetched)
         part = rows // 2 + 16
         third = lax.dynamic_slice_in_dim(fetched, core * (rows - part), part, 0)
         third = exchange_along(third, 1, 2)
-        passed = exchange_in_plane(fetched)
-        fetched_other = exchange(fetched, "ctx", 1)
-    else:
-        half = lax.dynamic_slice_in_dim(out_weight, core * rows, rows, 0)
-        half = lax.all_gather(half, "fsdp", axis=1, tiled=True)
-
-    own_same, own_other, *by_chip = pack(queries, key_rows, value_rows)
-    same = [exchange(array, "ctx", flip) for flip, array in zip(FLIPS[1:], by_chip)]
-    same, own_other = lax.optimization_barrier((same, exchange(own_other, "ctx", 1)))
+        third_passed = exchange_in_plane(third)
+    same, own_other = lax.optimization_barrier((same, own_other))
     other = [own_other, *(exchange(array, "ctx", 1) for array in same)]
 
     groups = ctx // HEADS
@@ -250,21 +253,20 @@
         rest = lax.all_gather(jnp.stack(pairs), "ctx", axis=0, axis_index_groups=across, tiled=True)
     mixed = attend(lengths, [own_same, *same], other, rest, groups)
 
+    heads = [exchange(array, "ctx", flip) for flip, array in zip(FLIPS[1:], mixed[1:])]
     own = []
     if split_columns:
-        third, passed, last = lax.optimization_barrier((third, passed, mixed[2]))
-        mixed = [*mixed[:2], last, mixed[3]]
-        third_passed = exchange_in_plane(third)
-    heads = [exchange(array, "ctx", flip) for flip, array in zip(FLIPS[1:], mixed[1:])]
-    if split_columns:
-        heads, third_passed = lax.optimization_barrier((heads, third_passed))
-        pieces = [fetched, passed, third, third_passed]
-        pieces += [fetched_other, *(exchange(array, "ctx", 1) for array in pieces[1:])]
+        heads, fetched, passed, third = lax.optimization_barrier((heads, fetched, passed, third))
+        pieces = [fetched, passed, third]
+        others = [exchange(array, "ctx", 1) for array in pieces]
+    heads_same = [mixed[0], *heads]
+    heads_other = exchange(second_entries(heads_same), "ctx", 1)
+    if split_columns:
+        third_passed, heads_other = lax.optimization_barrier((third_passed, heads_other))
+        pieces += [third_passed, *others, exchange(third_passed, "ctx", 1)]
         own = [out_weight]
     else:
         pieces = [half, exchange(half, "ctx", 1)]
-    heads_same = [mixed[0], *heads]
-    heads_other = exchange(second_entries(heads_same), "ctx", 1)
     return project(heads_same, heads_other, pieces, own, fsdp if split_columns else 1)
 
 

time: 36.3 us -> 33.8 us (0.931)
  starting transfers between devices: 18.3 us -> 16.2 us
    ppermute x2, waiting for transfers between devices: 2.81 us -> 0.47 us  [exchange_along(): return lax.ppermute(array, ('ctx', 'fsdp'), pairs)]
    ppermute x15, waiting for transfers between devices: 8.07 us -> 9.88 us  [exchange(): return lax.ppermute(array, axis, [(i, i ^ flip) for i in range(size)])]
    ppermute x15, starting transfers between devices: 10.3 us -> 8.84 us  [exchange(): return lax.ppermute(array, axis, [(i, i ^ flip) for i in range(size)])]
    ppermute x2, starting transfers between devices: 5.83 us -> 5.42 us  [exchange_along(): return lax.ppermute(array, ('ctx', 'fsdp'), pairs)]
  transfers between devices with their start and end apart: 19 -> 19, of which waited for: 9 -> 10; matrix products, arithmetic and copies ran while one was open for 0% -> 0% of each run, Pallas kernels for 10% -> 10%
where the time goes in v8:
time: 33.8 us; the launch traced here: 33.7 us
  starting transfers between devices  16.2 us (48%)
  waiting for transfers between devices  10.7 us (32%)
  Pallas kernels  5.05 us (15%)
  local copies, waits for them, and re-layouts  1.02 us (3%)
  between operations  0.74 us (2%)
    ppermute x15, waiting for transfers between devices, exchange(): return lax.ppermute(array, axis, [(i, i ^ flip) for i in range(size)])  9.88 us
    ppermute x15, starting transfers between devices, exchange(): return lax.ppermute(array, axis, [(i, i ^ flip) for i in range(size)])  8.84 us
    ppermute x2, starting transfers between devices, exchange_along(): return lax.ppermute(array, ('ctx', 'fsdp'), pairs)  5.42 us
    pallas_call x1, Pallas kernels, attend(): pl.pallas_call(functools.partial(attention_kernel, groups), out_shape=[ja...  2.22 us
    ppermute x2, starting transfers between devices, exchange_in_plane(): lax.ppermute(array, 'ctx', [(i, i ^ (4 if i % 2 else 2)) for i in range(c...  1.9 us
    pallas_call x1, Pallas kernels, project(): pl.pallas_call(functools.partial(project_kernel, shards), out_shape=jax.S...  1.52 us
    pallas_call x1, Pallas kernels, pack(): pl.pallas_call(pack_kernel, out_shape=[own] * 2 + [two] * (len(FLIPS) - 1...  1.31 us
    dynamic_slice x1, local copies, waits for them, and re-layouts, per_device(): lax.dynamic_slice_in_dim(out_weight, parity_of(place) * rows, rows, 0)  0.99 us
  transfers between devices with their start and end apart: 19, of which 10 were waited for; matrix products, arithmetic and copies ran while one was open for 0% of the time, Pallas kernels for 10%

profile of v8, /device:TPU:0, one launch (start us, length us, event | category | flops | bytes accessed | tf_op | source)
XLA Modules:
  0.0 33.7 jit_solution(2308757925851030837)
XLA Ops:
  0.0 1.0 %constant_dynamic-slice_fusion.1 = bf16[384,384]{1,0:T(8,128)(2,1)S(1)} fusion(bf16[768,384]{1,0:T(8,128)(2,1)} %refs_13_.1, s32[]{:T(128)S(6)} %select_n.14), kind=kLoop, calls=%fused_computation.1 | loop fusion | bytes 589828 | tf_op jit(solution)/shard_map/dynamic_slice | solution.py:227
  1.0 4.1 %collective-permute-start.3 = (bf16[384,384]{1,0:T(8,128)(2,1)S(1)}, bf16[384,384]{1,0:T(8,128)(2,1)S(1)}, u32[]{:S(2)}, u32[]{:S(2)}) collective-permute-start(bf16[384,384]{1,0:T(8,128)(2,1)S(1)} %constant_dynamic-slice_fusion.1), channel_id=1, source_target_pairs={{0,2},{1,3},{2,0},{3,1},{4,5},{5,4},{6,7},{7,6},{8,10},{9,11},{10,... | collective-permute-start | bytes 884744 | tf_op jit(solution)/shard_map/ppermute | solution.py:219
  5.1 1.3 %pack_heads.1 = (bf16[3,96,128]{2,1,0:T(8,128)(2,1)S(1)}, bf16[3,96,128]{2,1,0:T(8,128)(2,1)S(1)}, bf16[2,3,96,128]{3,2,1,0:T(8,128)(2,1)S(1)}, bf16[2,3,96,128]...) custom-call(bf16[1,128,768]{2,1,0:T(8,128)(2,1)} %query_ref.1, bf16[1,128,768]{2,1,0:T(8,128)(2,1)} %key_ref.1, ...), custom_call_target="tpu_custom_call" | custom-call | tf_op jit(solution)/shard_map/pack_heads/pallas_call | solution.py:50
  6.4 1.6 %collective-permute-start = (bf16[2,3,96,128]{3,2,1,0:T(8,128)(2,1)S(1)}, bf16[2,3,96,128]{3,2,1,0:T(8,128)(2,1)S(1)}, u32[]{:S(2)}, u32[]{:S(2)}) collective-permute-start(bf16[2,3,96,128]{3,2,1,0:T(8,128)(2,1)S(1)} %get-tuple-element.29), channel_id=1, source_target_pairs={{0,8},{4,12},{8,0},{12,4},{16,24},{20,28},{24,16},{28,20},{1,9},{5... | collective-permute-start | bytes 442376 | tf_op jit(solution)/shard_map/ppermute | solution.py:212
  8.0 1.5 %collective-permute-start.1 = (bf16[2,3,96,128]{3,2,1,0:T(8,128)(2,1)S(1)}, bf16[2,3,96,128]{3,2,1,0:T(8,128)(2,1)S(1)}, u32[]{:S(2)}, u32[]{:S(2)}) collective-permute-start(bf16[2,3,96,128]{3,2,1,0:T(8,128)(2,1)S(1)} %get-tuple-element.30), channel_id=1, source_target_pairs={{0,16},{4,20},{8,24},{12,28},{16,0},{20,4},{24,8},{28,12},{1,17},{... | collective-permute-start | bytes 442376 | tf_op jit(solution)/shard_map/ppermute | solution.py:212
  9.5 0.5 %collective-permute-start.2 = (bf16[2,3,96,128]{3,2,1,0:T(8,128)(2,1)S(1)}, bf16[2,3,96,128]{3,2,1,0:T(8,128)(2,1)S(1)}, u32[]{:S(2)}, u32[]{:S(2)}) collective-permute-start(bf16[2,3,96,128]{3,2,1,0:T(8,128)(2,1)S(1)} %get-tuple-element.31), channel_id=1, source_target_pairs={{0,24},{4,28},{8,16},{12,20},{16,8},{20,12},{24,0},{28,4},{1,25},{... | collective-permute-start | bytes 442376 | tf_op jit(solution)/shard_map/ppermute | solution.py:212
  10.0 0.0 collective-permute-start.4
  10.0 1.3 %collective-permute-done.4.refs_4_ = bf16[3,96,128]{2,1,0:T(8,128)(2,1)S(1)} collective-permute-done((bf16[3,96,128]{2,1,0:T(8,128)(2,1)S(1)}, bf16[3,96,128]{2,1,0:T(8,128)(2,1)S(1)}, u32[]{:S(2)}, u32[]{:S(2)}) %collective-permute-start.4) | collective-permute-done | bytes 73760 | tf_op jit(solution)/shard_map/ppermute | solution.py:212
  11.2 0.5 %collective-permute-done.3.refs_5_ = bf16[384,384]{1,0:T(8,128)(2,1)S(1)} collective-permute-done((bf16[384,384]{1,0:T(8,128)(2,1)S(1)}, bf16[384,384]{1,0:T(8,128)(2,1)S(1)}, u32[]{:S(2)}, u32[]{:S(2)}) %collective-permute-start.3) | collective-permute-done | bytes 294944 | tf_op jit(solution)/shard_map/ppermute | solution.py:219
  11.7 1.5 %collective-permute-done.refs_1_ = bf16[2,3,96,128]{3,2,1,0:T(8,128)(2,1)S(1)} collective-permute-done((bf16[2,3,96,128]{3,2,1,0:T(8,128)(2,1)S(1)}, bf16[2,3,96,128]{3,2,1,0:T(8,128)(2,1)S(1)}, u32[]{:S(2)}, u32[]{:S(2)}) %collective-permute-start) | collective-permute-done | bytes 147488 | tf_op jit(solution)/shard_map/ppermute | solution.py:212
  13.2 2.8 %collective-permute-done.1.refs_2_ = bf16[2,3,96,128]{3,2,1,0:T(8,128)(2,1)S(1)} collective-permute-done((bf16[2,3,96,128]{3,2,1,0:T(8,128)(2,1)S(1)}, bf16[2,3,96,128]{3,2,1,0:T(8,128)(2,1)S(1)}, u32[]{:S(2)}, u32[]{:S(2)}) %collective-permute-start.1) | collective-permute-done | bytes 147488 | tf_op jit(solution)/shard_map/ppermute | solution.py:212
  16.0 0.0 collective-permute-done.2.refs_3_
  16.0 0.0 collective-permute-start.5
  16.0 0.5 %collective-permute-start.6 = (bf16[2,3,96,128]{3,2,1,0:T(8,128)(2,1)S(1)}, bf16[2,3,96,128]{3,2,1,0:T(8,128)(2,1)S(1)}, u32[]{:S(2)}, u32[]{:S(2)}) collective-permute-start(bf16[2,3,96,128]{3,2,1,0:T(8,128)(2,1)S(1)} %collective-permute-done.1.refs_2_), channel_id=1, source_target_pairs={{0,4},{4,0},{8,12},{12,8},{16,20},{20,16},{24,28},{28,24},{1,5},{5... | collective-permute-start | bytes 442376 | tf_op jit(solution)/shard_map/ppermute | solution.py:212
  16.5 0.0 collective-permute-start.7
  16.5 0.4 %collective-permute-start.11 = (bf16[384,384]{1,0:T(8,128)(2,1)S(1)}, bf16[384,384]{1,0:T(8,128)(2,1)S(1)}, u32[]{:S(2)}, u32[]{:S(2)}) collective-permute-start(bf16[384,384]{1,0:T(8,128)(2,1)S(1)} %collective-permute-done.3.refs_5_), channel_id=1, source_target_pairs={{0,8},{4,20},{8,0},{12,28},{16,24},{20,4},{24,16},{28,12},{1,9},{5... | collective-permute-start | bytes 884744 | tf_op jit(solution)/shard_map/ppermute | solution.py:215
  16.9 1.3 %collective-permute-start.12 = (bf16[208,384]{1,0:T(8,128)(2,1)S(1)}, bf16[208,384]{1,0:T(8,128)(2,1)S(1)}, u32[]{:S(2)}, u32[]{:S(2)}) collective-permute-start(bf16[208,384]{1,0:T(8,128)(2,1)S(1)} %constant_dynamic-slice_fusion), channel_id=1, source_target_pairs={{0,1},{1,0},{2,3},{3,2},{4,6},{5,7},{6,4},{7,5},{8,9},{9,8},{10,11... | collective-permute-start | bytes 479240 | tf_op jit(solution)/shard_map/ppermute | solution.py:219
  18.9 0.0 collective-permute-done.5.refs_5_
  18.9 0.0 collective-permute-done.6.refs_6_
  18.9 0.0 collective-permute-done.7.refs_7_
  18.9 0.0 copy-start
  19.0 2.2 %attend_one_head.1 = (bf16[2,96,128]{2,1,0:T(8,128)(2,1)S(1)}, bf16[2,96,128]{2,1,0:T(8,128)(2,1)S(1)}, bf16[2,96,128]{2,1,0:T(8,128)(2,1)S(1)}, bf16[2,96,128]{2,1,0:T(8,128)(2,1)S(1)}) custom-call(s32[8,128]{1,0:T(8,128)S(1)} %broadcast_in_dim.2.lengths_ref, bf16[3,96,128]{2,1,0:T(8,128)(2,1)S(1)} %get-tuple-element.28.refs_0_, ...), custom_call_target="tpu_custom_call" | custom-call | tf_op jit(solution)/shard_map/attend_one_head/pallas_call | solution.py:114
  21.2 1.6 %collective-permute-start.8 = (bf16[2,96,128]{2,1,0:T(8,128)(2,1)S(1)}, bf16[2,96,128]{2,1,0:T(8,128)(2,1)S(1)}, u32[]{:S(2)}, u32[]{:S(2)}) collective-permute-start(bf16[2,96,128]{2,1,0:T(8,128)(2,1)S(1)} %get-tuple-element.39), channel_id=1, source_target_pairs={{0,8},{4,12},{8,0},{12,4},{16,24},{20,28},{24,16},{28,20},{1,9},{5... | collective-permute-start | bytes 147464 | tf_op jit(solution)/shard_map/ppermute | solution.py:212
  22.7 0.7 %collective-permute-start.9 = (bf16[2,96,128]{2,1,0:T(8,128)(2,1)S(1)}, bf16[2,96,128]{2,1,0:T(8,128)(2,1)S(1)}, u32[]{:S(2)}, u32[]{:S(2)}) collective-permute-start(bf16[2,96,128]{2,1,0:T(8,128)(2,1)S(1)} %get-tuple-element.40), channel_id=1, source_target_pairs={{0,16},{4,20},{8,24},{12,28},{16,0},{20,4},{24,8},{28,12},{1,17},{... | collective-permute-start | bytes 147464 | tf_op jit(solution)/shard_map/ppermute | solution.py:212
  23.4 1.3 %collective-permute-start.10 = (bf16[2,96,128]{2,1,0:T(8,128)(2,1)S(1)}, bf16[2,96,128]{2,1,0:T(8,128)(2,1)S(1)}, u32[]{:S(2)}, u32[]{:S(2)}) collective-permute-start(bf16[2,96,128]{2,1,0:T(8,128)(2,1)S(1)} %get-tuple-element.41), channel_id=1, source_target_pairs={{0,24},{4,28},{8,16},{12,20},{16,8},{20,12},{24,0},{28,4},{1,25},{... | collective-permute-start | bytes 147464 | tf_op jit(solution)/shard_map/ppermute | solution.py:212
  24.7 0.0 collective-permute-done.12.refs_7_
  24.7 1.5 %collective-permute-start.13 = (bf16[208,384]{1,0:T(8,128)(2,1)S(1)}, bf16[208,384]{1,0:T(8,128)(2,1)S(1)}, u32[]{:S(2)}, u32[]{:S(2)}) collective-permute-start(bf16[208,384]{1,0:T(8,128)(2,1)S(1)} %collective-permute-done.12.refs_7_), channel_id=1, source_target_pairs={{0,8},{4,20},{8,0},{12,28},{16,24},{20,4},{24,16},{28,12},{1,9},{5... | collective-permute-start | bytes 479240 | tf_op jit(solution)/shard_map/ppermute | solution.py:215
  26.2 0.0 collective-permute-done.8.refs_1_
  26.2 0.6 %collective-permute-done.9.refs_2_ = bf16[2,96,128]{2,1,0:T(8,128)(2,1)S(1)} collective-permute-done((bf16[2,96,128]{2,1,0:T(8,128)(2,1)S(1)}, bf16[2,96,128]{2,1,0:T(8,128)(2,1)S(1)}, u32[]{:S(2)}, u32[]{:S(2)}) %collective-permute-start.9) | collective-permute-done | bytes 49184 | tf_op jit(solution)/shard_map/ppermute | solution.py:212
  26.8 1.8 %collective-permute-done.10.refs_3_ = bf16[2,96,128]{2,1,0:T(8,128)(2,1)S(1)} collective-permute-done((bf16[2,96,128]{2,1,0:T(8,128)(2,1)S(1)}, bf16[2,96,128]{2,1,0:T(8,128)(2,1)S(1)}, u32[]{:S(2)}, u32[]{:S(2)}) %collective-permute-start.10) | collective-permute-done | bytes 49184 | tf_op jit(solution)/shard_map/ppermute | solution.py:212
  28.6 0.0 collective-permute-done.11.refs_6_
  28.6 0.0 collective-permute-start.15
  28.6 0.5 %collective-permute-start.16 = (bf16[384,384]{1,0:T(8,128)(2,1)S(1)}, bf16[384,384]{1,0:T(8,128)(2,1)S(1)}, u32[]{:S(2)}, u32[]{:S(2)}) collective-permute-start(bf16[384,384]{1,0:T(8,128)(2,1)S(1)} %collective-permute-done.11.refs_6_), channel_id=1, source_target_pairs={{0,4},{4,0},{8,12},{12,8},{16,20},{20,16},{24,28},{28,24},{1,5},{5... | collective-permute-start | bytes 884744 | tf_op jit(solution)/shard_map/ppermute | solution.py:212
  29.1 0.1 collective-permute-start.14
  29.2 0.5 %collective-permute-start.17 = (bf16[208,384]{1,0:T(8,128)(2,1)S(1)}, bf16[208,384]{1,0:T(8,128)(2,1)S(1)}, u32[]{:S(2)}, u32[]{:S(2)}) collective-permute-start(bf16[208,384]{1,0:T(8,128)(2,1)S(1)} %collective-permute-done.12.refs_7_), channel_id=1, source_target_pairs={{0,4},{4,0},{8,12},{12,8},{16,20},{20,16},{24,28},{28,24},{1,5},{5... | collective-permute-start | bytes 479240 | tf_op jit(solution)/shard_map/ppermute | solution.py:212
  29.7 0.3 collective-permute-done.13.refs_8_
  30.0 0.7 %collective-permute-done.14.refs_4_ = bf16[4,96,128]{2,1,0:T(8,128)(2,1)S(1)} collective-permute-done((bf16[4,96,128]{2,1,0:T(8,128)(2,1)S(1)}, bf16[4,96,128]{2,1,0:T(8,128)(2,1)S(1)}, u32[]{:S(2)}, u32[]{:S(2)}) %collective-permute-start.14) | collective-permute-done | bytes 98336 | tf_op jit(solution)/shard_map/ppermute | solution.py:212
  30.7 0.1 collective-permute-start.18
  30.9 0.1 collective-permute-done.17.refs_11_
  31.0 1.2 %collective-permute-done.18.refs_12_ = bf16[208,384]{1,0:T(8,128)(2,1)S(1)} collective-permute-done((bf16[208,384]{1,0:T(8,128)(2,1)S(1)}, bf16[208,384]{1,0:T(8,128)(2,1)S(1)}, u32[]{:S(2)}, u32[]{:S(2)}) %collective-permute-start.18) | collective-permute-done | bytes 159776 | tf_op jit(solution)/shard_map/ppermute | solution.py:212
  32.1 0.0 collective-permute-done.15.refs_9_
  32.1 0.0 collective-permute-done.16.refs_10_
  32.1 0.0 copy-done
  32.1 1.5 %project_heads.1 = bf16[1,128,1536]{2,1,0:T(8,128)(2,1)} custom-call(bf16[2,96,128]{2,1,0:T(8,128)(2,1)S(1)} %get-tuple-element.38.refs_0_, bf16[2,96,128]{2,1,0:T(8,128)(2,1)S(1)} %collective-permute-done.8.refs_1_, bf16[2,96,128]{2,1,0:T(8,128)(2,1)S(1)} %collective-permute-done.9.refs_2_, bf16[2,96,128]{2,1,0:T(8,128)(2,1)S(1)} %collective-permute-done.10.refs_3_, ...), custom_call_target="tpu_custom_call" | custom-call | flops 301989888 | bytes 2359296 | tf_op jit(solution)/shard_map/project_heads/pallas_call | solution.py:195
  (3 shorter events, 0.0 us)
Async XLA Ops:
  1.0 10.7 %collective-permute-start.3 = (bf16[384,384]{1,0:T(8,128)(2,1)S(1)}, bf16[384,384]{1,0:T(8,128)(2,1)S(1)}, u32[]{:S(2)}, u32[]{:S(2)}) collective-permute-start(bf16[384,384]{1,0:T(8,128)(2,1)S(1)} %constant_dynamic-slice_fusion.1), channel_id=1, source_target_pairs={{0,2},{1,3},{2,0},{3,1},{4,5},{5,4},{6,7},{7,6},{8,10},{9,11},{10,... | collective-permute-start | bytes 884744 | tf_op jit(solution)/shard_map/ppermute | solution.py:219
  6.4 6.8 %collective-permute-start = (bf16[2,3,96,128]{3,2,1,0:T(8,128)(2,1)S(1)}, bf16[2,3,96,128]{3,2,1,0:T(8,128)(2,1)S(1)}, u32[]{:S(2)}, u32[]{:S(2)}) collective-permute-start(bf16[2,3,96,128]{3,2,1,0:T(8,128)(2,1)S(1)} %get-tuple-element.29), channel_id=1, source_target_pairs={{0,8},{4,12},{8,0},{12,4},{16,24},{20,28},{24,16},{28,20},{1,9},{5... | collective-permute-start | bytes 442376 | tf_op jit(solution)/shard_map/ppermute | solution.py:212
  8.0 8.0 %collective-permute-start.1 = (bf16[2,3,96,128]{3,2,1,0:T(8,128)(2,1)S(1)}, bf16[2,3,96,128]{3,2,1,0:T(8,128)(2,1)S(1)}, u32[]{:S(2)}, u32[]{:S(2)}) collective-permute-start(bf16[2,3,96,128]{3,2,1,0:T(8,128)(2,1)S(1)} %get-tuple-element.30), channel_id=1, source_target_pairs={{0,16},{4,20},{8,24},{12,28},{16,0},{20,4},{24,8},{28,12},{1,17},{... | collective-permute-start | bytes 442376 | tf_op jit(solution)/shard_map/ppermute | solution.py:212
  9.5 6.5 %collective-permute-start.2 = (bf16[2,3,96,128]{3,2,1,0:T(8,128)(2,1)S(1)}, bf16[2,3,96,128]{3,2,1,0:T(8,128)(2,1)S(1)}, u32[]{:S(2)}, u32[]{:S(2)}) collective-permute-start(bf16[2,3,96,128]{3,2,1,0:T(8,128)(2,1)S(1)} %get-tuple-element.31), channel_id=1, source_target_pairs={{0,24},{4,28},{8,16},{12,20},{16,8},{20,12},{24,0},{28,4},{1,25},{... | collective-permute-start | bytes 442376 | tf_op jit(solution)/shard_map/ppermute | solution.py:212
  10.0 1.3 %collective-permute-start.4 = (bf16[3,96,128]{2,1,0:T(8,128)(2,1)S(1)}, bf16[3,96,128]{2,1,0:T(8,128)(2,1)S(1)}, u32[]{:S(2)}, u32[]{:S(2)}) collective-permute-start(bf16[3,96,128]{2,1,0:T(8,128)(2,1)S(1)} %get-tuple-element.32), channel_id=1, source_target_pairs={{0,4},{4,0},{8,12},{12,8},{16,20},{20,16},{24,28},{28,24},{1,5},{5... | collective-permute-start | bytes 221192 | tf_op jit(solution)/shard_map/ppermute | solution.py:212
  16.0 2.9 %collective-permute-start.5 = (bf16[2,3,96,128]{3,2,1,0:T(8,128)(2,1)S(1)}, bf16[2,3,96,128]{3,2,1,0:T(8,128)(2,1)S(1)}, u32[]{:S(2)}, u32[]{:S(2)}) collective-permute-start(bf16[2,3,96,128]{3,2,1,0:T(8,128)(2,1)S(1)} %collective-permute-done.refs_1_), channel_id=1, source_target_pairs={{0,4},{4,0},{8,12},{12,8},{16,20},{20,16},{24,28},{28,24},{1,5},{5... | collective-permute-start | bytes 442376 | tf_op jit(solution)/shard_map/ppermute | solution.py:212
  16.0 2.9 %collective-permute-start.6 = (bf16[2,3,96,128]{3,2,1,0:T(8,128)(2,1)S(1)}, bf16[2,3,96,128]{3,2,1,0:T(8,128)(2,1)S(1)}, u32[]{:S(2)}, u32[]{:S(2)}) collective-permute-start(bf16[2,3,96,128]{3,2,1,0:T(8,128)(2,1)S(1)} %collective-permute-done.1.refs_2_), channel_id=1, source_target_pairs={{0,4},{4,0},{8,12},{12,8},{16,20},{20,16},{24,28},{28,24},{1,5},{5... | collective-permute-start | bytes 442376 | tf_op jit(solution)/shard_map/ppermute | solution.py:212
  16.5 2.4 %collective-permute-start.7 = (bf16[2,3,96,128]{3,2,1,0:T(8,128)(2,1)S(1)}, bf16[2,3,96,128]{3,2,1,0:T(8,128)(2,1)S(1)}, u32[]{:S(2)}, u32[]{:S(2)}) collective-permute-start(bf16[2,3,96,128]{3,2,1,0:T(8,128)(2,1)S(1)} %collective-permute-done.2.refs_3_), channel_id=1, source_target_pairs={{0,4},{4,0},{8,12},{12,8},{16,20},{20,16},{24,28},{28,24},{1,5},{5... | collective-permute-start | bytes 442376 | tf_op jit(solution)/shard_map/ppermute | solution.py:212
  16.5 12.1 %collective-permute-start.11 = (bf16[384,384]{1,0:T(8,128)(2,1)S(1)}, bf16[384,384]{1,0:T(8,128)(2,1)S(1)}, u32[]{:S(2)}, u32[]{:S(2)}) collective-permute-start(bf16[384,384]{1,0:T(8,128)(2,1)S(1)} %collective-permute-done.3.refs_5_), channel_id=1, source_target_pairs={{0,8},{4,20},{8,0},{12,28},{16,24},{20,4},{24,16},{28,12},{1,9},{5... | collective-permute-start | bytes 884744 | tf_op jit(solution)/shard_map/ppermute | solution.py:215
  16.9 7.8 %collective-permute-start.12 = (bf16[208,384]{1,0:T(8,128)(2,1)S(1)}, bf16[208,384]{1,0:T(8,128)(2,1)S(1)}, u32[]{:S(2)}, u32[]{:S(2)}) collective-permute-start(bf16[208,384]{1,0:T(8,128)(2,1)S(1)} %constant_dynamic-slice_fusion), channel_id=1, source_target_pairs={{0,1},{1,0},{2,3},{3,2},{4,6},{5,7},{6,4},{7,5},{8,9},{9,8},{10,11... | collective-permute-start | bytes 479240 | tf_op jit(solution)/shard_map/ppermute | solution.py:219
  18.9 13.2 %copy-start = (bf16[768,384]{1,0:T(8,128)(2,1)S(1)}, bf16[768,384]{1,0:T(8,128)(2,1)}, u32[]{:S(2)}) copy-start(bf16[768,384]{1,0:T(8,128)(2,1)} %refs_13_.1) | copy-start | bytes 1769476
  21.2 5.1 %collective-permute-start.8 = (bf16[2,96,128]{2,1,0:T(8,128)(2,1)S(1)}, bf16[2,96,128]{2,1,0:T(8,128)(2,1)S(1)}, u32[]{:S(2)}, u32[]{:S(2)}) collective-permute-start(bf16[2,96,128]{2,1,0:T(8,128)(2,1)S(1)} %get-tuple-element.39), channel_id=1, source_target_pairs={{0,8},{4,12},{8,0},{12,4},{16,24},{20,28},{24,16},{28,20},{1,9},{5... | collective-permute-start | bytes 147464 | tf_op jit(solution)/shard_map/ppermute | solution.py:212
  22.7 4.1 %collective-permute-start.9 = (bf16[2,96,128]{2,1,0:T(8,128)(2,1)S(1)}, bf16[2,96,128]{2,1,0:T(8,128)(2,1)S(1)}, u32[]{:S(2)}, u32[]{:S(2)}) collective-permute-start(bf16[2,96,128]{2,1,0:T(8,128)(2,1)S(1)} %get-tuple-element.40), channel_id=1, source_target_pairs={{0,16},{4,20},{8,24},{12,28},{16,0},{20,4},{24,8},{28,12},{1,17},{... | collective-permute-start | bytes 147464 | tf_op jit(solution)/shard_map/ppermute | solution.py:212
  23.4 5.2 %collective-permute-start.10 = (bf16[2,96,128]{2,1,0:T(8,128)(2,1)S(1)}, bf16[2,96,128]{2,1,0:T(8,128)(2,1)S(1)}, u32[]{:S(2)}, u32[]{:S(2)}) collective-permute-start(bf16[2,96,128]{2,1,0:T(8,128)(2,1)S(1)} %get-tuple-element.41), channel_id=1, source_target_pairs={{0,24},{4,28},{8,16},{12,20},{16,8},{20,12},{24,0},{28,4},{1,25},{... | collective-permute-start | bytes 147464 | tf_op jit(solution)/shard_map/ppermute | solution.py:212
  24.7 5.3 %collective-permute-start.13 = (bf16[208,384]{1,0:T(8,128)(2,1)S(1)}, bf16[208,384]{1,0:T(8,128)(2,1)S(1)}, u32[]{:S(2)}, u32[]{:S(2)}) collective-permute-start(bf16[208,384]{1,0:T(8,128)(2,1)S(1)} %collective-permute-done.12.refs_7_), channel_id=1, source_target_pairs={{0,8},{4,20},{8,0},{12,28},{16,24},{20,4},{24,16},{28,12},{1,9},{5... | collective-permute-start | bytes 479240 | tf_op jit(solution)/shard_map/ppermute | solution.py:215
  28.6 3.5 %collective-permute-start.15 = (bf16[384,384]{1,0:T(8,128)(2,1)S(1)}, bf16[384,384]{1,0:T(8,128)(2,1)S(1)}, u32[]{:S(2)}, u32[]{:S(2)}) collective-permute-start(bf16[384,384]{1,0:T(8,128)(2,1)S(1)} %collective-permute-done.3.refs_5_), channel_id=1, source_target_pairs={{0,4},{4,0},{8,12},{12,8},{16,20},{20,16},{24,28},{28,24},{1,5},{5... | collective-permute-start | bytes 884744 | tf_op jit(solution)/shard_map/ppermute | solution.py:212
  28.6 3.5 %collective-permute-start.16 = (bf16[384,384]{1,0:T(8,128)(2,1)S(1)}, bf16[384,384]{1,0:T(8,128)(2,1)S(1)}, u32[]{:S(2)}, u32[]{:S(2)}) collective-permute-start(bf16[384,384]{1,0:T(8,128)(2,1)S(1)} %collective-permute-done.11.refs_6_), channel_id=1, source_target_pairs={{0,4},{4,0},{8,12},{12,8},{16,20},{20,16},{24,28},{28,24},{1,5},{5... | collective-permute-start | bytes 884744 | tf_op jit(solution)/shard_map/ppermute | solution.py:212
  29.1 1.6 %collective-permute-start.14 = (bf16[4,96,128]{2,1,0:T(8,128)(2,1)S(1)}, bf16[4,96,128]{2,1,0:T(8,128)(2,1)S(1)}, u32[]{:S(2)}, u32[]{:S(2)}) collective-permute-start(bf16[4,96,128]{2,1,0:T(8,128)(2,1)S(1)} %second_entries.1), channel_id=1, source_target_pairs={{0,4},{4,0},{8,12},{12,8},{16,20},{20,16},{24,28},{28,24},{1,5},{5... | collective-permute-start | bytes 294920 | tf_op jit(solution)/shard_map/ppermute | solution.py:212
  29.2 1.8 %collective-permute-start.17 = (bf16[208,384]{1,0:T(8,128)(2,1)S(1)}, bf16[208,384]{1,0:T(8,128)(2,1)S(1)}, u32[]{:S(2)}, u32[]{:S(2)}) collective-permute-start(bf16[208,384]{1,0:T(8,128)(2,1)S(1)} %collective-permute-done.12.refs_7_), channel_id=1, source_target_pairs={{0,4},{4,0},{8,12},{12,8},{16,20},{20,16},{24,28},{28,24},{1,5},{5... | collective-permute-start | bytes 479240 | tf_op jit(solution)/shard_map/ppermute | solution.py:212
  30.7 1.4 %collective-permute-start.18 = (bf16[208,384]{1,0:T(8,128)(2,1)S(1)}, bf16[208,384]{1,0:T(8,128)(2,1)S(1)}, u32[]{:S(2)}, u32[]{:S(2)}) collective-permute-start(bf16[208,384]{1,0:T(8,128)(2,1)S(1)} %collective-permute-done.13.refs_8_), channel_id=1, source_target_pairs={{0,4},{4,0},{8,12},{12,8},{16,20},{20,16},{24,28},{28,24},{1,5},{5... | collective-permute-start | bytes 479240 | tf_op jit(solution)/shard_map/ppermute | solution.py:212

commit v9 on v8

--- a/solution.py
+++ b/solution.py
@@ -146,70 +146,136 @@
     return ((place >> 2) ^ (place >> 1)) & 1
 
 
-def project_kernel(shards, *refs):
-    each = len(FLIPS)
-    heads_same, heads_other, pieces = refs[:each], refs[each], refs[each + 1 : -3]
-    out_ref, turned, weight = refs[-3:]
+def gather_heads(heads_same, heads_other, turned):
     place = place_in_group()
-    core, parity = place & 1, parity_of(place)
     rows = turned.shape[0] // HEADS
     for flip in range(HEADS):
         here = pl.ds(pl.multiple_of((place ^ flip) * rows, 32), rows)
         turned[here, :] = heads_other[flip // 2] if flip % 2 else heads_same[flip // 2][0]
+
+
+def project_kernel(*refs):
+    each = len(FLIPS)
+    heads_same, heads_other, halves = refs[:each], refs[each], refs[each + 1 : each + 3]
+    out_ref, turned, weight = refs[each + 3 :]
+    gather_heads(heads_same, heads_other, turned)
     half = weight.shape[0] // 2
-    if shards == 1:
-        for other, ref in enumerate(pieces):
-            weight[pl.ds(pl.multiple_of((core ^ other) * half, 32), half), :] = ref[...]
-    else:
-        *pieces, own_ref = pieces
-        columns = own_ref.shape[1]
-        part = pieces[2].shape[0]
-        for other in range(2):
-            fetched, passed, third, third_passed = pieces[4 * other : 4 * other + 4]
-            near = pl.ds(pl.multiple_of((1 - (core ^ other)) * columns, 128), columns)
-            last = slice(2 * columns, 3 * columns)
-            for flip, whole_ref, part_ref in ((0, fetched, third), (1, passed, third_passed)):
-                first = (parity ^ flip) * half
-                weight[pl.ds(pl.multiple_of(first, 32), half), near] = whole_ref[...]
-                first = first + (core ^ other) * (half - part)
-                weight[pl.ds(pl.multiple_of(first, 16), part), last] = part_ref[...]
-    attention = turned[...].T
-    foreign = jnp.dot(attention, weight[...], preferred_element_type=jnp.float32).astype(out_ref.dtype)
-    if shards == 1:
-        out_ref[0] = foreign
-        return
-    shard = lax.axis_index("fsdp")
-    own = jnp.dot(attention, own_ref[...], preferred_element_type=jnp.float32).astype(out_ref.dtype)
-    out_ref[0, :, pl.ds(pl.multiple_of(shard * columns, 128), columns)] = own
-    for flip in range(1, shards):
+    for other, ref in enumerate(halves):
+        weight[pl.ds(pl.multiple_of(((place_in_group() & 1) ^ other) * half, 32), half), :] = ref[...]
+    out_ref[0] = jnp.dot(turned[...].T, weight[...], preferred_element_type=jnp.float32).astype(out_ref.dtype)
+
+
+def project_near_kernel(*refs):
+    each = len(FLIPS)
+    heads_same, heads_other, own_ref, pieces = refs[:each], refs[each], refs[each + 1], refs[each + 2 : each + 6]
+    out_ref, attention_ref, turned, weight, blocks, sems = refs[each + 6 :]
+    gather_heads(heads_same, heads_other, turned)
+    attention_ref[...] = turned[...].T
+    place, shard = place_in_group(), lax.axis_index("fsdp")
+    half, columns = pieces[0].shape
+    beside = (place & 1) ^ 1
+    copies = []
+    for at, flip in enumerate((0, 1, 2)):
+        if flip == 0:
+            block = own_ref[...]
+        else:
+            mine = beside == flip - 1
+            for other in range(2):
+                here = pl.ds(pl.multiple_of((parity_of(place) ^ other) * half, 32), half)
+                weight[flip - 1, here, :] = jnp.where(mine, pieces[other][...], pieces[2 + other][...])
+            block = weight[flip - 1]
+        blocks[at] = jnp.dot(attention_ref[...], block, preferred_element_type=jnp.float32).astype(blocks.dtype)
         here = pl.ds(pl.multiple_of((shard ^ flip) * columns, 128), columns)
-        out_ref[0, :, here] = foreign[:, (flip - 1) * columns : flip * columns]
-
-
-def project(heads_same, heads_other, pieces, own, shards):
+        copies.append(pltpu.make_async_copy(blocks.at[at], out_ref.at[0, :, here], sems.at[at]))
+        copies[-1].start()
+    for copy in copies:
+        copy.wait()
+
+
+def project_third_kernel(so_far_ref, attention_ref, *refs):
+    pieces, (out_ref, weight, block, sem) = refs[:4], refs[4:]
+    place, shard = place_in_group(), lax.axis_index("fsdp")
+    part, columns = pieces[0].shape
+    half = weight.shape[0] // 2
+    for other in range(2):
+        for flip in range(2):
+            first = (parity_of(place) ^ flip) * half + ((place & 1) ^ other) * (half - part)
+            weight[pl.ds(pl.multiple_of(first, 16), part), :] = pieces[2 * other + flip][...]
+    block[...] = jnp.dot(attention_ref[...], weight[...], preferred_element_type=jnp.float32).astype(block.dtype)
+    here = pl.ds(pl.multiple_of((shard ^ 3) * columns, 128), columns)
+    copy = pltpu.make_async_copy(block, out_ref.at[0, :, here], sem)
+    copy.start()
+    copy.wait()
+
+
+def projection_cost(frames, features, columns):
+    return pl.CostEstimate(
+        flops=2 * features * frames * columns, bytes_accessed=2 * features * columns, transcendentals=0
+    )
+
+
+def project(heads_same, heads_other, halves):
     _, rows, frames = heads_other.shape
-    foreign = (shards - 1) * own[0].shape[1] if own else pieces[0].shape[1]
-    width = foreign + (own[0].shape[1] if own else 0)
-    features = HEADS * rows
-    pieces = [*heads_same, heads_other, *pieces, *own]
-    return pl.pallas_call(
-        functools.partial(project_kernel, shards),
+    features, width = HEADS * rows, halves[0].shape[1]
+    return pl.pallas_call(
+        project_kernel,
         out_shape=jax.ShapeDtypeStruct((1, frames, width), jnp.bfloat16),
-        in_specs=[WHOLE] * len(pieces),
+        in_specs=[WHOLE] * (len(FLIPS) + 3),
         out_specs=WHOLE,
-        scratch_shapes=[pltpu.VMEM((features, frames), jnp.bfloat16), pltpu.VMEM((features, foreign), jnp.bfloat16)],
-        compiler_params=params(24),
-        cost_estimate=pl.CostEstimate(
-            flops=2 * features * frames * width, bytes_accessed=2 * features * width, transcendentals=0
-        ),
+        scratch_shapes=[pltpu.VMEM((features, frames), jnp.bfloat16), pltpu.VMEM((features, width), jnp.bfloat16)],
+        compiler_params=params(24),
+        cost_estimate=projection_cost(frames, features, width),
         name="project_heads",
-    )(*pieces)
+    )(*heads_same, heads_other, *halves)
+
+
+def project_near(heads_same, heads_other, own, pieces):
+    _, rows, frames = heads_other.shape
+    features, columns = own.shape
+    return pl.pallas_call(
+        project_near_kernel,
+        out_shape=[jax.ShapeDtypeStruct((1, frames, 4 * columns), jnp.bfloat16), pltpu.VMEM((frames, features), jnp.bfloat16)],
+        in_specs=[WHOLE] * (len(FLIPS) + 6),
+        out_specs=[IN_HBM, WHOLE],
+        scratch_shapes=[
+            pltpu.VMEM((features, frames), jnp.bfloat16),
+            pltpu.VMEM((2, features, columns), jnp.bfloat16),
+            pltpu.VMEM((3, frames, columns), jnp.bfloat16),
+            pltpu.SemaphoreType.DMA((3,)),
+        ],
+        compiler_params=params(24),
+        cost_estimate=projection_cost(frames, features, 3 * columns),
+        name="project_near_shards",
+    )(*heads_same, heads_other, own, *pieces)
+
+
+def project_third(so_far, attention, pieces):
+    frames, features = attention.shape
+    columns = pieces[0].shape[1]
+    return pl.pallas_call(
+        project_third_kernel,
+        out_shape=jax.ShapeDtypeStruct(so_far.shape, so_far.dtype),
+        in_specs=[IN_HBM] + [WHOLE] * 5,
+        out_specs=IN_HBM,
+        input_output_aliases={0: 0},
+        scratch_shapes=[
+            pltpu.VMEM((features, columns), jnp.bfloat16),
+            pltpu.VMEM((frames, columns), jnp.bfloat16),
+            pltpu.SemaphoreType.DMA,
+        ],
+        compiler_params=params(24),
+        cost_estimate=projection_cost(frames, features, columns),
+        name="project_third_shard",
+    )(so_far, attention, *pieces)
 
 
 def per_device(ctx, fsdp, queries, key_rows, value_rows, lengths, out_weight):
     def exchange(array, axis, flip):
         size = ctx if axis == "ctx" else fsdp
         return lax.ppermute(array, axis, [(i, i ^ flip) for i in range(size)])
+
+    def exchange_chips(arrays):
+        return [exchange(array, "ctx", flip) for flip, array in zip(FLIPS[1:], arrays)]
 
     def exchange_in_plane(array):
         return lax.ppermute(array, "ctx", [(i, i ^ (4 if i % 2 else 2)) for i in range(ctx)])
@@ -231,10 +297,10 @@
         half = lax.all_gather(half, "fsdp", axis=1, tiled=True)
 
     own_same, own_other, *by_chip = pack(queries, key_rows, value_rows)
-    same = [exchange(array, "ctx", flip) for flip, array in zip(FLIPS[1:], by_chip)]
+    same = exchange_chips(by_chip)
     own_other = exchange(own_other, "ctx", 1)
     if split_columns:
-        fetched, own_other = lax.optimization_barrier((fetched, own_other))
+        fetched, own_other, lengths = lax.optimization_barrier((fetched, own_other, lengths))
         passed = exchange_in_plane(fetched)
         part = rows // 2 + 16
         third = lax.dynamic_slice_in_dim(fetched, core * (rows - part), part, 0)
@@ -253,21 +319,20 @@
         rest = lax.all_gather(jnp.stack(pairs), "ctx", axis=0, axis_index_groups=across, tiled=True)
     mixed = attend(lengths, [own_same, *same], other, rest, groups)
 
-    heads = [exchange(array, "ctx", flip) for flip, array in zip(FLIPS[1:], mixed[1:])]
-    own = []
+    heads = exchange_chips(mixed[1:])
     if split_columns:
-        heads, fetched, passed, third = lax.optimization_barrier((heads, fetched, passed, third))
-        pieces = [fetched, passed, third]
-        others = [exchange(array, "ctx", 1) for array in pieces]
+        heads, *arrived = lax.optimization_barrier((heads, fetched, passed, third))
+        fetched, passed, third = arrived
+        fetched_other, passed_other, third_other = (exchange(array, "ctx", 1) for array in arrived)
     heads_same = [mixed[0], *heads]
     heads_other = exchange(second_entries(heads_same), "ctx", 1)
-    if split_columns:
-        third_passed, heads_other = lax.optimization_barrier((third_passed, heads_other))
-        pieces += [third_passed, *others, exchange(third_passed, "ctx", 1)]
-        own = [out_weight]
-    else:
-        pieces = [half, exchange(half, "ctx", 1)]
-    return project(heads_same, heads_other, pieces, own, fsdp if split_columns else 1)
+    if not split_columns:
+        return project(heads_same, heads_other, [half, exchange(half, "ctx", 1)])
+    third_passed, heads_other = lax.optimization_barrier((third_passed, heads_other))
+    third_passed_other = exchange(third_passed, "ctx", 1)
+    near = [fetched, passed, fetched_other, passed_other]
+    so_far, attention = project_near(heads_same, heads_other, out_weight, near)
+    return project_third(so_far, attention, [third, third_passed, third_other, third_passed_other])
 
 
 def solution(mesh):

time: 33.8 us -> 32.7 us (0.967)
  waiting for transfers between devices: 10.7 us -> 8.61 us
  Pallas kernels: 5.05 us -> 5.94 us
    ppermute x15, waiting for transfers between devices: 9.88 us -> 7.86 us  [exchange(): return lax.ppermute(array, axis, [(i, i ^ flip) for i in range(size)])]
    pallas_call x1 -> x2, Pallas kernels: 1.52 us -> 2.42 us  [the longest x1 1.41 us: project_near(): pl.pallas_call(project_near_kernel, out_shape=[jax.ShapeDtypeStruct((1, f...]
    ppermute x2, starting transfers between devices: 1.9 us -> 2.33 us  [exchange_in_plane(): lax.ppermute(array, 'ctx', [(i, i ^ (4 if i % 2 else 2)) for i in range(c...]
  transfers between devices with their start and end apart: 19 -> 19, of which waited for: 10 -> 9; matrix products, arithmetic and copies ran while one was open for 0% -> 0% of each run, Pallas kernels for 10% -> 15%
where the time goes in v9:
time: 32.7 us; the launch traced here: 32.6 us
  starting transfers between devices  16.3 us (50%)
  waiting for transfers between devices  8.61 us (26%)
  Pallas kernels  5.94 us (18%)
  local copies, waits for them, and re-layouts  1.01 us (3%)
  between operations  0.73 us (2%)
    ppermute x15, starting transfers between devices, exchange(): return lax.ppermute(array, axis, [(i, i ^ flip) for i in range(size)])  8.84 us
    ppermute x15, waiting for transfers between devices, exchange(): return lax.ppermute(array, axis, [(i, i ^ flip) for i in range(size)])  7.86 us
    ppermute x2, starting transfers between devices, exchange_along(): return lax.ppermute(array, ('ctx', 'fsdp'), pairs)  5.12 us
    ppermute x2, starting transfers between devices, exchange_in_plane(): lax.ppermute(array, 'ctx', [(i, i ^ (4 if i % 2 else 2)) for i in range(c...  2.33 us
    pallas_call x1, Pallas kernels, attend(): pl.pallas_call(functools.partial(attention_kernel, groups), out_shape=[ja...  2.21 us
    pallas_call x1, Pallas kernels, project_near(): pl.pallas_call(project_near_kernel, out_shape=[jax.ShapeDtypeStruct((1, f...  1.41 us
    pallas_call x1, Pallas kernels, pack(): pl.pallas_call(pack_kernel, out_shape=[own] * 2 + [two] * (len(FLIPS) - 1...  1.31 us
    pallas_call x1, Pallas kernels, project_third(): pl.pallas_call(project_third_kernel, out_shape=jax.ShapeDtypeStruct(so_fa...  1 us
  transfers between devices with their start and end apart: 19, of which 9 were waited for; matrix products, arithmetic and copies ran while one was open for 0% of the time, Pallas kernels for 15%

profile of v9, /device:TPU:0, one launch (start us, length us, event | category | flops | bytes accessed | tf_op | source)
XLA Modules:
  0.0 32.6 jit_solution(13345898696173672625)
XLA Ops:
  0.0 1.0 %constant_dynamic-slice_fusion.1 = bf16[384,384]{1,0:T(8,128)(2,1)S(1)} fusion(bf16[768,384]{1,0:T(8,128)(2,1)} %refs_5_.1, s32[]{:T(128)S(6)} %select_n.14), kind=kLoop, calls=%fused_computation.1 | loop fusion | bytes 589828 | tf_op jit(solution)/shard_map/dynamic_slice | solution.py:293
  1.0 4.1 %collective-permute-start = (bf16[384,384]{1,0:T(8,128)(2,1)S(1)}, bf16[384,384]{1,0:T(8,128)(2,1)S(1)}, u32[]{:S(2)}, u32[]{:S(2)}) collective-permute-start(bf16[384,384]{1,0:T(8,128)(2,1)S(1)} %constant_dynamic-slice_fusion.1), channel_id=1, source_target_pairs={{0,2},{1,3},{2,0},{3,1},{4,5},{5,4},{6,7},{7,6},{8,10},{9,11},{10,... | collective-permute-start | bytes 884744 | tf_op jit(solution)/shard_map/ppermute | solution.py:285
  5.1 1.3 %pack_heads.1 = (bf16[3,96,128]{2,1,0:T(8,128)(2,1)S(1)}, bf16[3,96,128]{2,1,0:T(8,128)(2,1)S(1)}, bf16[2,3,96,128]{3,2,1,0:T(8,128)(2,1)S(1)}, bf16[2,3,96,128]...) custom-call(bf16[1,128,768]{2,1,0:T(8,128)(2,1)} %query_ref.1, bf16[1,128,768]{2,1,0:T(8,128)(2,1)} %key_ref.1, ...), custom_call_target="tpu_custom_call" | custom-call | tf_op jit(solution)/shard_map/pack_heads/pallas_call | solution.py:50
  6.4 1.6 %collective-permute-start.2 = (bf16[2,3,96,128]{3,2,1,0:T(8,128)(2,1)S(1)}, bf16[2,3,96,128]{3,2,1,0:T(8,128)(2,1)S(1)}, u32[]{:S(2)}, u32[]{:S(2)}) collective-permute-start(bf16[2,3,96,128]{3,2,1,0:T(8,128)(2,1)S(1)} %get-tuple-element.34), channel_id=1, source_target_pairs={{0,8},{4,12},{8,0},{12,4},{16,24},{20,28},{24,16},{28,20},{1,9},{5... | collective-permute-start | bytes 442376 | tf_op jit(solution)/shard_map/ppermute | solution.py:275
  8.0 1.5 %collective-permute-start.3 = (bf16[2,3,96,128]{3,2,1,0:T(8,128)(2,1)S(1)}, bf16[2,3,96,128]{3,2,1,0:T(8,128)(2,1)S(1)}, u32[]{:S(2)}, u32[]{:S(2)}) collective-permute-start(bf16[2,3,96,128]{3,2,1,0:T(8,128)(2,1)S(1)} %get-tuple-element.35), channel_id=1, source_target_pairs={{0,16},{4,20},{8,24},{12,28},{16,0},{20,4},{24,8},{28,12},{1,17},{... | collective-permute-start | bytes 442376 | tf_op jit(solution)/shard_map/ppermute | solution.py:275
  9.5 0.5 %collective-permute-start.4 = (bf16[2,3,96,128]{3,2,1,0:T(8,128)(2,1)S(1)}, bf16[2,3,96,128]{3,2,1,0:T(8,128)(2,1)S(1)}, u32[]{:S(2)}, u32[]{:S(2)}) collective-permute-start(bf16[2,3,96,128]{3,2,1,0:T(8,128)(2,1)S(1)} %get-tuple-element.36), channel_id=1, source_target_pairs={{0,24},{4,28},{8,16},{12,20},{16,8},{20,12},{24,0},{28,4},{1,25},{... | collective-permute-start | bytes 442376 | tf_op jit(solution)/shard_map/ppermute | solution.py:275
  10.0 0.0 collective-permute-start.1
  10.6 0.6 %collective-permute-done.1.refs_4_ = bf16[3,96,128]{2,1,0:T(8,128)(2,1)S(1)} collective-permute-done((bf16[3,96,128]{2,1,0:T(8,128)(2,1)S(1)}, bf16[3,96,128]{2,1,0:T(8,128)(2,1)S(1)}, u32[]{:S(2)}, u32[]{:S(2)}) %collective-permute-start.1) | collective-permute-done | bytes 73760 | tf_op jit(solution)/shard_map/ppermute | solution.py:275
  11.2 0.5 %collective-permute-done.refs_6_ = bf16[384,384]{1,0:T(8,128)(2,1)S(1)} collective-permute-done((bf16[384,384]{1,0:T(8,128)(2,1)S(1)}, bf16[384,384]{1,0:T(8,128)(2,1)S(1)}, u32[]{:S(2)}, u32[]{:S(2)}) %collective-permute-start) | collective-permute-done | bytes 294944 | tf_op jit(solution)/shard_map/ppermute | solution.py:285
  11.7 2.1 %collective-permute-start.11 = (bf16[384,384]{1,0:T(8,128)(2,1)S(1)}, bf16[384,384]{1,0:T(8,128)(2,1)S(1)}, u32[]{:S(2)}, u32[]{:S(2)}) collective-permute-start(bf16[384,384]{1,0:T(8,128)(2,1)S(1)} %collective-permute-done.refs_6_), channel_id=1, source_target_pairs={{0,8},{4,20},{8,0},{12,28},{16,24},{20,4},{24,16},{28,12},{1,9},{5... | collective-permute-start | bytes 884744 | tf_op jit(solution)/shard_map/ppermute | solution.py:281
  13.8 0.0 collective-permute-done.2.refs_1_
  13.8 2.5 %collective-permute-done.3.refs_2_ = bf16[2,3,96,128]{3,2,1,0:T(8,128)(2,1)S(1)} collective-permute-done((bf16[2,3,96,128]{3,2,1,0:T(8,128)(2,1)S(1)}, bf16[2,3,96,128]{3,2,1,0:T(8,128)(2,1)S(1)}, u32[]{:S(2)}, u32[]{:S(2)}) %collective-permute-start.3) | collective-permute-done | bytes 147488 | tf_op jit(solution)/shard_map/ppermute | solution.py:275
  16.3 0.0 collective-permute-done.4.refs_3_
  16.3 0.0 collective-permute-start.5
  16.3 0.5 %collective-permute-start.6 = (bf16[2,3,96,128]{3,2,1,0:T(8,128)(2,1)S(1)}, bf16[2,3,96,128]{3,2,1,0:T(8,128)(2,1)S(1)}, u32[]{:S(2)}, u32[]{:S(2)}) collective-permute-start(bf16[2,3,96,128]{3,2,1,0:T(8,128)(2,1)S(1)} %collective-permute-done.3.refs_2_), channel_id=1, source_target_pairs={{0,4},{4,0},{8,12},{12,8},{16,20},{20,16},{24,28},{28,24},{1,5},{5... | collective-permute-start | bytes 442376 | tf_op jit(solution)/shard_map/ppermute | solution.py:275
  16.8 0.0 collective-permute-start.7
  16.8 1.0 %collective-permute-start.12 = (bf16[208,384]{1,0:T(8,128)(2,1)S(1)}, bf16[208,384]{1,0:T(8,128)(2,1)S(1)}, u32[]{:S(2)}, u32[]{:S(2)}) collective-permute-start(bf16[208,384]{1,0:T(8,128)(2,1)S(1)} %constant_dynamic-slice_fusion), channel_id=1, source_target_pairs={{0,1},{1,0},{2,3},{3,2},{4,6},{5,7},{6,4},{7,5},{8,9},{9,8},{10,11... | collective-permute-start | bytes 479240 | tf_op jit(solution)/shard_map/ppermute | solution.py:285
  17.8 0.0 collective-permute-done.5.refs_5_
  17.8 0.0 collective-permute-done.6.refs_6_
  17.9 0.3 collective-permute-done.7.refs_7_
  18.2 0.0 copy-start
  18.2 2.2 %attend_one_head.1 = (bf16[2,96,128]{2,1,0:T(8,128)(2,1)S(1)}, bf16[2,96,128]{2,1,0:T(8,128)(2,1)S(1)}, bf16[2,96,128]{2,1,0:T(8,128)(2,1)S(1)}, bf16[2,96,128]{2,1,0:T(8,128)(2,1)S(1)}) custom-call(s32[8,128]{1,0:T(8,128)S(1)} %broadcast_in_dim.2.lengths_ref, bf16[3,96,128]{2,1,0:T(8,128)(2,1)S(1)} %get-tuple-element.33.refs_0_, ...), custom_call_target="tpu_custom_call" | custom-call | tf_op jit(solution)/shard_map/attend_one_head/pallas_call | solution.py:114
  20.4 0.6 %collective-permute-start.10 = (bf16[2,96,128]{2,1,0:T(8,128)(2,1)S(1)}, bf16[2,96,128]{2,1,0:T(8,128)(2,1)S(1)}, u32[]{:S(2)}, u32[]{:S(2)}) collective-permute-start(bf16[2,96,128]{2,1,0:T(8,128)(2,1)S(1)} %get-tuple-element.45), channel_id=1, source_target_pairs={{0,24},{4,28},{8,16},{12,20},{16,8},{20,12},{24,0},{28,4},{1,25},{... | collective-permute-start | bytes 147464 | tf_op jit(solution)/shard_map/ppermute | solution.py:275
  20.9 2.4 %collective-permute-start.8 = (bf16[2,96,128]{2,1,0:T(8,128)(2,1)S(1)}, bf16[2,96,128]{2,1,0:T(8,128)(2,1)S(1)}, u32[]{:S(2)}, u32[]{:S(2)}) collective-permute-start(bf16[2,96,128]{2,1,0:T(8,128)(2,1)S(1)} %get-tuple-element.43), channel_id=1, source_target_pairs={{0,8},{4,12},{8,0},{12,4},{16,24},{20,28},{24,16},{28,20},{1,9},{5... | collective-permute-start | bytes 147464 | tf_op jit(solution)/shard_map/ppermute | solution.py:275
  23.3 0.6 %collective-permute-start.9 = (bf16[2,96,128]{2,1,0:T(8,128)(2,1)S(1)}, bf16[2,96,128]{2,1,0:T(8,128)(2,1)S(1)}, u32[]{:S(2)}, u32[]{:S(2)}) collective-permute-start(bf16[2,96,128]{2,1,0:T(8,128)(2,1)S(1)} %get-tuple-element.44), channel_id=1, source_target_pairs={{0,16},{4,20},{8,24},{12,28},{16,0},{20,4},{24,8},{28,12},{1,17},{... | collective-permute-start | bytes 147464 | tf_op jit(solution)/shard_map/ppermute | solution.py:275
  23.9 0.0 collective-permute-done.12.refs_0_
  23.9 0.2 collective-permute-start.13
  24.1 1.5 %collective-permute-done.10.refs_3_ = bf16[2,96,128]{2,1,0:T(8,128)(2,1)S(1)} collective-permute-done((bf16[2,96,128]{2,1,0:T(8,128)(2,1)S(1)}, bf16[2,96,128]{2,1,0:T(8,128)(2,1)S(1)}, u32[]{:S(2)}, u32[]{:S(2)}) %collective-permute-start.10) | collective-permute-done | bytes 49184 | tf_op jit(solution)/shard_map/ppermute | solution.py:275
  25.6 1.3 %collective-permute-done.8.refs_1_ = bf16[2,96,128]{2,1,0:T(8,128)(2,1)S(1)} collective-permute-done((bf16[2,96,128]{2,1,0:T(8,128)(2,1)S(1)}, bf16[2,96,128]{2,1,0:T(8,128)(2,1)S(1)}, u32[]{:S(2)}, u32[]{:S(2)}) %collective-permute-start.8) | collective-permute-done | bytes 49184 | tf_op jit(solution)/shard_map/ppermute | solution.py:275
  26.9 0.9 %collective-permute-done.9.refs_2_ = bf16[2,96,128]{2,1,0:T(8,128)(2,1)S(1)} collective-permute-done((bf16[2,96,128]{2,1,0:T(8,128)(2,1)S(1)}, bf16[2,96,128]{2,1,0:T(8,128)(2,1)S(1)}, u32[]{:S(2)}, u32[]{:S(2)}) %collective-permute-start.9) | collective-permute-done | bytes 49184 | tf_op jit(solution)/shard_map/ppermute | solution.py:275
  27.8 0.0 collective-permute-done.11.refs_7_
  27.8 0.0 collective-permute-start.15
  27.8 0.5 %collective-permute-start.16 = (bf16[384,384]{1,0:T(8,128)(2,1)S(1)}, bf16[384,384]{1,0:T(8,128)(2,1)S(1)}, u32[]{:S(2)}, u32[]{:S(2)}) collective-permute-start(bf16[384,384]{1,0:T(8,128)(2,1)S(1)} %collective-permute-done.11.refs_7_), channel_id=1, source_target_pairs={{0,4},{4,0},{8,12},{12,8},{16,20},{20,16},{24,28},{28,24},{1,5},{5... | collective-permute-start | bytes 884744 | tf_op jit(solution)/shard_map/ppermute | solution.py:275
  28.4 0.1 collective-permute-start.14
  28.4 0.5 %collective-permute-start.17 = (bf16[208,384]{1,0:T(8,128)(2,1)S(1)}, bf16[208,384]{1,0:T(8,128)(2,1)S(1)}, u32[]{:S(2)}, u32[]{:S(2)}) collective-permute-start(bf16[208,384]{1,0:T(8,128)(2,1)S(1)} %collective-permute-done.12.refs_0_), channel_id=1, source_target_pairs={{0,4},{4,0},{8,12},{12,8},{16,20},{20,16},{24,28},{28,24},{1,5},{5... | collective-permute-start | bytes 479240 | tf_op jit(solution)/shard_map/ppermute | solution.py:275
  28.9 0.3 collective-permute-done.13.refs_1_
  29.2 0.8 %collective-permute-done.14.refs_4_ = bf16[4,96,128]{2,1,0:T(8,128)(2,1)S(1)} collective-permute-done((bf16[4,96,128]{2,1,0:T(8,128)(2,1)S(1)}, bf16[4,96,128]{2,1,0:T(8,128)(2,1)S(1)}, u32[]{:S(2)}, u32[]{:S(2)}) %collective-permute-start.14) | collective-permute-done | bytes 98336 | tf_op jit(solution)/shard_map/ppermute | solution.py:275
  30.0 0.1 collective-permute-start.18
  30.1 0.0 collective-permute-done.15.refs_8_
  30.1 0.0 collective-permute-done.16.refs_9_
  30.1 0.0 copy-done
  30.1 1.4 %project_near_shards.1 = (bf16[1,128,1536]{2,1,0:T(8,128)(2,1)}, bf16[128,768]{1,0:T(8,128)(2,1)S(1)}) custom-call(bf16[2,96,128]{2,1,0:T(8,128)(2,1)S(1)} %get-tuple-element.42.refs_0_, bf16[2,96,128]{2,1,0:T(8,128)(2,1)S(1)} %collective-permute-done.8.refs_1_, bf16[2,96,128]{2,1,0:T(8,128)(2,1)S(1)} %collective-permute-done.9.refs_2_, ...), custom_call_target="tpu_custom_call" | custom-call | flops 226492416 | bytes 1769472 | tf_op jit(solution)/shard_map/project_near_shards/pallas_call | solution.py:235
  31.6 0.0 collective-permute-done.17.refs_2_
  31.6 0.0 collective-permute-done.18.refs_3_
  31.6 1.0 %project_third_shard.1 = bf16[1,128,1536]{2,1,0:T(8,128)(2,1)} custom-call(bf16[1,128,1536]{2,1,0:T(8,128)(2,1)} %get-tuple-element.53.so_far_ref, bf16[128,768]{1,0:T(8,128)(2,1)S(1)} %get-tuple-element.54.attention_ref, bf16[208,384]{1,0:T(8,128)(2,1)S(1)} %collective-permute-done.12.refs_0_, ...), custom_call_target="tpu_custom_call", output_to_operand_aliasing={{}: (0, {})} | custom-call | flops 75497472 | bytes 589824 | tf_op jit(solution)/shard_map/project_third_shard/pallas_call | solution.py:255
  (3 shorter events, 0.0 us)
Async XLA Ops:
  1.0 10.7 %collective-permute-start = (bf16[384,384]{1,0:T(8,128)(2,1)S(1)}, bf16[384,384]{1,0:T(8,128)(2,1)S(1)}, u32[]{:S(2)}, u32[]{:S(2)}) collective-permute-start(bf16[384,384]{1,0:T(8,128)(2,1)S(1)} %constant_dynamic-slice_fusion.1), channel_id=1, source_target_pairs={{0,2},{1,3},{2,0},{3,1},{4,5},{5,4},{6,7},{7,6},{8,10},{9,11},{10,... | collective-permute-start | bytes 884744 | tf_op jit(solution)/shard_map/ppermute | solution.py:285
  6.4 7.4 %collective-permute-start.2 = (bf16[2,3,96,128]{3,2,1,0:T(8,128)(2,1)S(1)}, bf16[2,3,96,128]{3,2,1,0:T(8,128)(2,1)S(1)}, u32[]{:S(2)}, u32[]{:S(2)}) collective-permute-start(bf16[2,3,96,128]{3,2,1,0:T(8,128)(2,1)S(1)} %get-tuple-element.34), channel_id=1, source_target_pairs={{0,8},{4,12},{8,0},{12,4},{16,24},{20,28},{24,16},{28,20},{1,9},{5... | collective-permute-start | bytes 442376 | tf_op jit(solution)/shard_map/ppermute | solution.py:275
  8.0 8.3 %collective-permute-start.3 = (bf16[2,3,96,128]{3,2,1,0:T(8,128)(2,1)S(1)}, bf16[2,3,96,128]{3,2,1,0:T(8,128)(2,1)S(1)}, u32[]{:S(2)}, u32[]{:S(2)}) collective-permute-start(bf16[2,3,96,128]{3,2,1,0:T(8,128)(2,1)S(1)} %get-tuple-element.35), channel_id=1, source_target_pairs={{0,16},{4,20},{8,24},{12,28},{16,0},{20,4},{24,8},{28,12},{1,17},{... | collective-permute-start | bytes 442376 | tf_op jit(solution)/shard_map/ppermute | solution.py:275
  9.5 6.8 %collective-permute-start.4 = (bf16[2,3,96,128]{3,2,1,0:T(8,128)(2,1)S(1)}, bf16[2,3,96,128]{3,2,1,0:T(8,128)(2,1)S(1)}, u32[]{:S(2)}, u32[]{:S(2)}) collective-permute-start(bf16[2,3,96,128]{3,2,1,0:T(8,128)(2,1)S(1)} %get-tuple-element.36), channel_id=1, source_target_pairs={{0,24},{4,28},{8,16},{12,20},{16,8},{20,12},{24,0},{28,4},{1,25},{... | collective-permute-start | bytes 442376 | tf_op jit(solution)/shard_map/ppermute | solution.py:275
  10.0 1.3 %collective-permute-start.1 = (bf16[3,96,128]{2,1,0:T(8,128)(2,1)S(1)}, bf16[3,96,128]{2,1,0:T(8,128)(2,1)S(1)}, u32[]{:S(2)}, u32[]{:S(2)}) collective-permute-start(bf16[3,96,128]{2,1,0:T(8,128)(2,1)S(1)} %get-tuple-element.31), channel_id=1, source_target_pairs={{0,4},{4,0},{8,12},{12,8},{16,20},{20,16},{24,28},{28,24},{1,5},{5... | collective-permute-start | bytes 221192 | tf_op jit(solution)/shard_map/ppermute | solution.py:275
  11.7 16.1 %collective-permute-start.11 = (bf16[384,384]{1,0:T(8,128)(2,1)S(1)}, bf16[384,384]{1,0:T(8,128)(2,1)S(1)}, u32[]{:S(2)}, u32[]{:S(2)}) collective-permute-start(bf16[384,384]{1,0:T(8,128)(2,1)S(1)} %collective-permute-done.refs_6_), channel_id=1, source_target_pairs={{0,8},{4,20},{8,0},{12,28},{16,24},{20,4},{24,16},{28,12},{1,9},{5... | collective-permute-start | bytes 884744 | tf_op jit(solution)/shard_map/ppermute | solution.py:281
  16.3 1.6 %collective-permute-start.5 = (bf16[2,3,96,128]{3,2,1,0:T(8,128)(2,1)S(1)}, bf16[2,3,96,128]{3,2,1,0:T(8,128)(2,1)S(1)}, u32[]{:S(2)}, u32[]{:S(2)}) collective-permute-start(bf16[2,3,96,128]{3,2,1,0:T(8,128)(2,1)S(1)} %collective-permute-done.2.refs_1_), channel_id=1, source_target_pairs={{0,4},{4,0},{8,12},{12,8},{16,20},{20,16},{24,28},{28,24},{1,5},{5... | collective-permute-start | bytes 442376 | tf_op jit(solution)/shard_map/ppermute | solution.py:275
  16.3 1.6 %collective-permute-start.6 = (bf16[2,3,96,128]{3,2,1,0:T(8,128)(2,1)S(1)}, bf16[2,3,96,128]{3,2,1,0:T(8,128)(2,1)S(1)}, u32[]{:S(2)}, u32[]{:S(2)}) collective-permute-start(bf16[2,3,96,128]{3,2,1,0:T(8,128)(2,1)S(1)} %collective-permute-done.3.refs_2_), channel_id=1, source_target_pairs={{0,4},{4,0},{8,12},{12,8},{16,20},{20,16},{24,28},{28,24},{1,5},{5... | collective-permute-start | bytes 442376 | tf_op jit(solution)/shard_map/ppermute | solution.py:275
  16.8 1.4 %collective-permute-start.7 = (bf16[2,3,96,128]{3,2,1,0:T(8,128)(2,1)S(1)}, bf16[2,3,96,128]{3,2,1,0:T(8,128)(2,1)S(1)}, u32[]{:S(2)}, u32[]{:S(2)}) collective-permute-start(bf16[2,3,96,128]{3,2,1,0:T(8,128)(2,1)S(1)} %collective-permute-done.4.refs_3_), channel_id=1, source_target_pairs={{0,4},{4,0},{8,12},{12,8},{16,20},{20,16},{24,28},{28,24},{1,5},{5... | collective-permute-start | bytes 442376 | tf_op jit(solution)/shard_map/ppermute | solution.py:275
  16.8 7.1 %collective-permute-start.12 = (bf16[208,384]{1,0:T(8,128)(2,1)S(1)}, bf16[208,384]{1,0:T(8,128)(2,1)S(1)}, u32[]{:S(2)}, u32[]{:S(2)}) collective-permute-start(bf16[208,384]{1,0:T(8,128)(2,1)S(1)} %constant_dynamic-slice_fusion), channel_id=1, source_target_pairs={{0,1},{1,0},{2,3},{3,2},{4,6},{5,7},{6,4},{7,5},{8,9},{9,8},{10,11... | collective-permute-start | bytes 479240 | tf_op jit(solution)/shard_map/ppermute | solution.py:285
  18.2 12.0 %copy-start = (bf16[768,384]{1,0:T(8,128)(2,1)S(1)}, bf16[768,384]{1,0:T(8,128)(2,1)}, u32[]{:S(2)}) copy-start(bf16[768,384]{1,0:T(8,128)(2,1)} %refs_5_.1) | copy-start | bytes 1769476
  20.4 5.3 %collective-permute-start.10 = (bf16[2,96,128]{2,1,0:T(8,128)(2,1)S(1)}, bf16[2,96,128]{2,1,0:T(8,128)(2,1)S(1)}, u32[]{:S(2)}, u32[]{:S(2)}) collective-permute-start(bf16[2,96,128]{2,1,0:T(8,128)(2,1)S(1)} %get-tuple-element.45), channel_id=1, source_target_pairs={{0,24},{4,28},{8,16},{12,20},{16,8},{20,12},{24,0},{28,4},{1,25},{... | collective-permute-start | bytes 147464 | tf_op jit(solution)/shard_map/ppermute | solution.py:275
  20.9 6.0 %collective-permute-start.8 = (bf16[2,96,128]{2,1,0:T(8,128)(2,1)S(1)}, bf16[2,96,128]{2,1,0:T(8,128)(2,1)S(1)}, u32[]{:S(2)}, u32[]{:S(2)}) collective-permute-start(bf16[2,96,128]{2,1,0:T(8,128)(2,1)S(1)} %get-tuple-element.43), channel_id=1, source_target_pairs={{0,8},{4,12},{8,0},{12,4},{16,24},{20,28},{24,16},{28,20},{1,9},{5... | collective-permute-start | bytes 147464 | tf_op jit(solution)/shard_map/ppermute | solution.py:275
  23.3 4.5 %collective-permute-start.9 = (bf16[2,96,128]{2,1,0:T(8,128)(2,1)S(1)}, bf16[2,96,128]{2,1,0:T(8,128)(2,1)S(1)}, u32[]{:S(2)}, u32[]{:S(2)}) collective-permute-start(bf16[2,96,128]{2,1,0:T(8,128)(2,1)S(1)} %get-tuple-element.44), channel_id=1, source_target_pairs={{0,16},{4,20},{8,24},{12,28},{16,0},{20,4},{24,8},{28,12},{1,17},{... | collective-permute-start | bytes 147464 | tf_op jit(solution)/shard_map/ppermute | solution.py:275
  23.9 5.3 %collective-permute-start.13 = (bf16[208,384]{1,0:T(8,128)(2,1)S(1)}, bf16[208,384]{1,0:T(8,128)(2,1)S(1)}, u32[]{:S(2)}, u32[]{:S(2)}) collective-permute-start(bf16[208,384]{1,0:T(8,128)(2,1)S(1)} %collective-permute-done.12.refs_0_), channel_id=1, source_target_pairs={{0,8},{4,20},{8,0},{12,28},{16,24},{20,4},{24,16},{28,12},{1,9},{5... | collective-permute-start | bytes 479240 | tf_op jit(solution)/shard_map/ppermute | solution.py:281
  27.8 2.3 %collective-permute-start.15 = (bf16[384,384]{1,0:T(8,128)(2,1)S(1)}, bf16[384,384]{1,0:T(8,128)(2,1)S(1)}, u32[]{:S(2)}, u32[]{:S(2)}) collective-permute-start(bf16[384,384]{1,0:T(8,128)(2,1)S(1)} %collective-permute-done.refs_6_), channel_id=1, source_target_pairs={{0,4},{4,0},{8,12},{12,8},{16,20},{20,16},{24,28},{28,24},{1,5},{5... | collective-permute-start | bytes 884744 | tf_op jit(solution)/shard_map/ppermute | solution.py:275
  27.8 2.3 %collective-permute-start.16 = (bf16[384,384]{1,0:T(8,128)(2,1)S(1)}, bf16[384,384]{1,0:T(8,128)(2,1)S(1)}, u32[]{:S(2)}, u32[]{:S(2)}) collective-permute-start(bf16[384,384]{1,0:T(8,128)(2,1)S(1)} %collective-permute-done.11.refs_7_), channel_id=1, source_target_pairs={{0,4},{4,0},{8,12},{12,8},{16,20},{20,16},{24,28},{28,24},{1,5},{5... | collective-permute-start | bytes 884744 | tf_op jit(solution)/shard_map/ppermute | solution.py:275
  28.4 1.6 %collective-permute-start.14 = (bf16[4,96,128]{2,1,0:T(8,128)(2,1)S(1)}, bf16[4,96,128]{2,1,0:T(8,128)(2,1)S(1)}, u32[]{:S(2)}, u32[]{:S(2)}) collective-permute-start(bf16[4,96,128]{2,1,0:T(8,128)(2,1)S(1)} %second_entries.1), channel_id=1, source_target_pairs={{0,4},{4,0},{8,12},{12,8},{16,20},{20,16},{24,28},{28,24},{1,5},{5... | collective-permute-start | bytes 294920 | tf_op jit(solution)/shard_map/ppermute | solution.py:275
  28.4 3.1 %collective-permute-start.17 = (bf16[208,384]{1,0:T(8,128)(2,1)S(1)}, bf16[208,384]{1,0:T(8,128)(2,1)S(1)}, u32[]{:S(2)}, u32[]{:S(2)}) collective-permute-start(bf16[208,384]{1,0:T(8,128)(2,1)S(1)} %collective-permute-done.12.refs_0_), channel_id=1, source_target_pairs={{0,4},{4,0},{8,12},{12,8},{16,20},{20,16},{24,28},{28,24},{1,5},{5... | collective-permute-start | bytes 479240 | tf_op jit(solution)/shard_map/ppermute | solution.py:275
  30.0 1.6 %collective-permute-start.18 = (bf16[208,384]{1,0:T(8,128)(2,1)S(1)}, bf16[208,384]{1,0:T(8,128)(2,1)S(1)}, u32[]{:S(2)}, u32[]{:S(2)}) collective-permute-start(bf16[208,384]{1,0:T(8,128)(2,1)S(1)} %collective-permute-done.13.refs_1_), channel_id=1, source_target_pairs={{0,4},{4,0},{8,12},{12,8},{16,20},{20,16},{24,28},{28,24},{1,5},{5... | collective-permute-start | bytes 479240 | tf_op jit(solution)/shard_map/ppermute | solution.py:275

commit v10 on v9

v10 whole, which is shorter than its diff:
```python
import functools
import math

import jax
import jax.numpy as jnp
from jax import lax
from jax.experimental import pallas as pl
from jax.experimental.pallas import tpu as pltpu
from jax.sharding import PartitionSpec as P

HEADS = 8
FLIPS = tuple(range(0, HEADS, 2))
WHOLE = pl.BlockSpec(memory_space=pltpu.VMEM)
IN_HBM = pl.BlockSpec(memory_space=pltpu.HBM)


def params(mebibytes=48):
    return pltpu.CompilerParams(vmem_limit_bytes=mebibytes * 1024 * 1024)


def place_in_group():
    return lax.axis_index("ctx") % HEADS


def parity_of(place):
    return ((place >> 2) ^ (place >> 1)) & 1


def copy_in_kernel(by_parity, query_ref, key_ref, value_ref, weight_ref, rows_ref, half_ref, sems):
    place = place_in_group()
    first = (parity_of(place) if by_parity else place & 1) * half_ref.shape[0]
    copies = [pltpu.make_async_copy(weight_ref.at[pl.ds(pl.multiple_of(first, 32), half_ref.shape[0])], half_ref, sems.at[3])]
    for part, ref in enumerate((query_ref, key_ref, value_ref)):
        copies.append(pltpu.make_async_copy(ref.at[0], rows_ref.at[part], sems.at[part]))
    for copy in copies:
        copy.start()
    for copy in copies:
        copy.wait()


def copy_in(queries, key_rows, value_rows, out_weight, by_parity):
    _, frames, features = queries.shape
    half = (out_weight.shape[0] // 2, out_weight.shape[1])
    arrays = [pltpu.with_memory_space_constraint(array, pltpu.HBM) for array in (queries, key_rows, value_rows, out_weight)]
    return pl.pallas_call(
        functools.partial(copy_in_kernel, by_parity),
        out_shape=[pltpu.VMEM((3, frames, features), queries.dtype), pltpu.VMEM(half, out_weight.dtype)],
        in_specs=[IN_HBM] * 4,
        out_specs=[WHOLE] * 2,
        scratch_shapes=[pltpu.SemaphoreType.DMA((4,))],
        compiler_params=params(16),
        name="copy_in",
    )(*arrays)


def turn_kernel(rows_ref, *refs):
    outs, turned = refs[:-1], refs[-1]
    features = outs[0].shape[1]
    chip = place_in_group() >> 1
    for part in range(3):
        turned[part] = rows_ref[part].T
        for flip, out_ref in zip(FLIPS, outs):
            first = pl.multiple_of((chip ^ (flip >> 1)) * features, 32)
            out_ref[part] = turned[part, pl.ds(first, features), :]


def turn(rows):
    _, frames, features = rows.shape
    return pl.pallas_call(
        turn_kernel,
        out_shape=[pltpu.VMEM((3, features // len(FLIPS), frames), rows.dtype)] * len(FLIPS),
        in_specs=[WHOLE],
        out_specs=[WHOLE] * len(FLIPS),
        scratch_shapes=[pltpu.VMEM((3, features, frames), rows.dtype)],
        compiler_params=params(16),
        name="turn_heads",
    )(rows)


def attention_kernel(groups, lengths_ref, *refs):
    each = len(FLIPS)
    same, other = refs[:each], refs[each : 2 * each]
    rest_ref = refs[2 * each] if groups > 1 else None
    outs, (keys, values) = refs[-2 - each : -2], refs[-2:]
    block = outs[0].shape[1]
    head_size = outs[0].shape[0] // 2
    place = place_in_group()
    scale = jnp.float32(math.log2(math.e) / math.sqrt(head_size))
    pad = keys.shape[2] - head_size

    def piece(at, head, part):
        rows = slice(head * head_size, (head + 1) * head_size)
        if groups > 1:
            return rest_ref[at, part - 1, rows, :]
        return other[at // 2][part - 1, rows, :] if at % 2 else same[at // 2][part, rows, :]

    ones = jnp.where(lax.broadcasted_iota(jnp.int32, (pad, block), 0) == 0, 1.0, 0.0).astype(keys.dtype)
    at_frame = lax.broadcasted_iota(jnp.int32, (block, pad), 0)
    at_feature = lax.broadcasted_iota(jnp.int32, (block, pad), 1)
    for at in range(groups * HEADS):
        here = slice(at * block, (at + 1) * block)
        frame = (at // HEADS * HEADS + (place ^ (at % HEADS))) * block + at_frame
        bias = jnp.where((at_feature == 0) & (frame >= lengths_ref[:1, :pad]), -1e30, 0.0).astype(keys.dtype)
        for head in range(2):
            keys[head, here, :head_size] = piece(at, head, 1).T
            keys[head, here, head_size:] = bias
            values[head, :head_size, here] = piece(at, head, 2)
            values[head, head_size:, here] = ones

    def score(head, flips):
        rows = slice(head * head_size, (head + 1) * head_size)
        query = [jnp.concatenate([same[flip // 2][0, rows, :], ones], axis=0) for flip in flips]
        return jnp.dot(keys[head], jnp.concatenate(query, axis=1), preferred_element_type=jnp.float32)

    chunks = [(head, flips) for head in range(2) for flips in (FLIPS[:2], FLIPS[2:])]
    later = score(*chunks[0])
    for at, (head, flips) in enumerate(chunks):
        scores = later
        if at + 1 < len(chunks):
            later = score(*chunks[at + 1])
        row_max = jnp.max(scores, axis=0, keepdims=True) * scale
        probs = jnp.exp2(scores * scale - row_max).astype(jnp.bfloat16)
        mixed = jnp.dot(values[head], probs, preferred_element_type=jnp.float32)
        mixed = (mixed[:head_size] / mixed[head_size : head_size + 1]).astype(jnp.bfloat16)
        for half, flip in enumerate(flips):
            outs[flip // 2][head * head_size : (head + 1) * head_size, :] = mixed[:, half * block : (half + 1) * block]


def attend(lengths, same, other, rest, groups):
    _, features, block = same[0].shape
    keys = groups * HEADS * block
    padded = features // 2 + 32
    rest = [] if rest is None else [rest]
    return pl.pallas_call(
        functools.partial(attention_kernel, groups),
        out_shape=[pltpu.VMEM((features, block), jnp.bfloat16)] * len(FLIPS),
        in_specs=[WHOLE] * (1 + 2 * len(FLIPS) + len(rest)),
        out_specs=[WHOLE] * len(FLIPS),
        scratch_shapes=[pltpu.VMEM((2, keys, padded), jnp.bfloat16), pltpu.VMEM((2, padded, keys), jnp.bfloat16)],
        compiler_params=params(32),
        cost_estimate=pl.CostEstimate(flops=8 * keys * keys * features, bytes_accessed=0, transcendentals=0),
        name="attend_two_heads",
    )(lengths, *same, *other, *rest)


def gather_heads(heads, turned):
    rows = heads[0].shape[0]
    for flip, ref in zip(FLIPS, heads):
        first = pl.multiple_of(((place_in_group() ^ flip) >> 1) * rows, 32)
        turned[pl.ds(first, rows), :] = ref[...]


def project_kernel(*refs):
    each = len(FLIPS)
    heads, halves, (out_ref, turned, weight) = refs[:each], refs[each : each + 2], refs[each + 2 :]
    gather_heads(heads, turned)
    half = weight.shape[0] // 2
    for other, ref in enumerate(halves):
        weight[pl.ds(pl.multiple_of(((place_in_group() & 1) ^ other) * half, 32), half), :] = ref[...]
    out_ref[0] = jnp.dot(turned[...].T, weight[...], preferred_element_type=jnp.float32).astype(out_ref.dtype)


def project_near_kernel(*refs):
    each = len(FLIPS)
    heads, own_ref, pieces = refs[:each], refs[each], refs[each + 1 : each + 5]
    out_ref, attention_ref, turned, weight, blocks, sems = refs[each + 5 :]
    gather_heads(heads, turned)
    attention_ref[...] = turned[...].T
    place, shard = place_in_group(), lax.axis_index("fsdp")
    half, columns = pieces[0].shape
    beside = (place & 1) ^ 1
    copies = []
    for at, flip in enumerate((0, 1, 2)):
        if flip == 0:
            block = own_ref[...]
        else:
            mine = beside == flip - 1
            for other in range(2):
                here = pl.ds(pl.multiple_of((parity_of(place) ^ other) * half, 32), half)
                weight[flip - 1, here, :] = jnp.where(mine, pieces[other][...], pieces[2 + other][...])
            block = weight[flip - 1]
        blocks[at] = jnp.dot(attention_ref[...], block, preferred_element_type=jnp.float32).astype(blocks.dtype)
        here = pl.ds(pl.multiple_of((shard ^ flip) * columns, 128), columns)
        copies.append(pltpu.make_async_copy(blocks.at[at], out_ref.at[0, :, here], sems.at[at]))
        copies[-1].start()
    for copy in copies:
        copy.wait()


def project_third_kernel(so_far_ref, attention_ref, *refs):
    pieces, (out_ref, weight, block, sem) = refs[:4], refs[4:]
    place, shard = place_in_group(), lax.axis_index("fsdp")
    part, columns = pieces[0].shape
    half = weight.shape[0] // 2
    for other in range(2):
        for flip in range(2):
            first = (parity_of(place) ^ flip) * half + ((place & 1) ^ other) * (half - part)
            weight[pl.ds(pl.multiple_of(first, 16), part), :] = pieces[2 * other + flip][...]
    block[...] = jnp.dot(attention_ref[...], weight[...], preferred_element_type=jnp.float32).astype(block.dtype)
    here = pl.ds(pl.multiple_of((shard ^ 3) * columns, 128), columns)
    copy = pltpu.make_async_copy(block, out_ref.at[0, :, here], sem)
    copy.start()
    copy.wait()


def projection_cost(frames, features, columns):
    return pl.CostEstimate(
        flops=2 * features * frames * columns, bytes_accessed=2 * features * columns, transcendentals=0
    )


def project(heads, halves):
    rows, frames = heads[0].shape
    features, width = len(FLIPS) * rows, halves[0].shape[1]
    return pl.pallas_call(
        project_kernel,
        out_shape=jax.ShapeDtypeStruct((1, frames, width), jnp.bfloat16),
        in_specs=[WHOLE] * (len(FLIPS) + 2),
        out_specs=WHOLE,
        scratch_shapes=[pltpu.VMEM((features, frames), jnp.bfloat16), pltpu.VMEM((features, width), jnp.bfloat16)],
        compiler_params=params(24),
        cost_estimate=projection_cost(frames, features, width),
        name="project_heads",
    )(*heads, *halves)


def project_near(heads, own, pieces):
    frames = heads[0].shape[1]
    features, columns = own.shape
    return pl.pallas_call(
        project_near_kernel,
        out_shape=[jax.ShapeDtypeStruct((1, frames, 4 * columns), jnp.bfloat16), pltpu.VMEM((frames, features), jnp.bfloat16)],
        in_specs=[WHOLE] * (len(FLIPS) + 5),
        out_specs=[IN_HBM, WHOLE],
        scratch_shapes=[
            pltpu.VMEM((features, frames), jnp.bfloat16),
            pltpu.VMEM((2, features, columns), jnp.bfloat16),
            pltpu.VMEM((3, frames, columns), jnp.bfloat16),
            pltpu.SemaphoreType.DMA((3,)),
        ],
        compiler_params=params(24),
        cost_estimate=projection_cost(frames, features, 3 * columns),
        name="project_near_shards",
    )(*heads, own, *pieces)


def project_third(so_far, attention, pieces):
    frames, features = attention.shape
    columns = pieces[0].shape[1]
    return pl.pallas_call(
        project_third_kernel,
        out_shape=jax.ShapeDtypeStruct(so_far.shape, so_far.dtype),
        in_specs=[IN_HBM] + [WHOLE] * 5,
        out_specs=IN_HBM,
        input_output_aliases={0: 0},
        scratch_shapes=[
            pltpu.VMEM((features, columns), jnp.bfloat16),
            pltpu.VMEM((frames, columns), jnp.bfloat16),
            pltpu.SemaphoreType.DMA,
        ],
        compiler_params=params(24),
        cost_estimate=projection_cost(frames, features, columns),
        name="project_third_shard",
    )(so_far, attention, *pieces)


def per_device(ctx, fsdp, queries, key_rows, value_rows, lengths, out_weight):
    def exchange(array, axis, flip):
        size = ctx if axis == "ctx" else fsdp
        return lax.ppermute(array, axis, [(i, i ^ flip) for i in range(size)])

    def exchange_chips(arrays):
        return [exchange(array, "ctx", flip) for flip, array in zip(FLIPS[1:], arrays)]

    def exchange_in_plane(array):
        return lax.ppermute(array, "ctx", [(i, i ^ (4 if i % 2 else 2)) for i in range(ctx)])

    def exchange_along(array, *flips):
        pairs = [(i * fsdp + z, i * fsdp + (z ^ flips[i % 2])) for i in range(ctx) for z in range(fsdp)]
        return lax.ppermute(array, ("ctx", "fsdp"), pairs)

    core = place_in_group() & 1
    split_columns = fsdp == 4
    lengths = jnp.broadcast_to(lengths, (8, 128))
    rows, half = copy_in(queries, key_rows, value_rows, out_weight, split_columns)
    if split_columns:
        fetched = exchange_along(half, 2, 1)
    else:
        half = lax.all_gather(half, "fsdp", axis=1, tiled=True)

    own, *by_chip = turn(rows)
    same = exchange_chips(by_chip)
    own_other = exchange(own[1:], "ctx", 1)
    if split_columns:
        fetched, own_other, lengths = lax.optimization_barrier((fetched, own_other, lengths))
        passed = exchange_in_plane(fetched)
        depth = half.shape[0]
        part = depth // 2 + 16
        third = lax.dynamic_slice_in_dim(fetched, core * (depth - part), part, 0)
        third = exchange_along(third, 1, 2)
    same, own_other = lax.optimization_barrier((same, own_other))
    other = [own_other, *(exchange(array[1:], "ctx", 1) for array in same)]
    same = [own, *same]

    groups = ctx // HEADS
    rest = None
    if groups > 1:
        pairs = [array for one, two in zip(same, other) for array in (one[1:], two)]
        across = [[head + first for first in range(0, ctx, HEADS)] for head in range(HEADS)]
        rest = lax.all_gather(jnp.stack(pairs), "ctx", axis=0, axis_index_groups=across, tiled=True)
    mixed = attend(lengths, same, other, rest, groups)

    heads = [mixed[0], *exchange_chips(mixed[1:])]
    if not split_columns:
        return project(heads, [half, exchange(half, "ctx", 1)])
    third_passed = exchange_in_plane(third)
    heads, fetched, passed, third = lax.optimization_barrier((heads, fetched, passed, third))
    fetched_other, passed_other, third_other, third_passed_other = (
        exchange(array, "ctx", 1) for array in (fetched, passed, third, third_passed)
    )
    so_far, attention = project_near(heads, out_weight, [fetched, passed, fetched_other, passed_other])
    return project_third(so_far, attention, [third, third_passed, third_other, third_passed_other])


def solution(mesh):
    return jax.shard_map(
        functools.partial(per_device, mesh.shape["ctx"], mesh.shape["fsdp"]),
        mesh=mesh,
        in_specs=(
            P("fsdp", "ctx", None),
            P("fsdp", "ctx", None),
            P("fsdp", "ctx", None),
            P("fsdp"),
            P(None, "fsdp"),
        ),
        out_specs=P("fsdp", "ctx", None),
        check_vma=False,
    )
```

time: 32.7 us -> 31.5 us (0.963)
  local copies, waits for them, and re-layouts: 1.01 us -> 0.06 us
  starting transfers between devices: 16.3 us -> 15.8 us
    ppermute x15 -> x14, waiting for transfers between devices: 7.86 us -> 5.45 us  [exchange(): return lax.ppermute(array, axis, [(i, i ^ flip) for i in range(size)])]
    ppermute x2, waiting for transfers between devices: 0.28 us -> 1.68 us  [exchange_in_plane(): lax.ppermute(array, 'ctx', [(i, i ^ (4 if i % 2 else 2)) for i in range(c...]
    dynamic_slice x2 -> x1, local copies, waits for them, and re-layouts: 1.01 us -> 0.02 us  [per_device(): third = lax.dynamic_slice_in_dim(fetched, core * (depth - part), part, 0)]
    ppermute x2, waiting for transfers between devices: 0.47 us -> 1.42 us  [exchange_along(): return lax.ppermute(array, ('ctx', 'fsdp'), pairs)]
    ppermute x15 -> x14, starting transfers between devices: 8.84 us -> 8.4 us  [exchange(): return lax.ppermute(array, axis, [(i, i ^ flip) for i in range(size)])]
    ppermute x2, starting transfers between devices: 2.33 us -> 1.95 us  [exchange_in_plane(): lax.ppermute(array, 'ctx', [(i, i ^ (4 if i % 2 else 2)) for i in range(c...]
  transfers between devices with their start and end apart: 19 -> 18, of which waited for: 9 -> 8; matrix products, arithmetic and copies ran while one was open for 0% -> 0% of each run, Pallas kernels for 15% -> 12%
where the time goes in v10:
time: 31.5 us; the launch traced here: 31.3 us
  starting transfers between devices  15.8 us (50%)
  waiting for transfers between devices  8.55 us (27%)
  Pallas kernels  6.13 us (19%)
  between operations  0.78 us (2%)
    ppermute x14, starting transfers between devices, exchange(): return lax.ppermute(array, axis, [(i, i ^ flip) for i in range(size)])  8.4 us
    ppermute x14, waiting for transfers between devices, exchange(): return lax.ppermute(array, axis, [(i, i ^ flip) for i in range(size)])  5.45 us
    ppermute x2, starting transfers between devices, exchange_along(): return lax.ppermute(array, ('ctx', 'fsdp'), pairs)  5.43 us
    pallas_call x1, Pallas kernels, attend(): pl.pallas_call(functools.partial(attention_kernel, groups), out_shape=[pl...  2.21 us
    ppermute x2, starting transfers between devices, exchange_in_plane(): lax.ppermute(array, 'ctx', [(i, i ^ (4 if i % 2 else 2)) for i in range(c...  1.95 us
    ppermute x2, waiting for transfers between devices, exchange_in_plane(): lax.ppermute(array, 'ctx', [(i, i ^ (4 if i % 2 else 2)) for i in range(c...  1.68 us
    pallas_call x1, Pallas kernels, project_near(): pl.pallas_call(project_near_kernel, out_shape=[jax.ShapeDtypeStruct((1, f...  1.44 us
    ppermute x2, waiting for transfers between devices, exchange_along(): return lax.ppermute(array, ('ctx', 'fsdp'), pairs)  1.42 us
  transfers between devices with their start and end apart: 18, of which 8 were waited for; matrix products, arithmetic and copies ran while one was open for 0% of the time, Pallas kernels for 12%

profile of v10, /device:TPU:0, one launch (start us, length us, event | category | flops | bytes accessed | tf_op | source)
XLA Modules:
  0.0 31.3 jit_solution(10403781763431253897)
XLA Ops:
  0.0 1.2 %copy_in.1 = (bf16[3,128,768]{2,1,0:T(8,128)(2,1)S(1)}, bf16[384,384]{1,0:T(8,128)(2,1)S(1)}) custom-call(bf16[1,128,768]{2,1,0:T(8,128)(2,1)} %query_ref.1, bf16[1,128,768]{2,1,0:T(8,128)(2,1)} %key_ref.1, bf16[1,128,768]{2,1,0:T(8,128)(2,1)} %value_ref.1, bf16[768,384]{1,0:T(8,128)(2,1)} %refs_4_.1), custom_call_target="tpu_custom_call" | custom-call | tf_op jit(solution)/shard_map/copy_in/pallas_call | solution.py:45
  1.2 4.1 %collective-permute-start = (bf16[384,384]{1,0:T(8,128)(2,1)S(1)}, bf16[384,384]{1,0:T(8,128)(2,1)S(1)}, u32[]{:S(2)}, u32[]{:S(2)}) collective-permute-start(bf16[384,384]{1,0:T(8,128)(2,1)S(1)} %get-tuple-element.31), channel_id=1, source_target_pairs={{0,2},{1,3},{2,0},{3,1},{4,5},{5,4},{6,7},{7,6},{8,10},{9,11},{10,... | collective-permute-start | bytes 884744 | tf_op jit(solution)/shard_map/ppermute | solution.py:280
  5.3 0.2 turn_heads.1
  5.6 1.6 %collective-permute-start.2 = (bf16[3,192,128]{2,1,0:T(8,128)(2,1)S(1)}, bf16[3,192,128]{2,1,0:T(8,128)(2,1)S(1)}, u32[]{:S(2)}, u32[]{:S(2)}) collective-permute-start(bf16[3,192,128]{2,1,0:T(8,128)(2,1)S(1)} %get-tuple-element.35), channel_id=1, source_target_pairs={{0,8},{4,12},{8,0},{12,4},{16,24},{20,28},{24,16},{28,20},{1,9},{5... | collective-permute-start | bytes 442376 | tf_op jit(solution)/shard_map/ppermute | solution.py:270
  7.2 1.5 %collective-permute-start.3 = (bf16[3,192,128]{2,1,0:T(8,128)(2,1)S(1)}, bf16[3,192,128]{2,1,0:T(8,128)(2,1)S(1)}, u32[]{:S(2)}, u32[]{:S(2)}) collective-permute-start(bf16[3,192,128]{2,1,0:T(8,128)(2,1)S(1)} %get-tuple-element.36), channel_id=1, source_target_pairs={{0,16},{4,20},{8,24},{12,28},{16,0},{20,4},{24,8},{28,12},{1,17},{... | collective-permute-start | bytes 442376 | tf_op jit(solution)/shard_map/ppermute | solution.py:270
  8.7 0.5 %collective-permute-start.4 = (bf16[3,192,128]{2,1,0:T(8,128)(2,1)S(1)}, bf16[3,192,128]{2,1,0:T(8,128)(2,1)S(1)}, u32[]{:S(2)}, u32[]{:S(2)}) collective-permute-start(bf16[3,192,128]{2,1,0:T(8,128)(2,1)S(1)} %get-tuple-element.37), channel_id=1, source_target_pairs={{0,24},{4,28},{8,16},{12,20},{16,8},{20,12},{24,0},{28,4},{1,25},{... | collective-permute-start | bytes 442376 | tf_op jit(solution)/shard_map/ppermute | solution.py:270
  9.2 0.1 collective-permute-start.1
  9.9 0.6 %collective-permute-done.1.refs_4_ = bf16[2,192,128]{2,1,0:T(8,128)(2,1)S(1)} collective-permute-done((bf16[2,192,128]{2,1,0:T(8,128)(2,1)S(1)}, bf16[2,192,128]{2,1,0:T(8,128)(2,1)S(1)}, u32[]{:S(2)}, u32[]{:S(2)}) %collective-permute-start.1) | collective-permute-done | bytes 98336 | tf_op jit(solution)/shard_map/ppermute | solution.py:270
  10.5 1.4 %collective-permute-done.refs_5_ = bf16[384,384]{1,0:T(8,128)(2,1)S(1)} collective-permute-done((bf16[384,384]{1,0:T(8,128)(2,1)S(1)}, bf16[384,384]{1,0:T(8,128)(2,1)S(1)}, u32[]{:S(2)}, u32[]{:S(2)}) %collective-permute-start) | collective-permute-done | bytes 294944 | tf_op jit(solution)/shard_map/ppermute | solution.py:280
  12.0 0.4 %collective-permute-done.2.refs_1_ = bf16[3,192,128]{2,1,0:T(8,128)(2,1)S(1)} collective-permute-done((bf16[3,192,128]{2,1,0:T(8,128)(2,1)S(1)}, bf16[3,192,128]{2,1,0:T(8,128)(2,1)S(1)}, u32[]{:S(2)}, u32[]{:S(2)}) %collective-permute-start.2) | collective-permute-done | bytes 147488 | tf_op jit(solution)/shard_map/ppermute | solution.py:270
  12.4 2.8 %collective-permute-done.3.refs_2_ = bf16[3,192,128]{2,1,0:T(8,128)(2,1)S(1)} collective-permute-done((bf16[3,192,128]{2,1,0:T(8,128)(2,1)S(1)}, bf16[3,192,128]{2,1,0:T(8,128)(2,1)S(1)}, u32[]{:S(2)}, u32[]{:S(2)}) %collective-permute-start.3) | collective-permute-done | bytes 147488 | tf_op jit(solution)/shard_map/ppermute | solution.py:270
  15.2 0.0 collective-permute-done.4.refs_3_
  15.2 0.1 collective-permute-start.5
  15.3 0.5 %collective-permute-start.6 = (bf16[2,192,128]{2,1,0:T(8,128)(2,1)S(1)}, bf16[2,192,128]{2,1,0:T(8,128)(2,1)S(1)}, u32[]{:S(2)}, u32[]{:S(2)}) collective-permute-start(bf16[2,192,128]{2,1,0:T(8,128)(2,1)S(1)} %slice.14), channel_id=1, source_target_pairs={{0,4},{4,0},{8,12},{12,8},{16,20},{20,16},{24,28},{28,24},{1,5},{5... | collective-permute-start | bytes 294920 | tf_op jit(solution)/shard_map/ppermute | solution.py:270
  15.8 0.1 collective-permute-start.7
  15.9 0.5 %collective-permute-start.11 = (bf16[384,384]{1,0:T(8,128)(2,1)S(1)}, bf16[384,384]{1,0:T(8,128)(2,1)S(1)}, u32[]{:S(2)}, u32[]{:S(2)}) collective-permute-start(bf16[384,384]{1,0:T(8,128)(2,1)S(1)} %collective-permute-done.refs_5_), channel_id=1, source_target_pairs={{0,8},{4,20},{8,0},{12,28},{16,24},{20,4},{24,16},{28,12},{1,9},{5... | collective-permute-start | bytes 884744 | tf_op jit(solution)/shard_map/ppermute | solution.py:276
  16.4 0.0 copy-start
  16.4 1.3 %collective-permute-start.12 = (bf16[208,384]{1,0:T(8,128)(2,1)S(1)}, bf16[208,384]{1,0:T(8,128)(2,1)S(1)}, u32[]{:S(2)}, u32[]{:S(2)}) collective-permute-start(bf16[208,384]{1,0:T(8,128)(2,1)S(1)} %constant_dynamic-slice_fusion), channel_id=1, source_target_pairs={{0,1},{1,0},{2,3},{3,2},{4,6},{5,7},{6,4},{7,5},{8,9},{9,8},{10,11... | collective-permute-start | bytes 479240 | tf_op jit(solution)/shard_map/ppermute | solution.py:280
  17.7 0.0 collective-permute-done.5.refs_5_
  17.7 0.0 collective-permute-done.6.refs_6_
  17.7 0.0 collective-permute-done.7.refs_7_
  17.7 2.2 %attend_two_heads.1 = (bf16[192,128]{1,0:T(8,128)(2,1)S(1)}, bf16[192,128]{1,0:T(8,128)(2,1)S(1)}, bf16[192,128]{1,0:T(8,128)(2,1)S(1)}, bf16[192,128]{1,0:T(8,128)(2,1)S(1)}) custom-call(s32[8,128]{1,0:T(8,128)S(1)} %broadcast_in_dim.2.lengths_ref, bf16[3,192,128]{2,1,0:T(8,128)(2,1)S(1)} %get-tuple-element.33.refs_0_, ...), custom_call_target="tpu_custom_call" | custom-call | flops 1610612736 | tf_op jit(solution)/shard_map/attend_two_heads/pallas_call | solution.py:134
  20.0 1.7 %collective-permute-start.10 = (bf16[192,128]{1,0:T(8,128)(2,1)S(1)}, bf16[192,128]{1,0:T(8,128)(2,1)S(1)}, u32[]{:S(2)}, u32[]{:S(2)}) collective-permute-start(bf16[192,128]{1,0:T(8,128)(2,1)S(1)} %get-tuple-element.46), channel_id=1, source_target_pairs={{0,24},{4,28},{8,16},{12,20},{16,8},{20,12},{24,0},{28,4},{1,25},{... | collective-permute-start | bytes 147464 | tf_op jit(solution)/shard_map/ppermute | solution.py:270
  21.6 0.5 %collective-permute-start.8 = (bf16[192,128]{1,0:T(8,128)(2,1)S(1)}, bf16[192,128]{1,0:T(8,128)(2,1)S(1)}, u32[]{:S(2)}, u32[]{:S(2)}) collective-permute-start(bf16[192,128]{1,0:T(8,128)(2,1)S(1)} %get-tuple-element.44), channel_id=1, source_target_pairs={{0,8},{4,12},{8,0},{12,4},{16,24},{20,28},{24,16},{28,20},{1,9},{5... | collective-permute-start | bytes 147464 | tf_op jit(solution)/shard_map/ppermute | solution.py:270
  22.2 1.3 %collective-permute-start.9 = (bf16[192,128]{1,0:T(8,128)(2,1)S(1)}, bf16[192,128]{1,0:T(8,128)(2,1)S(1)}, u32[]{:S(2)}, u32[]{:S(2)}) collective-permute-start(bf16[192,128]{1,0:T(8,128)(2,1)S(1)} %get-tuple-element.45), channel_id=1, source_target_pairs={{0,16},{4,20},{8,24},{12,28},{16,0},{20,4},{24,8},{28,12},{1,17},{... | collective-permute-start | bytes 147464 | tf_op jit(solution)/shard_map/ppermute | solution.py:270
  23.5 0.0 collective-permute-done.12.refs_0_
  23.5 1.5 %collective-permute-start.15 = (bf16[208,384]{1,0:T(8,128)(2,1)S(1)}, bf16[208,384]{1,0:T(8,128)(2,1)S(1)}, u32[]{:S(2)}, u32[]{:S(2)}) collective-permute-start(bf16[208,384]{1,0:T(8,128)(2,1)S(1)} %collective-permute-done.12.refs_0_), channel_id=1, source_target_pairs={{0,8},{4,20},{8,0},{12,28},{16,24},{20,4},{24,16},{28,12},{1,9},{5... | collective-permute-start | bytes 479240 | tf_op jit(solution)/shard_map/ppermute | solution.py:276
  25.0 0.1 collective-permute-done.10.refs_3_
  25.1 1.0 %collective-permute-done.8.refs_1_ = bf16[192,128]{1,0:T(8,128)(2,1)S(1)} collective-permute-done((bf16[192,128]{1,0:T(8,128)(2,1)S(1)}, bf16[192,128]{1,0:T(8,128)(2,1)S(1)}, u32[]{:S(2)}, u32[]{:S(2)}) %collective-permute-start.8) | collective-permute-done | bytes 49184 | tf_op jit(solution)/shard_map/ppermute | solution.py:270
  26.1 0.5 %collective-permute-done.9.refs_2_ = bf16[192,128]{1,0:T(8,128)(2,1)S(1)} collective-permute-done((bf16[192,128]{1,0:T(8,128)(2,1)S(1)}, bf16[192,128]{1,0:T(8,128)(2,1)S(1)}, u32[]{:S(2)}, u32[]{:S(2)}) %collective-permute-start.9) | collective-permute-done | bytes 49184 | tf_op jit(solution)/shard_map/ppermute | solution.py:270
  26.6 0.0 collective-permute-done.11.refs_6_
  26.6 0.0 collective-permute-start.13
  26.6 0.5 %collective-permute-start.14 = (bf16[384,384]{1,0:T(8,128)(2,1)S(1)}, bf16[384,384]{1,0:T(8,128)(2,1)S(1)}, u32[]{:S(2)}, u32[]{:S(2)}) collective-permute-start(bf16[384,384]{1,0:T(8,128)(2,1)S(1)} %collective-permute-done.11.refs_6_), channel_id=1, source_target_pairs={{0,4},{4,0},{8,12},{12,8},{16,20},{20,16},{24,28},{28,24},{1,5},{5... | collective-permute-start | bytes 884744 | tf_op jit(solution)/shard_map/ppermute | solution.py:270
  27.1 0.0 collective-permute-start.16
  27.1 1.7 %collective-permute-done.15.refs_1_ = bf16[208,384]{1,0:T(8,128)(2,1)S(1)} collective-permute-done((bf16[208,384]{1,0:T(8,128)(2,1)S(1)}, bf16[208,384]{1,0:T(8,128)(2,1)S(1)}, u32[]{:S(2)}, u32[]{:S(2)}) %collective-permute-start.15) | collective-permute-done | bytes 159776 | tf_op jit(solution)/shard_map/ppermute | solution.py:276
  28.8 0.0 collective-permute-start.17
  28.8 0.0 collective-permute-done.13.refs_7_
  28.8 0.0 collective-permute-done.14.refs_8_
  28.8 0.0 copy-done
  28.8 1.4 %project_near_shards.1 = (bf16[1,128,1536]{2,1,0:T(8,128)(2,1)}, bf16[128,768]{1,0:T(8,128)(2,1)S(1)}) custom-call(bf16[192,128]{1,0:T(8,128)(2,1)S(1)} %get-tuple-element.48.refs_0_, bf16[192,128]{1,0:T(8,128)(2,1)S(1)} %collective-permute-done.8.refs_1_, bf16[192,128]{1,0:T(8,128)(2,1)S(1)} %collective-permute-done.9.refs_2_, ...), custom_call_target="tpu_custom_call" | custom-call | flops 226492416 | bytes 1769472 | tf_op jit(solution)/shard_map/project_near_shards/pallas_call | solution.py:230
  30.3 0.0 collective-permute-done.16.refs_2_
  30.3 0.0 collective-permute-done.17.refs_3_
  30.3 1.0 %project_third_shard.1 = bf16[1,128,1536]{2,1,0:T(8,128)(2,1)} custom-call(bf16[1,128,1536]{2,1,0:T(8,128)(2,1)} %get-tuple-element.54.so_far_ref, bf16[128,768]{1,0:T(8,128)(2,1)S(1)} %get-tuple-element.55.attention_ref, bf16[208,384]{1,0:T(8,128)(2,1)S(1)} %collective-permute-done.12.refs_0_, ...), custom_call_target="tpu_custom_call", output_to_operand_aliasing={{}: (0, {})} | custom-call | flops 75497472 | bytes 589824 | tf_op jit(solution)/shard_map/project_third_shard/pallas_call | solution.py:250
  (6 shorter events, 0.0 us)
Async XLA Ops:
  1.2 10.7 %collective-permute-start = (bf16[384,384]{1,0:T(8,128)(2,1)S(1)}, bf16[384,384]{1,0:T(8,128)(2,1)S(1)}, u32[]{:S(2)}, u32[]{:S(2)}) collective-permute-start(bf16[384,384]{1,0:T(8,128)(2,1)S(1)} %get-tuple-element.31), channel_id=1, source_target_pairs={{0,2},{1,3},{2,0},{3,1},{4,5},{5,4},{6,7},{7,6},{8,10},{9,11},{10,... | collective-permute-start | bytes 884744 | tf_op jit(solution)/shard_map/ppermute | solution.py:280
  5.6 6.8 %collective-permute-start.2 = (bf16[3,192,128]{2,1,0:T(8,128)(2,1)S(1)}, bf16[3,192,128]{2,1,0:T(8,128)(2,1)S(1)}, u32[]{:S(2)}, u32[]{:S(2)}) collective-permute-start(bf16[3,192,128]{2,1,0:T(8,128)(2,1)S(1)} %get-tuple-element.35), channel_id=1, source_target_pairs={{0,8},{4,12},{8,0},{12,4},{16,24},{20,28},{24,16},{28,20},{1,9},{5... | collective-permute-start | bytes 442376 | tf_op jit(solution)/shard_map/ppermute | solution.py:270
  7.2 8.0 %collective-permute-start.3 = (bf16[3,192,128]{2,1,0:T(8,128)(2,1)S(1)}, bf16[3,192,128]{2,1,0:T(8,128)(2,1)S(1)}, u32[]{:S(2)}, u32[]{:S(2)}) collective-permute-start(bf16[3,192,128]{2,1,0:T(8,128)(2,1)S(1)} %get-tuple-element.36), channel_id=1, source_target_pairs={{0,16},{4,20},{8,24},{12,28},{16,0},{20,4},{24,8},{28,12},{1,17},{... | collective-permute-start | bytes 442376 | tf_op jit(solution)/shard_map/ppermute | solution.py:270
  8.7 6.5 %collective-permute-start.4 = (bf16[3,192,128]{2,1,0:T(8,128)(2,1)S(1)}, bf16[3,192,128]{2,1,0:T(8,128)(2,1)S(1)}, u32[]{:S(2)}, u32[]{:S(2)}) collective-permute-start(bf16[3,192,128]{2,1,0:T(8,128)(2,1)S(1)} %get-tuple-element.37), channel_id=1, source_target_pairs={{0,24},{4,28},{8,16},{12,20},{16,8},{20,12},{24,0},{28,4},{1,25},{... | collective-permute-start | bytes 442376 | tf_op jit(solution)/shard_map/ppermute | solution.py:270
  9.2 1.4 %collective-permute-start.1 = (bf16[2,192,128]{2,1,0:T(8,128)(2,1)S(1)}, bf16[2,192,128]{2,1,0:T(8,128)(2,1)S(1)}, u32[]{:S(2)}, u32[]{:S(2)}) collective-permute-start(bf16[2,192,128]{2,1,0:T(8,128)(2,1)S(1)} %slice.12), channel_id=1, source_target_pairs={{0,4},{4,0},{8,12},{12,8},{16,20},{20,16},{24,28},{28,24},{1,5},{5... | collective-permute-start | bytes 294920 | tf_op jit(solution)/shard_map/ppermute | solution.py:270
  15.2 2.6 %collective-permute-start.5 = (bf16[2,192,128]{2,1,0:T(8,128)(2,1)S(1)}, bf16[2,192,128]{2,1,0:T(8,128)(2,1)S(1)}, u32[]{:S(2)}, u32[]{:S(2)}) collective-permute-start(bf16[2,192,128]{2,1,0:T(8,128)(2,1)S(1)} %slice.13), channel_id=1, source_target_pairs={{0,4},{4,0},{8,12},{12,8},{16,20},{20,16},{24,28},{28,24},{1,5},{5... | collective-permute-start | bytes 294920 | tf_op jit(solution)/shard_map/ppermute | solution.py:270
  15.3 2.5 %collective-permute-start.6 = (bf16[2,192,128]{2,1,0:T(8,128)(2,1)S(1)}, bf16[2,192,128]{2,1,0:T(8,128)(2,1)S(1)}, u32[]{:S(2)}, u32[]{:S(2)}) collective-permute-start(bf16[2,192,128]{2,1,0:T(8,128)(2,1)S(1)} %slice.14), channel_id=1, source_target_pairs={{0,4},{4,0},{8,12},{12,8},{16,20},{20,16},{24,28},{28,24},{1,5},{5... | collective-permute-start | bytes 294920 | tf_op jit(solution)/shard_map/ppermute | solution.py:270
  15.8 1.9 %collective-permute-start.7 = (bf16[2,192,128]{2,1,0:T(8,128)(2,1)S(1)}, bf16[2,192,128]{2,1,0:T(8,128)(2,1)S(1)}, u32[]{:S(2)}, u32[]{:S(2)}) collective-permute-start(bf16[2,192,128]{2,1,0:T(8,128)(2,1)S(1)} %slice.15), channel_id=1, source_target_pairs={{0,4},{4,0},{8,12},{12,8},{16,20},{20,16},{24,28},{28,24},{1,5},{5... | collective-permute-start | bytes 294920 | tf_op jit(solution)/shard_map/ppermute | solution.py:270
  15.9 10.7 %collective-permute-start.11 = (bf16[384,384]{1,0:T(8,128)(2,1)S(1)}, bf16[384,384]{1,0:T(8,128)(2,1)S(1)}, u32[]{:S(2)}, u32[]{:S(2)}) collective-permute-start(bf16[384,384]{1,0:T(8,128)(2,1)S(1)} %collective-permute-done.refs_5_), channel_id=1, source_target_pairs={{0,8},{4,20},{8,0},{12,28},{16,24},{20,4},{24,16},{28,12},{1,9},{5... | collective-permute-start | bytes 884744 | tf_op jit(solution)/shard_map/ppermute | solution.py:276
  16.4 12.4 %copy-start = (bf16[768,384]{1,0:T(8,128)(2,1)S(1)}, bf16[768,384]{1,0:T(8,128)(2,1)}, u32[]{:S(2)}) copy-start(bf16[768,384]{1,0:T(8,128)(2,1)} %refs_4_.1) | copy-start | bytes 1769476
  16.4 7.1 %collective-permute-start.12 = (bf16[208,384]{1,0:T(8,128)(2,1)S(1)}, bf16[208,384]{1,0:T(8,128)(2,1)S(1)}, u32[]{:S(2)}, u32[]{:S(2)}) collective-permute-start(bf16[208,384]{1,0:T(8,128)(2,1)S(1)} %constant_dynamic-slice_fusion), channel_id=1, source_target_pairs={{0,1},{1,0},{2,3},{3,2},{4,6},{5,7},{6,4},{7,5},{8,9},{9,8},{10,11... | collective-permute-start | bytes 479240 | tf_op jit(solution)/shard_map/ppermute | solution.py:280
  20.0 5.1 %collective-permute-start.10 = (bf16[192,128]{1,0:T(8,128)(2,1)S(1)}, bf16[192,128]{1,0:T(8,128)(2,1)S(1)}, u32[]{:S(2)}, u32[]{:S(2)}) collective-permute-start(bf16[192,128]{1,0:T(8,128)(2,1)S(1)} %get-tuple-element.46), channel_id=1, source_target_pairs={{0,24},{4,28},{8,16},{12,20},{16,8},{20,12},{24,0},{28,4},{1,25},{... | collective-permute-start | bytes 147464 | tf_op jit(solution)/shard_map/ppermute | solution.py:270
  21.6 4.4 %collective-permute-start.8 = (bf16[192,128]{1,0:T(8,128)(2,1)S(1)}, bf16[192,128]{1,0:T(8,128)(2,1)S(1)}, u32[]{:S(2)}, u32[]{:S(2)}) collective-permute-start(bf16[192,128]{1,0:T(8,128)(2,1)S(1)} %get-tuple-element.44), channel_id=1, source_target_pairs={{0,8},{4,12},{8,0},{12,4},{16,24},{20,28},{24,16},{28,20},{1,9},{5... | collective-permute-start | bytes 147464 | tf_op jit(solution)/shard_map/ppermute | solution.py:270
  22.2 4.4 %collective-permute-start.9 = (bf16[192,128]{1,0:T(8,128)(2,1)S(1)}, bf16[192,128]{1,0:T(8,128)(2,1)S(1)}, u32[]{:S(2)}, u32[]{:S(2)}) collective-permute-start(bf16[192,128]{1,0:T(8,128)(2,1)S(1)} %get-tuple-element.45), channel_id=1, source_target_pairs={{0,16},{4,20},{8,24},{12,28},{16,0},{20,4},{24,8},{28,12},{1,17},{... | collective-permute-start | bytes 147464 | tf_op jit(solution)/shard_map/ppermute | solution.py:270
  23.5 5.3 %collective-permute-start.15 = (bf16[208,384]{1,0:T(8,128)(2,1)S(1)}, bf16[208,384]{1,0:T(8,128)(2,1)S(1)}, u32[]{:S(2)}, u32[]{:S(2)}) collective-permute-start(bf16[208,384]{1,0:T(8,128)(2,1)S(1)} %collective-permute-done.12.refs_0_), channel_id=1, source_target_pairs={{0,8},{4,20},{8,0},{12,28},{16,24},{20,4},{24,16},{28,12},{1,9},{5... | collective-permute-start | bytes 479240 | tf_op jit(solution)/shard_map/ppermute | solution.py:276
  26.6 2.2 %collective-permute-start.13 = (bf16[384,384]{1,0:T(8,128)(2,1)S(1)}, bf16[384,384]{1,0:T(8,128)(2,1)S(1)}, u32[]{:S(2)}, u32[]{:S(2)}) collective-permute-start(bf16[384,384]{1,0:T(8,128)(2,1)S(1)} %collective-permute-done.refs_5_), channel_id=1, source_target_pairs={{0,4},{4,0},{8,12},{12,8},{16,20},{20,16},{24,28},{28,24},{1,5},{5... | collective-permute-start | bytes 884744 | tf_op jit(solution)/shard_map/ppermute | solution.py:270
  26.6 2.2 %collective-permute-start.14 = (bf16[384,384]{1,0:T(8,128)(2,1)S(1)}, bf16[384,384]{1,0:T(8,128)(2,1)S(1)}, u32[]{:S(2)}, u32[]{:S(2)}) collective-permute-start(bf16[384,384]{1,0:T(8,128)(2,1)S(1)} %collective-permute-done.11.refs_6_), channel_id=1, source_target_pairs={{0,4},{4,0},{8,12},{12,8},{16,20},{20,16},{24,28},{28,24},{1,5},{5... | collective-permute-start | bytes 884744 | tf_op jit(solution)/shard_map/ppermute | solution.py:270
  27.1 3.2 %collective-permute-start.16 = (bf16[208,384]{1,0:T(8,128)(2,1)S(1)}, bf16[208,384]{1,0:T(8,128)(2,1)S(1)}, u32[]{:S(2)}, u32[]{:S(2)}) collective-permute-start(bf16[208,384]{1,0:T(8,128)(2,1)S(1)} %collective-permute-done.12.refs_0_), channel_id=1, source_target_pairs={{0,4},{4,0},{8,12},{12,8},{16,20},{20,16},{24,28},{28,24},{1,5},{5... | collective-permute-start | bytes 479240 | tf_op jit(solution)/shard_map/ppermute | solution.py:270
  28.8 1.5 %collective-permute-start.17 = (bf16[208,384]{1,0:T(8,128)(2,1)S(1)}, bf16[208,384]{1,0:T(8,128)(2,1)S(1)}, u32[]{:S(2)}, u32[]{:S(2)}) collective-permute-start(bf16[208,384]{1,0:T(8,128)(2,1)S(1)} %collective-permute-done.15.refs_1_), channel_id=1, source_target_pairs={{0,4},{4,0},{8,12},{12,8},{16,20},{20,16},{24,28},{28,24},{1,5},{5... | collective-permute-start | bytes 479240 | tf_op jit(solution)/shard_map/ppermute | solution.py:270

commit v11 on v10

--- a/solution.py
+++ b/solution.py
@@ -95,17 +95,15 @@
         return other[at // 2][part - 1, rows, :] if at % 2 else same[at // 2][part, rows, :]
 
     ones = jnp.where(lax.broadcasted_iota(jnp.int32, (pad, block), 0) == 0, 1.0, 0.0).astype(keys.dtype)
-    at_frame = lax.broadcasted_iota(jnp.int32, (block, pad), 0)
-    at_feature = lax.broadcasted_iota(jnp.int32, (block, pad), 1)
+    at_feature = lax.broadcasted_iota(jnp.int32, (pad, block), 0)
+    at_frame = lax.broadcasted_iota(jnp.int32, (pad, block), 1)
     for at in range(groups * HEADS):
         here = slice(at * block, (at + 1) * block)
         frame = (at // HEADS * HEADS + (place ^ (at % HEADS))) * block + at_frame
-        bias = jnp.where((at_feature == 0) & (frame >= lengths_ref[:1, :pad]), -1e30, 0.0).astype(keys.dtype)
+        bias = jnp.where((at_feature == 0) & (frame >= lengths_ref[:1, :]), -1e30, 0.0).astype(keys.dtype)
         for head in range(2):
-            keys[head, here, :head_size] = piece(at, head, 1).T
-            keys[head, here, head_size:] = bias
-            values[head, :head_size, here] = piece(at, head, 2)
-            values[head, head_size:, here] = ones
+            keys[head, here, :] = jnp.concatenate([piece(at, head, 1), bias], axis=0).T
+            values[head, :, here] = jnp.concatenate([piece(at, head, 2), ones], axis=0)
 
     def score(head, flips):
         rows = slice(head * head_size, (head + 1) * head_size)
@@ -163,44 +161,42 @@
 def project_near_kernel(*refs):
     each = len(FLIPS)
     heads, own_ref, pieces = refs[:each], refs[each], refs[each + 1 : each + 5]
-    out_ref, attention_ref, turned, weight, blocks, sems = refs[each + 5 :]
+    blocks_ref, attention_ref, turned, weight = refs[each + 5 :]
     gather_heads(heads, turned)
-    attention_ref[...] = turned[...].T
-    place, shard = place_in_group(), lax.axis_index("fsdp")
-    half, columns = pieces[0].shape
-    beside = (place & 1) ^ 1
-    copies = []
-    for at, flip in enumerate((0, 1, 2)):
-        if flip == 0:
-            block = own_ref[...]
-        else:
-            mine = beside == flip - 1
-            for other in range(2):
-                here = pl.ds(pl.multiple_of((parity_of(place) ^ other) * half, 32), half)
-                weight[flip - 1, here, :] = jnp.where(mine, pieces[other][...], pieces[2 + other][...])
-            block = weight[flip - 1]
-        blocks[at] = jnp.dot(attention_ref[...], block, preferred_element_type=jnp.float32).astype(blocks.dtype)
-        here = pl.ds(pl.multiple_of((shard ^ flip) * columns, 128), columns)
-        copies.append(pltpu.make_async_copy(blocks.at[at], out_ref.at[0, :, here], sems.at[at]))
-        copies[-1].start()
-    for copy in copies:
-        copy.wait()
-
-
-def project_third_kernel(so_far_ref, attention_ref, *refs):
-    pieces, (out_ref, weight, block, sem) = refs[:4], refs[4:]
+    attention = turned[...].T
+    attention_ref[...] = attention
+    place = place_in_group()
+    half = pieces[0].shape[0]
+    for flip in (1, 2):
+        mine = (place & 1) == 2 - flip
+        for other in range(2):
+            here = pl.ds(pl.multiple_of((parity_of(place) ^ other) * half, 32), half)
+            weight[flip - 1, here, :] = jnp.where(mine, pieces[other][...], pieces[2 + other][...])
+    for flip, block in enumerate((own_ref[...], weight[0], weight[1])):
+        blocks_ref[flip] = jnp.dot(attention, block, preferred_element_type=jnp.float32).astype(blocks_ref.dtype)
+
+
+def project_third_kernel(blocks_ref, attention_ref, *refs):
+    pieces, (out_ref, weight, last, sems) = refs[:4], refs[4:]
     place, shard = place_in_group(), lax.axis_index("fsdp")
     part, columns = pieces[0].shape
     half = weight.shape[0] // 2
+
+    def copy_out(flip, block_ref):
+        here = pl.ds(pl.multiple_of((shard ^ flip) * columns, 128), columns)
+        copy = pltpu.make_async_copy(block_ref, out_ref.at[0, :, here], sems.at[flip])
+        copy.start()
+        return copy
+
+    copies = [copy_out(flip, blocks_ref.at[flip]) for flip in range(3)]
     for other in range(2):
         for flip in range(2):
             first = (parity_of(place) ^ flip) * half + ((place & 1) ^ other) * (half - part)
             weight[pl.ds(pl.multiple_of(first, 16), part), :] = pieces[2 * other + flip][...]
-    block[...] = jnp.dot(attention_ref[...], weight[...], preferred_element_type=jnp.float32).astype(block.dtype)
-    here = pl.ds(pl.multiple_of((shard ^ 3) * columns, 128), columns)
-    copy = pltpu.make_async_copy(block, out_ref.at[0, :, here], sem)
-    copy.start()
-    copy.wait()
+    last[...] = jnp.dot(attention_ref[...], weight[...], preferred_element_type=jnp.float32).astype(last.dtype)
+    copies.append(copy_out(3, last))
+    for copy in copies:
+        copy.wait()
 
 
 def projection_cost(frames, features, columns):
@@ -229,14 +225,12 @@
     features, columns = own.shape
     return pl.pallas_call(
         project_near_kernel,
-        out_shape=[jax.ShapeDtypeStruct((1, frames, 4 * columns), jnp.bfloat16), pltpu.VMEM((frames, features), jnp.bfloat16)],
+        out_shape=[pltpu.VMEM((3, frames, columns), jnp.bfloat16), pltpu.VMEM((frames, features), jnp.bfloat16)],
         in_specs=[WHOLE] * (len(FLIPS) + 5),
-        out_specs=[IN_HBM, WHOLE],
+        out_specs=[WHOLE] * 2,
         scratch_shapes=[
             pltpu.VMEM((features, frames), jnp.bfloat16),
             pltpu.VMEM((2, features, columns), jnp.bfloat16),
-            pltpu.VMEM((3, frames, columns), jnp.bfloat16),
-            pltpu.SemaphoreType.DMA((3,)),
         ],
         compiler_params=params(24),
         cost_estimate=projection_cost(frames, features, 3 * columns),
@@ -244,24 +238,23 @@
     )(*heads, own, *pieces)
 
 
-def project_third(so_far, attention, pieces):
+def project_third(blocks, attention, pieces):
     frames, features = attention.shape
     columns = pieces[0].shape[1]
     return pl.pallas_call(
         project_third_kernel,
-        out_shape=jax.ShapeDtypeStruct(so_far.shape, so_far.dtype),
-        in_specs=[IN_HBM] + [WHOLE] * 5,
+        out_shape=jax.ShapeDtypeStruct((1, frames, 4 * columns), blocks.dtype),
+        in_specs=[WHOLE] * 6,
         out_specs=IN_HBM,
-        input_output_aliases={0: 0},
         scratch_shapes=[
             pltpu.VMEM((features, columns), jnp.bfloat16),
             pltpu.VMEM((frames, columns), jnp.bfloat16),
-            pltpu.SemaphoreType.DMA,
+            pltpu.SemaphoreType.DMA((4,)),
         ],
         compiler_params=params(24),
         cost_estimate=projection_cost(frames, features, columns),
         name="project_third_shard",
-    )(so_far, attention, *pieces)
+    )(blocks, attention, *pieces)
 
 
 def per_device(ctx, fsdp, queries, key_rows, value_rows, lengths, out_weight):
@@ -318,8 +311,8 @@
     fetched_other, passed_other, third_other, third_passed_other = (
         exchange(array, "ctx", 1) for array in (fetched, passed, third, third_passed)
     )
-    so_far, attention = project_near(heads, out_weight, [fetched, passed, fetched_other, passed_other])
-    return project_third(so_far, attention, [third, third_passed, third_other, third_passed_other])
+    blocks, attention = project_near(heads, out_weight, [fetched, passed, fetched_other, passed_other])
+    return project_third(blocks, attention, [third, third_passed, third_other, third_passed_other])
 
 
 def solution(mesh):

time: 31.5 us -> 31.4 us (level)
  Pallas kernels: 6.13 us -> 5.44 us
  waiting for transfers between devices: 8.55 us -> 9.18 us
    pallas_call x2, Pallas kernels: 2.44 us -> 1.74 us  [the longest x1 1.02 us: project_third(): pl.pallas_call(project_third_kernel, out_shape=jax.ShapeDtypeStruct((1, f...]
    ppermute x14, waiting for transfers between devices: 5.45 us -> 6.08 us  [exchange(): return lax.ppermute(array, axis, [(i, i ^ flip) for i in range(size)])]
  transfers between devices with their start and end apart: 18 -> 18, of which waited for: 8 -> 9; matrix products, arithmetic and copies ran while one was open for 0% -> 0% of each run, Pallas kernels for 12% -> 10%
where the time goes in v11:
time: 31.4 us; the launch traced here: 31.2 us
  starting transfers between devices  15.8 us (50%)
  waiting for transfers between devices  9.18 us (29%)
  Pallas kernels  5.44 us (17%)
  between operations  0.77 us (2%)
    ppermute x14, starting transfers between devices, exchange(): return lax.ppermute(array, axis, [(i, i ^ flip) for i in range(size)])  8.4 us
    ppermute x14, waiting for transfers between devices, exchange(): return lax.ppermute(array, axis, [(i, i ^ flip) for i in range(size)])  6.08 us
    ppermute x2, starting transfers between devices, exchange_along(): return lax.ppermute(array, ('ctx', 'fsdp'), pairs)  5.43 us
    pallas_call x1, Pallas kernels, attend(): pl.pallas_call(functools.partial(attention_kernel, groups), out_shape=[pl...  2.22 us
    ppermute x2, starting transfers between devices, exchange_in_plane(): lax.ppermute(array, 'ctx', [(i, i ^ (4 if i % 2 else 2)) for i in range(c...  1.95 us
    ppermute x2, waiting for transfers between devices, exchange_in_plane(): lax.ppermute(array, 'ctx', [(i, i ^ (4 if i % 2 else 2)) for i in range(c...  1.68 us
    ppermute x2, waiting for transfers between devices, exchange_along(): return lax.ppermute(array, ('ctx', 'fsdp'), pairs)  1.42 us
    pallas_call x1, Pallas kernels, copy_in(): pl.pallas_call(functools.partial(copy_in_kernel, by_parity), out_shape=[p...  1.24 us
  transfers between devices with their start and end apart: 18, of which 9 were waited for; matrix products, arithmetic and copies ran while one was open for 0% of the time, Pallas kernels for 10%

profile of v11, /device:TPU:0, one launch (start us, length us, event | category | flops | bytes accessed | tf_op | source)
XLA Modules:
  0.0 31.2 jit_solution(6528829431634289351)
XLA Ops:
  0.0 1.2 %copy_in.1 = (bf16[3,128,768]{2,1,0:T(8,128)(2,1)S(1)}, bf16[384,384]{1,0:T(8,128)(2,1)S(1)}) custom-call(bf16[1,128,768]{2,1,0:T(8,128)(2,1)} %query_ref.1, bf16[1,128,768]{2,1,0:T(8,128)(2,1)} %key_ref.1, bf16[1,128,768]{2,1,0:T(8,128)(2,1)} %value_ref.1, bf16[768,384]{1,0:T(8,128)(2,1)} %refs_4_.1), custom_call_target="tpu_custom_call" | custom-call | tf_op jit(solution)/shard_map/copy_in/pallas_call | solution.py:45
  1.2 4.1 %collective-permute-start = (bf16[384,384]{1,0:T(8,128)(2,1)S(1)}, bf16[384,384]{1,0:T(8,128)(2,1)S(1)}, u32[]{:S(2)}, u32[]{:S(2)}) collective-permute-start(bf16[384,384]{1,0:T(8,128)(2,1)S(1)} %get-tuple-element.31), channel_id=1, source_target_pairs={{0,2},{1,3},{2,0},{3,1},{4,5},{5,4},{6,7},{7,6},{8,10},{9,11},{10,... | collective-permute-start | bytes 884744 | tf_op jit(solution)/shard_map/ppermute | solution.py:273
  5.3 0.2 turn_heads.1
  5.6 1.6 %collective-permute-start.2 = (bf16[3,192,128]{2,1,0:T(8,128)(2,1)S(1)}, bf16[3,192,128]{2,1,0:T(8,128)(2,1)S(1)}, u32[]{:S(2)}, u32[]{:S(2)}) collective-permute-start(bf16[3,192,128]{2,1,0:T(8,128)(2,1)S(1)} %get-tuple-element.35), channel_id=1, source_target_pairs={{0,8},{4,12},{8,0},{12,4},{16,24},{20,28},{24,16},{28,20},{1,9},{5... | collective-permute-start | bytes 442376 | tf_op jit(solution)/shard_map/ppermute | solution.py:263
  7.2 1.5 %collective-permute-start.3 = (bf16[3,192,128]{2,1,0:T(8,128)(2,1)S(1)}, bf16[3,192,128]{2,1,0:T(8,128)(2,1)S(1)}, u32[]{:S(2)}, u32[]{:S(2)}) collective-permute-start(bf16[3,192,128]{2,1,0:T(8,128)(2,1)S(1)} %get-tuple-element.36), channel_id=1, source_target_pairs={{0,16},{4,20},{8,24},{12,28},{16,0},{20,4},{24,8},{28,12},{1,17},{... | collective-permute-start | bytes 442376 | tf_op jit(solution)/shard_map/ppermute | solution.py:263
  8.7 0.5 %collective-permute-start.4 = (bf16[3,192,128]{2,1,0:T(8,128)(2,1)S(1)}, bf16[3,192,128]{2,1,0:T(8,128)(2,1)S(1)}, u32[]{:S(2)}, u32[]{:S(2)}) collective-permute-start(bf16[3,192,128]{2,1,0:T(8,128)(2,1)S(1)} %get-tuple-element.37), channel_id=1, source_target_pairs={{0,24},{4,28},{8,16},{12,20},{16,8},{20,12},{24,0},{28,4},{1,25},{... | collective-permute-start | bytes 442376 | tf_op jit(solution)/shard_map/ppermute | solution.py:263
  9.2 0.1 collective-permute-start.1
  9.9 0.6 %collective-permute-done.1.refs_4_ = bf16[2,192,128]{2,1,0:T(8,128)(2,1)S(1)} collective-permute-done((bf16[2,192,128]{2,1,0:T(8,128)(2,1)S(1)}, bf16[2,192,128]{2,1,0:T(8,128)(2,1)S(1)}, u32[]{:S(2)}, u32[]{:S(2)}) %collective-permute-start.1) | collective-permute-done | bytes 98336 | tf_op jit(solution)/shard_map/ppermute | solution.py:263
  10.5 1.4 %collective-permute-done.refs_5_ = bf16[384,384]{1,0:T(8,128)(2,1)S(1)} collective-permute-done((bf16[384,384]{1,0:T(8,128)(2,1)S(1)}, bf16[384,384]{1,0:T(8,128)(2,1)S(1)}, u32[]{:S(2)}, u32[]{:S(2)}) %collective-permute-start) | collective-permute-done | bytes 294944 | tf_op jit(solution)/shard_map/ppermute | solution.py:273
  12.0 0.4 %collective-permute-done.2.refs_1_ = bf16[3,192,128]{2,1,0:T(8,128)(2,1)S(1)} collective-permute-done((bf16[3,192,128]{2,1,0:T(8,128)(2,1)S(1)}, bf16[3,192,128]{2,1,0:T(8,128)(2,1)S(1)}, u32[]{:S(2)}, u32[]{:S(2)}) %collective-permute-start.2) | collective-permute-done | bytes 147488 | tf_op jit(solution)/shard_map/ppermute | solution.py:263
  12.4 2.8 %collective-permute-done.3.refs_2_ = bf16[3,192,128]{2,1,0:T(8,128)(2,1)S(1)} collective-permute-done((bf16[3,192,128]{2,1,0:T(8,128)(2,1)S(1)}, bf16[3,192,128]{2,1,0:T(8,128)(2,1)S(1)}, u32[]{:S(2)}, u32[]{:S(2)}) %collective-permute-start.3) | collective-permute-done | bytes 147488 | tf_op jit(solution)/shard_map/ppermute | solution.py:263
  15.2 0.0 collective-permute-done.4.refs_3_
  15.2 0.1 collective-permute-start.5
  15.3 0.5 %collective-permute-start.6 = (bf16[2,192,128]{2,1,0:T(8,128)(2,1)S(1)}, bf16[2,192,128]{2,1,0:T(8,128)(2,1)S(1)}, u32[]{:S(2)}, u32[]{:S(2)}) collective-permute-start(bf16[2,192,128]{2,1,0:T(8,128)(2,1)S(1)} %slice.14), channel_id=1, source_target_pairs={{0,4},{4,0},{8,12},{12,8},{16,20},{20,16},{24,28},{28,24},{1,5},{5... | collective-permute-start | bytes 294920 | tf_op jit(solution)/shard_map/ppermute | solution.py:263
  15.8 0.1 collective-permute-start.7
  15.9 0.5 %collective-permute-start.11 = (bf16[384,384]{1,0:T(8,128)(2,1)S(1)}, bf16[384,384]{1,0:T(8,128)(2,1)S(1)}, u32[]{:S(2)}, u32[]{:S(2)}) collective-permute-start(bf16[384,384]{1,0:T(8,128)(2,1)S(1)} %collective-permute-done.refs_5_), channel_id=1, source_target_pairs={{0,8},{4,20},{8,0},{12,28},{16,24},{20,4},{24,16},{28,12},{1,9},{5... | collective-permute-start | bytes 884744 | tf_op jit(solution)/shard_map/ppermute | solution.py:269
  16.4 0.0 copy-start
  16.4 1.3 %collective-permute-start.12 = (bf16[208,384]{1,0:T(8,128)(2,1)S(1)}, bf16[208,384]{1,0:T(8,128)(2,1)S(1)}, u32[]{:S(2)}, u32[]{:S(2)}) collective-permute-start(bf16[208,384]{1,0:T(8,128)(2,1)S(1)} %constant_dynamic-slice_fusion), channel_id=1, source_target_pairs={{0,1},{1,0},{2,3},{3,2},{4,6},{5,7},{6,4},{7,5},{8,9},{9,8},{10,11... | collective-permute-start | bytes 479240 | tf_op jit(solution)/shard_map/ppermute | solution.py:273
  17.7 0.0 collective-permute-done.5.refs_5_
  17.7 0.0 collective-permute-done.6.refs_6_
  17.7 0.0 collective-permute-done.7.refs_7_
  17.7 2.2 %attend_two_heads.1 = (bf16[192,128]{1,0:T(8,128)(2,1)S(1)}, bf16[192,128]{1,0:T(8,128)(2,1)S(1)}, bf16[192,128]{1,0:T(8,128)(2,1)S(1)}, bf16[192,128]{1,0:T(8,128)(2,1)S(1)}) custom-call(s32[8,128]{1,0:T(8,128)S(1)} %broadcast_in_dim.2.lengths_ref, bf16[3,192,128]{2,1,0:T(8,128)(2,1)S(1)} %get-tuple-element.33.refs_0_, ...), custom_call_target="tpu_custom_call" | custom-call | flops 1610612736 | tf_op jit(solution)/shard_map/attend_two_heads/pallas_call | solution.py:132
  20.0 1.7 %collective-permute-start.10 = (bf16[192,128]{1,0:T(8,128)(2,1)S(1)}, bf16[192,128]{1,0:T(8,128)(2,1)S(1)}, u32[]{:S(2)}, u32[]{:S(2)}) collective-permute-start(bf16[192,128]{1,0:T(8,128)(2,1)S(1)} %get-tuple-element.46), channel_id=1, source_target_pairs={{0,24},{4,28},{8,16},{12,20},{16,8},{20,12},{24,0},{28,4},{1,25},{... | collective-permute-start | bytes 147464 | tf_op jit(solution)/shard_map/ppermute | solution.py:263
  21.7 0.5 %collective-permute-start.8 = (bf16[192,128]{1,0:T(8,128)(2,1)S(1)}, bf16[192,128]{1,0:T(8,128)(2,1)S(1)}, u32[]{:S(2)}, u32[]{:S(2)}) collective-permute-start(bf16[192,128]{1,0:T(8,128)(2,1)S(1)} %get-tuple-element.44), channel_id=1, source_target_pairs={{0,8},{4,12},{8,0},{12,4},{16,24},{20,28},{24,16},{28,20},{1,9},{5... | collective-permute-start | bytes 147464 | tf_op jit(solution)/shard_map/ppermute | solution.py:263
  22.2 1.3 %collective-permute-start.9 = (bf16[192,128]{1,0:T(8,128)(2,1)S(1)}, bf16[192,128]{1,0:T(8,128)(2,1)S(1)}, u32[]{:S(2)}, u32[]{:S(2)}) collective-permute-start(bf16[192,128]{1,0:T(8,128)(2,1)S(1)} %get-tuple-element.45), channel_id=1, source_target_pairs={{0,16},{4,20},{8,24},{12,28},{16,0},{20,4},{24,8},{28,12},{1,17},{... | collective-permute-start | bytes 147464 | tf_op jit(solution)/shard_map/ppermute | solution.py:263
  23.5 0.0 collective-permute-done.12.refs_0_
  23.5 1.5 %collective-permute-start.15 = (bf16[208,384]{1,0:T(8,128)(2,1)S(1)}, bf16[208,384]{1,0:T(8,128)(2,1)S(1)}, u32[]{:S(2)}, u32[]{:S(2)}) collective-permute-start(bf16[208,384]{1,0:T(8,128)(2,1)S(1)} %collective-permute-done.12.refs_0_), channel_id=1, source_target_pairs={{0,8},{4,20},{8,0},{12,28},{16,24},{20,4},{24,16},{28,12},{1,9},{5... | collective-permute-start | bytes 479240 | tf_op jit(solution)/shard_map/ppermute | solution.py:269
  25.0 0.1 collective-permute-done.10.refs_3_
  25.1 1.0 %collective-permute-done.8.refs_1_ = bf16[192,128]{1,0:T(8,128)(2,1)S(1)} collective-permute-done((bf16[192,128]{1,0:T(8,128)(2,1)S(1)}, bf16[192,128]{1,0:T(8,128)(2,1)S(1)}, u32[]{:S(2)}, u32[]{:S(2)}) %collective-permute-start.8) | collective-permute-done | bytes 49184 | tf_op jit(solution)/shard_map/ppermute | solution.py:263
  26.1 0.5 %collective-permute-done.9.refs_2_ = bf16[192,128]{1,0:T(8,128)(2,1)S(1)} collective-permute-done((bf16[192,128]{1,0:T(8,128)(2,1)S(1)}, bf16[192,128]{1,0:T(8,128)(2,1)S(1)}, u32[]{:S(2)}, u32[]{:S(2)}) %collective-permute-start.9) | collective-permute-done | bytes 49184 | tf_op jit(solution)/shard_map/ppermute | solution.py:263
  26.6 0.0 collective-permute-done.11.refs_6_
  26.6 0.0 collective-permute-start.13
  26.6 0.5 %collective-permute-start.14 = (bf16[384,384]{1,0:T(8,128)(2,1)S(1)}, bf16[384,384]{1,0:T(8,128)(2,1)S(1)}, u32[]{:S(2)}, u32[]{:S(2)}) collective-permute-start(bf16[384,384]{1,0:T(8,128)(2,1)S(1)} %collective-permute-done.11.refs_6_), channel_id=1, source_target_pairs={{0,4},{4,0},{8,12},{12,8},{16,20},{20,16},{24,28},{28,24},{1,5},{5... | collective-permute-start | bytes 884744 | tf_op jit(solution)/shard_map/ppermute | solution.py:263
  27.1 0.0 collective-permute-start.16
  27.1 1.7 %collective-permute-done.15.refs_1_ = bf16[208,384]{1,0:T(8,128)(2,1)S(1)} collective-permute-done((bf16[208,384]{1,0:T(8,128)(2,1)S(1)}, bf16[208,384]{1,0:T(8,128)(2,1)S(1)}, u32[]{:S(2)}, u32[]{:S(2)}) %collective-permute-start.15) | collective-permute-done | bytes 159776 | tf_op jit(solution)/shard_map/ppermute | solution.py:269
  28.8 0.0 collective-permute-start.17
  28.8 0.0 collective-permute-done.13.refs_7_
  28.8 0.0 collective-permute-done.14.refs_8_
  28.8 0.0 copy-done
  28.8 0.7 %project_near_shards.1 = (bf16[3,128,384]{2,1,0:T(8,128)(2,1)S(1)}, bf16[128,768]{1,0:T(8,128)(2,1)S(1)}) custom-call(bf16[192,128]{1,0:T(8,128)(2,1)S(1)} %get-tuple-element.48.refs_0_, bf16[192,128]{1,0:T(8,128)(2,1)S(1)} %collective-permute-done.8.refs_1_, bf16[192,128]{1,0:T(8,128)(2,1)S(1)} %collective-permute-done.9.refs_2_, ...), custom_call_target="tpu_custom_call" | custom-call | flops 226492416 | bytes 1769472 | tf_op jit(solution)/shard_map/project_near_shards/pallas_call | solution.py:226
  29.5 0.0 collective-permute-done.16.refs_2_
  29.6 0.6 %collective-permute-done.17.refs_3_ = bf16[208,384]{1,0:T(8,128)(2,1)S(1)} collective-permute-done((bf16[208,384]{1,0:T(8,128)(2,1)S(1)}, bf16[208,384]{1,0:T(8,128)(2,1)S(1)}, u32[]{:S(2)}, u32[]{:S(2)}) %collective-permute-start.17) | collective-permute-done | bytes 159776 | tf_op jit(solution)/shard_map/ppermute | solution.py:263
  30.2 1.0 %project_third_shard.1 = bf16[1,128,1536]{2,1,0:T(8,128)(2,1)} custom-call(bf16[3,128,384]{2,1,0:T(8,128)(2,1)S(1)} %get-tuple-element.54.blocks_ref, bf16[128,768]{1,0:T(8,128)(2,1)S(1)} %get-tuple-element.55.attention_ref, bf16[208,384]{1,0:T(8,128)(2,1)S(1)} %collective-permute-done.12.refs_0_, bf16[208,384]{1,0:T(8,128)(2,1)S(1)} %collective-permute-done.15.refs_1_, ...), custom_call_target="tpu_custom_call" | custom-call | flops 75497472 | bytes 589824 | tf_op jit(solution)/shard_map/project_third_shard/pallas_call | solution.py:244
  (6 shorter events, 0.0 us)
Async XLA Ops:
  1.2 10.7 %collective-permute-start = (bf16[384,384]{1,0:T(8,128)(2,1)S(1)}, bf16[384,384]{1,0:T(8,128)(2,1)S(1)}, u32[]{:S(2)}, u32[]{:S(2)}) collective-permute-start(bf16[384,384]{1,0:T(8,128)(2,1)S(1)} %get-tuple-element.31), channel_id=1, source_target_pairs={{0,2},{1,3},{2,0},{3,1},{4,5},{5,4},{6,7},{7,6},{8,10},{9,11},{10,... | collective-permute-start | bytes 884744 | tf_op jit(solution)/shard_map/ppermute | solution.py:273
  5.6 6.8 %collective-permute-start.2 = (bf16[3,192,128]{2,1,0:T(8,128)(2,1)S(1)}, bf16[3,192,128]{2,1,0:T(8,128)(2,1)S(1)}, u32[]{:S(2)}, u32[]{:S(2)}) collective-permute-start(bf16[3,192,128]{2,1,0:T(8,128)(2,1)S(1)} %get-tuple-element.35), channel_id=1, source_target_pairs={{0,8},{4,12},{8,0},{12,4},{16,24},{20,28},{24,16},{28,20},{1,9},{5... | collective-permute-start | bytes 442376 | tf_op jit(solution)/shard_map/ppermute | solution.py:263
  7.2 8.0 %collective-permute-start.3 = (bf16[3,192,128]{2,1,0:T(8,128)(2,1)S(1)}, bf16[3,192,128]{2,1,0:T(8,128)(2,1)S(1)}, u32[]{:S(2)}, u32[]{:S(2)}) collective-permute-start(bf16[3,192,128]{2,1,0:T(8,128)(2,1)S(1)} %get-tuple-element.36), channel_id=1, source_target_pairs={{0,16},{4,20},{8,24},{12,28},{16,0},{20,4},{24,8},{28,12},{1,17},{... | collective-permute-start | bytes 442376 | tf_op jit(solution)/shard_map/ppermute | solution.py:263
  8.7 6.5 %collective-permute-start.4 = (bf16[3,192,128]{2,1,0:T(8,128)(2,1)S(1)}, bf16[3,192,128]{2,1,0:T(8,128)(2,1)S(1)}, u32[]{:S(2)}, u32[]{:S(2)}) collective-permute-start(bf16[3,192,128]{2,1,0:T(8,128)(2,1)S(1)} %get-tuple-element.37), channel_id=1, source_target_pairs={{0,24},{4,28},{8,16},{12,20},{16,8},{20,12},{24,0},{28,4},{1,25},{... | collective-permute-start | bytes 442376 | tf_op jit(solution)/shard_map/ppermute | solution.py:263
  9.2 1.4 %collective-permute-start.1 = (bf16[2,192,128]{2,1,0:T(8,128)(2,1)S(1)}, bf16[2,192,128]{2,1,0:T(8,128)(2,1)S(1)}, u32[]{:S(2)}, u32[]{:S(2)}) collective-permute-start(bf16[2,192,128]{2,1,0:T(8,128)(2,1)S(1)} %slice.12), channel_id=1, source_target_pairs={{0,4},{4,0},{8,12},{12,8},{16,20},{20,16},{24,28},{28,24},{1,5},{5... | collective-permute-start | bytes 294920 | tf_op jit(solution)/shard_map/ppermute | solution.py:263
  15.2 2.6 %collective-permute-start.5 = (bf16[2,192,128]{2,1,0:T(8,128)(2,1)S(1)}, bf16[2,192,128]{2,1,0:T(8,128)(2,1)S(1)}, u32[]{:S(2)}, u32[]{:S(2)}) collective-permute-start(bf16[2,192,128]{2,1,0:T(8,128)(2,1)S(1)} %slice.13), channel_id=1, source_target_pairs={{0,4},{4,0},{8,12},{12,8},{16,20},{20,16},{24,28},{28,24},{1,5},{5... | collective-permute-start | bytes 294920 | tf_op jit(solution)/shard_map/ppermute | solution.py:263
  15.3 2.5 %collective-permute-start.6 = (bf16[2,192,128]{2,1,0:T(8,128)(2,1)S(1)}, bf16[2,192,128]{2,1,0:T(8,128)(2,1)S(1)}, u32[]{:S(2)}, u32[]{:S(2)}) collective-permute-start(bf16[2,192,128]{2,1,0:T(8,128)(2,1)S(1)} %slice.14), channel_id=1, source_target_pairs={{0,4},{4,0},{8,12},{12,8},{16,20},{20,16},{24,28},{28,24},{1,5},{5... | collective-permute-start | bytes 294920 | tf_op jit(solution)/shard_map/ppermute | solution.py:263
  15.8 1.9 %collective-permute-start.7 = (bf16[2,192,128]{2,1,0:T(8,128)(2,1)S(1)}, bf16[2,192,128]{2,1,0:T(8,128)(2,1)S(1)}, u32[]{:S(2)}, u32[]{:S(2)}) collective-permute-start(bf16[2,192,128]{2,1,0:T(8,128)(2,1)S(1)} %slice.15), channel_id=1, source_target_pairs={{0,4},{4,0},{8,12},{12,8},{16,20},{20,16},{24,28},{28,24},{1,5},{5... | collective-permute-start | bytes 294920 | tf_op jit(solution)/shard_map/ppermute | solution.py:263
  15.9 10.7 %collective-permute-start.11 = (bf16[384,384]{1,0:T(8,128)(2,1)S(1)}, bf16[384,384]{1,0:T(8,128)(2,1)S(1)}, u32[]{:S(2)}, u32[]{:S(2)}) collective-permute-start(bf16[384,384]{1,0:T(8,128)(2,1)S(1)} %collective-permute-done.refs_5_), channel_id=1, source_target_pairs={{0,8},{4,20},{8,0},{12,28},{16,24},{20,4},{24,16},{28,12},{1,9},{5... | collective-permute-start | bytes 884744 | tf_op jit(solution)/shard_map/ppermute | solution.py:269
  16.4 12.4 %copy-start = (bf16[768,384]{1,0:T(8,128)(2,1)S(1)}, bf16[768,384]{1,0:T(8,128)(2,1)}, u32[]{:S(2)}) copy-start(bf16[768,384]{1,0:T(8,128)(2,1)} %refs_4_.1) | copy-start | bytes 1769476
  16.4 7.1 %collective-permute-start.12 = (bf16[208,384]{1,0:T(8,128)(2,1)S(1)}, bf16[208,384]{1,0:T(8,128)(2,1)S(1)}, u32[]{:S(2)}, u32[]{:S(2)}) collective-permute-start(bf16[208,384]{1,0:T(8,128)(2,1)S(1)} %constant_dynamic-slice_fusion), channel_id=1, source_target_pairs={{0,1},{1,0},{2,3},{3,2},{4,6},{5,7},{6,4},{7,5},{8,9},{9,8},{10,11... | collective-permute-start | bytes 479240 | tf_op jit(solution)/shard_map/ppermute | solution.py:273
  20.0 5.1 %collective-permute-start.10 = (bf16[192,128]{1,0:T(8,128)(2,1)S(1)}, bf16[192,128]{1,0:T(8,128)(2,1)S(1)}, u32[]{:S(2)}, u32[]{:S(2)}) collective-permute-start(bf16[192,128]{1,0:T(8,128)(2,1)S(1)} %get-tuple-element.46), channel_id=1, source_target_pairs={{0,24},{4,28},{8,16},{12,20},{16,8},{20,12},{24,0},{28,4},{1,25},{... | collective-permute-start | bytes 147464 | tf_op jit(solution)/shard_map/ppermute | solution.py:263
  21.7 4.4 %collective-permute-start.8 = (bf16[192,128]{1,0:T(8,128)(2,1)S(1)}, bf16[192,128]{1,0:T(8,128)(2,1)S(1)}, u32[]{:S(2)}, u32[]{:S(2)}) collective-permute-start(bf16[192,128]{1,0:T(8,128)(2,1)S(1)} %get-tuple-element.44), channel_id=1, source_target_pairs={{0,8},{4,12},{8,0},{12,4},{16,24},{20,28},{24,16},{28,20},{1,9},{5... | collective-permute-start | bytes 147464 | tf_op jit(solution)/shard_map/ppermute | solution.py:263
  22.2 4.4 %collective-permute-start.9 = (bf16[192,128]{1,0:T(8,128)(2,1)S(1)}, bf16[192,128]{1,0:T(8,128)(2,1)S(1)}, u32[]{:S(2)}, u32[]{:S(2)}) collective-permute-start(bf16[192,128]{1,0:T(8,128)(2,1)S(1)} %get-tuple-element.45), channel_id=1, source_target_pairs={{0,16},{4,20},{8,24},{12,28},{16,0},{20,4},{24,8},{28,12},{1,17},{... | collective-permute-start | bytes 147464 | tf_op jit(solution)/shard_map/ppermute | solution.py:263
  23.5 5.3 %collective-permute-start.15 = (bf16[208,384]{1,0:T(8,128)(2,1)S(1)}, bf16[208,384]{1,0:T(8,128)(2,1)S(1)}, u32[]{:S(2)}, u32[]{:S(2)}) collective-permute-start(bf16[208,384]{1,0:T(8,128)(2,1)S(1)} %collective-permute-done.12.refs_0_), channel_id=1, source_target_pairs={{0,8},{4,20},{8,0},{12,28},{16,24},{20,4},{24,16},{28,12},{1,9},{5... | collective-permute-start | bytes 479240 | tf_op jit(solution)/shard_map/ppermute | solution.py:269
  26.6 2.2 %collective-permute-start.13 = (bf16[384,384]{1,0:T(8,128)(2,1)S(1)}, bf16[384,384]{1,0:T(8,128)(2,1)S(1)}, u32[]{:S(2)}, u32[]{:S(2)}) collective-permute-start(bf16[384,384]{1,0:T(8,128)(2,1)S(1)} %collective-permute-done.refs_5_), channel_id=1, source_target_pairs={{0,4},{4,0},{8,12},{12,8},{16,20},{20,16},{24,28},{28,24},{1,5},{5... | collective-permute-start | bytes 884744 | tf_op jit(solution)/shard_map/ppermute | solution.py:263
  26.6 2.2 %collective-permute-start.14 = (bf16[384,384]{1,0:T(8,128)(2,1)S(1)}, bf16[384,384]{1,0:T(8,128)(2,1)S(1)}, u32[]{:S(2)}, u32[]{:S(2)}) collective-permute-start(bf16[384,384]{1,0:T(8,128)(2,1)S(1)} %collective-permute-done.11.refs_6_), channel_id=1, source_target_pairs={{0,4},{4,0},{8,12},{12,8},{16,20},{20,16},{24,28},{28,24},{1,5},{5... | collective-permute-start | bytes 884744 | tf_op jit(solution)/shard_map/ppermute | solution.py:263
  27.1 2.4 %collective-permute-start.16 = (bf16[208,384]{1,0:T(8,128)(2,1)S(1)}, bf16[208,384]{1,0:T(8,128)(2,1)S(1)}, u32[]{:S(2)}, u32[]{:S(2)}) collective-permute-start(bf16[208,384]{1,0:T(8,128)(2,1)S(1)} %collective-permute-done.12.refs_0_), channel_id=1, source_target_pairs={{0,4},{4,0},{8,12},{12,8},{16,20},{20,16},{24,28},{28,24},{1,5},{5... | collective-permute-start | bytes 479240 | tf_op jit(solution)/shard_map/ppermute | solution.py:263
  28.8 1.4 %collective-permute-start.17 = (bf16[208,384]{1,0:T(8,128)(2,1)S(1)}, bf16[208,384]{1,0:T(8,128)(2,1)S(1)}, u32[]{:S(2)}, u32[]{:S(2)}) collective-permute-start(bf16[208,384]{1,0:T(8,128)(2,1)S(1)} %collective-permute-done.15.refs_1_), channel_id=1, source_target_pairs={{0,4},{4,0},{8,12},{12,8},{16,20},{20,16},{24,28},{28,24},{1,5},{5... | collective-permute-start | bytes 479240 | tf_op jit(solution)/shard_map/ppermute | solution.py:263

commit v12 on v11

--- a/solution.py
+++ b/solution.py
@@ -79,8 +79,8 @@
 
 def attention_kernel(groups, lengths_ref, *refs):
     each = len(FLIPS)
-    same, other = refs[:each], refs[each : 2 * each]
-    rest_ref = refs[2 * each] if groups > 1 else None
+    same, own_other, other = refs[:each], refs[each], refs[each + 1]
+    rest_ref = refs[each + 2] if groups > 1 else None
     outs, (keys, values) = refs[-2 - each : -2], refs[-2:]
     block = outs[0].shape[1]
     head_size = outs[0].shape[0] // 2
@@ -92,7 +92,9 @@
         rows = slice(head * head_size, (head + 1) * head_size)
         if groups > 1:
             return rest_ref[at, part - 1, rows, :]
-        return other[at // 2][part - 1, rows, :] if at % 2 else same[at // 2][part, rows, :]
+        if at % 2 == 0:
+            return same[at // 2][part, rows, :]
+        return other[at // 2 - 1, part - 1, rows, :] if at > 1 else own_other[part - 1, rows, :]
 
     ones = jnp.where(lax.broadcasted_iota(jnp.int32, (pad, block), 0) == 0, 1.0, 0.0).astype(keys.dtype)
     at_feature = lax.broadcasted_iota(jnp.int32, (pad, block), 0)
@@ -124,7 +126,24 @@
             outs[flip // 2][head * head_size : (head + 1) * head_size, :] = mixed[:, half * block : (half + 1) * block]
 
 
-def attend(lengths, same, other, rest, groups):
+def stack_kernel(*refs):
+    for at, ref in enumerate(refs[:-1]):
+        refs[-1][at] = ref[1:]
+
+
+def stack_keys_and_values(arrays):
+    parts, features, frames = arrays[0].shape
+    return pl.pallas_call(
+        stack_kernel,
+        out_shape=pltpu.VMEM((len(arrays), parts - 1, features, frames), arrays[0].dtype),
+        in_specs=[WHOLE] * len(arrays),
+        out_specs=WHOLE,
+        compiler_params=params(16),
+        name="stack_keys_and_values",
+    )(*arrays)
+
+
+def attend(lengths, same, own_other, other, rest, groups):
     _, features, block = same[0].shape
     keys = groups * HEADS * block
     padded = features // 2 + 32
@@ -132,13 +151,13 @@
     return pl.pallas_call(
         functools.partial(attention_kernel, groups),
         out_shape=[pltpu.VMEM((features, block), jnp.bfloat16)] * len(FLIPS),
-        in_specs=[WHOLE] * (1 + 2 * len(FLIPS) + len(rest)),
+        in_specs=[WHOLE] * (3 + len(FLIPS) + len(rest)),
         out_specs=[WHOLE] * len(FLIPS),
         scratch_shapes=[pltpu.VMEM((2, keys, padded), jnp.bfloat16), pltpu.VMEM((2, padded, keys), jnp.bfloat16)],
         compiler_params=params(32),
-        cost_estimate=pl.CostEstimate(flops=8 * keys * keys * features, bytes_accessed=0, transcendentals=0),
+        cost_estimate=pl.CostEstimate(flops=2 * keys * keys * features, bytes_accessed=0, transcendentals=0),
         name="attend_two_heads",
-    )(lengths, *same, *other, *rest)
+    )(lengths, *same, own_other, other, *rest)
 
 
 def gather_heads(heads, turned):
@@ -233,7 +252,7 @@
             pltpu.VMEM((2, features, columns), jnp.bfloat16),
         ],
         compiler_params=params(24),
-        cost_estimate=projection_cost(frames, features, 3 * columns),
+        cost_estimate=pl.CostEstimate(flops=0, bytes_accessed=0, transcendentals=0),
         name="project_near_shards",
     )(*heads, own, *pieces)
 
@@ -286,28 +305,34 @@
     own_other = exchange(own[1:], "ctx", 1)
     if split_columns:
         fetched, own_other, lengths = lax.optimization_barrier((fetched, own_other, lengths))
-        passed = exchange_in_plane(fetched)
+        passed = [exchange_in_plane(rows) for rows in (fetched[: half.shape[0] // 2], fetched[half.shape[0] // 2 :])]
         depth = half.shape[0]
         part = depth // 2 + 16
         third = lax.dynamic_slice_in_dim(fetched, core * (depth - part), part, 0)
         third = exchange_along(third, 1, 2)
     same, own_other = lax.optimization_barrier((same, own_other))
-    other = [own_other, *(exchange(array[1:], "ctx", 1) for array in same)]
+    other = exchange(stack_keys_and_values(same), "ctx", 1)
     same = [own, *same]
 
     groups = ctx // HEADS
     rest = None
     if groups > 1:
-        pairs = [array for one, two in zip(same, other) for array in (one[1:], two)]
+        pairs = [own[1:], own_other]
+        for at, array in enumerate(same[1:]):
+            pairs += [array[1:], other[at]]
         across = [[head + first for first in range(0, ctx, HEADS)] for head in range(HEADS)]
         rest = lax.all_gather(jnp.stack(pairs), "ctx", axis=0, axis_index_groups=across, tiled=True)
-    mixed = attend(lengths, same, other, rest, groups)
-
+    mixed = attend(lengths, same, own_other, other, rest, groups)
+
+    if split_columns:
+        third, own_heads = lax.optimization_barrier((third, mixed[0]))
+        mixed = [own_heads, *mixed[1:]]
     heads = [mixed[0], *exchange_chips(mixed[1:])]
     if not split_columns:
         return project(heads, [half, exchange(half, "ctx", 1)])
     third_passed = exchange_in_plane(third)
-    heads, fetched, passed, third = lax.optimization_barrier((heads, fetched, passed, third))
+    heads[3], fetched, passed = lax.optimization_barrier((heads[3], fetched, jnp.concatenate(passed, axis=0)))
+    heads[1], heads[2], third = lax.optimization_barrier((heads[1], heads[2], third))
     fetched_other, passed_other, third_other, third_passed_other = (
         exchange(array, "ctx", 1) for array in (fetched, passed, third, third_passed)
     )

time: 31.4 us -> 34.4 us (1.096)
  waiting for transfers between devices: 9.18 us -> 12.8 us
  starting transfers between devices: 15.8 us -> 15.2 us
    ppermute x14 -> x12, waiting for transfers between devices: 6.08 us -> 10.4 us  [exchange(): return lax.ppermute(array, axis, [(i, i ^ flip) for i in range(size)])]
    ppermute x2 -> x3, waiting for transfers between devices: 1.68 us -> 0.23 us  [exchange_in_plane(): lax.ppermute(array, 'ctx', [(i, i ^ (4 if i % 2 else 2)) for i in range(c...]
    ppermute x14 -> x12, starting transfers between devices: 8.4 us -> 7.01 us  [exchange(): return lax.ppermute(array, axis, [(i, i ^ flip) for i in range(size)])]
    ppermute x2 -> x3, starting transfers between devices: 1.95 us -> 2.89 us  [exchange_in_plane(): lax.ppermute(array, 'ctx', [(i, i ^ (4 if i % 2 else 2)) for i in range(c...]
    ppermute x2, waiting for transfers between devices: 1.42 us -> 2.13 us  [exchange_along(): return lax.ppermute(array, ('ctx', 'fsdp'), pairs)]
  transfers between devices with their start and end apart: 18 -> 17, of which waited for: 9 -> 11; matrix products, arithmetic and copies ran while one was open for 0% -> 0% of each run, Pallas kernels for 10% -> 9%
where the time goes in v12:
time: 34.4 us; the launch traced here: 34.3 us
  starting transfers between devices  15.2 us (44%)
  waiting for transfers between devices  12.8 us (37%)
  Pallas kernels  5.46 us (16%)
  between operations  0.75 us (2%)
    ppermute x12, waiting for transfers between devices, exchange(): return lax.ppermute(array, axis, [(i, i ^ flip) for i in range(size)])  10.4 us
    ppermute x12, starting transfers between devices, exchange(): return lax.ppermute(array, axis, [(i, i ^ flip) for i in range(size)])  7.01 us
    ppermute x2, starting transfers between devices, exchange_along(): return lax.ppermute(array, ('ctx', 'fsdp'), pairs)  5.3 us
    ppermute x3, starting transfers between devices, exchange_in_plane(): lax.ppermute(array, 'ctx', [(i, i ^ (4 if i % 2 else 2)) for i in range(c...  2.89 us
    pallas_call x1, Pallas kernels, attend(): pl.pallas_call(functools.partial(attention_kernel, groups), out_shape=[pl...  2.23 us
    ppermute x2, waiting for transfers between devices, exchange_along(): return lax.ppermute(array, ('ctx', 'fsdp'), pairs)  2.13 us
    pallas_call x1, Pallas kernels, copy_in(): pl.pallas_call(functools.partial(copy_in_kernel, by_parity), out_shape=[p...  1.24 us
    pallas_call x1, Pallas kernels, project_third(): pl.pallas_call(project_third_kernel, out_shape=jax.ShapeDtypeStruct((1, f...  1.02 us
  transfers between devices with their start and end apart: 17, of which 11 were waited for; matrix products, arithmetic and copies ran while one was open for 0% of the time, Pallas kernels for 9%

profile of v12, /device:TPU:0, one launch (start us, length us, event | category | flops | bytes accessed | tf_op | source)
XLA Modules:
  0.0 34.3 jit_solution(10142084566673683119)
XLA Ops:
  0.0 1.2 %copy_in.1 = (bf16[3,128,768]{2,1,0:T(8,128)(2,1)S(1)}, bf16[384,384]{1,0:T(8,128)(2,1)S(1)}) custom-call(bf16[1,128,768]{2,1,0:T(8,128)(2,1)} %query_ref.1, bf16[1,128,768]{2,1,0:T(8,128)(2,1)} %key_ref.1, bf16[1,128,768]{2,1,0:T(8,128)(2,1)} %value_ref.1, bf16[768,384]{1,0:T(8,128)(2,1)} %refs_4_.1), custom_call_target="tpu_custom_call" | custom-call | tf_op jit(solution)/shard_map/copy_in/pallas_call | solution.py:45
  1.2 4.1 %collective-permute-start = (bf16[384,384]{1,0:T(8,128)(2,1)S(1)}, bf16[384,384]{1,0:T(8,128)(2,1)S(1)}, u32[]{:S(2)}, u32[]{:S(2)}) collective-permute-start(bf16[384,384]{1,0:T(8,128)(2,1)S(1)} %get-tuple-element.32), channel_id=1, source_target_pairs={{0,2},{1,3},{2,0},{3,1},{4,5},{5,4},{6,7},{7,6},{8,10},{9,11},{10,... | collective-permute-start | bytes 884744 | tf_op jit(solution)/shard_map/ppermute | solution.py:292
  5.3 0.2 turn_heads.1
  5.6 1.6 %collective-permute-start.3 = (bf16[3,192,128]{2,1,0:T(8,128)(2,1)S(1)}, bf16[3,192,128]{2,1,0:T(8,128)(2,1)S(1)}, u32[]{:S(2)}, u32[]{:S(2)}) collective-permute-start(bf16[3,192,128]{2,1,0:T(8,128)(2,1)S(1)} %get-tuple-element.37), channel_id=1, source_target_pairs={{0,8},{4,12},{8,0},{12,4},{16,24},{20,28},{24,16},{28,20},{1,9},{5... | collective-permute-start | bytes 442376 | tf_op jit(solution)/shard_map/ppermute | solution.py:282
  7.2 1.5 %collective-permute-start.4 = (bf16[3,192,128]{2,1,0:T(8,128)(2,1)S(1)}, bf16[3,192,128]{2,1,0:T(8,128)(2,1)S(1)}, u32[]{:S(2)}, u32[]{:S(2)}) collective-permute-start(bf16[3,192,128]{2,1,0:T(8,128)(2,1)S(1)} %get-tuple-element.38), channel_id=1, source_target_pairs={{0,16},{4,20},{8,24},{12,28},{16,0},{20,4},{24,8},{28,12},{1,17},{... | collective-permute-start | bytes 442376 | tf_op jit(solution)/shard_map/ppermute | solution.py:282
  8.7 0.5 %collective-permute-start.5 = (bf16[3,192,128]{2,1,0:T(8,128)(2,1)S(1)}, bf16[3,192,128]{2,1,0:T(8,128)(2,1)S(1)}, u32[]{:S(2)}, u32[]{:S(2)}) collective-permute-start(bf16[3,192,128]{2,1,0:T(8,128)(2,1)S(1)} %get-tuple-element.39), channel_id=1, source_target_pairs={{0,24},{4,28},{8,16},{12,20},{16,8},{20,12},{24,0},{28,4},{1,25},{... | collective-permute-start | bytes 442376 | tf_op jit(solution)/shard_map/ppermute | solution.py:282
  9.2 0.1 collective-permute-start.1
  9.9 0.6 %collective-permute-done.1.refs_4_ = bf16[2,192,128]{2,1,0:T(8,128)(2,1)S(1)} collective-permute-done((bf16[2,192,128]{2,1,0:T(8,128)(2,1)S(1)}, bf16[2,192,128]{2,1,0:T(8,128)(2,1)S(1)}, u32[]{:S(2)}, u32[]{:S(2)}) %collective-permute-start.1) | collective-permute-done | bytes 98336 | tf_op jit(solution)/shard_map/ppermute | solution.py:282
  10.5 1.4 %collective-permute-done.refs_5_ = bf16[384,384]{1,0:T(8,128)(2,1)S(1)} collective-permute-done((bf16[384,384]{1,0:T(8,128)(2,1)S(1)}, bf16[384,384]{1,0:T(8,128)(2,1)S(1)}, u32[]{:S(2)}, u32[]{:S(2)}) %collective-permute-start) | collective-permute-done | bytes 294944 | tf_op jit(solution)/shard_map/ppermute | solution.py:292
  12.0 0.4 %collective-permute-done.3.refs_0_.refs_1_ = bf16[3,192,128]{2,1,0:T(8,128)(2,1)S(1)} collective-permute-done((bf16[3,192,128]{2,1,0:T(8,128)(2,1)S(1)}, bf16[3,192,128]{2,1,0:T(8,128)(2,1)S(1)}, u32[]{:S(2)}, u32[]{:S(2)}) %collective-permute-start.3) | collective-permute-done | bytes 147488 | tf_op jit(solution)/shard_map/ppermute | solution.py:282
  12.4 2.8 %collective-permute-done.4.refs_1_.refs_2_ = bf16[3,192,128]{2,1,0:T(8,128)(2,1)S(1)} collective-permute-done((bf16[3,192,128]{2,1,0:T(8,128)(2,1)S(1)}, bf16[3,192,128]{2,1,0:T(8,128)(2,1)S(1)}, u32[]{:S(2)}, u32[]{:S(2)}) %collective-permute-start.4) | collective-permute-done | bytes 147488 | tf_op jit(solution)/shard_map/ppermute | solution.py:282
  15.2 0.0 collective-permute-done.5.refs_2_.refs_3_
  15.2 0.1 collective-permute-start.6
  15.3 1.2 %collective-permute-start.2 = (bf16[208,384]{1,0:T(8,128)(2,1)S(1)}, bf16[208,384]{1,0:T(8,128)(2,1)S(1)}, u32[]{:S(2)}, u32[]{:S(2)}) collective-permute-start(bf16[208,384]{1,0:T(8,128)(2,1)S(1)} %constant_dynamic-slice_fusion), channel_id=1, source_target_pairs={{0,1},{1,0},{2,3},{3,2},{4,6},{5,7},{6,4},{7,5},{8,9},{9,8},{10,11... | collective-permute-start | bytes 479240 | tf_op jit(solution)/shard_map/ppermute | solution.py:292
  16.5 0.6 %collective-permute-start.10 = (bf16[192,384]{1,0:T(8,128)(2,1)S(1)}, bf16[192,384]{1,0:T(8,128)(2,1)S(1)}, u32[]{:S(2)}, u32[]{:S(2)}) collective-permute-start(bf16[192,384]{1,0:T(8,128)(2,1)S(1)} %get-tuple-element.59), channel_id=1, source_target_pairs={{0,8},{4,20},{8,0},{12,28},{16,24},{20,4},{24,16},{28,12},{1,9},{5... | collective-permute-start | bytes 442376 | tf_op jit(solution)/shard_map/ppermute | solution.py:288
  17.1 1.5 %collective-permute-start.11 = (bf16[192,384]{1,0:T(8,128)(2,1)S(1)}, bf16[192,384]{1,0:T(8,128)(2,1)S(1)}, u32[]{:S(2)}, u32[]{:S(2)}) collective-permute-start(bf16[192,384]{1,0:T(8,128)(2,1)S(1)} %get-tuple-element.60), channel_id=1, source_target_pairs={{0,8},{4,20},{8,0},{12,28},{16,24},{20,4},{24,16},{28,12},{1,9},{5... | collective-permute-start | bytes 442376 | tf_op jit(solution)/shard_map/ppermute | solution.py:288
  18.6 0.0 collective-permute-done.6.refs_5_
  18.6 2.2 %attend_two_heads.1 = (bf16[192,128]{1,0:T(8,128)(2,1)S(1)}, bf16[192,128]{1,0:T(8,128)(2,1)S(1)}, bf16[192,128]{1,0:T(8,128)(2,1)S(1)}, bf16[192,128]{1,0:T(8,128)(2,1)S(1)}) custom-call(s32[8,128]{1,0:T(8,128)S(1)} %broadcast_in_dim.2.lengths_ref, bf16[3,192,128]{2,1,0:T(8,128)(2,1)S(1)} %get-tuple-element.34.refs_0_, ...), custom_call_target="tpu_custom_call" | custom-call | flops 402653184 | tf_op jit(solution)/shard_map/attend_two_heads/pallas_call | solution.py:151
  20.9 0.0 copy-start
  20.9 0.7 %collective-permute-start.9 = (bf16[192,128]{1,0:T(8,128)(2,1)S(1)}, bf16[192,128]{1,0:T(8,128)(2,1)S(1)}, u32[]{:S(2)}, u32[]{:S(2)}) collective-permute-start(bf16[192,128]{1,0:T(8,128)(2,1)S(1)} %get-tuple-element.52), channel_id=1, source_target_pairs={{0,24},{4,28},{8,16},{12,20},{16,8},{20,12},{24,0},{28,4},{1,25},{... | collective-permute-start | bytes 147464 | tf_op jit(solution)/shard_map/ppermute | solution.py:282
  21.6 0.7 %collective-permute-done.2.refs_0_ = bf16[208,384]{1,0:T(8,128)(2,1)S(1)} collective-permute-done((bf16[208,384]{1,0:T(8,128)(2,1)S(1)}, bf16[208,384]{1,0:T(8,128)(2,1)S(1)}, u32[]{:S(2)}, u32[]{:S(2)}) %collective-permute-start.2) | collective-permute-done | bytes 159776 | tf_op jit(solution)/shard_map/ppermute | solution.py:292
  22.3 0.8 %collective-permute-start.14 = (bf16[208,384]{1,0:T(8,128)(2,1)S(1)}, bf16[208,384]{1,0:T(8,128)(2,1)S(1)}, u32[]{:S(2)}, u32[]{:S(2)}) collective-permute-start(bf16[208,384]{1,0:T(8,128)(2,1)S(1)} %collective-permute-done.2.refs_0_), channel_id=1, source_target_pairs={{0,8},{4,20},{8,0},{12,28},{16,24},{20,4},{24,16},{28,12},{1,9},{5... | collective-permute-start | bytes 479240 | tf_op jit(solution)/shard_map/ppermute | solution.py:288
  23.1 0.0 collective-permute-done.10
  23.1 0.2 collective-permute-done.11
  23.4 2.6 %collective-permute-done.9.refs_3_ = bf16[192,128]{1,0:T(8,128)(2,1)S(1)} collective-permute-done((bf16[192,128]{1,0:T(8,128)(2,1)S(1)}, bf16[192,128]{1,0:T(8,128)(2,1)S(1)}, u32[]{:S(2)}, u32[]{:S(2)}) %collective-permute-start.9) | collective-permute-done | bytes 49184 | tf_op jit(solution)/shard_map/ppermute | solution.py:282
  26.0 0.0 collective-permute-start.12
  26.0 0.5 %collective-permute-start.13 = (bf16[384,384]{1,0:T(8,128)(2,1)S(1)}, bf16[384,384]{1,0:T(8,128)(2,1)S(1)}, u32[]{:S(2)}, u32[]{:S(2)}) collective-permute-start(bf16[384,384]{1,0:T(8,128)(2,1)S(1)} %pad_maximum_fusion.refs_6_), channel_id=1, source_target_pairs={{0,4},{4,0},{8,12},{12,8},{16,20},{20,16},{24,28},{28,24},{1,5},{5... | collective-permute-start | bytes 884744 | tf_op jit(solution)/shard_map/ppermute | solution.py:282
  26.5 1.0 %collective-permute-start.7 = (bf16[192,128]{1,0:T(8,128)(2,1)S(1)}, bf16[192,128]{1,0:T(8,128)(2,1)S(1)}, u32[]{:S(2)}, u32[]{:S(2)}) collective-permute-start(bf16[192,128]{1,0:T(8,128)(2,1)S(1)} %get-tuple-element.47), channel_id=1, source_target_pairs={{0,8},{4,12},{8,0},{12,4},{16,24},{20,28},{24,16},{28,20},{1,9},{5... | collective-permute-start | bytes 147464 | tf_op jit(solution)/shard_map/ppermute | solution.py:282
  27.5 0.6 %collective-permute-start.8 = (bf16[192,128]{1,0:T(8,128)(2,1)S(1)}, bf16[192,128]{1,0:T(8,128)(2,1)S(1)}, u32[]{:S(2)}, u32[]{:S(2)}) collective-permute-start(bf16[192,128]{1,0:T(8,128)(2,1)S(1)} %get-tuple-element.48), channel_id=1, source_target_pairs={{0,16},{4,20},{8,24},{12,28},{16,0},{20,4},{24,8},{28,12},{1,17},{... | collective-permute-start | bytes 147464 | tf_op jit(solution)/shard_map/ppermute | solution.py:282
  28.1 2.5 %collective-permute-done.7.refs_1_ = bf16[192,128]{1,0:T(8,128)(2,1)S(1)} collective-permute-done((bf16[192,128]{1,0:T(8,128)(2,1)S(1)}, bf16[192,128]{1,0:T(8,128)(2,1)S(1)}, u32[]{:S(2)}, u32[]{:S(2)}) %collective-permute-start.7) | collective-permute-done | bytes 49184 | tf_op jit(solution)/shard_map/ppermute | solution.py:282
  30.6 1.0 %collective-permute-done.8.refs_2_ = bf16[192,128]{1,0:T(8,128)(2,1)S(1)} collective-permute-done((bf16[192,128]{1,0:T(8,128)(2,1)S(1)}, bf16[192,128]{1,0:T(8,128)(2,1)S(1)}, u32[]{:S(2)}, u32[]{:S(2)}) %collective-permute-start.8) | collective-permute-done | bytes 49184 | tf_op jit(solution)/shard_map/ppermute | solution.py:282
  31.6 0.0 collective-permute-start.15
  31.6 0.0 collective-permute-done.14.refs_1_
  31.6 0.5 %collective-permute-start.16 = (bf16[208,384]{1,0:T(8,128)(2,1)S(1)}, bf16[208,384]{1,0:T(8,128)(2,1)S(1)}, u32[]{:S(2)}, u32[]{:S(2)}) collective-permute-start(bf16[208,384]{1,0:T(8,128)(2,1)S(1)} %collective-permute-done.14.refs_1_), channel_id=1, source_target_pairs={{0,4},{4,0},{8,12},{12,8},{16,20},{20,16},{24,28},{28,24},{1,5},{5... | collective-permute-start | bytes 479240 | tf_op jit(solution)/shard_map/ppermute | solution.py:282
  32.1 0.0 collective-permute-done.12.refs_7_
  32.1 0.0 collective-permute-done.13.refs_8_
  32.1 0.0 copy-done
  32.2 0.7 %project_near_shards.1 = (bf16[3,128,384]{2,1,0:T(8,128)(2,1)S(1)}, bf16[128,768]{1,0:T(8,128)(2,1)S(1)}) custom-call(bf16[192,128]{1,0:T(8,128)(2,1)S(1)} %get-tuple-element.46.refs_0_, bf16[192,128]{1,0:T(8,128)(2,1)S(1)} %collective-permute-done.7.refs_1_, bf16[192,128]{1,0:T(8,128)(2,1)S(1)} %collective-permute-done.8.refs_2_, ...), custom_call_target="tpu_custom_call" | custom-call | tf_op jit(solution)/shard_map/project_near_shards/pallas_call | solution.py:245
  32.9 0.2 collective-permute-done.15.refs_2_
  33.0 0.2 collective-permute-done.16.refs_3_
  33.2 1.0 %project_third_shard.1 = bf16[1,128,1536]{2,1,0:T(8,128)(2,1)} custom-call(bf16[3,128,384]{2,1,0:T(8,128)(2,1)S(1)} %get-tuple-element.56.blocks_ref, bf16[128,768]{1,0:T(8,128)(2,1)S(1)} %get-tuple-element.57.attention_ref, bf16[208,384]{1,0:T(8,128)(2,1)S(1)} %collective-permute-done.2.refs_0_, bf16[208,384]{1,0:T(8,128)(2,1)S(1)} %collective-permute-done.14.refs_1_, ...), custom_call_target="tpu_custom_call" | custom-call | flops 75497472 | bytes 589824 | tf_op jit(solution)/shard_map/project_third_shard/pallas_call | solution.py:263
  (6 shorter events, 0.1 us)
Async XLA Ops:
  1.2 10.7 %collective-permute-start = (bf16[384,384]{1,0:T(8,128)(2,1)S(1)}, bf16[384,384]{1,0:T(8,128)(2,1)S(1)}, u32[]{:S(2)}, u32[]{:S(2)}) collective-permute-start(bf16[384,384]{1,0:T(8,128)(2,1)S(1)} %get-tuple-element.32), channel_id=1, source_target_pairs={{0,2},{1,3},{2,0},{3,1},{4,5},{5,4},{6,7},{7,6},{8,10},{9,11},{10,... | collective-permute-start | bytes 884744 | tf_op jit(solution)/shard_map/ppermute | solution.py:292
  5.6 6.8 %collective-permute-start.3 = (bf16[3,192,128]{2,1,0:T(8,128)(2,1)S(1)}, bf16[3,192,128]{2,1,0:T(8,128)(2,1)S(1)}, u32[]{:S(2)}, u32[]{:S(2)}) collective-permute-start(bf16[3,192,128]{2,1,0:T(8,128)(2,1)S(1)} %get-tuple-element.37), channel_id=1, source_target_pairs={{0,8},{4,12},{8,0},{12,4},{16,24},{20,28},{24,16},{28,20},{1,9},{5... | collective-permute-start | bytes 442376 | tf_op jit(solution)/shard_map/ppermute | solution.py:282
  7.2 8.0 %collective-permute-start.4 = (bf16[3,192,128]{2,1,0:T(8,128)(2,1)S(1)}, bf16[3,192,128]{2,1,0:T(8,128)(2,1)S(1)}, u32[]{:S(2)}, u32[]{:S(2)}) collective-permute-start(bf16[3,192,128]{2,1,0:T(8,128)(2,1)S(1)} %get-tuple-element.38), channel_id=1, source_target_pairs={{0,16},{4,20},{8,24},{12,28},{16,0},{20,4},{24,8},{28,12},{1,17},{... | collective-permute-start | bytes 442376 | tf_op jit(solution)/shard_map/ppermute | solution.py:282
  8.7 6.5 %collective-permute-start.5 = (bf16[3,192,128]{2,1,0:T(8,128)(2,1)S(1)}, bf16[3,192,128]{2,1,0:T(8,128)(2,1)S(1)}, u32[]{:S(2)}, u32[]{:S(2)}) collective-permute-start(bf16[3,192,128]{2,1,0:T(8,128)(2,1)S(1)} %get-tuple-element.39), channel_id=1, source_target_pairs={{0,24},{4,28},{8,16},{12,20},{16,8},{20,12},{24,0},{28,4},{1,25},{... | collective-permute-start | bytes 442376 | tf_op jit(solution)/shard_map/ppermute | solution.py:282
  9.2 1.4 %collective-permute-start.1 = (bf16[2,192,128]{2,1,0:T(8,128)(2,1)S(1)}, bf16[2,192,128]{2,1,0:T(8,128)(2,1)S(1)}, u32[]{:S(2)}, u32[]{:S(2)}) collective-permute-start(bf16[2,192,128]{2,1,0:T(8,128)(2,1)S(1)} %slice.9), channel_id=1, source_target_pairs={{0,4},{4,0},{8,12},{12,8},{16,20},{20,16},{24,28},{28,24},{1,5},{5... | collective-permute-start | bytes 294920 | tf_op jit(solution)/shard_map/ppermute | solution.py:282
  15.2 3.4 %collective-permute-start.6 = (bf16[3,2,192,128]{3,2,1,0:T(8,128)(2,1)S(1)}, bf16[3,2,192,128]{3,2,1,0:T(8,128)(2,1)S(1)}, u32[]{:S(2)}, u32[]{:S(2)}) collective-permute-start(bf16[3,2,192,128]{3,2,1,0:T(8,128)(2,1)S(1)} %stack_keys_and_values.1), channel_id=1, source_target_pairs={{0,4},{4,0},{8,12},{12,8},{16,20},{20,16},{24,28},{28,24},{1,5},{5... | collective-permute-start | bytes 884744 | tf_op jit(solution)/shard_map/ppermute | solution.py:282
  15.3 7.0 %collective-permute-start.2 = (bf16[208,384]{1,0:T(8,128)(2,1)S(1)}, bf16[208,384]{1,0:T(8,128)(2,1)S(1)}, u32[]{:S(2)}, u32[]{:S(2)}) collective-permute-start(bf16[208,384]{1,0:T(8,128)(2,1)S(1)} %constant_dynamic-slice_fusion), channel_id=1, source_target_pairs={{0,1},{1,0},{2,3},{3,2},{4,6},{5,7},{6,4},{7,5},{8,9},{9,8},{10,11... | collective-permute-start | bytes 479240 | tf_op jit(solution)/shard_map/ppermute | solution.py:292
  16.5 6.6 %collective-permute-start.10 = (bf16[192,384]{1,0:T(8,128)(2,1)S(1)}, bf16[192,384]{1,0:T(8,128)(2,1)S(1)}, u32[]{:S(2)}, u32[]{:S(2)}) collective-permute-start(bf16[192,384]{1,0:T(8,128)(2,1)S(1)} %get-tuple-element.59), channel_id=1, source_target_pairs={{0,8},{4,20},{8,0},{12,28},{16,24},{20,4},{24,16},{28,12},{1,9},{5... | collective-permute-start | bytes 442376 | tf_op jit(solution)/shard_map/ppermute | solution.py:288
  17.1 6.2 %collective-permute-start.11 = (bf16[192,384]{1,0:T(8,128)(2,1)S(1)}, bf16[192,384]{1,0:T(8,128)(2,1)S(1)}, u32[]{:S(2)}, u32[]{:S(2)}) collective-permute-start(bf16[192,384]{1,0:T(8,128)(2,1)S(1)} %get-tuple-element.60), channel_id=1, source_target_pairs={{0,8},{4,20},{8,0},{12,28},{16,24},{20,4},{24,16},{28,12},{1,9},{5... | collective-permute-start | bytes 442376 | tf_op jit(solution)/shard_map/ppermute | solution.py:288
  20.9 11.3 %copy-start = (bf16[768,384]{1,0:T(8,128)(2,1)S(1)}, bf16[768,384]{1,0:T(8,128)(2,1)}, u32[]{:S(2)}) copy-start(bf16[768,384]{1,0:T(8,128)(2,1)} %refs_4_.1) | copy-start | bytes 1769476
  20.9 5.1 %collective-permute-start.9 = (bf16[192,128]{1,0:T(8,128)(2,1)S(1)}, bf16[192,128]{1,0:T(8,128)(2,1)S(1)}, u32[]{:S(2)}, u32[]{:S(2)}) collective-permute-start(bf16[192,128]{1,0:T(8,128)(2,1)S(1)} %get-tuple-element.52), channel_id=1, source_target_pairs={{0,24},{4,28},{8,16},{12,20},{16,8},{20,12},{24,0},{28,4},{1,25},{... | collective-permute-start | bytes 147464 | tf_op jit(solution)/shard_map/ppermute | solution.py:282
  22.3 9.3 %collective-permute-start.14 = (bf16[208,384]{1,0:T(8,128)(2,1)S(1)}, bf16[208,384]{1,0:T(8,128)(2,1)S(1)}, u32[]{:S(2)}, u32[]{:S(2)}) collective-permute-start(bf16[208,384]{1,0:T(8,128)(2,1)S(1)} %collective-permute-done.2.refs_0_), channel_id=1, source_target_pairs={{0,8},{4,20},{8,0},{12,28},{16,24},{20,4},{24,16},{28,12},{1,9},{5... | collective-permute-start | bytes 479240 | tf_op jit(solution)/shard_map/ppermute | solution.py:288
  26.0 6.2 %collective-permute-start.12 = (bf16[384,384]{1,0:T(8,128)(2,1)S(1)}, bf16[384,384]{1,0:T(8,128)(2,1)S(1)}, u32[]{:S(2)}, u32[]{:S(2)}) collective-permute-start(bf16[384,384]{1,0:T(8,128)(2,1)S(1)} %collective-permute-done.refs_5_), channel_id=1, source_target_pairs={{0,4},{4,0},{8,12},{12,8},{16,20},{20,16},{24,28},{28,24},{1,5},{5... | collective-permute-start | bytes 884744 | tf_op jit(solution)/shard_map/ppermute | solution.py:282
  26.0 6.2 %collective-permute-start.13 = (bf16[384,384]{1,0:T(8,128)(2,1)S(1)}, bf16[384,384]{1,0:T(8,128)(2,1)S(1)}, u32[]{:S(2)}, u32[]{:S(2)}) collective-permute-start(bf16[384,384]{1,0:T(8,128)(2,1)S(1)} %pad_maximum_fusion.refs_6_), channel_id=1, source_target_pairs={{0,4},{4,0},{8,12},{12,8},{16,20},{20,16},{24,28},{28,24},{1,5},{5... | collective-permute-start | bytes 884744 | tf_op jit(solution)/shard_map/ppermute | solution.py:282
  26.5 4.1 %collective-permute-start.7 = (bf16[192,128]{1,0:T(8,128)(2,1)S(1)}, bf16[192,128]{1,0:T(8,128)(2,1)S(1)}, u32[]{:S(2)}, u32[]{:S(2)}) collective-permute-start(bf16[192,128]{1,0:T(8,128)(2,1)S(1)} %get-tuple-element.47), channel_id=1, source_target_pairs={{0,8},{4,12},{8,0},{12,4},{16,24},{20,28},{24,16},{28,20},{1,9},{5... | collective-permute-start | bytes 147464 | tf_op jit(solution)/shard_map/ppermute | solution.py:282
  27.5 4.1 %collective-permute-start.8 = (bf16[192,128]{1,0:T(8,128)(2,1)S(1)}, bf16[192,128]{1,0:T(8,128)(2,1)S(1)}, u32[]{:S(2)}, u32[]{:S(2)}) collective-permute-start(bf16[192,128]{1,0:T(8,128)(2,1)S(1)} %get-tuple-element.48), channel_id=1, source_target_pairs={{0,16},{4,20},{8,24},{12,28},{16,0},{20,4},{24,8},{28,12},{1,17},{... | collective-permute-start | bytes 147464 | tf_op jit(solution)/shard_map/ppermute | solution.py:282
  31.6 1.4 %collective-permute-start.15 = (bf16[208,384]{1,0:T(8,128)(2,1)S(1)}, bf16[208,384]{1,0:T(8,128)(2,1)S(1)}, u32[]{:S(2)}, u32[]{:S(2)}) collective-permute-start(bf16[208,384]{1,0:T(8,128)(2,1)S(1)} %collective-permute-done.2.refs_0_), channel_id=1, source_target_pairs={{0,4},{4,0},{8,12},{12,8},{16,20},{20,16},{24,28},{28,24},{1,5},{5... | collective-permute-start | bytes 479240 | tf_op jit(solution)/shard_map/ppermute | solution.py:282
  31.6 1.6 %collective-permute-start.16 = (bf16[208,384]{1,0:T(8,128)(2,1)S(1)}, bf16[208,384]{1,0:T(8,128)(2,1)S(1)}, u32[]{:S(2)}, u32[]{:S(2)}) collective-permute-start(bf16[208,384]{1,0:T(8,128)(2,1)S(1)} %collective-permute-done.14.refs_1_), channel_id=1, source_target_pairs={{0,4},{4,0},{8,12},{12,8},{16,20},{20,16},{24,28},{28,24},{1,5},{5... | collective-permute-start | bytes 479240 | tf_op jit(solution)/shard_map/ppermute | solution.py:282

commit v13 on v12

--- a/solution.py
+++ b/solution.py
@@ -99,11 +99,12 @@
     ones = jnp.where(lax.broadcasted_iota(jnp.int32, (pad, block), 0) == 0, 1.0, 0.0).astype(keys.dtype)
     at_feature = lax.broadcasted_iota(jnp.int32, (pad, block), 0)
     at_frame = lax.broadcasted_iota(jnp.int32, (pad, block), 1)
-    for at in range(groups * HEADS):
-        here = slice(at * block, (at + 1) * block)
-        frame = (at // HEADS * HEADS + (place ^ (at % HEADS))) * block + at_frame
-        bias = jnp.where((at_feature == 0) & (frame >= lengths_ref[:1, :]), -1e30, 0.0).astype(keys.dtype)
-        for head in range(2):
+
+    def prepare(head):
+        for at in range(groups * HEADS):
+            here = slice(at * block, (at + 1) * block)
+            frame = (at // HEADS * HEADS + (place ^ (at % HEADS))) * block + at_frame
+            bias = jnp.where((at_feature == 0) & (frame >= lengths_ref[:1, :]), -1e30, 0.0).astype(keys.dtype)
             keys[head, here, :] = jnp.concatenate([piece(at, head, 1), bias], axis=0).T
             values[head, :, here] = jnp.concatenate([piece(at, head, 2), ones], axis=0)
 
@@ -113,7 +114,9 @@
         return jnp.dot(keys[head], jnp.concatenate(query, axis=1), preferred_element_type=jnp.float32)
 
     chunks = [(head, flips) for head in range(2) for flips in (FLIPS[:2], FLIPS[2:])]
+    prepare(0)
     later = score(*chunks[0])
+    prepare(1)
     for at, (head, flips) in enumerate(chunks):
         scores = later
         if at + 1 < len(chunks):
@@ -155,7 +158,7 @@
         out_specs=[WHOLE] * len(FLIPS),
         scratch_shapes=[pltpu.VMEM((2, keys, padded), jnp.bfloat16), pltpu.VMEM((2, padded, keys), jnp.bfloat16)],
         compiler_params=params(32),
-        cost_estimate=pl.CostEstimate(flops=2 * keys * keys * features, bytes_accessed=0, transcendentals=0),
+        cost_estimate=pl.CostEstimate(flops=8 * keys * keys * features, bytes_accessed=0, transcendentals=0),
         name="attend_two_heads",
     )(lengths, *same, own_other, other, *rest)
 
@@ -252,7 +255,7 @@
             pltpu.VMEM((2, features, columns), jnp.bfloat16),
         ],
         compiler_params=params(24),
-        cost_estimate=pl.CostEstimate(flops=0, bytes_accessed=0, transcendentals=0),
+        cost_estimate=projection_cost(frames, features, 3 * columns),
         name="project_near_shards",
     )(*heads, own, *pieces)
 
@@ -305,7 +308,7 @@
     own_other = exchange(own[1:], "ctx", 1)
     if split_columns:
         fetched, own_other, lengths = lax.optimization_barrier((fetched, own_other, lengths))
-        passed = [exchange_in_plane(rows) for rows in (fetched[: half.shape[0] // 2], fetched[half.shape[0] // 2 :])]
+        passed = exchange_in_plane(fetched)
         depth = half.shape[0]
         part = depth // 2 + 16
         third = lax.dynamic_slice_in_dim(fetched, core * (depth - part), part, 0)
@@ -324,15 +327,12 @@
         rest = lax.all_gather(jnp.stack(pairs), "ctx", axis=0, axis_index_groups=across, tiled=True)
     mixed = attend(lengths, same, own_other, other, rest, groups)
 
-    if split_columns:
-        third, own_heads = lax.optimization_barrier((third, mixed[0]))
-        mixed = [own_heads, *mixed[1:]]
     heads = [mixed[0], *exchange_chips(mixed[1:])]
     if not split_columns:
         return project(heads, [half, exchange(half, "ctx", 1)])
     third_passed = exchange_in_plane(third)
-    heads[3], fetched, passed = lax.optimization_barrier((heads[3], fetched, jnp.concatenate(passed, axis=0)))
-    heads[1], heads[2], third = lax.optimization_barrier((heads[1], heads[2], third))
+    heads[3], fetched = lax.optimization_barrier((heads[3], fetched))
+    heads[1], heads[2], passed, third = lax.optimization_barrier((heads[1], heads[2], passed, third))
     fetched_other, passed_other, third_other, third_passed_other = (
         exchange(array, "ctx", 1) for array in (fetched, passed, third, third_passed)
     )

time: 34.4 us -> 31 us (0.901)
  waiting for transfers between devices: 12.8 us -> 9.18 us
    ppermute x12, waiting for transfers between devices: 10.4 us -> 5.55 us  [exchange(): return lax.ppermute(array, axis, [(i, i ^ flip) for i in range(size)])]
    ppermute x3 -> x2, waiting for transfers between devices: 0.23 us -> 2.2 us  [exchange_in_plane(): lax.ppermute(array, 'ctx', [(i, i ^ (4 if i % 2 else 2)) for i in range(c...]
    ppermute x12, starting transfers between devices: 7.01 us -> 8.03 us  [exchange(): return lax.ppermute(array, axis, [(i, i ^ flip) for i in range(size)])]
    ppermute x3 -> x2, starting transfers between devices: 2.89 us -> 1.96 us  [exchange_in_plane(): lax.ppermute(array, 'ctx', [(i, i ^ (4 if i % 2 else 2)) for i in range(c...]
    ppermute x2, waiting for transfers between devices: 2.13 us -> 1.42 us  [exchange_along(): return lax.ppermute(array, ('ctx', 'fsdp'), pairs)]
  transfers between devices with their start and end apart: 17 -> 16, of which waited for: 11 -> 10; matrix products, arithmetic and copies ran while one was open for 0% -> 0% of each run, Pallas kernels for 9% -> 10%
where the time goes in v13:
time: 31 us; the launch traced here: 30.8 us
  starting transfers between devices  15.4 us (50%)
  waiting for transfers between devices  9.18 us (30%)
  Pallas kernels  5.45 us (18%)
  between operations  0.74 us (2%)
    ppermute x12, starting transfers between devices, exchange(): return lax.ppermute(array, axis, [(i, i ^ flip) for i in range(size)])  8.03 us
    ppermute x12, waiting for transfers between devices, exchange(): return lax.ppermute(array, axis, [(i, i ^ flip) for i in range(size)])  5.55 us
    ppermute x2, starting transfers between devices, exchange_along(): return lax.ppermute(array, ('ctx', 'fsdp'), pairs)  5.43 us
    pallas_call x1, Pallas kernels, attend(): pl.pallas_call(functools.partial(attention_kernel, groups), out_shape=[pl...  2.2 us
    ppermute x2, waiting for transfers between devices, exchange_in_plane(): lax.ppermute(array, 'ctx', [(i, i ^ (4 if i % 2 else 2)) for i in range(c...  2.2 us
    ppermute x2, starting transfers between devices, exchange_in_plane(): lax.ppermute(array, 'ctx', [(i, i ^ (4 if i % 2 else 2)) for i in range(c...  1.96 us
    ppermute x2, waiting for transfers between devices, exchange_along(): return lax.ppermute(array, ('ctx', 'fsdp'), pairs)  1.42 us
    pallas_call x1, Pallas kernels, copy_in(): pl.pallas_call(functools.partial(copy_in_kernel, by_parity), out_shape=[p...  1.24 us
  transfers between devices with their start and end apart: 16, of which 10 were waited for; matrix products, arithmetic and copies ran while one was open for 0% of the time, Pallas kernels for 10%

profile of v13, /device:TPU:0, one launch (start us, length us, event | category | flops | bytes accessed | tf_op | source)
XLA Modules:
  0.0 30.8 jit_solution(8536703182222332876)
XLA Ops:
  0.0 1.2 %copy_in.1 = (bf16[3,128,768]{2,1,0:T(8,128)(2,1)S(1)}, bf16[384,384]{1,0:T(8,128)(2,1)S(1)}) custom-call(bf16[1,128,768]{2,1,0:T(8,128)(2,1)} %query_ref.1, bf16[1,128,768]{2,1,0:T(8,128)(2,1)} %key_ref.1, bf16[1,128,768]{2,1,0:T(8,128)(2,1)} %value_ref.1, bf16[768,384]{1,0:T(8,128)(2,1)} %refs_4_.1), custom_call_target="tpu_custom_call" | custom-call | tf_op jit(solution)/shard_map/copy_in/pallas_call | solution.py:45
  1.2 4.1 %collective-permute-start = (bf16[384,384]{1,0:T(8,128)(2,1)S(1)}, bf16[384,384]{1,0:T(8,128)(2,1)S(1)}, u32[]{:S(2)}, u32[]{:S(2)}) collective-permute-start(bf16[384,384]{1,0:T(8,128)(2,1)S(1)} %get-tuple-element.30), channel_id=1, source_target_pairs={{0,2},{1,3},{2,0},{3,1},{4,5},{5,4},{6,7},{7,6},{8,10},{9,11},{10,... | collective-permute-start | bytes 884744 | tf_op jit(solution)/shard_map/ppermute | solution.py:295
  5.3 0.2 turn_heads.1
  5.6 1.6 %collective-permute-start.2 = (bf16[3,192,128]{2,1,0:T(8,128)(2,1)S(1)}, bf16[3,192,128]{2,1,0:T(8,128)(2,1)S(1)}, u32[]{:S(2)}, u32[]{:S(2)}) collective-permute-start(bf16[3,192,128]{2,1,0:T(8,128)(2,1)S(1)} %get-tuple-element.34), channel_id=1, source_target_pairs={{0,8},{4,12},{8,0},{12,4},{16,24},{20,28},{24,16},{28,20},{1,9},{5... | collective-permute-start | bytes 442376 | tf_op jit(solution)/shard_map/ppermute | solution.py:285
  7.2 1.5 %collective-permute-start.3 = (bf16[3,192,128]{2,1,0:T(8,128)(2,1)S(1)}, bf16[3,192,128]{2,1,0:T(8,128)(2,1)S(1)}, u32[]{:S(2)}, u32[]{:S(2)}) collective-permute-start(bf16[3,192,128]{2,1,0:T(8,128)(2,1)S(1)} %get-tuple-element.35), channel_id=1, source_target_pairs={{0,16},{4,20},{8,24},{12,28},{16,0},{20,4},{24,8},{28,12},{1,17},{... | collective-permute-start | bytes 442376 | tf_op jit(solution)/shard_map/ppermute | solution.py:285
  8.7 0.5 %collective-permute-start.4 = (bf16[3,192,128]{2,1,0:T(8,128)(2,1)S(1)}, bf16[3,192,128]{2,1,0:T(8,128)(2,1)S(1)}, u32[]{:S(2)}, u32[]{:S(2)}) collective-permute-start(bf16[3,192,128]{2,1,0:T(8,128)(2,1)S(1)} %get-tuple-element.36), channel_id=1, source_target_pairs={{0,24},{4,28},{8,16},{12,20},{16,8},{20,12},{24,0},{28,4},{1,25},{... | collective-permute-start | bytes 442376 | tf_op jit(solution)/shard_map/ppermute | solution.py:285
  9.2 0.1 collective-permute-start.1
  9.9 0.6 %collective-permute-done.1.refs_4_ = bf16[2,192,128]{2,1,0:T(8,128)(2,1)S(1)} collective-permute-done((bf16[2,192,128]{2,1,0:T(8,128)(2,1)S(1)}, bf16[2,192,128]{2,1,0:T(8,128)(2,1)S(1)}, u32[]{:S(2)}, u32[]{:S(2)}) %collective-permute-start.1) | collective-permute-done | bytes 98336 | tf_op jit(solution)/shard_map/ppermute | solution.py:285
  10.5 1.4 %collective-permute-done.refs_5_ = bf16[384,384]{1,0:T(8,128)(2,1)S(1)} collective-permute-done((bf16[384,384]{1,0:T(8,128)(2,1)S(1)}, bf16[384,384]{1,0:T(8,128)(2,1)S(1)}, u32[]{:S(2)}, u32[]{:S(2)}) %collective-permute-start) | collective-permute-done | bytes 294944 | tf_op jit(solution)/shard_map/ppermute | solution.py:295
  12.0 0.4 %collective-permute-done.2.refs_0_.refs_1_ = bf16[3,192,128]{2,1,0:T(8,128)(2,1)S(1)} collective-permute-done((bf16[3,192,128]{2,1,0:T(8,128)(2,1)S(1)}, bf16[3,192,128]{2,1,0:T(8,128)(2,1)S(1)}, u32[]{:S(2)}, u32[]{:S(2)}) %collective-permute-start.2) | collective-permute-done | bytes 147488 | tf_op jit(solution)/shard_map/ppermute | solution.py:285
  12.4 2.8 %collective-permute-done.3.refs_1_.refs_2_ = bf16[3,192,128]{2,1,0:T(8,128)(2,1)S(1)} collective-permute-done((bf16[3,192,128]{2,1,0:T(8,128)(2,1)S(1)}, bf16[3,192,128]{2,1,0:T(8,128)(2,1)S(1)}, u32[]{:S(2)}, u32[]{:S(2)}) %collective-permute-start.3) | collective-permute-done | bytes 147488 | tf_op jit(solution)/shard_map/ppermute | solution.py:285
  15.2 0.0 collective-permute-done.4.refs_2_.refs_3_
  15.2 0.1 collective-permute-start.5
  15.3 0.5 %collective-permute-start.8 = (bf16[384,384]{1,0:T(8,128)(2,1)S(1)}, bf16[384,384]{1,0:T(8,128)(2,1)S(1)}, u32[]{:S(2)}, u32[]{:S(2)}) collective-permute-start(bf16[384,384]{1,0:T(8,128)(2,1)S(1)} %collective-permute-done.refs_5_), channel_id=1, source_target_pairs={{0,8},{4,20},{8,0},{12,28},{16,24},{20,4},{24,16},{28,12},{1,9},{5... | collective-permute-start | bytes 884744 | tf_op jit(solution)/shard_map/ppermute | solution.py:291
  15.8 0.0 copy-start
  15.8 1.3 %collective-permute-start.9 = (bf16[208,384]{1,0:T(8,128)(2,1)S(1)}, bf16[208,384]{1,0:T(8,128)(2,1)S(1)}, u32[]{:S(2)}, u32[]{:S(2)}) collective-permute-start(bf16[208,384]{1,0:T(8,128)(2,1)S(1)} %constant_dynamic-slice_fusion), channel_id=1, source_target_pairs={{0,1},{1,0},{2,3},{3,2},{4,6},{5,7},{6,4},{7,5},{8,9},{9,8},{10,11... | collective-permute-start | bytes 479240 | tf_op jit(solution)/shard_map/ppermute | solution.py:295
  17.1 0.0 collective-permute-done.5.refs_5_
  17.1 2.2 %attend_two_heads.1 = (bf16[192,128]{1,0:T(8,128)(2,1)S(1)}, bf16[192,128]{1,0:T(8,128)(2,1)S(1)}, bf16[192,128]{1,0:T(8,128)(2,1)S(1)}, bf16[192,128]{1,0:T(8,128)(2,1)S(1)}) custom-call(s32[8,128]{1,0:T(8,128)S(1)} %broadcast_in_dim.2.lengths_ref, bf16[3,192,128]{2,1,0:T(8,128)(2,1)S(1)} %get-tuple-element.32.refs_0_, ...), custom_call_target="tpu_custom_call" | custom-call | flops 1610612736 | tf_op jit(solution)/shard_map/attend_two_heads/pallas_call | solution.py:154
  19.3 1.7 %collective-permute-start.10 = (bf16[192,128]{1,0:T(8,128)(2,1)S(1)}, bf16[192,128]{1,0:T(8,128)(2,1)S(1)}, u32[]{:S(2)}, u32[]{:S(2)}) collective-permute-start(bf16[192,128]{1,0:T(8,128)(2,1)S(1)} %get-tuple-element.48), channel_id=1, source_target_pairs={{0,24},{4,28},{8,16},{12,20},{16,8},{20,12},{24,0},{28,4},{1,25},{... | collective-permute-start | bytes 147464 | tf_op jit(solution)/shard_map/ppermute | solution.py:285
  21.0 0.6 %collective-permute-start.6 = (bf16[192,128]{1,0:T(8,128)(2,1)S(1)}, bf16[192,128]{1,0:T(8,128)(2,1)S(1)}, u32[]{:S(2)}, u32[]{:S(2)}) collective-permute-start(bf16[192,128]{1,0:T(8,128)(2,1)S(1)} %get-tuple-element.43), channel_id=1, source_target_pairs={{0,8},{4,12},{8,0},{12,4},{16,24},{20,28},{24,16},{28,20},{1,9},{5... | collective-permute-start | bytes 147464 | tf_op jit(solution)/shard_map/ppermute | solution.py:285
  21.6 1.3 %collective-permute-start.7 = (bf16[192,128]{1,0:T(8,128)(2,1)S(1)}, bf16[192,128]{1,0:T(8,128)(2,1)S(1)}, u32[]{:S(2)}, u32[]{:S(2)}) collective-permute-start(bf16[192,128]{1,0:T(8,128)(2,1)S(1)} %get-tuple-element.44), channel_id=1, source_target_pairs={{0,16},{4,20},{8,24},{12,28},{16,0},{20,4},{24,8},{28,12},{1,17},{... | collective-permute-start | bytes 147464 | tf_op jit(solution)/shard_map/ppermute | solution.py:285
  22.9 0.0 collective-permute-done.9.refs_0_
  22.9 1.5 %collective-permute-start.13 = (bf16[208,384]{1,0:T(8,128)(2,1)S(1)}, bf16[208,384]{1,0:T(8,128)(2,1)S(1)}, u32[]{:S(2)}, u32[]{:S(2)}) collective-permute-start(bf16[208,384]{1,0:T(8,128)(2,1)S(1)} %collective-permute-done.9.refs_0_), channel_id=1, source_target_pairs={{0,8},{4,20},{8,0},{12,28},{16,24},{20,4},{24,16},{28,12},{1,9},{5... | collective-permute-start | bytes 479240 | tf_op jit(solution)/shard_map/ppermute | solution.py:291
  24.4 0.1 collective-permute-done.10.refs_3_
  24.5 0.3 collective-permute-start.11
  24.7 0.0 collective-permute-done.8.refs_6_
  24.7 0.7 %collective-permute-done.6.refs_1_ = bf16[192,128]{1,0:T(8,128)(2,1)S(1)} collective-permute-done((bf16[192,128]{1,0:T(8,128)(2,1)S(1)}, bf16[192,128]{1,0:T(8,128)(2,1)S(1)}, u32[]{:S(2)}, u32[]{:S(2)}) %collective-permute-start.6) | collective-permute-done | bytes 49184 | tf_op jit(solution)/shard_map/ppermute | solution.py:285
  25.4 0.6 %collective-permute-done.7.refs_2_ = bf16[192,128]{1,0:T(8,128)(2,1)S(1)} collective-permute-done((bf16[192,128]{1,0:T(8,128)(2,1)S(1)}, bf16[192,128]{1,0:T(8,128)(2,1)S(1)}, u32[]{:S(2)}, u32[]{:S(2)}) %collective-permute-start.7) | collective-permute-done | bytes 49184 | tf_op jit(solution)/shard_map/ppermute | solution.py:285
  26.0 0.0 collective-permute-start.12
  26.0 2.2 %collective-permute-done.13.refs_1_ = bf16[208,384]{1,0:T(8,128)(2,1)S(1)} collective-permute-done((bf16[208,384]{1,0:T(8,128)(2,1)S(1)}, bf16[208,384]{1,0:T(8,128)(2,1)S(1)}, u32[]{:S(2)}, u32[]{:S(2)}) %collective-permute-start.13) | collective-permute-done | bytes 159776 | tf_op jit(solution)/shard_map/ppermute | solution.py:291
  28.2 0.0 collective-permute-start.15
  28.2 0.5 %collective-permute-start.14 = (bf16[208,384]{1,0:T(8,128)(2,1)S(1)}, bf16[208,384]{1,0:T(8,128)(2,1)S(1)}, u32[]{:S(2)}, u32[]{:S(2)}) collective-permute-start(bf16[208,384]{1,0:T(8,128)(2,1)S(1)} %collective-permute-done.9.refs_0_), channel_id=1, source_target_pairs={{0,4},{4,0},{8,12},{12,8},{16,20},{20,16},{24,28},{28,24},{1,5},{5... | collective-permute-start | bytes 479240 | tf_op jit(solution)/shard_map/ppermute | solution.py:285
  28.7 0.0 collective-permute-done.11.refs_7_
  28.7 0.0 collective-permute-done.12.refs_8_
  28.7 0.0 copy-done
  28.7 0.7 %project_near_shards.1 = (bf16[3,128,384]{2,1,0:T(8,128)(2,1)S(1)}, bf16[128,768]{1,0:T(8,128)(2,1)S(1)}) custom-call(bf16[192,128]{1,0:T(8,128)(2,1)S(1)} %get-tuple-element.42.refs_0_, bf16[192,128]{1,0:T(8,128)(2,1)S(1)} %collective-permute-done.6.refs_1_, bf16[192,128]{1,0:T(8,128)(2,1)S(1)} %collective-permute-done.7.refs_2_, ...), custom_call_target="tpu_custom_call" | custom-call | flops 226492416 | bytes 1769472 | tf_op jit(solution)/shard_map/project_near_shards/pallas_call | solution.py:248
  29.4 0.1 collective-permute-done.15.refs_3_
  29.6 0.2 collective-permute-done.14.refs_2_
  29.8 1.0 %project_third_shard.1 = bf16[1,128,1536]{2,1,0:T(8,128)(2,1)} custom-call(bf16[3,128,384]{2,1,0:T(8,128)(2,1)S(1)} %get-tuple-element.52.blocks_ref, bf16[128,768]{1,0:T(8,128)(2,1)S(1)} %get-tuple-element.53.attention_ref, bf16[208,384]{1,0:T(8,128)(2,1)S(1)} %collective-permute-done.9.refs_0_, bf16[208,384]{1,0:T(8,128)(2,1)S(1)} %collective-permute-done.13.refs_1_, ...), custom_call_target="tpu_custom_call" | custom-call | flops 75497472 | bytes 589824 | tf_op jit(solution)/shard_map/project_third_shard/pallas_call | solution.py:266
  (4 shorter events, 0.0 us)
Async XLA Ops:
  1.2 10.7 %collective-permute-start = (bf16[384,384]{1,0:T(8,128)(2,1)S(1)}, bf16[384,384]{1,0:T(8,128)(2,1)S(1)}, u32[]{:S(2)}, u32[]{:S(2)}) collective-permute-start(bf16[384,384]{1,0:T(8,128)(2,1)S(1)} %get-tuple-element.30), channel_id=1, source_target_pairs={{0,2},{1,3},{2,0},{3,1},{4,5},{5,4},{6,7},{7,6},{8,10},{9,11},{10,... | collective-permute-start | bytes 884744 | tf_op jit(solution)/shard_map/ppermute | solution.py:295
  5.6 6.8 %collective-permute-start.2 = (bf16[3,192,128]{2,1,0:T(8,128)(2,1)S(1)}, bf16[3,192,128]{2,1,0:T(8,128)(2,1)S(1)}, u32[]{:S(2)}, u32[]{:S(2)}) collective-permute-start(bf16[3,192,128]{2,1,0:T(8,128)(2,1)S(1)} %get-tuple-element.34), channel_id=1, source_target_pairs={{0,8},{4,12},{8,0},{12,4},{16,24},{20,28},{24,16},{28,20},{1,9},{5... | collective-permute-start | bytes 442376 | tf_op jit(solution)/shard_map/ppermute | solution.py:285
  7.2 8.0 %collective-permute-start.3 = (bf16[3,192,128]{2,1,0:T(8,128)(2,1)S(1)}, bf16[3,192,128]{2,1,0:T(8,128)(2,1)S(1)}, u32[]{:S(2)}, u32[]{:S(2)}) collective-permute-start(bf16[3,192,128]{2,1,0:T(8,128)(2,1)S(1)} %get-tuple-element.35), channel_id=1, source_target_pairs={{0,16},{4,20},{8,24},{12,28},{16,0},{20,4},{24,8},{28,12},{1,17},{... | collective-permute-start | bytes 442376 | tf_op jit(solution)/shard_map/ppermute | solution.py:285
  8.7 6.5 %collective-permute-start.4 = (bf16[3,192,128]{2,1,0:T(8,128)(2,1)S(1)}, bf16[3,192,128]{2,1,0:T(8,128)(2,1)S(1)}, u32[]{:S(2)}, u32[]{:S(2)}) collective-permute-start(bf16[3,192,128]{2,1,0:T(8,128)(2,1)S(1)} %get-tuple-element.36), channel_id=1, source_target_pairs={{0,24},{4,28},{8,16},{12,20},{16,8},{20,12},{24,0},{28,4},{1,25},{... | collective-permute-start | bytes 442376 | tf_op jit(solution)/shard_map/ppermute | solution.py:285
  9.2 1.4 %collective-permute-start.1 = (bf16[2,192,128]{2,1,0:T(8,128)(2,1)S(1)}, bf16[2,192,128]{2,1,0:T(8,128)(2,1)S(1)}, u32[]{:S(2)}, u32[]{:S(2)}) collective-permute-start(bf16[2,192,128]{2,1,0:T(8,128)(2,1)S(1)} %slice.3), channel_id=1, source_target_pairs={{0,4},{4,0},{8,12},{12,8},{16,20},{20,16},{24,28},{28,24},{1,5},{5... | collective-permute-start | bytes 294920 | tf_op jit(solution)/shard_map/ppermute | solution.py:285
  15.2 1.9 %collective-permute-start.5 = (bf16[3,2,192,128]{3,2,1,0:T(8,128)(2,1)S(1)}, bf16[3,2,192,128]{3,2,1,0:T(8,128)(2,1)S(1)}, u32[]{:S(2)}, u32[]{:S(2)}) collective-permute-start(bf16[3,2,192,128]{3,2,1,0:T(8,128)(2,1)S(1)} %stack_keys_and_values.1), channel_id=1, source_target_pairs={{0,4},{4,0},{8,12},{12,8},{16,20},{20,16},{24,28},{28,24},{1,5},{5... | collective-permute-start | bytes 884744 | tf_op jit(solution)/shard_map/ppermute | solution.py:285
  15.3 9.4 %collective-permute-start.8 = (bf16[384,384]{1,0:T(8,128)(2,1)S(1)}, bf16[384,384]{1,0:T(8,128)(2,1)S(1)}, u32[]{:S(2)}, u32[]{:S(2)}) collective-permute-start(bf16[384,384]{1,0:T(8,128)(2,1)S(1)} %collective-permute-done.refs_5_), channel_id=1, source_target_pairs={{0,8},{4,20},{8,0},{12,28},{16,24},{20,4},{24,16},{28,12},{1,9},{5... | collective-permute-start | bytes 884744 | tf_op jit(solution)/shard_map/ppermute | solution.py:291
  15.8 12.9 %copy-start = (bf16[768,384]{1,0:T(8,128)(2,1)S(1)}, bf16[768,384]{1,0:T(8,128)(2,1)}, u32[]{:S(2)}) copy-start(bf16[768,384]{1,0:T(8,128)(2,1)} %refs_4_.1) | copy-start | bytes 1769476
  15.8 7.1 %collective-permute-start.9 = (bf16[208,384]{1,0:T(8,128)(2,1)S(1)}, bf16[208,384]{1,0:T(8,128)(2,1)S(1)}, u32[]{:S(2)}, u32[]{:S(2)}) collective-permute-start(bf16[208,384]{1,0:T(8,128)(2,1)S(1)} %constant_dynamic-slice_fusion), channel_id=1, source_target_pairs={{0,1},{1,0},{2,3},{3,2},{4,6},{5,7},{6,4},{7,5},{8,9},{9,8},{10,11... | collective-permute-start | bytes 479240 | tf_op jit(solution)/shard_map/ppermute | solution.py:295
  19.3 5.1 %collective-permute-start.10 = (bf16[192,128]{1,0:T(8,128)(2,1)S(1)}, bf16[192,128]{1,0:T(8,128)(2,1)S(1)}, u32[]{:S(2)}, u32[]{:S(2)}) collective-permute-start(bf16[192,128]{1,0:T(8,128)(2,1)S(1)} %get-tuple-element.48), channel_id=1, source_target_pairs={{0,24},{4,28},{8,16},{12,20},{16,8},{20,12},{24,0},{28,4},{1,25},{... | collective-permute-start | bytes 147464 | tf_op jit(solution)/shard_map/ppermute | solution.py:285
  21.0 4.4 %collective-permute-start.6 = (bf16[192,128]{1,0:T(8,128)(2,1)S(1)}, bf16[192,128]{1,0:T(8,128)(2,1)S(1)}, u32[]{:S(2)}, u32[]{:S(2)}) collective-permute-start(bf16[192,128]{1,0:T(8,128)(2,1)S(1)} %get-tuple-element.43), channel_id=1, source_target_pairs={{0,8},{4,12},{8,0},{12,4},{16,24},{20,28},{24,16},{28,20},{1,9},{5... | collective-permute-start | bytes 147464 | tf_op jit(solution)/shard_map/ppermute | solution.py:285
  21.6 4.4 %collective-permute-start.7 = (bf16[192,128]{1,0:T(8,128)(2,1)S(1)}, bf16[192,128]{1,0:T(8,128)(2,1)S(1)}, u32[]{:S(2)}, u32[]{:S(2)}) collective-permute-start(bf16[192,128]{1,0:T(8,128)(2,1)S(1)} %get-tuple-element.44), channel_id=1, source_target_pairs={{0,16},{4,20},{8,24},{12,28},{16,0},{20,4},{24,8},{28,12},{1,17},{... | collective-permute-start | bytes 147464 | tf_op jit(solution)/shard_map/ppermute | solution.py:285
  22.9 5.3 %collective-permute-start.13 = (bf16[208,384]{1,0:T(8,128)(2,1)S(1)}, bf16[208,384]{1,0:T(8,128)(2,1)S(1)}, u32[]{:S(2)}, u32[]{:S(2)}) collective-permute-start(bf16[208,384]{1,0:T(8,128)(2,1)S(1)} %collective-permute-done.9.refs_0_), channel_id=1, source_target_pairs={{0,8},{4,20},{8,0},{12,28},{16,24},{20,4},{24,16},{28,12},{1,9},{5... | collective-permute-start | bytes 479240 | tf_op jit(solution)/shard_map/ppermute | solution.py:291
  24.5 4.2 %collective-permute-start.11 = (bf16[384,384]{1,0:T(8,128)(2,1)S(1)}, bf16[384,384]{1,0:T(8,128)(2,1)S(1)}, u32[]{:S(2)}, u32[]{:S(2)}) collective-permute-start(bf16[384,384]{1,0:T(8,128)(2,1)S(1)} %collective-permute-done.refs_5_), channel_id=1, source_target_pairs={{0,4},{4,0},{8,12},{12,8},{16,20},{20,16},{24,28},{28,24},{1,5},{5... | collective-permute-start | bytes 884744 | tf_op jit(solution)/shard_map/ppermute | solution.py:285
  26.0 2.7 %collective-permute-start.12 = (bf16[384,384]{1,0:T(8,128)(2,1)S(1)}, bf16[384,384]{1,0:T(8,128)(2,1)S(1)}, u32[]{:S(2)}, u32[]{:S(2)}) collective-permute-start(bf16[384,384]{1,0:T(8,128)(2,1)S(1)} %collective-permute-done.8.refs_6_), channel_id=1, source_target_pairs={{0,4},{4,0},{8,12},{12,8},{16,20},{20,16},{24,28},{28,24},{1,5},{5... | collective-permute-start | bytes 884744 | tf_op jit(solution)/shard_map/ppermute | solution.py:285
  28.2 1.4 %collective-permute-start.15 = (bf16[208,384]{1,0:T(8,128)(2,1)S(1)}, bf16[208,384]{1,0:T(8,128)(2,1)S(1)}, u32[]{:S(2)}, u32[]{:S(2)}) collective-permute-start(bf16[208,384]{1,0:T(8,128)(2,1)S(1)} %collective-permute-done.13.refs_1_), channel_id=1, source_target_pairs={{0,4},{4,0},{8,12},{12,8},{16,20},{20,16},{24,28},{28,24},{1,5},{5... | collective-permute-start | bytes 479240 | tf_op jit(solution)/shard_map/ppermute | solution.py:285
  28.2 1.6 %collective-permute-start.14 = (bf16[208,384]{1,0:T(8,128)(2,1)S(1)}, bf16[208,384]{1,0:T(8,128)(2,1)S(1)}, u32[]{:S(2)}, u32[]{:S(2)}) collective-permute-start(bf16[208,384]{1,0:T(8,128)(2,1)S(1)} %collective-permute-done.9.refs_0_), channel_id=1, source_target_pairs={{0,4},{4,0},{8,12},{12,8},{16,20},{20,16},{24,28},{28,24},{1,5},{5... | collective-permute-start | bytes 479240 | tf_op jit(solution)/shard_map/ppermute | solution.py:285

commit v14 on v13

--- a/solution.py
+++ b/solution.py
@@ -331,11 +331,12 @@
     if not split_columns:
         return project(heads, [half, exchange(half, "ctx", 1)])
     third_passed = exchange_in_plane(third)
-    heads[3], fetched = lax.optimization_barrier((heads[3], fetched))
-    heads[1], heads[2], passed, third = lax.optimization_barrier((heads[1], heads[2], passed, third))
+    heads[3], fetched, third = lax.optimization_barrier((heads[3], fetched, third))
+    heads[1], heads[2], passed = lax.optimization_barrier((heads[1], heads[2], passed))
     fetched_other, passed_other, third_other, third_passed_other = (
         exchange(array, "ctx", 1) for array in (fetched, passed, third, third_passed)
     )
+    third_other, passed_other = lax.optimization_barrier((third_other, passed_other))
     blocks, attention = project_near(heads, out_weight, [fetched, passed, fetched_other, passed_other])
     return project_third(blocks, attention, [third, third_passed, third_other, third_passed_other])
 

time: 31 us -> 30.7 us (level)
    ppermute x2, waiting for transfers between devices: 2.2 us -> 1.01 us  [exchange_in_plane(): lax.ppermute(array, 'ctx', [(i, i ^ (4 if i % 2 else 2)) for i in range(c...]
    ppermute x12, waiting for transfers between devices: 5.55 us -> 6.67 us  [exchange(): return lax.ppermute(array, axis, [(i, i ^ flip) for i in range(size)])]
  transfers between devices with their start and end apart: 16 -> 16, of which waited for: 10 -> 9; matrix products, arithmetic and copies ran while one was open for 0% -> 0% of each run, Pallas kernels for 10% -> 10%
where the time goes in v14:
time: 30.7 us; the launch traced here: 30.6 us
  starting transfers between devices  15.3 us (50%)
  waiting for transfers between devices  9.1 us (30%)
  Pallas kernels  5.45 us (18%)
  between operations  0.74 us (2%)
    ppermute x12, starting transfers between devices, exchange(): return lax.ppermute(array, axis, [(i, i ^ flip) for i in range(size)])  7.87 us
    ppermute x12, waiting for transfers between devices, exchange(): return lax.ppermute(array, axis, [(i, i ^ flip) for i in range(size)])  6.67 us
    ppermute x2, starting transfers between devices, exchange_along(): return lax.ppermute(array, ('ctx', 'fsdp'), pairs)  5.43 us
    pallas_call x1, Pallas kernels, attend(): pl.pallas_call(functools.partial(attention_kernel, groups), out_shape=[pl...  2.2 us
    ppermute x2, starting transfers between devices, exchange_in_plane(): lax.ppermute(array, 'ctx', [(i, i ^ (4 if i % 2 else 2)) for i in range(c...  1.96 us
    ppermute x2, waiting for transfers between devices, exchange_along(): return lax.ppermute(array, ('ctx', 'fsdp'), pairs)  1.42 us
    pallas_call x1, Pallas kernels, copy_in(): pl.pallas_call(functools.partial(copy_in_kernel, by_parity), out_shape=[p...  1.24 us
    pallas_call x1, Pallas kernels, project_third(): pl.pallas_call(project_third_kernel, out_shape=jax.ShapeDtypeStruct((1, f...  1.02 us
  transfers between devices with their start and end apart: 16, of which 9 were waited for; matrix products, arithmetic and copies ran while one was open for 0% of the time, Pallas kernels for 10%

profile of v14, /device:TPU:0, one launch (start us, length us, event | category | flops | bytes accessed | tf_op | source)
XLA Modules:
  0.0 30.6 jit_solution(13308885412999463706)
XLA Ops:
  0.0 1.2 %copy_in.1 = (bf16[3,128,768]{2,1,0:T(8,128)(2,1)S(1)}, bf16[384,384]{1,0:T(8,128)(2,1)S(1)}) custom-call(bf16[1,128,768]{2,1,0:T(8,128)(2,1)} %query_ref.1, bf16[1,128,768]{2,1,0:T(8,128)(2,1)} %key_ref.1, bf16[1,128,768]{2,1,0:T(8,128)(2,1)} %value_ref.1, bf16[768,384]{1,0:T(8,128)(2,1)} %refs_4_.1), custom_call_target="tpu_custom_call" | custom-call | tf_op jit(solution)/shard_map/copy_in/pallas_call | solution.py:45
  1.2 4.1 %collective-permute-start = (bf16[384,384]{1,0:T(8,128)(2,1)S(1)}, bf16[384,384]{1,0:T(8,128)(2,1)S(1)}, u32[]{:S(2)}, u32[]{:S(2)}) collective-permute-start(bf16[384,384]{1,0:T(8,128)(2,1)S(1)} %get-tuple-element.32), channel_id=1, source_target_pairs={{0,2},{1,3},{2,0},{3,1},{4,5},{5,4},{6,7},{7,6},{8,10},{9,11},{10,... | collective-permute-start | bytes 884744 | tf_op jit(solution)/shard_map/ppermute | solution.py:295
  5.3 0.2 turn_heads.1
  5.6 1.6 %collective-permute-start.2 = (bf16[3,192,128]{2,1,0:T(8,128)(2,1)S(1)}, bf16[3,192,128]{2,1,0:T(8,128)(2,1)S(1)}, u32[]{:S(2)}, u32[]{:S(2)}) collective-permute-start(bf16[3,192,128]{2,1,0:T(8,128)(2,1)S(1)} %get-tuple-element.36), channel_id=1, source_target_pairs={{0,8},{4,12},{8,0},{12,4},{16,24},{20,28},{24,16},{28,20},{1,9},{5... | collective-permute-start | bytes 442376 | tf_op jit(solution)/shard_map/ppermute | solution.py:285
  7.2 1.5 %collective-permute-start.3 = (bf16[3,192,128]{2,1,0:T(8,128)(2,1)S(1)}, bf16[3,192,128]{2,1,0:T(8,128)(2,1)S(1)}, u32[]{:S(2)}, u32[]{:S(2)}) collective-permute-start(bf16[3,192,128]{2,1,0:T(8,128)(2,1)S(1)} %get-tuple-element.37), channel_id=1, source_target_pairs={{0,16},{4,20},{8,24},{12,28},{16,0},{20,4},{24,8},{28,12},{1,17},{... | collective-permute-start | bytes 442376 | tf_op jit(solution)/shard_map/ppermute | solution.py:285
  8.7 0.5 %collective-permute-start.4 = (bf16[3,192,128]{2,1,0:T(8,128)(2,1)S(1)}, bf16[3,192,128]{2,1,0:T(8,128)(2,1)S(1)}, u32[]{:S(2)}, u32[]{:S(2)}) collective-permute-start(bf16[3,192,128]{2,1,0:T(8,128)(2,1)S(1)} %get-tuple-element.38), channel_id=1, source_target_pairs={{0,24},{4,28},{8,16},{12,20},{16,8},{20,12},{24,0},{28,4},{1,25},{... | collective-permute-start | bytes 442376 | tf_op jit(solution)/shard_map/ppermute | solution.py:285
  9.2 0.1 collective-permute-start.1
  9.9 0.6 %collective-permute-done.1.refs_4_ = bf16[2,192,128]{2,1,0:T(8,128)(2,1)S(1)} collective-permute-done((bf16[2,192,128]{2,1,0:T(8,128)(2,1)S(1)}, bf16[2,192,128]{2,1,0:T(8,128)(2,1)S(1)}, u32[]{:S(2)}, u32[]{:S(2)}) %collective-permute-start.1) | collective-permute-done | bytes 98336 | tf_op jit(solution)/shard_map/ppermute | solution.py:285
  10.5 1.4 %collective-permute-done.refs_5_ = bf16[384,384]{1,0:T(8,128)(2,1)S(1)} collective-permute-done((bf16[384,384]{1,0:T(8,128)(2,1)S(1)}, bf16[384,384]{1,0:T(8,128)(2,1)S(1)}, u32[]{:S(2)}, u32[]{:S(2)}) %collective-permute-start) | collective-permute-done | bytes 294944 | tf_op jit(solution)/shard_map/ppermute | solution.py:295
  12.0 0.4 %collective-permute-done.2.refs_0_.refs_1_ = bf16[3,192,128]{2,1,0:T(8,128)(2,1)S(1)} collective-permute-done((bf16[3,192,128]{2,1,0:T(8,128)(2,1)S(1)}, bf16[3,192,128]{2,1,0:T(8,128)(2,1)S(1)}, u32[]{:S(2)}, u32[]{:S(2)}) %collective-permute-start.2) | collective-permute-done | bytes 147488 | tf_op jit(solution)/shard_map/ppermute | solution.py:285
  12.4 2.8 %collective-permute-done.3.refs_1_.refs_2_ = bf16[3,192,128]{2,1,0:T(8,128)(2,1)S(1)} collective-permute-done((bf16[3,192,128]{2,1,0:T(8,128)(2,1)S(1)}, bf16[3,192,128]{2,1,0:T(8,128)(2,1)S(1)}, u32[]{:S(2)}, u32[]{:S(2)}) %collective-permute-start.3) | collective-permute-done | bytes 147488 | tf_op jit(solution)/shard_map/ppermute | solution.py:285
  15.2 0.0 collective-permute-done.4.refs_2_.refs_3_
  15.2 0.1 collective-permute-start.5
  15.3 0.5 %collective-permute-start.8 = (bf16[384,384]{1,0:T(8,128)(2,1)S(1)}, bf16[384,384]{1,0:T(8,128)(2,1)S(1)}, u32[]{:S(2)}, u32[]{:S(2)}) collective-permute-start(bf16[384,384]{1,0:T(8,128)(2,1)S(1)} %collective-permute-done.refs_5_), channel_id=1, source_target_pairs={{0,8},{4,20},{8,0},{12,28},{16,24},{20,4},{24,16},{28,12},{1,9},{5... | collective-permute-start | bytes 884744 | tf_op jit(solution)/shard_map/ppermute | solution.py:291
  15.8 0.0 copy-start
  15.8 1.3 %collective-permute-start.10 = (bf16[208,384]{1,0:T(8,128)(2,1)S(1)}, bf16[208,384]{1,0:T(8,128)(2,1)S(1)}, u32[]{:S(2)}, u32[]{:S(2)}) collective-permute-start(bf16[208,384]{1,0:T(8,128)(2,1)S(1)} %constant_dynamic-slice_fusion), channel_id=1, source_target_pairs={{0,1},{1,0},{2,3},{3,2},{4,6},{5,7},{6,4},{7,5},{8,9},{9,8},{10,11... | collective-permute-start | bytes 479240 | tf_op jit(solution)/shard_map/ppermute | solution.py:295
  17.1 0.0 collective-permute-done.5.refs_5_
  17.1 2.2 %attend_two_heads.1 = (bf16[192,128]{1,0:T(8,128)(2,1)S(1)}, bf16[192,128]{1,0:T(8,128)(2,1)S(1)}, bf16[192,128]{1,0:T(8,128)(2,1)S(1)}, bf16[192,128]{1,0:T(8,128)(2,1)S(1)}) custom-call(s32[8,128]{1,0:T(8,128)S(1)} %broadcast_in_dim.2.lengths_ref, bf16[3,192,128]{2,1,0:T(8,128)(2,1)S(1)} %get-tuple-element.34.refs_0_, ...), custom_call_target="tpu_custom_call" | custom-call | flops 1610612736 | tf_op jit(solution)/shard_map/attend_two_heads/pallas_call | solution.py:154
  19.3 1.6 %collective-permute-start.6 = (bf16[192,128]{1,0:T(8,128)(2,1)S(1)}, bf16[192,128]{1,0:T(8,128)(2,1)S(1)}, u32[]{:S(2)}, u32[]{:S(2)}) collective-permute-start(bf16[192,128]{1,0:T(8,128)(2,1)S(1)} %get-tuple-element.45), channel_id=1, source_target_pairs={{0,8},{4,12},{8,0},{12,4},{16,24},{20,28},{24,16},{28,20},{1,9},{5... | collective-permute-start | bytes 147464 | tf_op jit(solution)/shard_map/ppermute | solution.py:285
  20.9 0.7 %collective-permute-start.7 = (bf16[192,128]{1,0:T(8,128)(2,1)S(1)}, bf16[192,128]{1,0:T(8,128)(2,1)S(1)}, u32[]{:S(2)}, u32[]{:S(2)}) collective-permute-start(bf16[192,128]{1,0:T(8,128)(2,1)S(1)} %get-tuple-element.46), channel_id=1, source_target_pairs={{0,16},{4,20},{8,24},{12,28},{16,0},{20,4},{24,8},{28,12},{1,17},{... | collective-permute-start | bytes 147464 | tf_op jit(solution)/shard_map/ppermute | solution.py:285
  21.6 1.3 %collective-permute-start.9 = (bf16[192,128]{1,0:T(8,128)(2,1)S(1)}, bf16[192,128]{1,0:T(8,128)(2,1)S(1)}, u32[]{:S(2)}, u32[]{:S(2)}) collective-permute-start(bf16[192,128]{1,0:T(8,128)(2,1)S(1)} %get-tuple-element.50), channel_id=1, source_target_pairs={{0,24},{4,28},{8,16},{12,20},{16,8},{20,12},{24,0},{28,4},{1,25},{... | collective-permute-start | bytes 147464 | tf_op jit(solution)/shard_map/ppermute | solution.py:285
  22.9 0.0 collective-permute-done.10.refs_0_
  22.9 1.5 %collective-permute-start.14 = (bf16[208,384]{1,0:T(8,128)(2,1)S(1)}, bf16[208,384]{1,0:T(8,128)(2,1)S(1)}, u32[]{:S(2)}, u32[]{:S(2)}) collective-permute-start(bf16[208,384]{1,0:T(8,128)(2,1)S(1)} %collective-permute-done.10.refs_0_), channel_id=1, source_target_pairs={{0,8},{4,20},{8,0},{12,28},{16,24},{20,4},{24,16},{28,12},{1,9},{5... | collective-permute-start | bytes 479240 | tf_op jit(solution)/shard_map/ppermute | solution.py:291
  24.4 0.0 collective-permute-done.8.refs_6_
  24.4 0.0 collective-permute-done.6.refs_1_
  24.4 0.6 %collective-permute-done.7.refs_2_ = bf16[192,128]{1,0:T(8,128)(2,1)S(1)} collective-permute-done((bf16[192,128]{1,0:T(8,128)(2,1)S(1)}, bf16[192,128]{1,0:T(8,128)(2,1)S(1)}, u32[]{:S(2)}, u32[]{:S(2)}) %collective-permute-start.7) | collective-permute-done | bytes 49184 | tf_op jit(solution)/shard_map/ppermute | solution.py:285
  25.0 0.0 collective-permute-start.13
  25.0 1.7 %collective-permute-done.9.refs_3_ = bf16[192,128]{1,0:T(8,128)(2,1)S(1)} collective-permute-done((bf16[192,128]{1,0:T(8,128)(2,1)S(1)}, bf16[192,128]{1,0:T(8,128)(2,1)S(1)}, u32[]{:S(2)}, u32[]{:S(2)}) %collective-permute-start.9) | collective-permute-done | bytes 49184 | tf_op jit(solution)/shard_map/ppermute | solution.py:285
  26.6 0.0 collective-permute-start.11
  26.6 0.5 %collective-permute-start.12 = (bf16[208,384]{1,0:T(8,128)(2,1)S(1)}, bf16[208,384]{1,0:T(8,128)(2,1)S(1)}, u32[]{:S(2)}, u32[]{:S(2)}) collective-permute-start(bf16[208,384]{1,0:T(8,128)(2,1)S(1)} %collective-permute-done.10.refs_0_), channel_id=1, source_target_pairs={{0,4},{4,0},{8,12},{12,8},{16,20},{20,16},{24,28},{28,24},{1,5},{5... | collective-permute-start | bytes 479240 | tf_op jit(solution)/shard_map/ppermute | solution.py:285
  27.2 1.0 %collective-permute-done.14.refs_1_ = bf16[208,384]{1,0:T(8,128)(2,1)S(1)} collective-permute-done((bf16[208,384]{1,0:T(8,128)(2,1)S(1)}, bf16[208,384]{1,0:T(8,128)(2,1)S(1)}, u32[]{:S(2)}, u32[]{:S(2)}) %collective-permute-start.14) | collective-permute-done | bytes 159776 | tf_op jit(solution)/shard_map/ppermute | solution.py:291
  28.2 0.1 collective-permute-start.15
  28.3 0.2 collective-permute-done.12.refs_2_
  28.5 0.0 collective-permute-done.13.refs_8_
  28.5 0.0 collective-permute-done.11.refs_7_
  28.5 0.0 copy-done
  28.5 0.7 %project_near_shards.1 = (bf16[3,128,384]{2,1,0:T(8,128)(2,1)S(1)}, bf16[128,768]{1,0:T(8,128)(2,1)S(1)}) custom-call(bf16[192,128]{1,0:T(8,128)(2,1)S(1)} %get-tuple-element.44.refs_0_, bf16[192,128]{1,0:T(8,128)(2,1)S(1)} %collective-permute-done.6.refs_1_, bf16[192,128]{1,0:T(8,128)(2,1)S(1)} %collective-permute-done.7.refs_2_, ...), custom_call_target="tpu_custom_call" | custom-call | flops 226492416 | bytes 1769472 | tf_op jit(solution)/shard_map/project_near_shards/pallas_call | solution.py:248
  29.2 0.4 %collective-permute-done.15.refs_3_ = bf16[208,384]{1,0:T(8,128)(2,1)S(1)} collective-permute-done((bf16[208,384]{1,0:T(8,128)(2,1)S(1)}, bf16[208,384]{1,0:T(8,128)(2,1)S(1)}, u32[]{:S(2)}, u32[]{:S(2)}) %collective-permute-start.15) | collective-permute-done | bytes 159776 | tf_op jit(solution)/shard_map/ppermute | solution.py:285
  29.6 1.0 %project_third_shard.1 = bf16[1,128,1536]{2,1,0:T(8,128)(2,1)} custom-call(bf16[3,128,384]{2,1,0:T(8,128)(2,1)S(1)} %get-tuple-element.56.blocks_ref, bf16[128,768]{1,0:T(8,128)(2,1)S(1)} %get-tuple-element.57.attention_ref, bf16[208,384]{1,0:T(8,128)(2,1)S(1)} %collective-permute-done.10.refs_0_, bf16[208,384]{1,0:T(8,128)(2,1)S(1)} %collective-permute-done.14.refs_1_, ...), custom_call_target="tpu_custom_call" | custom-call | flops 75497472 | bytes 589824 | tf_op jit(solution)/shard_map/project_third_shard/pallas_call | solution.py:266
  (4 shorter events, 0.0 us)
Async XLA Ops:
  1.2 10.7 %collective-permute-start = (bf16[384,384]{1,0:T(8,128)(2,1)S(1)}, bf16[384,384]{1,0:T(8,128)(2,1)S(1)}, u32[]{:S(2)}, u32[]{:S(2)}) collective-permute-start(bf16[384,384]{1,0:T(8,128)(2,1)S(1)} %get-tuple-element.32), channel_id=1, source_target_pairs={{0,2},{1,3},{2,0},{3,1},{4,5},{5,4},{6,7},{7,6},{8,10},{9,11},{10,... | collective-permute-start | bytes 884744 | tf_op jit(solution)/shard_map/ppermute | solution.py:295
  5.6 6.8 %collective-permute-start.2 = (bf16[3,192,128]{2,1,0:T(8,128)(2,1)S(1)}, bf16[3,192,128]{2,1,0:T(8,128)(2,1)S(1)}, u32[]{:S(2)}, u32[]{:S(2)}) collective-permute-start(bf16[3,192,128]{2,1,0:T(8,128)(2,1)S(1)} %get-tuple-element.36), channel_id=1, source_target_pairs={{0,8},{4,12},{8,0},{12,4},{16,24},{20,28},{24,16},{28,20},{1,9},{5... | collective-permute-start | bytes 442376 | tf_op jit(solution)/shard_map/ppermute | solution.py:285
  7.2 8.0 %collective-permute-start.3 = (bf16[3,192,128]{2,1,0:T(8,128)(2,1)S(1)}, bf16[3,192,128]{2,1,0:T(8,128)(2,1)S(1)}, u32[]{:S(2)}, u32[]{:S(2)}) collective-permute-start(bf16[3,192,128]{2,1,0:T(8,128)(2,1)S(1)} %get-tuple-element.37), channel_id=1, source_target_pairs={{0,16},{4,20},{8,24},{12,28},{16,0},{20,4},{24,8},{28,12},{1,17},{... | collective-permute-start | bytes 442376 | tf_op jit(solution)/shard_map/ppermute | solution.py:285
  8.7 6.5 %collective-permute-start.4 = (bf16[3,192,128]{2,1,0:T(8,128)(2,1)S(1)}, bf16[3,192,128]{2,1,0:T(8,128)(2,1)S(1)}, u32[]{:S(2)}, u32[]{:S(2)}) collective-permute-start(bf16[3,192,128]{2,1,0:T(8,128)(2,1)S(1)} %get-tuple-element.38), channel_id=1, source_target_pairs={{0,24},{4,28},{8,16},{12,20},{16,8},{20,12},{24,0},{28,4},{1,25},{... | collective-permute-start | bytes 442376 | tf_op jit(solution)/shard_map/ppermute | solution.py:285
  9.2 1.4 %collective-permute-start.1 = (bf16[2,192,128]{2,1,0:T(8,128)(2,1)S(1)}, bf16[2,192,128]{2,1,0:T(8,128)(2,1)S(1)}, u32[]{:S(2)}, u32[]{:S(2)}) collective-permute-start(bf16[2,192,128]{2,1,0:T(8,128)(2,1)S(1)} %slice.3), channel_id=1, source_target_pairs={{0,4},{4,0},{8,12},{12,8},{16,20},{20,16},{24,28},{28,24},{1,5},{5... | collective-permute-start | bytes 294920 | tf_op jit(solution)/shard_map/ppermute | solution.py:285
  15.2 1.9 %collective-permute-start.5 = (bf16[3,2,192,128]{3,2,1,0:T(8,128)(2,1)S(1)}, bf16[3,2,192,128]{3,2,1,0:T(8,128)(2,1)S(1)}, u32[]{:S(2)}, u32[]{:S(2)}) collective-permute-start(bf16[3,2,192,128]{3,2,1,0:T(8,128)(2,1)S(1)} %stack_keys_and_values.1), channel_id=1, source_target_pairs={{0,4},{4,0},{8,12},{12,8},{16,20},{20,16},{24,28},{28,24},{1,5},{5... | collective-permute-start | bytes 884744 | tf_op jit(solution)/shard_map/ppermute | solution.py:285
  15.3 9.1 %collective-permute-start.8 = (bf16[384,384]{1,0:T(8,128)(2,1)S(1)}, bf16[384,384]{1,0:T(8,128)(2,1)S(1)}, u32[]{:S(2)}, u32[]{:S(2)}) collective-permute-start(bf16[384,384]{1,0:T(8,128)(2,1)S(1)} %collective-permute-done.refs_5_), channel_id=1, source_target_pairs={{0,8},{4,20},{8,0},{12,28},{16,24},{20,4},{24,16},{28,12},{1,9},{5... | collective-permute-start | bytes 884744 | tf_op jit(solution)/shard_map/ppermute | solution.py:291
  15.8 12.7 %copy-start = (bf16[768,384]{1,0:T(8,128)(2,1)S(1)}, bf16[768,384]{1,0:T(8,128)(2,1)}, u32[]{:S(2)}) copy-start(bf16[768,384]{1,0:T(8,128)(2,1)} %refs_4_.1) | copy-start | bytes 1769476
  15.8 7.1 %collective-permute-start.10 = (bf16[208,384]{1,0:T(8,128)(2,1)S(1)}, bf16[208,384]{1,0:T(8,128)(2,1)S(1)}, u32[]{:S(2)}, u32[]{:S(2)}) collective-permute-start(bf16[208,384]{1,0:T(8,128)(2,1)S(1)} %constant_dynamic-slice_fusion), channel_id=1, source_target_pairs={{0,1},{1,0},{2,3},{3,2},{4,6},{5,7},{6,4},{7,5},{8,9},{9,8},{10,11... | collective-permute-start | bytes 479240 | tf_op jit(solution)/shard_map/ppermute | solution.py:295
  19.3 5.1 %collective-permute-start.6 = (bf16[192,128]{1,0:T(8,128)(2,1)S(1)}, bf16[192,128]{1,0:T(8,128)(2,1)S(1)}, u32[]{:S(2)}, u32[]{:S(2)}) collective-permute-start(bf16[192,128]{1,0:T(8,128)(2,1)S(1)} %get-tuple-element.45), channel_id=1, source_target_pairs={{0,8},{4,12},{8,0},{12,4},{16,24},{20,28},{24,16},{28,20},{1,9},{5... | collective-permute-start | bytes 147464 | tf_op jit(solution)/shard_map/ppermute | solution.py:285
  20.9 4.1 %collective-permute-start.7 = (bf16[192,128]{1,0:T(8,128)(2,1)S(1)}, bf16[192,128]{1,0:T(8,128)(2,1)S(1)}, u32[]{:S(2)}, u32[]{:S(2)}) collective-permute-start(bf16[192,128]{1,0:T(8,128)(2,1)S(1)} %get-tuple-element.46), channel_id=1, source_target_pairs={{0,16},{4,20},{8,24},{12,28},{16,0},{20,4},{24,8},{28,12},{1,17},{... | collective-permute-start | bytes 147464 | tf_op jit(solution)/shard_map/ppermute | solution.py:285
  21.6 5.1 %collective-permute-start.9 = (bf16[192,128]{1,0:T(8,128)(2,1)S(1)}, bf16[192,128]{1,0:T(8,128)(2,1)S(1)}, u32[]{:S(2)}, u32[]{:S(2)}) collective-permute-start(bf16[192,128]{1,0:T(8,128)(2,1)S(1)} %get-tuple-element.50), channel_id=1, source_target_pairs={{0,24},{4,28},{8,16},{12,20},{16,8},{20,12},{24,0},{28,4},{1,25},{... | collective-permute-start | bytes 147464 | tf_op jit(solution)/shard_map/ppermute | solution.py:285
  22.9 5.3 %collective-permute-start.14 = (bf16[208,384]{1,0:T(8,128)(2,1)S(1)}, bf16[208,384]{1,0:T(8,128)(2,1)S(1)}, u32[]{:S(2)}, u32[]{:S(2)}) collective-permute-start(bf16[208,384]{1,0:T(8,128)(2,1)S(1)} %collective-permute-done.10.refs_0_), channel_id=1, source_target_pairs={{0,8},{4,20},{8,0},{12,28},{16,24},{20,4},{24,16},{28,12},{1,9},{5... | collective-permute-start | bytes 479240 | tf_op jit(solution)/shard_map/ppermute | solution.py:291
  25.0 3.5 %collective-permute-start.13 = (bf16[384,384]{1,0:T(8,128)(2,1)S(1)}, bf16[384,384]{1,0:T(8,128)(2,1)S(1)}, u32[]{:S(2)}, u32[]{:S(2)}) collective-permute-start(bf16[384,384]{1,0:T(8,128)(2,1)S(1)} %collective-permute-done.8.refs_6_), channel_id=1, source_target_pairs={{0,4},{4,0},{8,12},{12,8},{16,20},{20,16},{24,28},{28,24},{1,5},{5... | collective-permute-start | bytes 884744 | tf_op jit(solution)/shard_map/ppermute | solution.py:285
  26.6 1.8 %collective-permute-start.11 = (bf16[384,384]{1,0:T(8,128)(2,1)S(1)}, bf16[384,384]{1,0:T(8,128)(2,1)S(1)}, u32[]{:S(2)}, u32[]{:S(2)}) collective-permute-start(bf16[384,384]{1,0:T(8,128)(2,1)S(1)} %collective-permute-done.refs_5_), channel_id=1, source_target_pairs={{0,4},{4,0},{8,12},{12,8},{16,20},{20,16},{24,28},{28,24},{1,5},{5... | collective-permute-start | bytes 884744 | tf_op jit(solution)/shard_map/ppermute | solution.py:285
  26.6 1.8 %collective-permute-start.12 = (bf16[208,384]{1,0:T(8,128)(2,1)S(1)}, bf16[208,384]{1,0:T(8,128)(2,1)S(1)}, u32[]{:S(2)}, u32[]{:S(2)}) collective-permute-start(bf16[208,384]{1,0:T(8,128)(2,1)S(1)} %collective-permute-done.10.refs_0_), channel_id=1, source_target_pairs={{0,4},{4,0},{8,12},{12,8},{16,20},{20,16},{24,28},{28,24},{1,5},{5... | collective-permute-start | bytes 479240 | tf_op jit(solution)/shard_map/ppermute | solution.py:285
  28.2 1.4 %collective-permute-start.15 = (bf16[208,384]{1,0:T(8,128)(2,1)S(1)}, bf16[208,384]{1,0:T(8,128)(2,1)S(1)}, u32[]{:S(2)}, u32[]{:S(2)}) collective-permute-start(bf16[208,384]{1,0:T(8,128)(2,1)S(1)} %collective-permute-done.14.refs_1_), channel_id=1, source_target_pairs={{0,4},{4,0},{8,12},{12,8},{16,20},{20,16},{24,28},{28,24},{1,5},{5... | collective-permute-start | bytes 479240 | tf_op jit(solution)/shard_map/ppermute | solution.py:285

commit v15 on v14

--- a/solution.py
+++ b/solution.py
@@ -213,8 +213,11 @@
     copies = [copy_out(flip, blocks_ref.at[flip]) for flip in range(3)]
     for other in range(2):
         for flip in range(2):
-            first = (parity_of(place) ^ flip) * half + ((place & 1) ^ other) * (half - part)
-            weight[pl.ds(pl.multiple_of(first, 16), part), :] = pieces[2 * other + flip][...]
+            first = (parity_of(place) ^ flip) * half + ((place & 1) ^ other) * (half - part) // 2
+            ref = pieces[2 * other + flip]
+            for rest in range(2):
+                here = pl.ds(pl.multiple_of(first + rest * (half // 2), 16), part // 2)
+                weight[here, :] = ref[rest * (part // 2) : (rest + 1) * (part // 2), :]
     last[...] = jnp.dot(attention_ref[...], weight[...], preferred_element_type=jnp.float32).astype(last.dtype)
     copies.append(copy_out(3, last))
     for copy in copies:
@@ -299,7 +302,8 @@
     lengths = jnp.broadcast_to(lengths, (8, 128))
     rows, half = copy_in(queries, key_rows, value_rows, out_weight, split_columns)
     if split_columns:
-        fetched = exchange_along(half, 2, 1)
+        depth = half.shape[0]
+        fetched_first = exchange_along(half[: depth // 2], 2, 1)
     else:
         half = lax.all_gather(half, "fsdp", axis=1, tiled=True)
 
@@ -307,12 +311,21 @@
     same = exchange_chips(by_chip)
     own_other = exchange(own[1:], "ctx", 1)
     if split_columns:
-        fetched, own_other, lengths = lax.optimization_barrier((fetched, own_other, lengths))
+        fetched_first, own_other, lengths, rest = lax.optimization_barrier(
+            (fetched_first, own_other, lengths, half[depth // 2 :])
+        )
+        fetched_second = exchange_along(rest, 2, 1)
+
+        def forward(rows):
+            part = depth // 4 + 16
+            rows = lax.dynamic_slice_in_dim(rows, core * (depth // 2 - part), part, 0)
+            return exchange_along(rows, 1, 2)
+
+        third_first = forward(fetched_first)
+        fetched_second, third_first = lax.optimization_barrier((fetched_second, third_first))
+        fetched = jnp.concatenate([fetched_first, fetched_second], axis=0)
         passed = exchange_in_plane(fetched)
-        depth = half.shape[0]
-        part = depth // 2 + 16
-        third = lax.dynamic_slice_in_dim(fetched, core * (depth - part), part, 0)
-        third = exchange_along(third, 1, 2)
+        third = jnp.concatenate([third_first, forward(fetched_second)], axis=0)
     same, own_other = lax.optimization_barrier((same, own_other))
     other = exchange(stack_keys_and_values(same), "ctx", 1)
     same = [own, *same]

time: 30.7 us -> 35 us (1.14)
  starting transfers between devices: 15.3 us -> 18.7 us
  waiting for transfers between devices: 9.1 us -> 9.77 us
    ppermute x2 -> x4, starting transfers between devices: 5.43 us -> 8.77 us  [exchange_along(): return lax.ppermute(array, ('ctx', 'fsdp'), pairs)]
    ppermute x2 -> x4, waiting for transfers between devices: 1.42 us -> 2.9 us  [exchange_along(): return lax.ppermute(array, ('ctx', 'fsdp'), pairs)]
    ppermute x12, waiting for transfers between devices: 6.67 us -> 5.85 us  [exchange(): return lax.ppermute(array, axis, [(i, i ^ flip) for i in range(size)])]
  transfers between devices with their start and end apart: 16 -> 18, of which waited for: 9 -> 7; matrix products, arithmetic and copies ran while one was open for 0% -> 0% of each run, Pallas kernels for 10% -> 9%
where the time goes in v15:
time: 35 us; the launch traced here: 34.9 us
  starting transfers between devices  18.7 us (53%)
  waiting for transfers between devices  9.77 us (28%)
  Pallas kernels  5.45 us (16%)
  between operations  0.82 us (2%)
    ppermute x4, starting transfers between devices, exchange_along(): return lax.ppermute(array, ('ctx', 'fsdp'), pairs)  8.77 us
    ppermute x12, starting transfers between devices, exchange(): return lax.ppermute(array, axis, [(i, i ^ flip) for i in range(size)])  7.77 us
    ppermute x12, waiting for transfers between devices, exchange(): return lax.ppermute(array, axis, [(i, i ^ flip) for i in range(size)])  5.85 us
    ppermute x4, waiting for transfers between devices, exchange_along(): return lax.ppermute(array, ('ctx', 'fsdp'), pairs)  2.9 us
    pallas_call x1, Pallas kernels, attend(): pl.pallas_call(functools.partial(attention_kernel, groups), out_shape=[pl...  2.2 us
    ppermute x2, starting transfers between devices, exchange_in_plane(): lax.ppermute(array, 'ctx', [(i, i ^ (4 if i % 2 else 2)) for i in range(c...  2.16 us
    pallas_call x1, Pallas kernels, copy_in(): pl.pallas_call(functools.partial(copy_in_kernel, by_parity), out_shape=[p...  1.24 us
    pallas_call x1, Pallas kernels, project_third(): pl.pallas_call(project_third_kernel, out_shape=jax.ShapeDtypeStruct((1, f...  1.03 us
  transfers between devices with their start and end apart: 18, of which 7 were waited for; matrix products, arithmetic and copies ran while one was open for 0% of the time, Pallas kernels for 9%

profile of v15, /device:TPU:0, one launch (start us, length us, event | category | flops | bytes accessed | tf_op | source)
XLA Modules:
  0.0 34.9 jit_solution(5687578379642062871)
XLA Ops:
  0.0 1.2 %copy_in.1 = (bf16[3,128,768]{2,1,0:T(8,128)(2,1)S(1)}, bf16[384,384]{1,0:T(8,128)(2,1)S(1)}) custom-call(bf16[1,128,768]{2,1,0:T(8,128)(2,1)} %query_ref.1, bf16[1,128,768]{2,1,0:T(8,128)(2,1)} %key_ref.1, bf16[1,128,768]{2,1,0:T(8,128)(2,1)} %value_ref.1, bf16[768,384]{1,0:T(8,128)(2,1)} %refs_4_.1), custom_call_target="tpu_custom_call" | custom-call | tf_op jit(solution)/shard_map/copy_in/pallas_call | solution.py:45
  1.3 4.1 %collective-permute-start = (bf16[192,384]{1,0:T(8,128)(2,1)S(1)}, bf16[192,384]{1,0:T(8,128)(2,1)S(1)}, u32[]{:S(2)}, u32[]{:S(2)}) collective-permute-start(bf16[192,384]{1,0:T(8,128)(2,1)S(1)} %get-tuple-element.66), channel_id=1, source_target_pairs={{0,2},{1,3},{2,0},{3,1},{4,5},{5,4},{6,7},{7,6},{8,10},{9,11},{10,... | collective-permute-start | bytes 442376 | tf_op jit(solution)/shard_map/ppermute | solution.py:298
  5.4 0.2 turn_heads.1
  5.7 0.1 collective-permute-start.1
  5.7 1.6 %collective-permute-start.2 = (bf16[3,192,128]{2,1,0:T(8,128)(2,1)S(1)}, bf16[3,192,128]{2,1,0:T(8,128)(2,1)S(1)}, u32[]{:S(2)}, u32[]{:S(2)}) collective-permute-start(bf16[3,192,128]{2,1,0:T(8,128)(2,1)S(1)} %get-tuple-element.39), channel_id=1, source_target_pairs={{0,8},{4,12},{8,0},{12,4},{16,24},{20,28},{24,16},{28,20},{1,9},{5... | collective-permute-start | bytes 442376 | tf_op jit(solution)/shard_map/ppermute | solution.py:288
  7.3 1.5 %collective-permute-start.3 = (bf16[3,192,128]{2,1,0:T(8,128)(2,1)S(1)}, bf16[3,192,128]{2,1,0:T(8,128)(2,1)S(1)}, u32[]{:S(2)}, u32[]{:S(2)}) collective-permute-start(bf16[3,192,128]{2,1,0:T(8,128)(2,1)S(1)} %get-tuple-element.40), channel_id=1, source_target_pairs={{0,16},{4,20},{8,24},{12,28},{16,0},{20,4},{24,8},{28,12},{1,17},{... | collective-permute-start | bytes 442376 | tf_op jit(solution)/shard_map/ppermute | solution.py:288
  8.8 0.5 %collective-permute-start.4 = (bf16[3,192,128]{2,1,0:T(8,128)(2,1)S(1)}, bf16[3,192,128]{2,1,0:T(8,128)(2,1)S(1)}, u32[]{:S(2)}, u32[]{:S(2)}) collective-permute-start(bf16[3,192,128]{2,1,0:T(8,128)(2,1)S(1)} %get-tuple-element.41), channel_id=1, source_target_pairs={{0,24},{4,28},{8,16},{12,20},{16,8},{20,12},{24,0},{28,4},{1,25},{... | collective-permute-start | bytes 442376 | tf_op jit(solution)/shard_map/ppermute | solution.py:288
  9.9 0.0 collective-permute-done.1.refs_4_
  10.0 0.0 collective-permute-done
  10.0 1.6 %collective-permute-start.8 = (bf16[192,384]{1,0:T(8,128)(2,1)S(1)}, bf16[192,384]{1,0:T(8,128)(2,1)S(1)}, u32[]{:S(2)}, u32[]{:S(2)}) collective-permute-start(bf16[192,384]{1,0:T(8,128)(2,1)S(1)} %get-tuple-element.51), channel_id=1, source_target_pairs={{0,2},{1,3},{2,0},{3,1},{4,5},{5,4},{6,7},{7,6},{8,10},{9,11},{10,... | collective-permute-start | bytes 442376 | tf_op jit(solution)/shard_map/ppermute | solution.py:298
  11.5 3.0 %collective-permute-start.9 = (bf16[112,384]{1,0:T(8,128)(2,1)S(1)}, bf16[112,384]{1,0:T(8,128)(2,1)S(1)}, u32[]{:S(2)}, u32[]{:S(2)}) collective-permute-start(bf16[112,384]{1,0:T(8,128)(2,1)S(1)} %constant_dynamic-slice_fusion.1), channel_id=1, source_target_pairs={{0,1},{1,0},{2,3},{3,2},{4,6},{5,7},{6,4},{7,5},{8,9},{9,8},{10,11... | collective-permute-start | bytes 258056 | tf_op jit(solution)/shard_map/ppermute | solution.py:298
  14.6 0.0 collective-permute-done.2.refs_0_.refs_1_
  14.6 1.8 %collective-permute-done.3.refs_1_.refs_2_ = bf16[3,192,128]{2,1,0:T(8,128)(2,1)S(1)} collective-permute-done((bf16[3,192,128]{2,1,0:T(8,128)(2,1)S(1)}, bf16[3,192,128]{2,1,0:T(8,128)(2,1)S(1)}, u32[]{:S(2)}, u32[]{:S(2)}) %collective-permute-start.3) | collective-permute-done | bytes 147488 | tf_op jit(solution)/shard_map/ppermute | solution.py:288
  16.4 0.0 collective-permute-done.4.refs_2_.refs_3_
  16.4 0.1 collective-permute-start.5
  16.5 0.5 %collective-permute-done.9 = bf16[112,384]{1,0:T(8,128)(2,1)S(1)} collective-permute-done((bf16[112,384]{1,0:T(8,128)(2,1)S(1)}, bf16[112,384]{1,0:T(8,128)(2,1)S(1)}, u32[]{:S(2)}, u32[]{:S(2)}) %collective-permute-start.9) | collective-permute-done | bytes 86048 | tf_op jit(solution)/shard_map/ppermute | solution.py:298
  17.1 2.4 %collective-permute-done.8 = bf16[192,384]{1,0:T(8,128)(2,1)S(1)} collective-permute-done((bf16[192,384]{1,0:T(8,128)(2,1)S(1)}, bf16[192,384]{1,0:T(8,128)(2,1)S(1)}, u32[]{:S(2)}, u32[]{:S(2)}) %collective-permute-start.8) | collective-permute-done | bytes 147488 | tf_op jit(solution)/shard_map/ppermute | solution.py:298
  19.4 0.1 collective-permute-start.12
  19.5 1.6 %collective-permute-start.10 = (bf16[384,384]{1,0:T(8,128)(2,1)S(1)}, bf16[384,384]{1,0:T(8,128)(2,1)S(1)}, u32[]{:S(2)}, u32[]{:S(2)}) collective-permute-start(bf16[384,384]{1,0:T(8,128)(2,1)S(1)} %constant_dynamic-update-slice_fusion.refs_5_), channel_id=1, source_target_pairs={{0,8},{4,20},{8,0},{12,28},{16,24},{20,4},{24,16},{28,12},{1,9},{5... | collective-permute-start | bytes 884744 | tf_op jit(solution)/shard_map/ppermute | solution.py:294
  21.1 0.0 copy-start
  21.1 0.0 collective-permute-done.5.refs_5_
  21.1 2.2 %attend_two_heads.1 = (bf16[192,128]{1,0:T(8,128)(2,1)S(1)}, bf16[192,128]{1,0:T(8,128)(2,1)S(1)}, bf16[192,128]{1,0:T(8,128)(2,1)S(1)}, bf16[192,128]{1,0:T(8,128)(2,1)S(1)}) custom-call(s32[8,128]{1,0:T(8,128)S(1)} %broadcast_in_dim.2.lengths_ref, bf16[3,192,128]{2,1,0:T(8,128)(2,1)S(1)} %get-tuple-element.37.refs_0_, ...), custom_call_target="tpu_custom_call" | custom-call | flops 1610612736 | tf_op jit(solution)/shard_map/attend_two_heads/pallas_call | solution.py:154
  23.3 1.6 %collective-permute-start.11 = (bf16[192,128]{1,0:T(8,128)(2,1)S(1)}, bf16[192,128]{1,0:T(8,128)(2,1)S(1)}, u32[]{:S(2)}, u32[]{:S(2)}) collective-permute-start(bf16[192,128]{1,0:T(8,128)(2,1)S(1)} %get-tuple-element.55), channel_id=1, source_target_pairs={{0,24},{4,28},{8,16},{12,20},{16,8},{20,12},{24,0},{28,4},{1,25},{... | collective-permute-start | bytes 147464 | tf_op jit(solution)/shard_map/ppermute | solution.py:288
  24.9 1.5 %collective-permute-start.6 = (bf16[192,128]{1,0:T(8,128)(2,1)S(1)}, bf16[192,128]{1,0:T(8,128)(2,1)S(1)}, u32[]{:S(2)}, u32[]{:S(2)}) collective-permute-start(bf16[192,128]{1,0:T(8,128)(2,1)S(1)} %get-tuple-element.48), channel_id=1, source_target_pairs={{0,8},{4,12},{8,0},{12,4},{16,24},{20,28},{24,16},{28,20},{1,9},{5... | collective-permute-start | bytes 147464 | tf_op jit(solution)/shard_map/ppermute | solution.py:288
  26.4 0.5 %collective-permute-start.7 = (bf16[192,128]{1,0:T(8,128)(2,1)S(1)}, bf16[192,128]{1,0:T(8,128)(2,1)S(1)}, u32[]{:S(2)}, u32[]{:S(2)}) collective-permute-start(bf16[192,128]{1,0:T(8,128)(2,1)S(1)} %get-tuple-element.49), channel_id=1, source_target_pairs={{0,16},{4,20},{8,24},{12,28},{16,0},{20,4},{24,8},{28,12},{1,17},{... | collective-permute-start | bytes 147464 | tf_op jit(solution)/shard_map/ppermute | solution.py:288
  26.9 0.0 collective-permute-done.12
  26.9 0.6 %collective-permute-start.16 = (bf16[224,384]{1,0:T(8,128)(2,1)S(1)}, bf16[224,384]{1,0:T(8,128)(2,1)S(1)}, u32[]{:S(2)}, u32[]{:S(2)}) collective-permute-start(bf16[224,384]{1,0:T(8,128)(2,1)S(1)} %constant_dynamic-update-slice_fusion.2.refs_0_), channel_id=1, source_target_pairs={{0,8},{4,20},{8,0},{12,28},{16,24},{20,4},{24,16},{28,12},{1,9},{5... | collective-permute-start | bytes 516104 | tf_op jit(solution)/shard_map/ppermute | solution.py:294
  27.5 1.5 %collective-permute-done.11.refs_3_ = bf16[192,128]{1,0:T(8,128)(2,1)S(1)} collective-permute-done((bf16[192,128]{1,0:T(8,128)(2,1)S(1)}, bf16[192,128]{1,0:T(8,128)(2,1)S(1)}, u32[]{:S(2)}, u32[]{:S(2)}) %collective-permute-start.11) | collective-permute-done | bytes 49184 | tf_op jit(solution)/shard_map/ppermute | solution.py:288
  29.0 0.0 collective-permute-done.6.refs_1_
  29.0 1.9 %collective-permute-done.7.refs_2_ = bf16[192,128]{1,0:T(8,128)(2,1)S(1)} collective-permute-done((bf16[192,128]{1,0:T(8,128)(2,1)S(1)}, bf16[192,128]{1,0:T(8,128)(2,1)S(1)}, u32[]{:S(2)}, u32[]{:S(2)}) %collective-permute-start.7) | collective-permute-done | bytes 49184 | tf_op jit(solution)/shard_map/ppermute | solution.py:288
  30.8 0.0 collective-permute-done.10.refs_6_
  30.8 0.0 collective-permute-start.15
  30.8 0.5 %collective-permute-start.13 = (bf16[384,384]{1,0:T(8,128)(2,1)S(1)}, bf16[384,384]{1,0:T(8,128)(2,1)S(1)}, u32[]{:S(2)}, u32[]{:S(2)}) collective-permute-start(bf16[384,384]{1,0:T(8,128)(2,1)S(1)} %constant_dynamic-update-slice_fusion.refs_5_), channel_id=1, source_target_pairs={{0,4},{4,0},{8,12},{12,8},{16,20},{20,16},{24,28},{28,24},{1,5},{5... | collective-permute-start | bytes 884744 | tf_op jit(solution)/shard_map/ppermute | solution.py:288
  31.4 0.0 collective-permute-start.14
  31.4 1.0 %collective-permute-done.16.refs_1_ = bf16[224,384]{1,0:T(8,128)(2,1)S(1)} collective-permute-done((bf16[224,384]{1,0:T(8,128)(2,1)S(1)}, bf16[224,384]{1,0:T(8,128)(2,1)S(1)}, u32[]{:S(2)}, u32[]{:S(2)}) %collective-permute-start.16) | collective-permute-done | bytes 172064 | tf_op jit(solution)/shard_map/ppermute | solution.py:294
  32.4 0.0 collective-permute-start.17
  32.4 0.7 %collective-permute-done.14.refs_2_ = bf16[224,384]{1,0:T(8,128)(2,1)S(1)} collective-permute-done((bf16[224,384]{1,0:T(8,128)(2,1)S(1)}, bf16[224,384]{1,0:T(8,128)(2,1)S(1)}, u32[]{:S(2)}, u32[]{:S(2)}) %collective-permute-start.14) | collective-permute-done | bytes 172064 | tf_op jit(solution)/shard_map/ppermute | solution.py:288
  33.1 0.0 collective-permute-done.15.refs_8_
  33.1 0.0 collective-permute-done.13.refs_7_
  33.1 0.0 copy-done
  33.1 0.7 %project_near_shards.1 = (bf16[3,128,384]{2,1,0:T(8,128)(2,1)S(1)}, bf16[128,768]{1,0:T(8,128)(2,1)S(1)}) custom-call(bf16[192,128]{1,0:T(8,128)(2,1)S(1)} %get-tuple-element.47.refs_0_, bf16[192,128]{1,0:T(8,128)(2,1)S(1)} %collective-permute-done.6.refs_1_, bf16[192,128]{1,0:T(8,128)(2,1)S(1)} %collective-permute-done.7.refs_2_, ...), custom_call_target="tpu_custom_call" | custom-call | flops 226492416 | bytes 1769472 | tf_op jit(solution)/shard_map/project_near_shards/pallas_call | solution.py:251
  33.8 0.0 collective-permute-done.17.refs_3_
  33.8 1.0 %project_third_shard.1 = bf16[1,128,1536]{2,1,0:T(8,128)(2,1)} custom-call(bf16[3,128,384]{2,1,0:T(8,128)(2,1)S(1)} %get-tuple-element.62.blocks_ref, bf16[128,768]{1,0:T(8,128)(2,1)S(1)} %get-tuple-element.63.attention_ref, bf16[224,384]{1,0:T(8,128)(2,1)S(1)} %constant_dynamic-update-slice_fusion.2.refs_0_, ...), custom_call_target="tpu_custom_call" | custom-call | flops 75497472 | bytes 589824 | tf_op jit(solution)/shard_map/project_third_shard/pallas_call | solution.py:269
  (10 shorter events, 0.2 us)
Async XLA Ops:
  1.3 8.7 %collective-permute-start = (bf16[192,384]{1,0:T(8,128)(2,1)S(1)}, bf16[192,384]{1,0:T(8,128)(2,1)S(1)}, u32[]{:S(2)}, u32[]{:S(2)}) collective-permute-start(bf16[192,384]{1,0:T(8,128)(2,1)S(1)} %get-tuple-element.66), channel_id=1, source_target_pairs={{0,2},{1,3},{2,0},{3,1},{4,5},{5,4},{6,7},{7,6},{8,10},{9,11},{10,... | collective-permute-start | bytes 442376 | tf_op jit(solution)/shard_map/ppermute | solution.py:298
  5.7 4.3 %collective-permute-start.1 = (bf16[2,192,128]{2,1,0:T(8,128)(2,1)S(1)}, bf16[2,192,128]{2,1,0:T(8,128)(2,1)S(1)}, u32[]{:S(2)}, u32[]{:S(2)}) collective-permute-start(bf16[2,192,128]{2,1,0:T(8,128)(2,1)S(1)} %slice.10), channel_id=1, source_target_pairs={{0,4},{4,0},{8,12},{12,8},{16,20},{20,16},{24,28},{28,24},{1,5},{5... | collective-permute-start | bytes 294920 | tf_op jit(solution)/shard_map/ppermute | solution.py:288
  5.7 8.9 %collective-permute-start.2 = (bf16[3,192,128]{2,1,0:T(8,128)(2,1)S(1)}, bf16[3,192,128]{2,1,0:T(8,128)(2,1)S(1)}, u32[]{:S(2)}, u32[]{:S(2)}) collective-permute-start(bf16[3,192,128]{2,1,0:T(8,128)(2,1)S(1)} %get-tuple-element.39), channel_id=1, source_target_pairs={{0,8},{4,12},{8,0},{12,4},{16,24},{20,28},{24,16},{28,20},{1,9},{5... | collective-permute-start | bytes 442376 | tf_op jit(solution)/shard_map/ppermute | solution.py:288
  7.3 9.1 %collective-permute-start.3 = (bf16[3,192,128]{2,1,0:T(8,128)(2,1)S(1)}, bf16[3,192,128]{2,1,0:T(8,128)(2,1)S(1)}, u32[]{:S(2)}, u32[]{:S(2)}) collective-permute-start(bf16[3,192,128]{2,1,0:T(8,128)(2,1)S(1)} %get-tuple-element.40), channel_id=1, source_target_pairs={{0,16},{4,20},{8,24},{12,28},{16,0},{20,4},{24,8},{28,12},{1,17},{... | collective-permute-start | bytes 442376 | tf_op jit(solution)/shard_map/ppermute | solution.py:288
  8.8 7.6 %collective-permute-start.4 = (bf16[3,192,128]{2,1,0:T(8,128)(2,1)S(1)}, bf16[3,192,128]{2,1,0:T(8,128)(2,1)S(1)}, u32[]{:S(2)}, u32[]{:S(2)}) collective-permute-start(bf16[3,192,128]{2,1,0:T(8,128)(2,1)S(1)} %get-tuple-element.41), channel_id=1, source_target_pairs={{0,24},{4,28},{8,16},{12,20},{16,8},{20,12},{24,0},{28,4},{1,25},{... | collective-permute-start | bytes 442376 | tf_op jit(solution)/shard_map/ppermute | solution.py:288
  10.0 9.4 %collective-permute-start.8 = (bf16[192,384]{1,0:T(8,128)(2,1)S(1)}, bf16[192,384]{1,0:T(8,128)(2,1)S(1)}, u32[]{:S(2)}, u32[]{:S(2)}) collective-permute-start(bf16[192,384]{1,0:T(8,128)(2,1)S(1)} %get-tuple-element.51), channel_id=1, source_target_pairs={{0,2},{1,3},{2,0},{3,1},{4,5},{5,4},{6,7},{7,6},{8,10},{9,11},{10,... | collective-permute-start | bytes 442376 | tf_op jit(solution)/shard_map/ppermute | solution.py:298
  11.5 5.5 %collective-permute-start.9 = (bf16[112,384]{1,0:T(8,128)(2,1)S(1)}, bf16[112,384]{1,0:T(8,128)(2,1)S(1)}, u32[]{:S(2)}, u32[]{:S(2)}) collective-permute-start(bf16[112,384]{1,0:T(8,128)(2,1)S(1)} %constant_dynamic-slice_fusion.1), channel_id=1, source_target_pairs={{0,1},{1,0},{2,3},{3,2},{4,6},{5,7},{6,4},{7,5},{8,9},{9,8},{10,11... | collective-permute-start | bytes 258056 | tf_op jit(solution)/shard_map/ppermute | solution.py:298
  16.4 4.7 %collective-permute-start.5 = (bf16[3,2,192,128]{3,2,1,0:T(8,128)(2,1)S(1)}, bf16[3,2,192,128]{3,2,1,0:T(8,128)(2,1)S(1)}, u32[]{:S(2)}, u32[]{:S(2)}) collective-permute-start(bf16[3,2,192,128]{3,2,1,0:T(8,128)(2,1)S(1)} %stack_keys_and_values.1), channel_id=1, source_target_pairs={{0,4},{4,0},{8,12},{12,8},{16,20},{20,16},{24,28},{28,24},{1,5},{5... | collective-permute-start | bytes 884744 | tf_op jit(solution)/shard_map/ppermute | solution.py:288
  19.4 7.5 %collective-permute-start.12 = (bf16[112,384]{1,0:T(8,128)(2,1)S(1)}, bf16[112,384]{1,0:T(8,128)(2,1)S(1)}, u32[]{:S(2)}, u32[]{:S(2)}) collective-permute-start(bf16[112,384]{1,0:T(8,128)(2,1)S(1)} %constant_dynamic-slice_fusion), channel_id=1, source_target_pairs={{0,1},{1,0},{2,3},{3,2},{4,6},{5,7},{6,4},{7,5},{8,9},{9,8},{10,11... | collective-permute-start | bytes 258056 | tf_op jit(solution)/shard_map/ppermute | solution.py:298
  19.5 11.3 %collective-permute-start.10 = (bf16[384,384]{1,0:T(8,128)(2,1)S(1)}, bf16[384,384]{1,0:T(8,128)(2,1)S(1)}, u32[]{:S(2)}, u32[]{:S(2)}) collective-permute-start(bf16[384,384]{1,0:T(8,128)(2,1)S(1)} %constant_dynamic-update-slice_fusion.refs_5_), channel_id=1, source_target_pairs={{0,8},{4,20},{8,0},{12,28},{16,24},{20,4},{24,16},{28,12},{1,9},{5... | collective-permute-start | bytes 884744 | tf_op jit(solution)/shard_map/ppermute | solution.py:294
  21.1 12.0 %copy-start = (bf16[768,384]{1,0:T(8,128)(2,1)S(1)}, bf16[768,384]{1,0:T(8,128)(2,1)}, u32[]{:S(2)}) copy-start(bf16[768,384]{1,0:T(8,128)(2,1)} %refs_4_.1) | copy-start | bytes 1769476
  23.3 5.6 %collective-permute-start.11 = (bf16[192,128]{1,0:T(8,128)(2,1)S(1)}, bf16[192,128]{1,0:T(8,128)(2,1)S(1)}, u32[]{:S(2)}, u32[]{:S(2)}) collective-permute-start(bf16[192,128]{1,0:T(8,128)(2,1)S(1)} %get-tuple-element.55), channel_id=1, source_target_pairs={{0,24},{4,28},{8,16},{12,20},{16,8},{20,12},{24,0},{28,4},{1,25},{... | collective-permute-start | bytes 147464 | tf_op jit(solution)/shard_map/ppermute | solution.py:288
  24.9 4.1 %collective-permute-start.6 = (bf16[192,128]{1,0:T(8,128)(2,1)S(1)}, bf16[192,128]{1,0:T(8,128)(2,1)S(1)}, u32[]{:S(2)}, u32[]{:S(2)}) collective-permute-start(bf16[192,128]{1,0:T(8,128)(2,1)S(1)} %get-tuple-element.48), channel_id=1, source_target_pairs={{0,8},{4,12},{8,0},{12,4},{16,24},{20,28},{24,16},{28,20},{1,9},{5... | collective-permute-start | bytes 147464 | tf_op jit(solution)/shard_map/ppermute | solution.py:288
  26.4 4.4 %collective-permute-start.7 = (bf16[192,128]{1,0:T(8,128)(2,1)S(1)}, bf16[192,128]{1,0:T(8,128)(2,1)S(1)}, u32[]{:S(2)}, u32[]{:S(2)}) collective-permute-start(bf16[192,128]{1,0:T(8,128)(2,1)S(1)} %get-tuple-element.49), channel_id=1, source_target_pairs={{0,16},{4,20},{8,24},{12,28},{16,0},{20,4},{24,8},{28,12},{1,17},{... | collective-permute-start | bytes 147464 | tf_op jit(solution)/shard_map/ppermute | solution.py:288
  26.9 5.5 %collective-permute-start.16 = (bf16[224,384]{1,0:T(8,128)(2,1)S(1)}, bf16[224,384]{1,0:T(8,128)(2,1)S(1)}, u32[]{:S(2)}, u32[]{:S(2)}) collective-permute-start(bf16[224,384]{1,0:T(8,128)(2,1)S(1)} %constant_dynamic-update-slice_fusion.2.refs_0_), channel_id=1, source_target_pairs={{0,8},{4,20},{8,0},{12,28},{16,24},{20,4},{24,16},{28,12},{1,9},{5... | collective-permute-start | bytes 516104 | tf_op jit(solution)/shard_map/ppermute | solution.py:294
  30.8 2.3 %collective-permute-start.15 = (bf16[384,384]{1,0:T(8,128)(2,1)S(1)}, bf16[384,384]{1,0:T(8,128)(2,1)S(1)}, u32[]{:S(2)}, u32[]{:S(2)}) collective-permute-start(bf16[384,384]{1,0:T(8,128)(2,1)S(1)} %collective-permute-done.10.refs_6_), channel_id=1, source_target_pairs={{0,4},{4,0},{8,12},{12,8},{16,20},{20,16},{24,28},{28,24},{1,5},{5... | collective-permute-start | bytes 884744 | tf_op jit(solution)/shard_map/ppermute | solution.py:288
  30.8 2.3 %collective-permute-start.13 = (bf16[384,384]{1,0:T(8,128)(2,1)S(1)}, bf16[384,384]{1,0:T(8,128)(2,1)S(1)}, u32[]{:S(2)}, u32[]{:S(2)}) collective-permute-start(bf16[384,384]{1,0:T(8,128)(2,1)S(1)} %constant_dynamic-update-slice_fusion.refs_5_), channel_id=1, source_target_pairs={{0,4},{4,0},{8,12},{12,8},{16,20},{20,16},{24,28},{28,24},{1,5},{5... | collective-permute-start | bytes 884744 | tf_op jit(solution)/shard_map/ppermute | solution.py:288
  31.4 1.7 %collective-permute-start.14 = (bf16[224,384]{1,0:T(8,128)(2,1)S(1)}, bf16[224,384]{1,0:T(8,128)(2,1)S(1)}, u32[]{:S(2)}, u32[]{:S(2)}) collective-permute-start(bf16[224,384]{1,0:T(8,128)(2,1)S(1)} %constant_dynamic-update-slice_fusion.2.refs_0_), channel_id=1, source_target_pairs={{0,4},{4,0},{8,12},{12,8},{16,20},{20,16},{24,28},{28,24},{1,5},{5... | collective-permute-start | bytes 516104 | tf_op jit(solution)/shard_map/ppermute | solution.py:288
  32.4 1.5 %collective-permute-start.17 = (bf16[224,384]{1,0:T(8,128)(2,1)S(1)}, bf16[224,384]{1,0:T(8,128)(2,1)S(1)}, u32[]{:S(2)}, u32[]{:S(2)}) collective-permute-start(bf16[224,384]{1,0:T(8,128)(2,1)S(1)} %collective-permute-done.16.refs_1_), channel_id=1, source_target_pairs={{0,4},{4,0},{8,12},{12,8},{16,20},{20,16},{24,28},{28,24},{1,5},{5... | collective-permute-start | bytes 516104 | tf_op jit(solution)/shard_map/ppermute | solution.py:288

commit v16 on v14

--- a/solution.py
+++ b/solution.py
@@ -110,9 +110,10 @@
 
     def score(head, flips):
         rows = slice(head * head_size, (head + 1) * head_size)
-        query = [jnp.concatenate([same[flip // 2][0, rows, :], ones], axis=0) for flip in flips]
-        return jnp.dot(keys[head], jnp.concatenate(query, axis=1), preferred_element_type=jnp.float32)
-
+        query = jnp.concatenate([jnp.concatenate([same[flip // 2][0, rows, :], ones], axis=0) for flip in flips], axis=1)
+        return [jnp.dot(keys[head, part, :], query, preferred_element_type=jnp.float32) for part in parts]
+
+    parts = [slice(first, first + keys.shape[1] // 4) for first in range(0, keys.shape[1], keys.shape[1] // 4)]
     chunks = [(head, flips) for head in range(2) for flips in (FLIPS[:2], FLIPS[2:])]
     prepare(0)
     later = score(*chunks[0])
@@ -121,9 +122,11 @@
         scores = later
         if at + 1 < len(chunks):
             later = score(*chunks[at + 1])
-        row_max = jnp.max(scores, axis=0, keepdims=True) * scale
-        probs = jnp.exp2(scores * scale - row_max).astype(jnp.bfloat16)
-        mixed = jnp.dot(values[head], probs, preferred_element_type=jnp.float32)
+        row_max = functools.reduce(jnp.maximum, (jnp.max(part, axis=0, keepdims=True) for part in scores)) * scale
+        mixed = jnp.zeros((values.shape[1], scores[0].shape[1]), jnp.float32)
+        for part, part_scores in zip(parts, scores):
+            probs = jnp.exp2(part_scores * scale - row_max).astype(jnp.bfloat16)
+            mixed = mixed + jnp.dot(values[head, :, part], probs, preferred_element_type=jnp.float32)
         mixed = (mixed[:head_size] / mixed[head_size : head_size + 1]).astype(jnp.bfloat16)
         for half, flip in enumerate(flips):
             outs[flip // 2][head * head_size : (head + 1) * head_size, :] = mixed[:, half * block : (half + 1) * block]

time: 30.7 us -> 30.4 us (level)
  transfers between devices with their start and end apart: 16 -> 16, of which waited for: 9 -> 9; matrix products, arithmetic and copies ran while one was open for 0% -> 0% of each run, Pallas kernels for 10% -> 9%
where the time goes in v16:
time: 30.4 us; the launch traced here: 30.3 us
  starting transfers between devices  15.3 us (50%)
  waiting for transfers between devices  9.09 us (30%)
  Pallas kernels  5.16 us (17%)
  between operations  0.74 us (2%)
    ppermute x12, starting transfers between devices, exchange(): return lax.ppermute(array, axis, [(i, i ^ flip) for i in range(size)])  7.87 us
    ppermute x12, waiting for transfers between devices, exchange(): return lax.ppermute(array, axis, [(i, i ^ flip) for i in range(size)])  6.64 us
    ppermute x2, starting transfers between devices, exchange_along(): return lax.ppermute(array, ('ctx', 'fsdp'), pairs)  5.43 us
    ppermute x2, starting transfers between devices, exchange_in_plane(): lax.ppermute(array, 'ctx', [(i, i ^ (4 if i % 2 else 2)) for i in range(c...  1.97 us
    pallas_call x1, Pallas kernels, attend(): pl.pallas_call(functools.partial(attention_kernel, groups), out_shape=[pl...  1.91 us
    ppermute x2, waiting for transfers between devices, exchange_along(): return lax.ppermute(array, ('ctx', 'fsdp'), pairs)  1.42 us
    pallas_call x1, Pallas kernels, copy_in(): pl.pallas_call(functools.partial(copy_in_kernel, by_parity), out_shape=[p...  1.24 us
    ppermute x2, waiting for transfers between devices, exchange_in_plane(): lax.ppermute(array, 'ctx', [(i, i ^ (4 if i % 2 else 2)) for i in range(c...  1.02 us
  transfers between devices with their start and end apart: 16, of which 9 were waited for; matrix products, arithmetic and copies ran while one was open for 0% of the time, Pallas kernels for 9%

profile of v16, /device:TPU:0, one launch (start us, length us, event | category | flops | bytes accessed | tf_op | source)
XLA Modules:
  0.0 30.3 jit_solution(5098751043401924074)
XLA Ops:
  0.0 1.2 %copy_in.1 = (bf16[3,128,768]{2,1,0:T(8,128)(2,1)S(1)}, bf16[384,384]{1,0:T(8,128)(2,1)S(1)}) custom-call(bf16[1,128,768]{2,1,0:T(8,128)(2,1)} %query_ref.1, bf16[1,128,768]{2,1,0:T(8,128)(2,1)} %key_ref.1, bf16[1,128,768]{2,1,0:T(8,128)(2,1)} %value_ref.1, bf16[768,384]{1,0:T(8,128)(2,1)} %refs_4_.1), custom_call_target="tpu_custom_call" | custom-call | tf_op jit(solution)/shard_map/copy_in/pallas_call | solution.py:45
  1.2 4.1 %collective-permute-start = (bf16[384,384]{1,0:T(8,128)(2,1)S(1)}, bf16[384,384]{1,0:T(8,128)(2,1)S(1)}, u32[]{:S(2)}, u32[]{:S(2)}) collective-permute-start(bf16[384,384]{1,0:T(8,128)(2,1)S(1)} %get-tuple-element.32), channel_id=1, source_target_pairs={{0,2},{1,3},{2,0},{3,1},{4,5},{5,4},{6,7},{7,6},{8,10},{9,11},{10,... | collective-permute-start | bytes 884744 | tf_op jit(solution)/shard_map/ppermute | solution.py:298
  5.3 0.2 turn_heads.1
  5.6 1.6 %collective-permute-start.2 = (bf16[3,192,128]{2,1,0:T(8,128)(2,1)S(1)}, bf16[3,192,128]{2,1,0:T(8,128)(2,1)S(1)}, u32[]{:S(2)}, u32[]{:S(2)}) collective-permute-start(bf16[3,192,128]{2,1,0:T(8,128)(2,1)S(1)} %get-tuple-element.36), channel_id=1, source_target_pairs={{0,8},{4,12},{8,0},{12,4},{16,24},{20,28},{24,16},{28,20},{1,9},{5... | collective-permute-start | bytes 442376 | tf_op jit(solution)/shard_map/ppermute | solution.py:288
  7.2 1.5 %collective-permute-start.3 = (bf16[3,192,128]{2,1,0:T(8,128)(2,1)S(1)}, bf16[3,192,128]{2,1,0:T(8,128)(2,1)S(1)}, u32[]{:S(2)}, u32[]{:S(2)}) collective-permute-start(bf16[3,192,128]{2,1,0:T(8,128)(2,1)S(1)} %get-tuple-element.37), channel_id=1, source_target_pairs={{0,16},{4,20},{8,24},{12,28},{16,0},{20,4},{24,8},{28,12},{1,17},{... | collective-permute-start | bytes 442376 | tf_op jit(solution)/shard_map/ppermute | solution.py:288
  8.7 0.5 %collective-permute-start.4 = (bf16[3,192,128]{2,1,0:T(8,128)(2,1)S(1)}, bf16[3,192,128]{2,1,0:T(8,128)(2,1)S(1)}, u32[]{:S(2)}, u32[]{:S(2)}) collective-permute-start(bf16[3,192,128]{2,1,0:T(8,128)(2,1)S(1)} %get-tuple-element.38), channel_id=1, source_target_pairs={{0,24},{4,28},{8,16},{12,20},{16,8},{20,12},{24,0},{28,4},{1,25},{... | collective-permute-start | bytes 442376 | tf_op jit(solution)/shard_map/ppermute | solution.py:288
  9.2 0.1 collective-permute-start.1
  9.9 0.6 %collective-permute-done.1.refs_4_ = bf16[2,192,128]{2,1,0:T(8,128)(2,1)S(1)} collective-permute-done((bf16[2,192,128]{2,1,0:T(8,128)(2,1)S(1)}, bf16[2,192,128]{2,1,0:T(8,128)(2,1)S(1)}, u32[]{:S(2)}, u32[]{:S(2)}) %collective-permute-start.1) | collective-permute-done | bytes 98336 | tf_op jit(solution)/shard_map/ppermute | solution.py:288
  10.5 1.4 %collective-permute-done.refs_5_ = bf16[384,384]{1,0:T(8,128)(2,1)S(1)} collective-permute-done((bf16[384,384]{1,0:T(8,128)(2,1)S(1)}, bf16[384,384]{1,0:T(8,128)(2,1)S(1)}, u32[]{:S(2)}, u32[]{:S(2)}) %collective-permute-start) | collective-permute-done | bytes 294944 | tf_op jit(solution)/shard_map/ppermute | solution.py:298
  12.0 0.4 %collective-permute-done.2.refs_0_.refs_1_ = bf16[3,192,128]{2,1,0:T(8,128)(2,1)S(1)} collective-permute-done((bf16[3,192,128]{2,1,0:T(8,128)(2,1)S(1)}, bf16[3,192,128]{2,1,0:T(8,128)(2,1)S(1)}, u32[]{:S(2)}, u32[]{:S(2)}) %collective-permute-start.2) | collective-permute-done | bytes 147488 | tf_op jit(solution)/shard_map/ppermute | solution.py:288
  12.4 2.8 %collective-permute-done.3.refs_1_.refs_2_ = bf16[3,192,128]{2,1,0:T(8,128)(2,1)S(1)} collective-permute-done((bf16[3,192,128]{2,1,0:T(8,128)(2,1)S(1)}, bf16[3,192,128]{2,1,0:T(8,128)(2,1)S(1)}, u32[]{:S(2)}, u32[]{:S(2)}) %collective-permute-start.3) | collective-permute-done | bytes 147488 | tf_op jit(solution)/shard_map/ppermute | solution.py:288
  15.2 0.0 collective-permute-done.4.refs_2_.refs_3_
  15.2 0.1 collective-permute-start.5
  15.3 0.5 %collective-permute-start.8 = (bf16[384,384]{1,0:T(8,128)(2,1)S(1)}, bf16[384,384]{1,0:T(8,128)(2,1)S(1)}, u32[]{:S(2)}, u32[]{:S(2)}) collective-permute-start(bf16[384,384]{1,0:T(8,128)(2,1)S(1)} %collective-permute-done.refs_5_), channel_id=1, source_target_pairs={{0,8},{4,20},{8,0},{12,28},{16,24},{20,4},{24,16},{28,12},{1,9},{5... | collective-permute-start | bytes 884744 | tf_op jit(solution)/shard_map/ppermute | solution.py:294
  15.8 0.0 copy-start
  15.8 1.3 %collective-permute-start.10 = (bf16[208,384]{1,0:T(8,128)(2,1)S(1)}, bf16[208,384]{1,0:T(8,128)(2,1)S(1)}, u32[]{:S(2)}, u32[]{:S(2)}) collective-permute-start(bf16[208,384]{1,0:T(8,128)(2,1)S(1)} %constant_dynamic-slice_fusion), channel_id=1, source_target_pairs={{0,1},{1,0},{2,3},{3,2},{4,6},{5,7},{6,4},{7,5},{8,9},{9,8},{10,11... | collective-permute-start | bytes 479240 | tf_op jit(solution)/shard_map/ppermute | solution.py:298
  17.1 0.0 collective-permute-done.5.refs_5_
  17.1 1.9 %attend_two_heads.1 = (bf16[192,128]{1,0:T(8,128)(2,1)S(1)}, bf16[192,128]{1,0:T(8,128)(2,1)S(1)}, bf16[192,128]{1,0:T(8,128)(2,1)S(1)}, bf16[192,128]{1,0:T(8,128)(2,1)S(1)}) custom-call(s32[8,128]{1,0:T(8,128)S(1)} %broadcast_in_dim.2.lengths_ref, bf16[3,192,128]{2,1,0:T(8,128)(2,1)S(1)} %get-tuple-element.34.refs_0_, ...), custom_call_target="tpu_custom_call" | custom-call | flops 1610612736 | tf_op jit(solution)/shard_map/attend_two_heads/pallas_call | solution.py:157
  19.0 1.6 %collective-permute-start.6 = (bf16[192,128]{1,0:T(8,128)(2,1)S(1)}, bf16[192,128]{1,0:T(8,128)(2,1)S(1)}, u32[]{:S(2)}, u32[]{:S(2)}) collective-permute-start(bf16[192,128]{1,0:T(8,128)(2,1)S(1)} %get-tuple-element.45), channel_id=1, source_target_pairs={{0,8},{4,12},{8,0},{12,4},{16,24},{20,28},{24,16},{28,20},{1,9},{5... | collective-permute-start | bytes 147464 | tf_op jit(solution)/shard_map/ppermute | solution.py:288
  20.6 0.7 %collective-permute-start.7 = (bf16[192,128]{1,0:T(8,128)(2,1)S(1)}, bf16[192,128]{1,0:T(8,128)(2,1)S(1)}, u32[]{:S(2)}, u32[]{:S(2)}) collective-permute-start(bf16[192,128]{1,0:T(8,128)(2,1)S(1)} %get-tuple-element.46), channel_id=1, source_target_pairs={{0,16},{4,20},{8,24},{12,28},{16,0},{20,4},{24,8},{28,12},{1,17},{... | collective-permute-start | bytes 147464 | tf_op jit(solution)/shard_map/ppermute | solution.py:288
  21.3 1.3 %collective-permute-start.9 = (bf16[192,128]{1,0:T(8,128)(2,1)S(1)}, bf16[192,128]{1,0:T(8,128)(2,1)S(1)}, u32[]{:S(2)}, u32[]{:S(2)}) collective-permute-start(bf16[192,128]{1,0:T(8,128)(2,1)S(1)} %get-tuple-element.50), channel_id=1, source_target_pairs={{0,24},{4,28},{8,16},{12,20},{16,8},{20,12},{24,0},{28,4},{1,25},{... | collective-permute-start | bytes 147464 | tf_op jit(solution)/shard_map/ppermute | solution.py:288
  22.6 0.0 collective-permute-done.10.refs_0_
  22.6 1.5 %collective-permute-start.14 = (bf16[208,384]{1,0:T(8,128)(2,1)S(1)}, bf16[208,384]{1,0:T(8,128)(2,1)S(1)}, u32[]{:S(2)}, u32[]{:S(2)}) collective-permute-start(bf16[208,384]{1,0:T(8,128)(2,1)S(1)} %collective-permute-done.10.refs_0_), channel_id=1, source_target_pairs={{0,8},{4,20},{8,0},{12,28},{16,24},{20,4},{24,16},{28,12},{1,9},{5... | collective-permute-start | bytes 479240 | tf_op jit(solution)/shard_map/ppermute | solution.py:294
  24.1 0.0 collective-permute-done.8.refs_6_
  24.1 0.0 collective-permute-done.6.refs_1_
  24.1 0.6 %collective-permute-done.7.refs_2_ = bf16[192,128]{1,0:T(8,128)(2,1)S(1)} collective-permute-done((bf16[192,128]{1,0:T(8,128)(2,1)S(1)}, bf16[192,128]{1,0:T(8,128)(2,1)S(1)}, u32[]{:S(2)}, u32[]{:S(2)}) %collective-permute-start.7) | collective-permute-done | bytes 49184 | tf_op jit(solution)/shard_map/ppermute | solution.py:288
  24.7 0.0 collective-permute-start.13
  24.7 1.6 %collective-permute-done.9.refs_3_ = bf16[192,128]{1,0:T(8,128)(2,1)S(1)} collective-permute-done((bf16[192,128]{1,0:T(8,128)(2,1)S(1)}, bf16[192,128]{1,0:T(8,128)(2,1)S(1)}, u32[]{:S(2)}, u32[]{:S(2)}) %collective-permute-start.9) | collective-permute-done | bytes 49184 | tf_op jit(solution)/shard_map/ppermute | solution.py:288
  26.3 0.0 collective-permute-start.11
  26.3 0.5 %collective-permute-start.12 = (bf16[208,384]{1,0:T(8,128)(2,1)S(1)}, bf16[208,384]{1,0:T(8,128)(2,1)S(1)}, u32[]{:S(2)}, u32[]{:S(2)}) collective-permute-start(bf16[208,384]{1,0:T(8,128)(2,1)S(1)} %collective-permute-done.10.refs_0_), channel_id=1, source_target_pairs={{0,4},{4,0},{8,12},{12,8},{16,20},{20,16},{24,28},{28,24},{1,5},{5... | collective-permute-start | bytes 479240 | tf_op jit(solution)/shard_map/ppermute | solution.py:288
  26.8 1.0 %collective-permute-done.14.refs_1_ = bf16[208,384]{1,0:T(8,128)(2,1)S(1)} collective-permute-done((bf16[208,384]{1,0:T(8,128)(2,1)S(1)}, bf16[208,384]{1,0:T(8,128)(2,1)S(1)}, u32[]{:S(2)}, u32[]{:S(2)}) %collective-permute-start.14) | collective-permute-done | bytes 159776 | tf_op jit(solution)/shard_map/ppermute | solution.py:294
  27.9 0.1 collective-permute-start.15
  28.0 0.2 collective-permute-done.12.refs_2_
  28.1 0.0 collective-permute-done.13.refs_8_
  28.2 0.0 collective-permute-done.11.refs_7_
  28.2 0.0 copy-done
  28.2 0.7 %project_near_shards.1 = (bf16[3,128,384]{2,1,0:T(8,128)(2,1)S(1)}, bf16[128,768]{1,0:T(8,128)(2,1)S(1)}) custom-call(bf16[192,128]{1,0:T(8,128)(2,1)S(1)} %get-tuple-element.44.refs_0_, bf16[192,128]{1,0:T(8,128)(2,1)S(1)} %collective-permute-done.6.refs_1_, bf16[192,128]{1,0:T(8,128)(2,1)S(1)} %collective-permute-done.7.refs_2_, ...), custom_call_target="tpu_custom_call" | custom-call | flops 226492416 | bytes 1769472 | tf_op jit(solution)/shard_map/project_near_shards/pallas_call | solution.py:251
  28.9 0.4 %collective-permute-done.15.refs_3_ = bf16[208,384]{1,0:T(8,128)(2,1)S(1)} collective-permute-done((bf16[208,384]{1,0:T(8,128)(2,1)S(1)}, bf16[208,384]{1,0:T(8,128)(2,1)S(1)}, u32[]{:S(2)}, u32[]{:S(2)}) %collective-permute-start.15) | collective-permute-done | bytes 159776 | tf_op jit(solution)/shard_map/ppermute | solution.py:288
  29.3 1.0 %project_third_shard.1 = bf16[1,128,1536]{2,1,0:T(8,128)(2,1)} custom-call(bf16[3,128,384]{2,1,0:T(8,128)(2,1)S(1)} %get-tuple-element.56.blocks_ref, bf16[128,768]{1,0:T(8,128)(2,1)S(1)} %get-tuple-element.57.attention_ref, bf16[208,384]{1,0:T(8,128)(2,1)S(1)} %collective-permute-done.10.refs_0_, bf16[208,384]{1,0:T(8,128)(2,1)S(1)} %collective-permute-done.14.refs_1_, ...), custom_call_target="tpu_custom_call" | custom-call | flops 75497472 | bytes 589824 | tf_op jit(solution)/shard_map/project_third_shard/pallas_call | solution.py:269
  (4 shorter events, 0.0 us)
Async XLA Ops:
  1.2 10.7 %collective-permute-start = (bf16[384,384]{1,0:T(8,128)(2,1)S(1)}, bf16[384,384]{1,0:T(8,128)(2,1)S(1)}, u32[]{:S(2)}, u32[]{:S(2)}) collective-permute-start(bf16[384,384]{1,0:T(8,128)(2,1)S(1)} %get-tuple-element.32), channel_id=1, source_target_pairs={{0,2},{1,3},{2,0},{3,1},{4,5},{5,4},{6,7},{7,6},{8,10},{9,11},{10,... | collective-permute-start | bytes 884744 | tf_op jit(solution)/shard_map/ppermute | solution.py:298
  5.6 6.8 %collective-permute-start.2 = (bf16[3,192,128]{2,1,0:T(8,128)(2,1)S(1)}, bf16[3,192,128]{2,1,0:T(8,128)(2,1)S(1)}, u32[]{:S(2)}, u32[]{:S(2)}) collective-permute-start(bf16[3,192,128]{2,1,0:T(8,128)(2,1)S(1)} %get-tuple-element.36), channel_id=1, source_target_pairs={{0,8},{4,12},{8,0},{12,4},{16,24},{20,28},{24,16},{28,20},{1,9},{5... | collective-permute-start | bytes 442376 | tf_op jit(solution)/shard_map/ppermute | solution.py:288
  7.2 8.0 %collective-permute-start.3 = (bf16[3,192,128]{2,1,0:T(8,128)(2,1)S(1)}, bf16[3,192,128]{2,1,0:T(8,128)(2,1)S(1)}, u32[]{:S(2)}, u32[]{:S(2)}) collective-permute-start(bf16[3,192,128]{2,1,0:T(8,128)(2,1)S(1)} %get-tuple-element.37), channel_id=1, source_target_pairs={{0,16},{4,20},{8,24},{12,28},{16,0},{20,4},{24,8},{28,12},{1,17},{... | collective-permute-start | bytes 442376 | tf_op jit(solution)/shard_map/ppermute | solution.py:288
  8.7 6.5 %collective-permute-start.4 = (bf16[3,192,128]{2,1,0:T(8,128)(2,1)S(1)}, bf16[3,192,128]{2,1,0:T(8,128)(2,1)S(1)}, u32[]{:S(2)}, u32[]{:S(2)}) collective-permute-start(bf16[3,192,128]{2,1,0:T(8,128)(2,1)S(1)} %get-tuple-element.38), channel_id=1, source_target_pairs={{0,24},{4,28},{8,16},{12,20},{16,8},{20,12},{24,0},{28,4},{1,25},{... | collective-permute-start | bytes 442376 | tf_op jit(solution)/shard_map/ppermute | solution.py:288
  9.2 1.4 %collective-permute-start.1 = (bf16[2,192,128]{2,1,0:T(8,128)(2,1)S(1)}, bf16[2,192,128]{2,1,0:T(8,128)(2,1)S(1)}, u32[]{:S(2)}, u32[]{:S(2)}) collective-permute-start(bf16[2,192,128]{2,1,0:T(8,128)(2,1)S(1)} %slice.3), channel_id=1, source_target_pairs={{0,4},{4,0},{8,12},{12,8},{16,20},{20,16},{24,28},{28,24},{1,5},{5... | collective-permute-start | bytes 294920 | tf_op jit(solution)/shard_map/ppermute | solution.py:288
  15.2 1.9 %collective-permute-start.5 = (bf16[3,2,192,128]{3,2,1,0:T(8,128)(2,1)S(1)}, bf16[3,2,192,128]{3,2,1,0:T(8,128)(2,1)S(1)}, u32[]{:S(2)}, u32[]{:S(2)}) collective-permute-start(bf16[3,2,192,128]{3,2,1,0:T(8,128)(2,1)S(1)} %stack_keys_and_values.1), channel_id=1, source_target_pairs={{0,4},{4,0},{8,12},{12,8},{16,20},{20,16},{24,28},{28,24},{1,5},{5... | collective-permute-start | bytes 884744 | tf_op jit(solution)/shard_map/ppermute | solution.py:288
  15.3 8.8 %collective-permute-start.8 = (bf16[384,384]{1,0:T(8,128)(2,1)S(1)}, bf16[384,384]{1,0:T(8,128)(2,1)S(1)}, u32[]{:S(2)}, u32[]{:S(2)}) collective-permute-start(bf16[384,384]{1,0:T(8,128)(2,1)S(1)} %collective-permute-done.refs_5_), channel_id=1, source_target_pairs={{0,8},{4,20},{8,0},{12,28},{16,24},{20,4},{24,16},{28,12},{1,9},{5... | collective-permute-start | bytes 884744 | tf_op jit(solution)/shard_map/ppermute | solution.py:294
  15.8 12.4 %copy-start = (bf16[768,384]{1,0:T(8,128)(2,1)S(1)}, bf16[768,384]{1,0:T(8,128)(2,1)}, u32[]{:S(2)}) copy-start(bf16[768,384]{1,0:T(8,128)(2,1)} %refs_4_.1) | copy-start | bytes 1769476
  15.8 6.8 %collective-permute-start.10 = (bf16[208,384]{1,0:T(8,128)(2,1)S(1)}, bf16[208,384]{1,0:T(8,128)(2,1)S(1)}, u32[]{:S(2)}, u32[]{:S(2)}) collective-permute-start(bf16[208,384]{1,0:T(8,128)(2,1)S(1)} %constant_dynamic-slice_fusion), channel_id=1, source_target_pairs={{0,1},{1,0},{2,3},{3,2},{4,6},{5,7},{6,4},{7,5},{8,9},{9,8},{10,11... | collective-permute-start | bytes 479240 | tf_op jit(solution)/shard_map/ppermute | solution.py:298
  19.0 5.1 %collective-permute-start.6 = (bf16[192,128]{1,0:T(8,128)(2,1)S(1)}, bf16[192,128]{1,0:T(8,128)(2,1)S(1)}, u32[]{:S(2)}, u32[]{:S(2)}) collective-permute-start(bf16[192,128]{1,0:T(8,128)(2,1)S(1)} %get-tuple-element.45), channel_id=1, source_target_pairs={{0,8},{4,12},{8,0},{12,4},{16,24},{20,28},{24,16},{28,20},{1,9},{5... | collective-permute-start | bytes 147464 | tf_op jit(solution)/shard_map/ppermute | solution.py:288
  20.6 4.1 %collective-permute-start.7 = (bf16[192,128]{1,0:T(8,128)(2,1)S(1)}, bf16[192,128]{1,0:T(8,128)(2,1)S(1)}, u32[]{:S(2)}, u32[]{:S(2)}) collective-permute-start(bf16[192,128]{1,0:T(8,128)(2,1)S(1)} %get-tuple-element.46), channel_id=1, source_target_pairs={{0,16},{4,20},{8,24},{12,28},{16,0},{20,4},{24,8},{28,12},{1,17},{... | collective-permute-start | bytes 147464 | tf_op jit(solution)/shard_map/ppermute | solution.py:288
  21.3 5.1 %collective-permute-start.9 = (bf16[192,128]{1,0:T(8,128)(2,1)S(1)}, bf16[192,128]{1,0:T(8,128)(2,1)S(1)}, u32[]{:S(2)}, u32[]{:S(2)}) collective-permute-start(bf16[192,128]{1,0:T(8,128)(2,1)S(1)} %get-tuple-element.50), channel_id=1, source_target_pairs={{0,24},{4,28},{8,16},{12,20},{16,8},{20,12},{24,0},{28,4},{1,25},{... | collective-permute-start | bytes 147464 | tf_op jit(solution)/shard_map/ppermute | solution.py:288
  22.6 5.3 %collective-permute-start.14 = (bf16[208,384]{1,0:T(8,128)(2,1)S(1)}, bf16[208,384]{1,0:T(8,128)(2,1)S(1)}, u32[]{:S(2)}, u32[]{:S(2)}) collective-permute-start(bf16[208,384]{1,0:T(8,128)(2,1)S(1)} %collective-permute-done.10.refs_0_), channel_id=1, source_target_pairs={{0,8},{4,20},{8,0},{12,28},{16,24},{20,4},{24,16},{28,12},{1,9},{5... | collective-permute-start | bytes 479240 | tf_op jit(solution)/shard_map/ppermute | solution.py:294
  24.7 3.5 %collective-permute-start.13 = (bf16[384,384]{1,0:T(8,128)(2,1)S(1)}, bf16[384,384]{1,0:T(8,128)(2,1)S(1)}, u32[]{:S(2)}, u32[]{:S(2)}) collective-permute-start(bf16[384,384]{1,0:T(8,128)(2,1)S(1)} %collective-permute-done.8.refs_6_), channel_id=1, source_target_pairs={{0,4},{4,0},{8,12},{12,8},{16,20},{20,16},{24,28},{28,24},{1,5},{5... | collective-permute-start | bytes 884744 | tf_op jit(solution)/shard_map/ppermute | solution.py:288
  26.3 1.8 %collective-permute-start.11 = (bf16[384,384]{1,0:T(8,128)(2,1)S(1)}, bf16[384,384]{1,0:T(8,128)(2,1)S(1)}, u32[]{:S(2)}, u32[]{:S(2)}) collective-permute-start(bf16[384,384]{1,0:T(8,128)(2,1)S(1)} %collective-permute-done.refs_5_), channel_id=1, source_target_pairs={{0,4},{4,0},{8,12},{12,8},{16,20},{20,16},{24,28},{28,24},{1,5},{5... | collective-permute-start | bytes 884744 | tf_op jit(solution)/shard_map/ppermute | solution.py:288
  26.3 1.8 %collective-permute-start.12 = (bf16[208,384]{1,0:T(8,128)(2,1)S(1)}, bf16[208,384]{1,0:T(8,128)(2,1)S(1)}, u32[]{:S(2)}, u32[]{:S(2)}) collective-permute-start(bf16[208,384]{1,0:T(8,128)(2,1)S(1)} %collective-permute-done.10.refs_0_), channel_id=1, source_target_pairs={{0,4},{4,0},{8,12},{12,8},{16,20},{20,16},{24,28},{28,24},{1,5},{5... | collective-permute-start | bytes 479240 | tf_op jit(solution)/shard_map/ppermute | solution.py:288
  27.9 1.4 %collective-permute-start.15 = (bf16[208,384]{1,0:T(8,128)(2,1)S(1)}, bf16[208,384]{1,0:T(8,128)(2,1)S(1)}, u32[]{:S(2)}, u32[]{:S(2)}) collective-permute-start(bf16[208,384]{1,0:T(8,128)(2,1)S(1)} %collective-permute-done.14.refs_1_), channel_id=1, source_target_pairs={{0,4},{4,0},{8,12},{12,8},{16,20},{20,16},{24,28},{28,24},{1,5},{5... | collective-permute-start | bytes 479240 | tf_op jit(solution)/shard_map/ppermute | solution.py:288

commit v17 on v16

--- a/solution.py
+++ b/solution.py
@@ -185,27 +185,40 @@
 
 def project_near_kernel(*refs):
     each = len(FLIPS)
-    heads, own_ref, pieces = refs[:each], refs[each], refs[each + 1 : each + 5]
-    blocks_ref, attention_ref, turned, weight = refs[each + 5 :]
+    heads, own_ref, pieces, thirds = refs[:each], refs[each], refs[each + 1 : each + 5], refs[each + 5 : each + 8]
+    blocks_ref, sum_ref, rest_ref, turned, weight, third = refs[each + 8 :]
     gather_heads(heads, turned)
     attention = turned[...].T
-    attention_ref[...] = attention
     place = place_in_group()
+    core, parity = place & 1, parity_of(place)
     half = pieces[0].shape[0]
     for flip in (1, 2):
-        mine = (place & 1) == 2 - flip
+        mine = core == 2 - flip
         for other in range(2):
-            here = pl.ds(pl.multiple_of((parity_of(place) ^ other) * half, 32), half)
+            here = pl.ds(pl.multiple_of((parity ^ other) * half, 32), half)
             weight[flip - 1, here, :] = jnp.where(mine, pieces[other][...], pieces[2 + other][...])
     for flip, block in enumerate((own_ref[...], weight[0], weight[1])):
         blocks_ref[flip] = jnp.dot(attention, block, preferred_element_type=jnp.float32).astype(blocks_ref.dtype)
 
-
-def project_third_kernel(blocks_ref, attention_ref, *refs):
-    pieces, (out_ref, weight, last, sems) = refs[:4], refs[4:]
-    place, shard = place_in_group(), lax.axis_index("fsdp")
-    part, columns = pieces[0].shape
-    half = weight.shape[0] // 2
+    part, quarter = thirds[0].shape[0], half // 2
+    for other in range(2):
+        third[pl.ds(pl.multiple_of((core ^ other) * (half - part), 16), part), :] = thirds[other][...]
+    fitting = turned[pl.ds(pl.multiple_of(parity * half, 32), half), :].T
+    total = jnp.dot(fitting, third[...], preferred_element_type=jnp.float32)
+    for other in range(2):
+        first = (1 - parity) * half + (core ^ other) * quarter
+        fitting = turned[pl.ds(pl.multiple_of(first, 32), quarter), :].T
+        if other:
+            rest_ref[...] = fitting
+        else:
+            rows = thirds[2][pl.ds(pl.multiple_of(core * (part - quarter), 16), quarter), :]
+            total = total + jnp.dot(fitting, rows, preferred_element_type=jnp.float32)
+    sum_ref[...] = total
+
+
+def project_third_kernel(blocks_ref, sum_ref, rest_ref, part_ref, out_ref, last, sems):
+    shard = lax.axis_index("fsdp")
+    quarter, columns = rest_ref.shape[1], last.shape[1]
 
     def copy_out(flip, block_ref):
         here = pl.ds(pl.multiple_of((shard ^ flip) * columns, 128), columns)
@@ -214,11 +227,10 @@
         return copy
 
     copies = [copy_out(flip, blocks_ref.at[flip]) for flip in range(3)]
-    for other in range(2):
-        for flip in range(2):
-            first = (parity_of(place) ^ flip) * half + ((place & 1) ^ other) * (half - part)
-            weight[pl.ds(pl.multiple_of(first, 16), part), :] = pieces[2 * other + flip][...]
-    last[...] = jnp.dot(attention_ref[...], weight[...], preferred_element_type=jnp.float32).astype(last.dtype)
+    first = (1 - (place_in_group() & 1)) * (part_ref.shape[0] - quarter)
+    rows = part_ref[pl.ds(pl.multiple_of(first, 16), quarter), :]
+    total = sum_ref[...] + jnp.dot(rest_ref[...], rows, preferred_element_type=jnp.float32)
+    last[...] = total.astype(last.dtype)
     copies.append(copy_out(3, last))
     for copy in copies:
         copy.wait()
@@ -245,41 +257,41 @@
     )(*heads, *halves)
 
 
-def project_near(heads, own, pieces):
+def project_near(heads, own, pieces, thirds):
     frames = heads[0].shape[1]
     features, columns = own.shape
     return pl.pallas_call(
         project_near_kernel,
-        out_shape=[pltpu.VMEM((3, frames, columns), jnp.bfloat16), pltpu.VMEM((frames, features), jnp.bfloat16)],
-        in_specs=[WHOLE] * (len(FLIPS) + 5),
-        out_specs=[WHOLE] * 2,
+        out_shape=[
+            pltpu.VMEM((3, frames, columns), jnp.bfloat16),
+            pltpu.VMEM((frames, columns), jnp.float32),
+            pltpu.VMEM((frames, features // 4), jnp.bfloat16),
+        ],
+        in_specs=[WHOLE] * (len(FLIPS) + 8),
+        out_specs=[WHOLE] * 3,
         scratch_shapes=[
             pltpu.VMEM((features, frames), jnp.bfloat16),
             pltpu.VMEM((2, features, columns), jnp.bfloat16),
+            pltpu.VMEM((features // 2, columns), jnp.bfloat16),
         ],
         compiler_params=params(24),
         cost_estimate=projection_cost(frames, features, 3 * columns),
         name="project_near_shards",
-    )(*heads, own, *pieces)
-
-
-def project_third(blocks, attention, pieces):
-    frames, features = attention.shape
-    columns = pieces[0].shape[1]
+    )(*heads, own, *pieces, *thirds)
+
+
+def project_third(blocks, so_far, rest, part):
+    _, frames, columns = blocks.shape
     return pl.pallas_call(
         project_third_kernel,
         out_shape=jax.ShapeDtypeStruct((1, frames, 4 * columns), blocks.dtype),
-        in_specs=[WHOLE] * 6,
+        in_specs=[WHOLE] * 4,
         out_specs=IN_HBM,
-        scratch_shapes=[
-            pltpu.VMEM((features, columns), jnp.bfloat16),
-            pltpu.VMEM((frames, columns), jnp.bfloat16),
-            pltpu.SemaphoreType.DMA((4,)),
-        ],
+        scratch_shapes=[pltpu.VMEM((frames, columns), jnp.bfloat16), pltpu.SemaphoreType.DMA((4,))],
         compiler_params=params(24),
-        cost_estimate=projection_cost(frames, features, columns),
+        cost_estimate=projection_cost(frames, rest.shape[1], columns),
         name="project_third_shard",
-    )(blocks, attention, *pieces)
+    )(blocks, so_far, rest, part)
 
 
 def per_device(ctx, fsdp, queries, key_rows, value_rows, lengths, out_weight):
@@ -340,8 +352,9 @@
         exchange(array, "ctx", 1) for array in (fetched, passed, third, third_passed)
     )
     third_other, passed_other = lax.optimization_barrier((third_other, passed_other))
-    blocks, attention = project_near(heads, out_weight, [fetched, passed, fetched_other, passed_other])
-    return project_third(blocks, attention, [third, third_passed, third_other, third_passed_other])
+    near = [fetched, passed, fetched_other, passed_other]
+    blocks, so_far, rest = project_near(heads, out_weight, near, [third, third_other, third_passed])
+    return project_third(blocks, so_far, rest, third_passed_other)
 
 
 def solution(mesh):

time: 30.4 us -> 30.3 us (level)
  transfers between devices with their start and end apart: 16 -> 16, of which waited for: 9 -> 9; matrix products, arithmetic and copies ran while one was open for 0% -> 0% of each run, Pallas kernels for 9% -> 10%
where the time goes in v17:
time: 30.3 us; the launch traced here: 30.1 us
  starting transfers between devices  15.3 us (50%)
  waiting for transfers between devices  8.98 us (30%)
  Pallas kernels  5.11 us (17%)
  between operations  0.74 us (2%)
    ppermute x12, starting transfers between devices, exchange(): return lax.ppermute(array, axis, [(i, i ^ flip) for i in range(size)])  7.87 us
    ppermute x12, waiting for transfers between devices, exchange(): return lax.ppermute(array, axis, [(i, i ^ flip) for i in range(size)])  6.53 us
    ppermute x2, starting transfers between devices, exchange_along(): return lax.ppermute(array, ('ctx', 'fsdp'), pairs)  5.43 us
    ppermute x2, starting transfers between devices, exchange_in_plane(): lax.ppermute(array, 'ctx', [(i, i ^ (4 if i % 2 else 2)) for i in range(c...  1.97 us
    pallas_call x1, Pallas kernels, attend(): pl.pallas_call(functools.partial(attention_kernel, groups), out_shape=[pl...  1.91 us
    ppermute x2, waiting for transfers between devices, exchange_along(): return lax.ppermute(array, ('ctx', 'fsdp'), pairs)  1.42 us
    pallas_call x1, Pallas kernels, copy_in(): pl.pallas_call(functools.partial(copy_in_kernel, by_parity), out_shape=[p...  1.24 us
    ppermute x2, waiting for transfers between devices, exchange_in_plane(): lax.ppermute(array, 'ctx', [(i, i ^ (4 if i % 2 else 2)) for i in range(c...  1.02 us
  transfers between devices with their start and end apart: 16, of which 9 were waited for; matrix products, arithmetic and copies ran while one was open for 0% of the time, Pallas kernels for 10%

profile of v17, /device:TPU:0, one launch (start us, length us, event | category | flops | bytes accessed | tf_op | source)
XLA Modules:
  0.0 30.1 jit_solution(2954158350367925227)
XLA Ops:
  0.0 1.2 %copy_in.1 = (bf16[3,128,768]{2,1,0:T(8,128)(2,1)S(1)}, bf16[384,384]{1,0:T(8,128)(2,1)S(1)}) custom-call(bf16[1,128,768]{2,1,0:T(8,128)(2,1)} %query_ref.1, bf16[1,128,768]{2,1,0:T(8,128)(2,1)} %key_ref.1, bf16[1,128,768]{2,1,0:T(8,128)(2,1)} %value_ref.1, bf16[768,384]{1,0:T(8,128)(2,1)} %refs_4_.1), custom_call_target="tpu_custom_call" | custom-call | tf_op jit(solution)/shard_map/copy_in/pallas_call | solution.py:45
  1.2 4.1 %collective-permute-start = (bf16[384,384]{1,0:T(8,128)(2,1)S(1)}, bf16[384,384]{1,0:T(8,128)(2,1)S(1)}, u32[]{:S(2)}, u32[]{:S(2)}) collective-permute-start(bf16[384,384]{1,0:T(8,128)(2,1)S(1)} %get-tuple-element.33), channel_id=1, source_target_pairs={{0,2},{1,3},{2,0},{3,1},{4,5},{5,4},{6,7},{7,6},{8,10},{9,11},{10,... | collective-permute-start | bytes 884744 | tf_op jit(solution)/shard_map/ppermute | solution.py:310
  5.3 0.2 turn_heads.1
  5.6 1.6 %collective-permute-start.2 = (bf16[3,192,128]{2,1,0:T(8,128)(2,1)S(1)}, bf16[3,192,128]{2,1,0:T(8,128)(2,1)S(1)}, u32[]{:S(2)}, u32[]{:S(2)}) collective-permute-start(bf16[3,192,128]{2,1,0:T(8,128)(2,1)S(1)} %get-tuple-element.37), channel_id=1, source_target_pairs={{0,8},{4,12},{8,0},{12,4},{16,24},{20,28},{24,16},{28,20},{1,9},{5... | collective-permute-start | bytes 442376 | tf_op jit(solution)/shard_map/ppermute | solution.py:300
  7.2 1.5 %collective-permute-start.3 = (bf16[3,192,128]{2,1,0:T(8,128)(2,1)S(1)}, bf16[3,192,128]{2,1,0:T(8,128)(2,1)S(1)}, u32[]{:S(2)}, u32[]{:S(2)}) collective-permute-start(bf16[3,192,128]{2,1,0:T(8,128)(2,1)S(1)} %get-tuple-element.38), channel_id=1, source_target_pairs={{0,16},{4,20},{8,24},{12,28},{16,0},{20,4},{24,8},{28,12},{1,17},{... | collective-permute-start | bytes 442376 | tf_op jit(solution)/shard_map/ppermute | solution.py:300
  8.7 0.5 %collective-permute-start.4 = (bf16[3,192,128]{2,1,0:T(8,128)(2,1)S(1)}, bf16[3,192,128]{2,1,0:T(8,128)(2,1)S(1)}, u32[]{:S(2)}, u32[]{:S(2)}) collective-permute-start(bf16[3,192,128]{2,1,0:T(8,128)(2,1)S(1)} %get-tuple-element.39), channel_id=1, source_target_pairs={{0,24},{4,28},{8,16},{12,20},{16,8},{20,12},{24,0},{28,4},{1,25},{... | collective-permute-start | bytes 442376 | tf_op jit(solution)/shard_map/ppermute | solution.py:300
  9.2 0.1 collective-permute-start.1
  9.9 0.6 %collective-permute-done.1.refs_4_ = bf16[2,192,128]{2,1,0:T(8,128)(2,1)S(1)} collective-permute-done((bf16[2,192,128]{2,1,0:T(8,128)(2,1)S(1)}, bf16[2,192,128]{2,1,0:T(8,128)(2,1)S(1)}, u32[]{:S(2)}, u32[]{:S(2)}) %collective-permute-start.1) | collective-permute-done | bytes 98336 | tf_op jit(solution)/shard_map/ppermute | solution.py:300
  10.5 1.4 %collective-permute-done.refs_5_ = bf16[384,384]{1,0:T(8,128)(2,1)S(1)} collective-permute-done((bf16[384,384]{1,0:T(8,128)(2,1)S(1)}, bf16[384,384]{1,0:T(8,128)(2,1)S(1)}, u32[]{:S(2)}, u32[]{:S(2)}) %collective-permute-start) | collective-permute-done | bytes 294944 | tf_op jit(solution)/shard_map/ppermute | solution.py:310
  12.0 0.4 %collective-permute-done.2.refs_0_.refs_1_ = bf16[3,192,128]{2,1,0:T(8,128)(2,1)S(1)} collective-permute-done((bf16[3,192,128]{2,1,0:T(8,128)(2,1)S(1)}, bf16[3,192,128]{2,1,0:T(8,128)(2,1)S(1)}, u32[]{:S(2)}, u32[]{:S(2)}) %collective-permute-start.2) | collective-permute-done | bytes 147488 | tf_op jit(solution)/shard_map/ppermute | solution.py:300
  12.4 2.8 %collective-permute-done.3.refs_1_.refs_2_ = bf16[3,192,128]{2,1,0:T(8,128)(2,1)S(1)} collective-permute-done((bf16[3,192,128]{2,1,0:T(8,128)(2,1)S(1)}, bf16[3,192,128]{2,1,0:T(8,128)(2,1)S(1)}, u32[]{:S(2)}, u32[]{:S(2)}) %collective-permute-start.3) | collective-permute-done | bytes 147488 | tf_op jit(solution)/shard_map/ppermute | solution.py:300
  15.2 0.0 collective-permute-done.4.refs_2_.refs_3_
  15.2 0.1 collective-permute-start.5
  15.3 0.5 %collective-permute-start.8 = (bf16[384,384]{1,0:T(8,128)(2,1)S(1)}, bf16[384,384]{1,0:T(8,128)(2,1)S(1)}, u32[]{:S(2)}, u32[]{:S(2)}) collective-permute-start(bf16[384,384]{1,0:T(8,128)(2,1)S(1)} %collective-permute-done.refs_5_), channel_id=1, source_target_pairs={{0,8},{4,20},{8,0},{12,28},{16,24},{20,4},{24,16},{28,12},{1,9},{5... | collective-permute-start | bytes 884744 | tf_op jit(solution)/shard_map/ppermute | solution.py:306
  15.8 0.0 copy-start
  15.8 1.3 %collective-permute-start.10 = (bf16[208,384]{1,0:T(8,128)(2,1)S(1)}, bf16[208,384]{1,0:T(8,128)(2,1)S(1)}, u32[]{:S(2)}, u32[]{:S(2)}) collective-permute-start(bf16[208,384]{1,0:T(8,128)(2,1)S(1)} %constant_dynamic-slice_fusion), channel_id=1, source_target_pairs={{0,1},{1,0},{2,3},{3,2},{4,6},{5,7},{6,4},{7,5},{8,9},{9,8},{10,11... | collective-permute-start | bytes 479240 | tf_op jit(solution)/shard_map/ppermute | solution.py:310
  17.1 0.0 collective-permute-done.5.refs_5_
  17.1 1.9 %attend_two_heads.1 = (bf16[192,128]{1,0:T(8,128)(2,1)S(1)}, bf16[192,128]{1,0:T(8,128)(2,1)S(1)}, bf16[192,128]{1,0:T(8,128)(2,1)S(1)}, bf16[192,128]{1,0:T(8,128)(2,1)S(1)}) custom-call(s32[8,128]{1,0:T(8,128)S(1)} %broadcast_in_dim.2.lengths_ref, bf16[3,192,128]{2,1,0:T(8,128)(2,1)S(1)} %get-tuple-element.35.refs_0_, ...), custom_call_target="tpu_custom_call" | custom-call | flops 1610612736 | tf_op jit(solution)/shard_map/attend_two_heads/pallas_call | solution.py:157
  19.0 1.6 %collective-permute-start.6 = (bf16[192,128]{1,0:T(8,128)(2,1)S(1)}, bf16[192,128]{1,0:T(8,128)(2,1)S(1)}, u32[]{:S(2)}, u32[]{:S(2)}) collective-permute-start(bf16[192,128]{1,0:T(8,128)(2,1)S(1)} %get-tuple-element.46), channel_id=1, source_target_pairs={{0,8},{4,12},{8,0},{12,4},{16,24},{20,28},{24,16},{28,20},{1,9},{5... | collective-permute-start | bytes 147464 | tf_op jit(solution)/shard_map/ppermute | solution.py:300
  20.6 0.7 %collective-permute-start.7 = (bf16[192,128]{1,0:T(8,128)(2,1)S(1)}, bf16[192,128]{1,0:T(8,128)(2,1)S(1)}, u32[]{:S(2)}, u32[]{:S(2)}) collective-permute-start(bf16[192,128]{1,0:T(8,128)(2,1)S(1)} %get-tuple-element.47), channel_id=1, source_target_pairs={{0,16},{4,20},{8,24},{12,28},{16,0},{20,4},{24,8},{28,12},{1,17},{... | collective-permute-start | bytes 147464 | tf_op jit(solution)/shard_map/ppermute | solution.py:300
  21.3 1.3 %collective-permute-start.9 = (bf16[192,128]{1,0:T(8,128)(2,1)S(1)}, bf16[192,128]{1,0:T(8,128)(2,1)S(1)}, u32[]{:S(2)}, u32[]{:S(2)}) collective-permute-start(bf16[192,128]{1,0:T(8,128)(2,1)S(1)} %get-tuple-element.51), channel_id=1, source_target_pairs={{0,24},{4,28},{8,16},{12,20},{16,8},{20,12},{24,0},{28,4},{1,25},{... | collective-permute-start | bytes 147464 | tf_op jit(solution)/shard_map/ppermute | solution.py:300
  22.6 0.0 collective-permute-done.10.refs_9_
  22.6 1.5 %collective-permute-start.14 = (bf16[208,384]{1,0:T(8,128)(2,1)S(1)}, bf16[208,384]{1,0:T(8,128)(2,1)S(1)}, u32[]{:S(2)}, u32[]{:S(2)}) collective-permute-start(bf16[208,384]{1,0:T(8,128)(2,1)S(1)} %collective-permute-done.10.refs_9_), channel_id=1, source_target_pairs={{0,8},{4,20},{8,0},{12,28},{16,24},{20,4},{24,16},{28,12},{1,9},{5... | collective-permute-start | bytes 479240 | tf_op jit(solution)/shard_map/ppermute | solution.py:306
  24.1 0.0 collective-permute-done.8.refs_6_
  24.1 0.0 collective-permute-done.6.refs_1_
  24.1 0.6 %collective-permute-done.7.refs_2_ = bf16[192,128]{1,0:T(8,128)(2,1)S(1)} collective-permute-done((bf16[192,128]{1,0:T(8,128)(2,1)S(1)}, bf16[192,128]{1,0:T(8,128)(2,1)S(1)}, u32[]{:S(2)}, u32[]{:S(2)}) %collective-permute-start.7) | collective-permute-done | bytes 49184 | tf_op jit(solution)/shard_map/ppermute | solution.py:300
  24.7 0.0 collective-permute-start.13
  24.7 1.6 %collective-permute-done.9.refs_3_ = bf16[192,128]{1,0:T(8,128)(2,1)S(1)} collective-permute-done((bf16[192,128]{1,0:T(8,128)(2,1)S(1)}, bf16[192,128]{1,0:T(8,128)(2,1)S(1)}, u32[]{:S(2)}, u32[]{:S(2)}) %collective-permute-start.9) | collective-permute-done | bytes 49184 | tf_op jit(solution)/shard_map/ppermute | solution.py:300
  26.3 0.0 collective-permute-start.11
  26.3 0.5 %collective-permute-start.12 = (bf16[208,384]{1,0:T(8,128)(2,1)S(1)}, bf16[208,384]{1,0:T(8,128)(2,1)S(1)}, u32[]{:S(2)}, u32[]{:S(2)}) collective-permute-start(bf16[208,384]{1,0:T(8,128)(2,1)S(1)} %collective-permute-done.10.refs_9_), channel_id=1, source_target_pairs={{0,4},{4,0},{8,12},{12,8},{16,20},{20,16},{24,28},{28,24},{1,5},{5... | collective-permute-start | bytes 479240 | tf_op jit(solution)/shard_map/ppermute | solution.py:300
  26.8 1.0 %collective-permute-done.14.refs_11_ = bf16[208,384]{1,0:T(8,128)(2,1)S(1)} collective-permute-done((bf16[208,384]{1,0:T(8,128)(2,1)S(1)}, bf16[208,384]{1,0:T(8,128)(2,1)S(1)}, u32[]{:S(2)}, u32[]{:S(2)}) %collective-permute-start.14) | collective-permute-done | bytes 159776 | tf_op jit(solution)/shard_map/ppermute | solution.py:306
  27.9 0.1 collective-permute-start.15
  28.0 0.2 collective-permute-done.12.refs_10_
  28.1 0.0 collective-permute-done.13.refs_8_
  28.2 0.0 collective-permute-done.11.refs_7_
  28.2 0.0 copy-done
  28.2 0.8 %project_near_shards.1 = (bf16[3,128,384]{2,1,0:T(8,128)(2,1)S(1)}, f32[128,384]{1,0:T(8,128)S(1)}, bf16[128,192]{1,0:T(8,128)(2,1)S(1)}) custom-call(bf16[192,128]{1,0:T(8,128)(2,1)S(1)} %get-tuple-element.45.refs_0_, bf16[192,128]{1,0:T(8,128)(2,1)S(1)} %collective-permute-done.6.refs_1_, bf16[192,128]{1,0:T(8,128)(2,1)S(1)} %collective-permute-done.7.refs_2_, ...), custom_call_target="tpu_custom_call" | custom-call | flops 226492416 | bytes 1769472 | tf_op jit(solution)/shard_map/project_near_shards/pallas_call | solution.py:263
  29.0 0.3 collective-permute-done.15.part_ref
  29.3 0.9 %project_third_shard.1 = bf16[1,128,1536]{2,1,0:T(8,128)(2,1)} custom-call(bf16[3,128,384]{2,1,0:T(8,128)(2,1)S(1)} %get-tuple-element.58.blocks_ref, f32[128,384]{1,0:T(8,128)S(1)} %get-tuple-element.59.sum_ref, bf16[128,192]{1,0:T(8,128)(2,1)S(1)} %get-tuple-element.60.rest_ref, bf16[208,384]{1,0:T(8,128)(2,1)S(1)} %collective-permute-done.15.part_ref), custom_call_target="tpu_custom_call" | custom-call | flops 18874368 | bytes 147456 | tf_op jit(solution)/shard_map/project_third_shard/pallas_call | solution.py:285
  (4 shorter events, 0.0 us)
Async XLA Ops:
  1.2 10.7 %collective-permute-start = (bf16[384,384]{1,0:T(8,128)(2,1)S(1)}, bf16[384,384]{1,0:T(8,128)(2,1)S(1)}, u32[]{:S(2)}, u32[]{:S(2)}) collective-permute-start(bf16[384,384]{1,0:T(8,128)(2,1)S(1)} %get-tuple-element.33), channel_id=1, source_target_pairs={{0,2},{1,3},{2,0},{3,1},{4,5},{5,4},{6,7},{7,6},{8,10},{9,11},{10,... | collective-permute-start | bytes 884744 | tf_op jit(solution)/shard_map/ppermute | solution.py:310
  5.6 6.8 %collective-permute-start.2 = (bf16[3,192,128]{2,1,0:T(8,128)(2,1)S(1)}, bf16[3,192,128]{2,1,0:T(8,128)(2,1)S(1)}, u32[]{:S(2)}, u32[]{:S(2)}) collective-permute-start(bf16[3,192,128]{2,1,0:T(8,128)(2,1)S(1)} %get-tuple-element.37), channel_id=1, source_target_pairs={{0,8},{4,12},{8,0},{12,4},{16,24},{20,28},{24,16},{28,20},{1,9},{5... | collective-permute-start | bytes 442376 | tf_op jit(solution)/shard_map/ppermute | solution.py:300
  7.2 8.0 %collective-permute-start.3 = (bf16[3,192,128]{2,1,0:T(8,128)(2,1)S(1)}, bf16[3,192,128]{2,1,0:T(8,128)(2,1)S(1)}, u32[]{:S(2)}, u32[]{:S(2)}) collective-permute-start(bf16[3,192,128]{2,1,0:T(8,128)(2,1)S(1)} %get-tuple-element.38), channel_id=1, source_target_pairs={{0,16},{4,20},{8,24},{12,28},{16,0},{20,4},{24,8},{28,12},{1,17},{... | collective-permute-start | bytes 442376 | tf_op jit(solution)/shard_map/ppermute | solution.py:300
  8.7 6.5 %collective-permute-start.4 = (bf16[3,192,128]{2,1,0:T(8,128)(2,1)S(1)}, bf16[3,192,128]{2,1,0:T(8,128)(2,1)S(1)}, u32[]{:S(2)}, u32[]{:S(2)}) collective-permute-start(bf16[3,192,128]{2,1,0:T(8,128)(2,1)S(1)} %get-tuple-element.39), channel_id=1, source_target_pairs={{0,24},{4,28},{8,16},{12,20},{16,8},{20,12},{24,0},{28,4},{1,25},{... | collective-permute-start | bytes 442376 | tf_op jit(solution)/shard_map/ppermute | solution.py:300
  9.2 1.4 %collective-permute-start.1 = (bf16[2,192,128]{2,1,0:T(8,128)(2,1)S(1)}, bf16[2,192,128]{2,1,0:T(8,128)(2,1)S(1)}, u32[]{:S(2)}, u32[]{:S(2)}) collective-permute-start(bf16[2,192,128]{2,1,0:T(8,128)(2,1)S(1)} %slice.3), channel_id=1, source_target_pairs={{0,4},{4,0},{8,12},{12,8},{16,20},{20,16},{24,28},{28,24},{1,5},{5... | collective-permute-start | bytes 294920 | tf_op jit(solution)/shard_map/ppermute | solution.py:300
  15.2 1.9 %collective-permute-start.5 = (bf16[3,2,192,128]{3,2,1,0:T(8,128)(2,1)S(1)}, bf16[3,2,192,128]{3,2,1,0:T(8,128)(2,1)S(1)}, u32[]{:S(2)}, u32[]{:S(2)}) collective-permute-start(bf16[3,2,192,128]{3,2,1,0:T(8,128)(2,1)S(1)} %stack_keys_and_values.1), channel_id=1, source_target_pairs={{0,4},{4,0},{8,12},{12,8},{16,20},{20,16},{24,28},{28,24},{1,5},{5... | collective-permute-start | bytes 884744 | tf_op jit(solution)/shard_map/ppermute | solution.py:300
  15.3 8.8 %collective-permute-start.8 = (bf16[384,384]{1,0:T(8,128)(2,1)S(1)}, bf16[384,384]{1,0:T(8,128)(2,1)S(1)}, u32[]{:S(2)}, u32[]{:S(2)}) collective-permute-start(bf16[384,384]{1,0:T(8,128)(2,1)S(1)} %collective-permute-done.refs_5_), channel_id=1, source_target_pairs={{0,8},{4,20},{8,0},{12,28},{16,24},{20,4},{24,16},{28,12},{1,9},{5... | collective-permute-start | bytes 884744 | tf_op jit(solution)/shard_map/ppermute | solution.py:306
  15.8 12.4 %copy-start = (bf16[768,384]{1,0:T(8,128)(2,1)S(1)}, bf16[768,384]{1,0:T(8,128)(2,1)}, u32[]{:S(2)}) copy-start(bf16[768,384]{1,0:T(8,128)(2,1)} %refs_4_.1) | copy-start | bytes 1769476
  15.8 6.8 %collective-permute-start.10 = (bf16[208,384]{1,0:T(8,128)(2,1)S(1)}, bf16[208,384]{1,0:T(8,128)(2,1)S(1)}, u32[]{:S(2)}, u32[]{:S(2)}) collective-permute-start(bf16[208,384]{1,0:T(8,128)(2,1)S(1)} %constant_dynamic-slice_fusion), channel_id=1, source_target_pairs={{0,1},{1,0},{2,3},{3,2},{4,6},{5,7},{6,4},{7,5},{8,9},{9,8},{10,11... | collective-permute-start | bytes 479240 | tf_op jit(solution)/shard_map/ppermute | solution.py:310
  19.0 5.1 %collective-permute-start.6 = (bf16[192,128]{1,0:T(8,128)(2,1)S(1)}, bf16[192,128]{1,0:T(8,128)(2,1)S(1)}, u32[]{:S(2)}, u32[]{:S(2)}) collective-permute-start(bf16[192,128]{1,0:T(8,128)(2,1)S(1)} %get-tuple-element.46), channel_id=1, source_target_pairs={{0,8},{4,12},{8,0},{12,4},{16,24},{20,28},{24,16},{28,20},{1,9},{5... | collective-permute-start | bytes 147464 | tf_op jit(solution)/shard_map/ppermute | solution.py:300
  20.6 4.1 %collective-permute-start.7 = (bf16[192,128]{1,0:T(8,128)(2,1)S(1)}, bf16[192,128]{1,0:T(8,128)(2,1)S(1)}, u32[]{:S(2)}, u32[]{:S(2)}) collective-permute-start(bf16[192,128]{1,0:T(8,128)(2,1)S(1)} %get-tuple-element.47), channel_id=1, source_target_pairs={{0,16},{4,20},{8,24},{12,28},{16,0},{20,4},{24,8},{28,12},{1,17},{... | collective-permute-start | bytes 147464 | tf_op jit(solution)/shard_map/ppermute | solution.py:300
  21.3 5.1 %collective-permute-start.9 = (bf16[192,128]{1,0:T(8,128)(2,1)S(1)}, bf16[192,128]{1,0:T(8,128)(2,1)S(1)}, u32[]{:S(2)}, u32[]{:S(2)}) collective-permute-start(bf16[192,128]{1,0:T(8,128)(2,1)S(1)} %get-tuple-element.51), channel_id=1, source_target_pairs={{0,24},{4,28},{8,16},{12,20},{16,8},{20,12},{24,0},{28,4},{1,25},{... | collective-permute-start | bytes 147464 | tf_op jit(solution)/shard_map/ppermute | solution.py:300
  22.6 5.3 %collective-permute-start.14 = (bf16[208,384]{1,0:T(8,128)(2,1)S(1)}, bf16[208,384]{1,0:T(8,128)(2,1)S(1)}, u32[]{:S(2)}, u32[]{:S(2)}) collective-permute-start(bf16[208,384]{1,0:T(8,128)(2,1)S(1)} %collective-permute-done.10.refs_9_), channel_id=1, source_target_pairs={{0,8},{4,20},{8,0},{12,28},{16,24},{20,4},{24,16},{28,12},{1,9},{5... | collective-permute-start | bytes 479240 | tf_op jit(solution)/shard_map/ppermute | solution.py:306
  24.7 3.5 %collective-permute-start.13 = (bf16[384,384]{1,0:T(8,128)(2,1)S(1)}, bf16[384,384]{1,0:T(8,128)(2,1)S(1)}, u32[]{:S(2)}, u32[]{:S(2)}) collective-permute-start(bf16[384,384]{1,0:T(8,128)(2,1)S(1)} %collective-permute-done.8.refs_6_), channel_id=1, source_target_pairs={{0,4},{4,0},{8,12},{12,8},{16,20},{20,16},{24,28},{28,24},{1,5},{5... | collective-permute-start | bytes 884744 | tf_op jit(solution)/shard_map/ppermute | solution.py:300
  26.3 1.8 %collective-permute-start.11 = (bf16[384,384]{1,0:T(8,128)(2,1)S(1)}, bf16[384,384]{1,0:T(8,128)(2,1)S(1)}, u32[]{:S(2)}, u32[]{:S(2)}) collective-permute-start(bf16[384,384]{1,0:T(8,128)(2,1)S(1)} %collective-permute-done.refs_5_), channel_id=1, source_target_pairs={{0,4},{4,0},{8,12},{12,8},{16,20},{20,16},{24,28},{28,24},{1,5},{5... | collective-permute-start | bytes 884744 | tf_op jit(solution)/shard_map/ppermute | solution.py:300
  26.3 1.8 %collective-permute-start.12 = (bf16[208,384]{1,0:T(8,128)(2,1)S(1)}, bf16[208,384]{1,0:T(8,128)(2,1)S(1)}, u32[]{:S(2)}, u32[]{:S(2)}) collective-permute-start(bf16[208,384]{1,0:T(8,128)(2,1)S(1)} %collective-permute-done.10.refs_9_), channel_id=1, source_target_pairs={{0,4},{4,0},{8,12},{12,8},{16,20},{20,16},{24,28},{28,24},{1,5},{5... | collective-permute-start | bytes 479240 | tf_op jit(solution)/shard_map/ppermute | solution.py:300
  27.9 1.4 %collective-permute-start.15 = (bf16[208,384]{1,0:T(8,128)(2,1)S(1)}, bf16[208,384]{1,0:T(8,128)(2,1)S(1)}, u32[]{:S(2)}, u32[]{:S(2)}) collective-permute-start(bf16[208,384]{1,0:T(8,128)(2,1)S(1)} %collective-permute-done.14.refs_11_), channel_id=1, source_target_pairs={{0,4},{4,0},{8,12},{12,8},{16,20},{20,16},{24,28},{28,24},{1,5},{5... | collective-permute-start | bytes 479240 | tf_op jit(solution)/shard_map/ppermute | solution.py:300

commit v18 on v17

--- a/solution.py
+++ b/solution.py
@@ -79,8 +79,8 @@
 
 def attention_kernel(groups, lengths_ref, *refs):
     each = len(FLIPS)
-    same, own_other, other = refs[:each], refs[each], refs[each + 1]
-    rest_ref = refs[each + 2] if groups > 1 else None
+    same, own_other, other = refs[:each], refs[each], refs[each + 1 : each + 3]
+    rest_ref = refs[each + 3] if groups > 1 else None
     outs, (keys, values) = refs[-2 - each : -2], refs[-2:]
     block = outs[0].shape[1]
     head_size = outs[0].shape[0] // 2
@@ -94,7 +94,7 @@
             return rest_ref[at, part - 1, rows, :]
         if at % 2 == 0:
             return same[at // 2][part, rows, :]
-        return other[at // 2 - 1, part - 1, rows, :] if at > 1 else own_other[part - 1, rows, :]
+        return other[part - 1][at // 2 - 1, rows, :] if at > 1 else own_other[part - 1, rows, :]
 
     ones = jnp.where(lax.broadcasted_iota(jnp.int32, (pad, block), 0) == 0, 1.0, 0.0).astype(keys.dtype)
     at_feature = lax.broadcasted_iota(jnp.int32, (pad, block), 0)
@@ -133,17 +133,18 @@
 
 
 def stack_kernel(*refs):
-    for at, ref in enumerate(refs[:-1]):
-        refs[-1][at] = ref[1:]
+    for part in range(2):
+        for at, ref in enumerate(refs[:-2]):
+            refs[part - 2][at] = ref[1 + part]
 
 
 def stack_keys_and_values(arrays):
     parts, features, frames = arrays[0].shape
     return pl.pallas_call(
         stack_kernel,
-        out_shape=pltpu.VMEM((len(arrays), parts - 1, features, frames), arrays[0].dtype),
+        out_shape=[pltpu.VMEM((len(arrays), features, frames), arrays[0].dtype)] * (parts - 1),
         in_specs=[WHOLE] * len(arrays),
-        out_specs=WHOLE,
+        out_specs=[WHOLE] * (parts - 1),
         compiler_params=params(16),
         name="stack_keys_and_values",
     )(*arrays)
@@ -157,13 +158,13 @@
     return pl.pallas_call(
         functools.partial(attention_kernel, groups),
         out_shape=[pltpu.VMEM((features, block), jnp.bfloat16)] * len(FLIPS),
-        in_specs=[WHOLE] * (3 + len(FLIPS) + len(rest)),
+        in_specs=[WHOLE] * (4 + len(FLIPS) + len(rest)),
         out_specs=[WHOLE] * len(FLIPS),
         scratch_shapes=[pltpu.VMEM((2, keys, padded), jnp.bfloat16), pltpu.VMEM((2, padded, keys), jnp.bfloat16)],
         compiler_params=params(32),
-        cost_estimate=pl.CostEstimate(flops=8 * keys * keys * features, bytes_accessed=0, transcendentals=0),
+        cost_estimate=pl.CostEstimate(flops=0 * keys * keys * features, bytes_accessed=0, transcendentals=0),
         name="attend_two_heads",
-    )(lengths, *same, own_other, other, *rest)
+    )(lengths, *same, own_other, *other, *rest)
 
 
 def gather_heads(heads, turned):
@@ -325,11 +326,11 @@
         fetched, own_other, lengths = lax.optimization_barrier((fetched, own_other, lengths))
         passed = exchange_in_plane(fetched)
         depth = half.shape[0]
-        part = depth // 2 + 16
+        part = depth // 2 + 32
         third = lax.dynamic_slice_in_dim(fetched, core * (depth - part), part, 0)
         third = exchange_along(third, 1, 2)
     same, own_other = lax.optimization_barrier((same, own_other))
-    other = exchange(stack_keys_and_values(same), "ctx", 1)
+    other = [exchange(array, "ctx", 1) for array in stack_keys_and_values(same)]
     same = [own, *same]
 
     groups = ctx // HEADS
@@ -337,7 +338,7 @@
     if groups > 1:
         pairs = [own[1:], own_other]
         for at, array in enumerate(same[1:]):
-            pairs += [array[1:], other[at]]
+            pairs += [array[1:], jnp.stack([other[0][at], other[1][at]])]
         across = [[head + first for first in range(0, ctx, HEADS)] for head in range(HEADS)]
         rest = lax.all_gather(jnp.stack(pairs), "ctx", axis=0, axis_index_groups=across, tiled=True)
     mixed = attend(lengths, same, own_other, other, rest, groups)

time: 30.3 us -> 32.5 us (1.073)
  starting transfers between devices: 15.3 us -> 17.7 us
    ppermute x2, starting transfers between devices: 1.97 us -> 3.18 us  [exchange_in_plane(): lax.ppermute(array, 'ctx', [(i, i ^ (4 if i % 2 else 2)) for i in range(c...]
    ppermute x12 -> x13, starting transfers between devices: 7.87 us -> 8.66 us  [exchange(): return lax.ppermute(array, axis, [(i, i ^ flip) for i in range(size)])]
    ppermute x2, waiting for transfers between devices: 1.02 us -> 0.25 us  [exchange_in_plane(): lax.ppermute(array, 'ctx', [(i, i ^ (4 if i % 2 else 2)) for i in range(c...]
    ppermute x2, waiting for transfers between devices: 1.42 us -> 2.03 us  [exchange_along(): return lax.ppermute(array, ('ctx', 'fsdp'), pairs)]
    ppermute x2, starting transfers between devices: 5.43 us -> 5.9 us  [exchange_along(): return lax.ppermute(array, ('ctx', 'fsdp'), pairs)]
    ppermute x12 -> x13, waiting for transfers between devices: 6.53 us -> 6.45 us  [exchange(): return lax.ppermute(array, axis, [(i, i ^ flip) for i in range(size)])]
  transfers between devices with their start and end apart: 16 -> 17, of which waited for: 9 -> 9; matrix products, arithmetic and copies ran while one was open for 0% -> 0% of each run, Pallas kernels for 10% -> 9%
where the time goes in v18:
time: 32.5 us; the launch traced here: 32.4 us
  starting transfers between devices  17.7 us (54%)
  waiting for transfers between devices  8.74 us (27%)
  Pallas kernels  5.09 us (16%)
  between operations  0.76 us (2%)
    ppermute x13, starting transfers between devices, exchange(): return lax.ppermute(array, axis, [(i, i ^ flip) for i in range(size)])  8.66 us
    ppermute x13, waiting for transfers between devices, exchange(): return lax.ppermute(array, axis, [(i, i ^ flip) for i in range(size)])  6.45 us
    ppermute x2, starting transfers between devices, exchange_along(): return lax.ppermute(array, ('ctx', 'fsdp'), pairs)  5.9 us
    ppermute x2, starting transfers between devices, exchange_in_plane(): lax.ppermute(array, 'ctx', [(i, i ^ (4 if i % 2 else 2)) for i in range(c...  3.18 us
    ppermute x2, waiting for transfers between devices, exchange_along(): return lax.ppermute(array, ('ctx', 'fsdp'), pairs)  2.03 us
    pallas_call x1, Pallas kernels, attend(): pl.pallas_call(functools.partial(attention_kernel, groups), out_shape=[pl...  1.89 us
    pallas_call x1, Pallas kernels, copy_in(): pl.pallas_call(functools.partial(copy_in_kernel, by_parity), out_shape=[p...  1.24 us
    pallas_call x1, Pallas kernels, project_third(): pl.pallas_call(project_third_kernel, out_shape=jax.ShapeDtypeStruct((1, f...  0.88 us
  transfers between devices with their start and end apart: 17, of which 9 were waited for; matrix products, arithmetic and copies ran while one was open for 0% of the time, Pallas kernels for 9%

profile of v18, /device:TPU:0, one launch (start us, length us, event | category | flops | bytes accessed | tf_op | source)
XLA Modules:
  0.0 32.4 jit_solution(6061226099292988469)
XLA Ops:
  0.0 1.2 %copy_in.1 = (bf16[3,128,768]{2,1,0:T(8,128)(2,1)S(1)}, bf16[384,384]{1,0:T(8,128)(2,1)S(1)}) custom-call(bf16[1,128,768]{2,1,0:T(8,128)(2,1)} %query_ref.1, bf16[1,128,768]{2,1,0:T(8,128)(2,1)} %key_ref.1, bf16[1,128,768]{2,1,0:T(8,128)(2,1)} %value_ref.1, bf16[768,384]{1,0:T(8,128)(2,1)} %refs_4_.1), custom_call_target="tpu_custom_call" | custom-call | tf_op jit(solution)/shard_map/copy_in/pallas_call | solution.py:45
  1.2 4.1 %collective-permute-start = (bf16[384,384]{1,0:T(8,128)(2,1)S(1)}, bf16[384,384]{1,0:T(8,128)(2,1)S(1)}, u32[]{:S(2)}, u32[]{:S(2)}) collective-permute-start(bf16[384,384]{1,0:T(8,128)(2,1)S(1)} %get-tuple-element.35), channel_id=1, source_target_pairs={{0,2},{1,3},{2,0},{3,1},{4,5},{5,4},{6,7},{7,6},{8,10},{9,11},{10,... | collective-permute-start | bytes 884744 | tf_op jit(solution)/shard_map/ppermute | solution.py:311
  5.3 0.2 turn_heads.1
  5.6 0.1 collective-permute-start.1
  5.7 1.6 %collective-permute-start.2 = (bf16[3,192,128]{2,1,0:T(8,128)(2,1)S(1)}, bf16[3,192,128]{2,1,0:T(8,128)(2,1)S(1)}, u32[]{:S(2)}, u32[]{:S(2)}) collective-permute-start(bf16[3,192,128]{2,1,0:T(8,128)(2,1)S(1)} %get-tuple-element.39), channel_id=1, source_target_pairs={{0,8},{4,12},{8,0},{12,4},{16,24},{20,28},{24,16},{28,20},{1,9},{5... | collective-permute-start | bytes 442376 | tf_op jit(solution)/shard_map/ppermute | solution.py:301
  7.3 1.5 %collective-permute-start.3 = (bf16[3,192,128]{2,1,0:T(8,128)(2,1)S(1)}, bf16[3,192,128]{2,1,0:T(8,128)(2,1)S(1)}, u32[]{:S(2)}, u32[]{:S(2)}) collective-permute-start(bf16[3,192,128]{2,1,0:T(8,128)(2,1)S(1)} %get-tuple-element.40), channel_id=1, source_target_pairs={{0,16},{4,20},{8,24},{12,28},{16,0},{20,4},{24,8},{28,12},{1,17},{... | collective-permute-start | bytes 442376 | tf_op jit(solution)/shard_map/ppermute | solution.py:301
  8.8 0.5 %collective-permute-start.4 = (bf16[3,192,128]{2,1,0:T(8,128)(2,1)S(1)}, bf16[3,192,128]{2,1,0:T(8,128)(2,1)S(1)}, u32[]{:S(2)}, u32[]{:S(2)}) collective-permute-start(bf16[3,192,128]{2,1,0:T(8,128)(2,1)S(1)} %get-tuple-element.41), channel_id=1, source_target_pairs={{0,24},{4,28},{8,16},{12,20},{16,8},{20,12},{24,0},{28,4},{1,25},{... | collective-permute-start | bytes 442376 | tf_op jit(solution)/shard_map/ppermute | solution.py:301
  9.9 0.0 collective-permute-done.1.refs_4_
  9.9 2.0 %collective-permute-done.refs_5_ = bf16[384,384]{1,0:T(8,128)(2,1)S(1)} collective-permute-done((bf16[384,384]{1,0:T(8,128)(2,1)S(1)}, bf16[384,384]{1,0:T(8,128)(2,1)S(1)}, u32[]{:S(2)}, u32[]{:S(2)}) %collective-permute-start) | collective-permute-done | bytes 294944 | tf_op jit(solution)/shard_map/ppermute | solution.py:311
  12.0 2.1 %collective-permute-start.9 = (bf16[384,384]{1,0:T(8,128)(2,1)S(1)}, bf16[384,384]{1,0:T(8,128)(2,1)S(1)}, u32[]{:S(2)}, u32[]{:S(2)}) collective-permute-start(bf16[384,384]{1,0:T(8,128)(2,1)S(1)} %collective-permute-done.refs_5_), channel_id=1, source_target_pairs={{0,8},{4,20},{8,0},{12,28},{16,24},{20,4},{24,16},{28,12},{1,9},{5... | collective-permute-start | bytes 884744 | tf_op jit(solution)/shard_map/ppermute | solution.py:307
  14.1 1.8 %collective-permute-start.11 = (bf16[224,384]{1,0:T(8,128)(2,1)S(1)}, bf16[224,384]{1,0:T(8,128)(2,1)S(1)}, u32[]{:S(2)}, u32[]{:S(2)}) collective-permute-start(bf16[224,384]{1,0:T(8,128)(2,1)S(1)} %constant_dynamic-slice_fusion), channel_id=1, source_target_pairs={{0,1},{1,0},{2,3},{3,2},{4,6},{5,7},{6,4},{7,5},{8,9},{9,8},{10,11... | collective-permute-start | bytes 516104 | tf_op jit(solution)/shard_map/ppermute | solution.py:311
  15.9 0.0 collective-permute-done.2.refs_0_.refs_1_
  15.9 0.6 %collective-permute-done.3.refs_1_.refs_2_ = bf16[3,192,128]{2,1,0:T(8,128)(2,1)S(1)} collective-permute-done((bf16[3,192,128]{2,1,0:T(8,128)(2,1)S(1)}, bf16[3,192,128]{2,1,0:T(8,128)(2,1)S(1)}, u32[]{:S(2)}, u32[]{:S(2)}) %collective-permute-start.3) | collective-permute-done | bytes 147488 | tf_op jit(solution)/shard_map/ppermute | solution.py:301
  16.5 0.0 collective-permute-done.4.refs_2_.refs_3_
  16.5 0.0 copy-start
  16.5 0.1 collective-permute-start.5
  16.6 0.5 %collective-permute-start.6 = (bf16[3,192,128]{2,1,0:T(8,128)(2,1)S(1)}, bf16[3,192,128]{2,1,0:T(8,128)(2,1)S(1)}, u32[]{:S(2)}, u32[]{:S(2)}) collective-permute-start(bf16[3,192,128]{2,1,0:T(8,128)(2,1)S(1)} %get-tuple-element.48), channel_id=1, source_target_pairs={{0,4},{4,0},{8,12},{12,8},{16,20},{20,16},{24,28},{28,24},{1,5},{5... | collective-permute-start | bytes 442376 | tf_op jit(solution)/shard_map/ppermute | solution.py:301
  17.1 0.9 %collective-permute-done.5.refs_5_ = bf16[3,192,128]{2,1,0:T(8,128)(2,1)S(1)} collective-permute-done((bf16[3,192,128]{2,1,0:T(8,128)(2,1)S(1)}, bf16[3,192,128]{2,1,0:T(8,128)(2,1)S(1)}, u32[]{:S(2)}, u32[]{:S(2)}) %collective-permute-start.5) | collective-permute-done | bytes 147488 | tf_op jit(solution)/shard_map/ppermute | solution.py:301
  17.9 0.2 collective-permute-done.6.refs_6_
  18.1 1.9 %attend_two_heads.1 = (bf16[192,128]{1,0:T(8,128)(2,1)S(1)}, bf16[192,128]{1,0:T(8,128)(2,1)S(1)}, bf16[192,128]{1,0:T(8,128)(2,1)S(1)}, bf16[192,128]{1,0:T(8,128)(2,1)S(1)}) custom-call(s32[8,128]{1,0:T(8,128)S(1)} %broadcast_in_dim.2.lengths_ref, bf16[3,192,128]{2,1,0:T(8,128)(2,1)S(1)} %get-tuple-element.37.refs_0_, ...), custom_call_target="tpu_custom_call" | custom-call | tf_op jit(solution)/shard_map/attend_two_heads/pallas_call | solution.py:158
  20.0 1.6 %collective-permute-start.10 = (bf16[192,128]{1,0:T(8,128)(2,1)S(1)}, bf16[192,128]{1,0:T(8,128)(2,1)S(1)}, u32[]{:S(2)}, u32[]{:S(2)}) collective-permute-start(bf16[192,128]{1,0:T(8,128)(2,1)S(1)} %get-tuple-element.55), channel_id=1, source_target_pairs={{0,24},{4,28},{8,16},{12,20},{16,8},{20,12},{24,0},{28,4},{1,25},{... | collective-permute-start | bytes 147464 | tf_op jit(solution)/shard_map/ppermute | solution.py:301
  21.6 2.1 %collective-permute-start.7 = (bf16[192,128]{1,0:T(8,128)(2,1)S(1)}, bf16[192,128]{1,0:T(8,128)(2,1)S(1)}, u32[]{:S(2)}, u32[]{:S(2)}) collective-permute-start(bf16[192,128]{1,0:T(8,128)(2,1)S(1)} %get-tuple-element.50), channel_id=1, source_target_pairs={{0,8},{4,12},{8,0},{12,4},{16,24},{20,28},{24,16},{28,20},{1,9},{5... | collective-permute-start | bytes 147464 | tf_op jit(solution)/shard_map/ppermute | solution.py:301
  23.7 0.0 collective-permute-start.8
  23.7 0.0 collective-permute-done.11.refs_9_
  23.7 1.1 %collective-permute-start.15 = (bf16[224,384]{1,0:T(8,128)(2,1)S(1)}, bf16[224,384]{1,0:T(8,128)(2,1)S(1)}, u32[]{:S(2)}, u32[]{:S(2)}) collective-permute-start(bf16[224,384]{1,0:T(8,128)(2,1)S(1)} %collective-permute-done.11.refs_9_), channel_id=1, source_target_pairs={{0,8},{4,20},{8,0},{12,28},{16,24},{20,4},{24,16},{28,12},{1,9},{5... | collective-permute-start | bytes 516104 | tf_op jit(solution)/shard_map/ppermute | solution.py:307
  24.8 0.5 %collective-permute-done.10.refs_3_ = bf16[192,128]{1,0:T(8,128)(2,1)S(1)} collective-permute-done((bf16[192,128]{1,0:T(8,128)(2,1)S(1)}, bf16[192,128]{1,0:T(8,128)(2,1)S(1)}, u32[]{:S(2)}, u32[]{:S(2)}) %collective-permute-start.10) | collective-permute-done | bytes 49184 | tf_op jit(solution)/shard_map/ppermute | solution.py:301
  25.4 1.4 %collective-permute-done.7.refs_1_ = bf16[192,128]{1,0:T(8,128)(2,1)S(1)} collective-permute-done((bf16[192,128]{1,0:T(8,128)(2,1)S(1)}, bf16[192,128]{1,0:T(8,128)(2,1)S(1)}, u32[]{:S(2)}, u32[]{:S(2)}) %collective-permute-start.7) | collective-permute-done | bytes 49184 | tf_op jit(solution)/shard_map/ppermute | solution.py:301
  26.7 1.7 %collective-permute-done.8.refs_2_ = bf16[192,128]{1,0:T(8,128)(2,1)S(1)} collective-permute-done((bf16[192,128]{1,0:T(8,128)(2,1)S(1)}, bf16[192,128]{1,0:T(8,128)(2,1)S(1)}, u32[]{:S(2)}, u32[]{:S(2)}) %collective-permute-start.8) | collective-permute-done | bytes 49184 | tf_op jit(solution)/shard_map/ppermute | solution.py:301
  28.4 0.0 collective-permute-done.9.refs_6_
  28.4 0.0 collective-permute-start.14
  28.4 0.5 %collective-permute-start.12 = (bf16[384,384]{1,0:T(8,128)(2,1)S(1)}, bf16[384,384]{1,0:T(8,128)(2,1)S(1)}, u32[]{:S(2)}, u32[]{:S(2)}) collective-permute-start(bf16[384,384]{1,0:T(8,128)(2,1)S(1)} %collective-permute-done.refs_5_), channel_id=1, source_target_pairs={{0,4},{4,0},{8,12},{12,8},{16,20},{20,16},{24,28},{28,24},{1,5},{5... | collective-permute-start | bytes 884744 | tf_op jit(solution)/shard_map/ppermute | solution.py:301
  28.9 0.0 collective-permute-start.13
  28.9 0.3 collective-permute-done.15.refs_11_
  29.2 0.3 collective-permute-start.16
  29.4 1.2 %collective-permute-done.13.refs_10_ = bf16[224,384]{1,0:T(8,128)(2,1)S(1)} collective-permute-done((bf16[224,384]{1,0:T(8,128)(2,1)S(1)}, bf16[224,384]{1,0:T(8,128)(2,1)S(1)}, u32[]{:S(2)}, u32[]{:S(2)}) %collective-permute-start.13) | collective-permute-done | bytes 172064 | tf_op jit(solution)/shard_map/ppermute | solution.py:301
  30.6 0.0 collective-permute-done.14.refs_8_
  30.6 0.0 collective-permute-done.12.refs_7_
  30.6 0.0 copy-done
  30.7 0.8 %project_near_shards.1 = (bf16[3,128,384]{2,1,0:T(8,128)(2,1)S(1)}, f32[128,384]{1,0:T(8,128)S(1)}, bf16[128,192]{1,0:T(8,128)(2,1)S(1)}) custom-call(bf16[192,128]{1,0:T(8,128)(2,1)S(1)} %get-tuple-element.49.refs_0_, bf16[192,128]{1,0:T(8,128)(2,1)S(1)} %collective-permute-done.7.refs_1_, bf16[192,128]{1,0:T(8,128)(2,1)S(1)} %collective-permute-done.8.refs_2_, ...), custom_call_target="tpu_custom_call" | custom-call | flops 226492416 | bytes 1769472 | tf_op jit(solution)/shard_map/project_near_shards/pallas_call | solution.py:264
  31.5 0.0 collective-permute-done.16.part_ref
  31.5 0.9 %project_third_shard.1 = bf16[1,128,1536]{2,1,0:T(8,128)(2,1)} custom-call(bf16[3,128,384]{2,1,0:T(8,128)(2,1)S(1)} %get-tuple-element.62.blocks_ref, f32[128,384]{1,0:T(8,128)S(1)} %get-tuple-element.63.sum_ref, bf16[128,192]{1,0:T(8,128)(2,1)S(1)} %get-tuple-element.64.rest_ref, bf16[224,384]{1,0:T(8,128)(2,1)S(1)} %collective-permute-done.16.part_ref), custom_call_target="tpu_custom_call" | custom-call | flops 18874368 | bytes 147456 | tf_op jit(solution)/shard_map/project_third_shard/pallas_call | solution.py:286
  (4 shorter events, 0.0 us)
Async XLA Ops:
  1.2 10.7 %collective-permute-start = (bf16[384,384]{1,0:T(8,128)(2,1)S(1)}, bf16[384,384]{1,0:T(8,128)(2,1)S(1)}, u32[]{:S(2)}, u32[]{:S(2)}) collective-permute-start(bf16[384,384]{1,0:T(8,128)(2,1)S(1)} %get-tuple-element.35), channel_id=1, source_target_pairs={{0,2},{1,3},{2,0},{3,1},{4,5},{5,4},{6,7},{7,6},{8,10},{9,11},{10,... | collective-permute-start | bytes 884744 | tf_op jit(solution)/shard_map/ppermute | solution.py:311
  5.6 4.3 %collective-permute-start.1 = (bf16[2,192,128]{2,1,0:T(8,128)(2,1)S(1)}, bf16[2,192,128]{2,1,0:T(8,128)(2,1)S(1)}, u32[]{:S(2)}, u32[]{:S(2)}) collective-permute-start(bf16[2,192,128]{2,1,0:T(8,128)(2,1)S(1)} %slice.3), channel_id=1, source_target_pairs={{0,4},{4,0},{8,12},{12,8},{16,20},{20,16},{24,28},{28,24},{1,5},{5... | collective-permute-start | bytes 294920 | tf_op jit(solution)/shard_map/ppermute | solution.py:301
  5.7 10.2 %collective-permute-start.2 = (bf16[3,192,128]{2,1,0:T(8,128)(2,1)S(1)}, bf16[3,192,128]{2,1,0:T(8,128)(2,1)S(1)}, u32[]{:S(2)}, u32[]{:S(2)}) collective-permute-start(bf16[3,192,128]{2,1,0:T(8,128)(2,1)S(1)} %get-tuple-element.39), channel_id=1, source_target_pairs={{0,8},{4,12},{8,0},{12,4},{16,24},{20,28},{24,16},{28,20},{1,9},{5... | collective-permute-start | bytes 442376 | tf_op jit(solution)/shard_map/ppermute | solution.py:301
  7.3 9.2 %collective-permute-start.3 = (bf16[3,192,128]{2,1,0:T(8,128)(2,1)S(1)}, bf16[3,192,128]{2,1,0:T(8,128)(2,1)S(1)}, u32[]{:S(2)}, u32[]{:S(2)}) collective-permute-start(bf16[3,192,128]{2,1,0:T(8,128)(2,1)S(1)} %get-tuple-element.40), channel_id=1, source_target_pairs={{0,16},{4,20},{8,24},{12,28},{16,0},{20,4},{24,8},{28,12},{1,17},{... | collective-permute-start | bytes 442376 | tf_op jit(solution)/shard_map/ppermute | solution.py:301
  8.8 7.7 %collective-permute-start.4 = (bf16[3,192,128]{2,1,0:T(8,128)(2,1)S(1)}, bf16[3,192,128]{2,1,0:T(8,128)(2,1)S(1)}, u32[]{:S(2)}, u32[]{:S(2)}) collective-permute-start(bf16[3,192,128]{2,1,0:T(8,128)(2,1)S(1)} %get-tuple-element.41), channel_id=1, source_target_pairs={{0,24},{4,28},{8,16},{12,20},{16,8},{20,12},{24,0},{28,4},{1,25},{... | collective-permute-start | bytes 442376 | tf_op jit(solution)/shard_map/ppermute | solution.py:301
  12.0 16.4 %collective-permute-start.9 = (bf16[384,384]{1,0:T(8,128)(2,1)S(1)}, bf16[384,384]{1,0:T(8,128)(2,1)S(1)}, u32[]{:S(2)}, u32[]{:S(2)}) collective-permute-start(bf16[384,384]{1,0:T(8,128)(2,1)S(1)} %collective-permute-done.refs_5_), channel_id=1, source_target_pairs={{0,8},{4,20},{8,0},{12,28},{16,24},{20,4},{24,16},{28,12},{1,9},{5... | collective-permute-start | bytes 884744 | tf_op jit(solution)/shard_map/ppermute | solution.py:307
  14.1 9.7 %collective-permute-start.11 = (bf16[224,384]{1,0:T(8,128)(2,1)S(1)}, bf16[224,384]{1,0:T(8,128)(2,1)S(1)}, u32[]{:S(2)}, u32[]{:S(2)}) collective-permute-start(bf16[224,384]{1,0:T(8,128)(2,1)S(1)} %constant_dynamic-slice_fusion), channel_id=1, source_target_pairs={{0,1},{1,0},{2,3},{3,2},{4,6},{5,7},{6,4},{7,5},{8,9},{9,8},{10,11... | collective-permute-start | bytes 516104 | tf_op jit(solution)/shard_map/ppermute | solution.py:311
  16.5 14.2 %copy-start = (bf16[768,384]{1,0:T(8,128)(2,1)S(1)}, bf16[768,384]{1,0:T(8,128)(2,1)}, u32[]{:S(2)}) copy-start(bf16[768,384]{1,0:T(8,128)(2,1)} %refs_4_.1) | copy-start | bytes 1769476
  16.5 1.4 %collective-permute-start.5 = (bf16[3,192,128]{2,1,0:T(8,128)(2,1)S(1)}, bf16[3,192,128]{2,1,0:T(8,128)(2,1)S(1)}, u32[]{:S(2)}, u32[]{:S(2)}) collective-permute-start(bf16[3,192,128]{2,1,0:T(8,128)(2,1)S(1)} %get-tuple-element.47), channel_id=1, source_target_pairs={{0,4},{4,0},{8,12},{12,8},{16,20},{20,16},{24,28},{28,24},{1,5},{5... | collective-permute-start | bytes 442376 | tf_op jit(solution)/shard_map/ppermute | solution.py:301
  16.6 1.6 %collective-permute-start.6 = (bf16[3,192,128]{2,1,0:T(8,128)(2,1)S(1)}, bf16[3,192,128]{2,1,0:T(8,128)(2,1)S(1)}, u32[]{:S(2)}, u32[]{:S(2)}) collective-permute-start(bf16[3,192,128]{2,1,0:T(8,128)(2,1)S(1)} %get-tuple-element.48), channel_id=1, source_target_pairs={{0,4},{4,0},{8,12},{12,8},{16,20},{20,16},{24,28},{28,24},{1,5},{5... | collective-permute-start | bytes 442376 | tf_op jit(solution)/shard_map/ppermute | solution.py:301
  20.0 5.3 %collective-permute-start.10 = (bf16[192,128]{1,0:T(8,128)(2,1)S(1)}, bf16[192,128]{1,0:T(8,128)(2,1)S(1)}, u32[]{:S(2)}, u32[]{:S(2)}) collective-permute-start(bf16[192,128]{1,0:T(8,128)(2,1)S(1)} %get-tuple-element.55), channel_id=1, source_target_pairs={{0,24},{4,28},{8,16},{12,20},{16,8},{20,12},{24,0},{28,4},{1,25},{... | collective-permute-start | bytes 147464 | tf_op jit(solution)/shard_map/ppermute | solution.py:301
  21.6 5.1 %collective-permute-start.7 = (bf16[192,128]{1,0:T(8,128)(2,1)S(1)}, bf16[192,128]{1,0:T(8,128)(2,1)S(1)}, u32[]{:S(2)}, u32[]{:S(2)}) collective-permute-start(bf16[192,128]{1,0:T(8,128)(2,1)S(1)} %get-tuple-element.50), channel_id=1, source_target_pairs={{0,8},{4,12},{8,0},{12,4},{16,24},{20,28},{24,16},{28,20},{1,9},{5... | collective-permute-start | bytes 147464 | tf_op jit(solution)/shard_map/ppermute | solution.py:301
  23.7 4.6 %collective-permute-start.8 = (bf16[192,128]{1,0:T(8,128)(2,1)S(1)}, bf16[192,128]{1,0:T(8,128)(2,1)S(1)}, u32[]{:S(2)}, u32[]{:S(2)}) collective-permute-start(bf16[192,128]{1,0:T(8,128)(2,1)S(1)} %get-tuple-element.51), channel_id=1, source_target_pairs={{0,16},{4,20},{8,24},{12,28},{16,0},{20,4},{24,8},{28,12},{1,17},{... | collective-permute-start | bytes 147464 | tf_op jit(solution)/shard_map/ppermute | solution.py:301
  23.7 5.4 %collective-permute-start.15 = (bf16[224,384]{1,0:T(8,128)(2,1)S(1)}, bf16[224,384]{1,0:T(8,128)(2,1)S(1)}, u32[]{:S(2)}, u32[]{:S(2)}) collective-permute-start(bf16[224,384]{1,0:T(8,128)(2,1)S(1)} %collective-permute-done.11.refs_9_), channel_id=1, source_target_pairs={{0,8},{4,20},{8,0},{12,28},{16,24},{20,4},{24,16},{28,12},{1,9},{5... | collective-permute-start | bytes 516104 | tf_op jit(solution)/shard_map/ppermute | solution.py:307
  28.4 2.3 %collective-permute-start.14 = (bf16[384,384]{1,0:T(8,128)(2,1)S(1)}, bf16[384,384]{1,0:T(8,128)(2,1)S(1)}, u32[]{:S(2)}, u32[]{:S(2)}) collective-permute-start(bf16[384,384]{1,0:T(8,128)(2,1)S(1)} %collective-permute-done.9.refs_6_), channel_id=1, source_target_pairs={{0,4},{4,0},{8,12},{12,8},{16,20},{20,16},{24,28},{28,24},{1,5},{5... | collective-permute-start | bytes 884744 | tf_op jit(solution)/shard_map/ppermute | solution.py:301
  28.4 2.3 %collective-permute-start.12 = (bf16[384,384]{1,0:T(8,128)(2,1)S(1)}, bf16[384,384]{1,0:T(8,128)(2,1)S(1)}, u32[]{:S(2)}, u32[]{:S(2)}) collective-permute-start(bf16[384,384]{1,0:T(8,128)(2,1)S(1)} %collective-permute-done.refs_5_), channel_id=1, source_target_pairs={{0,4},{4,0},{8,12},{12,8},{16,20},{20,16},{24,28},{28,24},{1,5},{5... | collective-permute-start | bytes 884744 | tf_op jit(solution)/shard_map/ppermute | solution.py:301
  28.9 1.7 %collective-permute-start.13 = (bf16[224,384]{1,0:T(8,128)(2,1)S(1)}, bf16[224,384]{1,0:T(8,128)(2,1)S(1)}, u32[]{:S(2)}, u32[]{:S(2)}) collective-permute-start(bf16[224,384]{1,0:T(8,128)(2,1)S(1)} %collective-permute-done.11.refs_9_), channel_id=1, source_target_pairs={{0,4},{4,0},{8,12},{12,8},{16,20},{20,16},{24,28},{28,24},{1,5},{5... | collective-permute-start | bytes 516104 | tf_op jit(solution)/shard_map/ppermute | solution.py:301
  29.2 2.3 %collective-permute-start.16 = (bf16[224,384]{1,0:T(8,128)(2,1)S(1)}, bf16[224,384]{1,0:T(8,128)(2,1)S(1)}, u32[]{:S(2)}, u32[]{:S(2)}) collective-permute-start(bf16[224,384]{1,0:T(8,128)(2,1)S(1)} %collective-permute-done.15.refs_11_), channel_id=1, source_target_pairs={{0,4},{4,0},{8,12},{12,8},{16,20},{20,16},{24,28},{28,24},{1,5},{5... | collective-permute-start | bytes 516104 | tf_op jit(solution)/shard_map/ppermute | solution.py:301

commit v19 on v17

--- a/solution.py
+++ b/solution.py
@@ -100,8 +100,8 @@
     at_feature = lax.broadcasted_iota(jnp.int32, (pad, block), 0)
     at_frame = lax.broadcasted_iota(jnp.int32, (pad, block), 1)
 
-    def prepare(head):
-        for at in range(groups * HEADS):
+    def prepare(head, pieces):
+        for at in pieces:
             here = slice(at * block, (at + 1) * block)
             frame = (at // HEADS * HEADS + (place ^ (at % HEADS))) * block + at_frame
             bias = jnp.where((at_feature == 0) & (frame >= lengths_ref[:1, :]), -1e30, 0.0).astype(keys.dtype)
@@ -111,13 +111,16 @@
     def score(head, flips):
         rows = slice(head * head_size, (head + 1) * head_size)
         query = jnp.concatenate([jnp.concatenate([same[flip // 2][0, rows, :], ones], axis=0) for flip in flips], axis=1)
-        return [jnp.dot(keys[head, part, :], query, preferred_element_type=jnp.float32) for part in parts]
+        scores = []
+        for part in parts:
+            if flips == FLIPS[:2]:
+                prepare(head, range(part.start // block, part.stop // block))
+            scores.append(jnp.dot(keys[head, part, :], query, preferred_element_type=jnp.float32))
+        return scores
 
     parts = [slice(first, first + keys.shape[1] // 4) for first in range(0, keys.shape[1], keys.shape[1] // 4)]
     chunks = [(head, flips) for head in range(2) for flips in (FLIPS[:2], FLIPS[2:])]
-    prepare(0)
     later = score(*chunks[0])
-    prepare(1)
     for at, (head, flips) in enumerate(chunks):
         scores = later
         if at + 1 < len(chunks):
@@ -346,8 +349,8 @@
     if not split_columns:
         return project(heads, [half, exchange(half, "ctx", 1)])
     third_passed = exchange_in_plane(third)
-    heads[3], fetched, third = lax.optimization_barrier((heads[3], fetched, third))
-    heads[1], heads[2], passed = lax.optimization_barrier((heads[1], heads[2], passed))
+    heads[3], fetched = lax.optimization_barrier((heads[3], fetched))
+    heads[1], heads[2], passed, third = lax.optimization_barrier((heads[1], heads[2], passed, third))
     fetched_other, passed_other, third_other, third_passed_other = (
         exchange(array, "ctx", 1) for array in (fetched, passed, third, third_passed)
     )

time: 30.3 us -> 30.3 us (level)
  no operation moved by 1% of the time
where the time goes in v19:
time: 30.3 us; the launch traced here: 30.1 us
  starting transfers between devices  15.3 us (50%)
  waiting for transfers between devices  8.98 us (30%)
  Pallas kernels  5.11 us (17%)
  between operations  0.74 us (2%)
    ppermute x12, starting transfers between devices, exchange(): return lax.ppermute(array, axis, [(i, i ^ flip) for i in range(size)])  7.87 us
    ppermute x12, waiting for transfers between devices, exchange(): return lax.ppermute(array, axis, [(i, i ^ flip) for i in range(size)])  6.53 us
    ppermute x2, starting transfers between devices, exchange_along(): return lax.ppermute(array, ('ctx', 'fsdp'), pairs)  5.43 us
    ppermute x2, starting transfers between devices, exchange_in_plane(): lax.ppermute(array, 'ctx', [(i, i ^ (4 if i % 2 else 2)) for i in range(c...  1.97 us
    pallas_call x1, Pallas kernels, attend(): pl.pallas_call(functools.partial(attention_kernel, groups), out_shape=[pl...  1.91 us
    ppermute x2, waiting for transfers between devices, exchange_along(): return lax.ppermute(array, ('ctx', 'fsdp'), pairs)  1.42 us
    pallas_call x1, Pallas kernels, copy_in(): pl.pallas_call(functools.partial(copy_in_kernel, by_parity), out_shape=[p...  1.24 us
    ppermute x2, waiting for transfers between devices, exchange_in_plane(): lax.ppermute(array, 'ctx', [(i, i ^ (4 if i % 2 else 2)) for i in range(c...  1.02 us
  transfers between devices with their start and end apart: 16, of which 9 were waited for; matrix products, arithmetic and copies ran while one was open for 0% of the time, Pallas kernels for 10%

profile of v19, /device:TPU:0, one launch (start us, length us, event | category | flops | bytes accessed | tf_op | source)
XLA Modules:
  0.0 30.1 jit_solution(2982783698343550582)
XLA Ops:
  0.0 1.2 %copy_in.1 = (bf16[3,128,768]{2,1,0:T(8,128)(2,1)S(1)}, bf16[384,384]{1,0:T(8,128)(2,1)S(1)}) custom-call(bf16[1,128,768]{2,1,0:T(8,128)(2,1)} %query_ref.1, bf16[1,128,768]{2,1,0:T(8,128)(2,1)} %key_ref.1, bf16[1,128,768]{2,1,0:T(8,128)(2,1)} %value_ref.1, bf16[768,384]{1,0:T(8,128)(2,1)} %refs_4_.1), custom_call_target="tpu_custom_call" | custom-call | tf_op jit(solution)/shard_map/copy_in/pallas_call | solution.py:45
  1.2 4.1 %collective-permute-start = (bf16[384,384]{1,0:T(8,128)(2,1)S(1)}, bf16[384,384]{1,0:T(8,128)(2,1)S(1)}, u32[]{:S(2)}, u32[]{:S(2)}) collective-permute-start(bf16[384,384]{1,0:T(8,128)(2,1)S(1)} %get-tuple-element.33), channel_id=1, source_target_pairs={{0,2},{1,3},{2,0},{3,1},{4,5},{5,4},{6,7},{7,6},{8,10},{9,11},{10,... | collective-permute-start | bytes 884744 | tf_op jit(solution)/shard_map/ppermute | solution.py:313
  5.3 0.2 turn_heads.1
  5.6 1.6 %collective-permute-start.2 = (bf16[3,192,128]{2,1,0:T(8,128)(2,1)S(1)}, bf16[3,192,128]{2,1,0:T(8,128)(2,1)S(1)}, u32[]{:S(2)}, u32[]{:S(2)}) collective-permute-start(bf16[3,192,128]{2,1,0:T(8,128)(2,1)S(1)} %get-tuple-element.37), channel_id=1, source_target_pairs={{0,8},{4,12},{8,0},{12,4},{16,24},{20,28},{24,16},{28,20},{1,9},{5... | collective-permute-start | bytes 442376 | tf_op jit(solution)/shard_map/ppermute | solution.py:303
  7.2 1.5 %collective-permute-start.3 = (bf16[3,192,128]{2,1,0:T(8,128)(2,1)S(1)}, bf16[3,192,128]{2,1,0:T(8,128)(2,1)S(1)}, u32[]{:S(2)}, u32[]{:S(2)}) collective-permute-start(bf16[3,192,128]{2,1,0:T(8,128)(2,1)S(1)} %get-tuple-element.38), channel_id=1, source_target_pairs={{0,16},{4,20},{8,24},{12,28},{16,0},{20,4},{24,8},{28,12},{1,17},{... | collective-permute-start | bytes 442376 | tf_op jit(solution)/shard_map/ppermute | solution.py:303
  8.7 0.5 %collective-permute-start.4 = (bf16[3,192,128]{2,1,0:T(8,128)(2,1)S(1)}, bf16[3,192,128]{2,1,0:T(8,128)(2,1)S(1)}, u32[]{:S(2)}, u32[]{:S(2)}) collective-permute-start(bf16[3,192,128]{2,1,0:T(8,128)(2,1)S(1)} %get-tuple-element.39), channel_id=1, source_target_pairs={{0,24},{4,28},{8,16},{12,20},{16,8},{20,12},{24,0},{28,4},{1,25},{... | collective-permute-start | bytes 442376 | tf_op jit(solution)/shard_map/ppermute | solution.py:303
  9.2 0.1 collective-permute-start.1
  9.9 0.6 %collective-permute-done.1.refs_4_ = bf16[2,192,128]{2,1,0:T(8,128)(2,1)S(1)} collective-permute-done((bf16[2,192,128]{2,1,0:T(8,128)(2,1)S(1)}, bf16[2,192,128]{2,1,0:T(8,128)(2,1)S(1)}, u32[]{:S(2)}, u32[]{:S(2)}) %collective-permute-start.1) | collective-permute-done | bytes 98336 | tf_op jit(solution)/shard_map/ppermute | solution.py:303
  10.5 1.4 %collective-permute-done.refs_5_ = bf16[384,384]{1,0:T(8,128)(2,1)S(1)} collective-permute-done((bf16[384,384]{1,0:T(8,128)(2,1)S(1)}, bf16[384,384]{1,0:T(8,128)(2,1)S(1)}, u32[]{:S(2)}, u32[]{:S(2)}) %collective-permute-start) | collective-permute-done | bytes 294944 | tf_op jit(solution)/shard_map/ppermute | solution.py:313
  12.0 0.4 %collective-permute-done.2.refs_0_.refs_1_ = bf16[3,192,128]{2,1,0:T(8,128)(2,1)S(1)} collective-permute-done((bf16[3,192,128]{2,1,0:T(8,128)(2,1)S(1)}, bf16[3,192,128]{2,1,0:T(8,128)(2,1)S(1)}, u32[]{:S(2)}, u32[]{:S(2)}) %collective-permute-start.2) | collective-permute-done | bytes 147488 | tf_op jit(solution)/shard_map/ppermute | solution.py:303
  12.4 2.8 %collective-permute-done.3.refs_1_.refs_2_ = bf16[3,192,128]{2,1,0:T(8,128)(2,1)S(1)} collective-permute-done((bf16[3,192,128]{2,1,0:T(8,128)(2,1)S(1)}, bf16[3,192,128]{2,1,0:T(8,128)(2,1)S(1)}, u32[]{:S(2)}, u32[]{:S(2)}) %collective-permute-start.3) | collective-permute-done | bytes 147488 | tf_op jit(solution)/shard_map/ppermute | solution.py:303
  15.2 0.0 collective-permute-done.4.refs_2_.refs_3_
  15.2 0.1 collective-permute-start.5
  15.3 0.5 %collective-permute-start.8 = (bf16[384,384]{1,0:T(8,128)(2,1)S(1)}, bf16[384,384]{1,0:T(8,128)(2,1)S(1)}, u32[]{:S(2)}, u32[]{:S(2)}) collective-permute-start(bf16[384,384]{1,0:T(8,128)(2,1)S(1)} %collective-permute-done.refs_5_), channel_id=1, source_target_pairs={{0,8},{4,20},{8,0},{12,28},{16,24},{20,4},{24,16},{28,12},{1,9},{5... | collective-permute-start | bytes 884744 | tf_op jit(solution)/shard_map/ppermute | solution.py:309
  15.8 0.0 copy-start
  15.8 1.3 %collective-permute-start.9 = (bf16[208,384]{1,0:T(8,128)(2,1)S(1)}, bf16[208,384]{1,0:T(8,128)(2,1)S(1)}, u32[]{:S(2)}, u32[]{:S(2)}) collective-permute-start(bf16[208,384]{1,0:T(8,128)(2,1)S(1)} %constant_dynamic-slice_fusion), channel_id=1, source_target_pairs={{0,1},{1,0},{2,3},{3,2},{4,6},{5,7},{6,4},{7,5},{8,9},{9,8},{10,11... | collective-permute-start | bytes 479240 | tf_op jit(solution)/shard_map/ppermute | solution.py:313
  17.1 0.0 collective-permute-done.5.refs_5_
  17.1 1.9 %attend_two_heads.1 = (bf16[192,128]{1,0:T(8,128)(2,1)S(1)}, bf16[192,128]{1,0:T(8,128)(2,1)S(1)}, bf16[192,128]{1,0:T(8,128)(2,1)S(1)}, bf16[192,128]{1,0:T(8,128)(2,1)S(1)}) custom-call(s32[8,128]{1,0:T(8,128)S(1)} %broadcast_in_dim.2.lengths_ref, bf16[3,192,128]{2,1,0:T(8,128)(2,1)S(1)} %get-tuple-element.35.refs_0_, ...), custom_call_target="tpu_custom_call" | custom-call | flops 1610612736 | tf_op jit(solution)/shard_map/attend_two_heads/pallas_call | solution.py:160
  19.0 1.6 %collective-permute-start.6 = (bf16[192,128]{1,0:T(8,128)(2,1)S(1)}, bf16[192,128]{1,0:T(8,128)(2,1)S(1)}, u32[]{:S(2)}, u32[]{:S(2)}) collective-permute-start(bf16[192,128]{1,0:T(8,128)(2,1)S(1)} %get-tuple-element.46), channel_id=1, source_target_pairs={{0,8},{4,12},{8,0},{12,4},{16,24},{20,28},{24,16},{28,20},{1,9},{5... | collective-permute-start | bytes 147464 | tf_op jit(solution)/shard_map/ppermute | solution.py:303
  20.6 0.7 %collective-permute-start.7 = (bf16[192,128]{1,0:T(8,128)(2,1)S(1)}, bf16[192,128]{1,0:T(8,128)(2,1)S(1)}, u32[]{:S(2)}, u32[]{:S(2)}) collective-permute-start(bf16[192,128]{1,0:T(8,128)(2,1)S(1)} %get-tuple-element.47), channel_id=1, source_target_pairs={{0,16},{4,20},{8,24},{12,28},{16,0},{20,4},{24,8},{28,12},{1,17},{... | collective-permute-start | bytes 147464 | tf_op jit(solution)/shard_map/ppermute | solution.py:303
  21.3 1.3 %collective-permute-start.10 = (bf16[192,128]{1,0:T(8,128)(2,1)S(1)}, bf16[192,128]{1,0:T(8,128)(2,1)S(1)}, u32[]{:S(2)}, u32[]{:S(2)}) collective-permute-start(bf16[192,128]{1,0:T(8,128)(2,1)S(1)} %get-tuple-element.51), channel_id=1, source_target_pairs={{0,24},{4,28},{8,16},{12,20},{16,8},{20,12},{24,0},{28,4},{1,25},{... | collective-permute-start | bytes 147464 | tf_op jit(solution)/shard_map/ppermute | solution.py:303
  22.6 0.0 collective-permute-done.9.refs_9_
  22.6 1.5 %collective-permute-start.14 = (bf16[208,384]{1,0:T(8,128)(2,1)S(1)}, bf16[208,384]{1,0:T(8,128)(2,1)S(1)}, u32[]{:S(2)}, u32[]{:S(2)}) collective-permute-start(bf16[208,384]{1,0:T(8,128)(2,1)S(1)} %collective-permute-done.9.refs_9_), channel_id=1, source_target_pairs={{0,8},{4,20},{8,0},{12,28},{16,24},{20,4},{24,16},{28,12},{1,9},{5... | collective-permute-start | bytes 479240 | tf_op jit(solution)/shard_map/ppermute | solution.py:309
  24.1 0.0 collective-permute-done.8.refs_6_
  24.1 0.0 collective-permute-done.6.refs_1_
  24.1 0.6 %collective-permute-done.7.refs_2_ = bf16[192,128]{1,0:T(8,128)(2,1)S(1)} collective-permute-done((bf16[192,128]{1,0:T(8,128)(2,1)S(1)}, bf16[192,128]{1,0:T(8,128)(2,1)S(1)}, u32[]{:S(2)}, u32[]{:S(2)}) %collective-permute-start.7) | collective-permute-done | bytes 49184 | tf_op jit(solution)/shard_map/ppermute | solution.py:303
  24.7 0.0 collective-permute-start.13
  24.7 1.6 %collective-permute-done.10.refs_3_ = bf16[192,128]{1,0:T(8,128)(2,1)S(1)} collective-permute-done((bf16[192,128]{1,0:T(8,128)(2,1)S(1)}, bf16[192,128]{1,0:T(8,128)(2,1)S(1)}, u32[]{:S(2)}, u32[]{:S(2)}) %collective-permute-start.10) | collective-permute-done | bytes 49184 | tf_op jit(solution)/shard_map/ppermute | solution.py:303
  26.3 0.0 collective-permute-start.11
  26.3 0.5 %collective-permute-start.12 = (bf16[208,384]{1,0:T(8,128)(2,1)S(1)}, bf16[208,384]{1,0:T(8,128)(2,1)S(1)}, u32[]{:S(2)}, u32[]{:S(2)}) collective-permute-start(bf16[208,384]{1,0:T(8,128)(2,1)S(1)} %collective-permute-done.9.refs_9_), channel_id=1, source_target_pairs={{0,4},{4,0},{8,12},{12,8},{16,20},{20,16},{24,28},{28,24},{1,5},{5... | collective-permute-start | bytes 479240 | tf_op jit(solution)/shard_map/ppermute | solution.py:303
  26.8 1.0 %collective-permute-done.14.refs_11_ = bf16[208,384]{1,0:T(8,128)(2,1)S(1)} collective-permute-done((bf16[208,384]{1,0:T(8,128)(2,1)S(1)}, bf16[208,384]{1,0:T(8,128)(2,1)S(1)}, u32[]{:S(2)}, u32[]{:S(2)}) %collective-permute-start.14) | collective-permute-done | bytes 159776 | tf_op jit(solution)/shard_map/ppermute | solution.py:309
  27.9 0.1 collective-permute-start.15
  28.0 0.2 collective-permute-done.12.refs_10_
  28.1 0.0 collective-permute-done.13.refs_8_
  28.1 0.0 collective-permute-done.11.refs_7_
  28.2 0.0 copy-done
  28.2 0.8 %project_near_shards.1 = (bf16[3,128,384]{2,1,0:T(8,128)(2,1)S(1)}, f32[128,384]{1,0:T(8,128)S(1)}, bf16[128,192]{1,0:T(8,128)(2,1)S(1)}) custom-call(bf16[192,128]{1,0:T(8,128)(2,1)S(1)} %get-tuple-element.45.refs_0_, bf16[192,128]{1,0:T(8,128)(2,1)S(1)} %collective-permute-done.6.refs_1_, bf16[192,128]{1,0:T(8,128)(2,1)S(1)} %collective-permute-done.7.refs_2_, ...), custom_call_target="tpu_custom_call" | custom-call | flops 226492416 | bytes 1769472 | tf_op jit(solution)/shard_map/project_near_shards/pallas_call | solution.py:266
  29.0 0.3 collective-permute-done.15.part_ref
  29.3 0.9 %project_third_shard.1 = bf16[1,128,1536]{2,1,0:T(8,128)(2,1)} custom-call(bf16[3,128,384]{2,1,0:T(8,128)(2,1)S(1)} %get-tuple-element.58.blocks_ref, f32[128,384]{1,0:T(8,128)S(1)} %get-tuple-element.59.sum_ref, bf16[128,192]{1,0:T(8,128)(2,1)S(1)} %get-tuple-element.60.rest_ref, bf16[208,384]{1,0:T(8,128)(2,1)S(1)} %collective-permute-done.15.part_ref), custom_call_target="tpu_custom_call" | custom-call | flops 18874368 | bytes 147456 | tf_op jit(solution)/shard_map/project_third_shard/pallas_call | solution.py:288
  (4 shorter events, 0.0 us)
Async XLA Ops:
  1.2 10.7 %collective-permute-start = (bf16[384,384]{1,0:T(8,128)(2,1)S(1)}, bf16[384,384]{1,0:T(8,128)(2,1)S(1)}, u32[]{:S(2)}, u32[]{:S(2)}) collective-permute-start(bf16[384,384]{1,0:T(8,128)(2,1)S(1)} %get-tuple-element.33), channel_id=1, source_target_pairs={{0,2},{1,3},{2,0},{3,1},{4,5},{5,4},{6,7},{7,6},{8,10},{9,11},{10,... | collective-permute-start | bytes 884744 | tf_op jit(solution)/shard_map/ppermute | solution.py:313
  5.6 6.8 %collective-permute-start.2 = (bf16[3,192,128]{2,1,0:T(8,128)(2,1)S(1)}, bf16[3,192,128]{2,1,0:T(8,128)(2,1)S(1)}, u32[]{:S(2)}, u32[]{:S(2)}) collective-permute-start(bf16[3,192,128]{2,1,0:T(8,128)(2,1)S(1)} %get-tuple-element.37), channel_id=1, source_target_pairs={{0,8},{4,12},{8,0},{12,4},{16,24},{20,28},{24,16},{28,20},{1,9},{5... | collective-permute-start | bytes 442376 | tf_op jit(solution)/shard_map/ppermute | solution.py:303
  7.2 8.0 %collective-permute-start.3 = (bf16[3,192,128]{2,1,0:T(8,128)(2,1)S(1)}, bf16[3,192,128]{2,1,0:T(8,128)(2,1)S(1)}, u32[]{:S(2)}, u32[]{:S(2)}) collective-permute-start(bf16[3,192,128]{2,1,0:T(8,128)(2,1)S(1)} %get-tuple-element.38), channel_id=1, source_target_pairs={{0,16},{4,20},{8,24},{12,28},{16,0},{20,4},{24,8},{28,12},{1,17},{... | collective-permute-start | bytes 442376 | tf_op jit(solution)/shard_map/ppermute | solution.py:303
  8.7 6.5 %collective-permute-start.4 = (bf16[3,192,128]{2,1,0:T(8,128)(2,1)S(1)}, bf16[3,192,128]{2,1,0:T(8,128)(2,1)S(1)}, u32[]{:S(2)}, u32[]{:S(2)}) collective-permute-start(bf16[3,192,128]{2,1,0:T(8,128)(2,1)S(1)} %get-tuple-element.39), channel_id=1, source_target_pairs={{0,24},{4,28},{8,16},{12,20},{16,8},{20,12},{24,0},{28,4},{1,25},{... | collective-permute-start | bytes 442376 | tf_op jit(solution)/shard_map/ppermute | solution.py:303
  9.2 1.4 %collective-permute-start.1 = (bf16[2,192,128]{2,1,0:T(8,128)(2,1)S(1)}, bf16[2,192,128]{2,1,0:T(8,128)(2,1)S(1)}, u32[]{:S(2)}, u32[]{:S(2)}) collective-permute-start(bf16[2,192,128]{2,1,0:T(8,128)(2,1)S(1)} %slice.3), channel_id=1, source_target_pairs={{0,4},{4,0},{8,12},{12,8},{16,20},{20,16},{24,28},{28,24},{1,5},{5... | collective-permute-start | bytes 294920 | tf_op jit(solution)/shard_map/ppermute | solution.py:303
  15.2 1.9 %collective-permute-start.5 = (bf16[3,2,192,128]{3,2,1,0:T(8,128)(2,1)S(1)}, bf16[3,2,192,128]{3,2,1,0:T(8,128)(2,1)S(1)}, u32[]{:S(2)}, u32[]{:S(2)}) collective-permute-start(bf16[3,2,192,128]{3,2,1,0:T(8,128)(2,1)S(1)} %stack_keys_and_values.1), channel_id=1, source_target_pairs={{0,4},{4,0},{8,12},{12,8},{16,20},{20,16},{24,28},{28,24},{1,5},{5... | collective-permute-start | bytes 884744 | tf_op jit(solution)/shard_map/ppermute | solution.py:303
  15.3 8.8 %collective-permute-start.8 = (bf16[384,384]{1,0:T(8,128)(2,1)S(1)}, bf16[384,384]{1,0:T(8,128)(2,1)S(1)}, u32[]{:S(2)}, u32[]{:S(2)}) collective-permute-start(bf16[384,384]{1,0:T(8,128)(2,1)S(1)} %collective-permute-done.refs_5_), channel_id=1, source_target_pairs={{0,8},{4,20},{8,0},{12,28},{16,24},{20,4},{24,16},{28,12},{1,9},{5... | collective-permute-start | bytes 884744 | tf_op jit(solution)/shard_map/ppermute | solution.py:309
  15.8 12.4 %copy-start = (bf16[768,384]{1,0:T(8,128)(2,1)S(1)}, bf16[768,384]{1,0:T(8,128)(2,1)}, u32[]{:S(2)}) copy-start(bf16[768,384]{1,0:T(8,128)(2,1)} %refs_4_.1) | copy-start | bytes 1769476
  15.8 6.8 %collective-permute-start.9 = (bf16[208,384]{1,0:T(8,128)(2,1)S(1)}, bf16[208,384]{1,0:T(8,128)(2,1)S(1)}, u32[]{:S(2)}, u32[]{:S(2)}) collective-permute-start(bf16[208,384]{1,0:T(8,128)(2,1)S(1)} %constant_dynamic-slice_fusion), channel_id=1, source_target_pairs={{0,1},{1,0},{2,3},{3,2},{4,6},{5,7},{6,4},{7,5},{8,9},{9,8},{10,11... | collective-permute-start | bytes 479240 | tf_op jit(solution)/shard_map/ppermute | solution.py:313
  19.0 5.1 %collective-permute-start.6 = (bf16[192,128]{1,0:T(8,128)(2,1)S(1)}, bf16[192,128]{1,0:T(8,128)(2,1)S(1)}, u32[]{:S(2)}, u32[]{:S(2)}) collective-permute-start(bf16[192,128]{1,0:T(8,128)(2,1)S(1)} %get-tuple-element.46), channel_id=1, source_target_pairs={{0,8},{4,12},{8,0},{12,4},{16,24},{20,28},{24,16},{28,20},{1,9},{5... | collective-permute-start | bytes 147464 | tf_op jit(solution)/shard_map/ppermute | solution.py:303
  20.6 4.1 %collective-permute-start.7 = (bf16[192,128]{1,0:T(8,128)(2,1)S(1)}, bf16[192,128]{1,0:T(8,128)(2,1)S(1)}, u32[]{:S(2)}, u32[]{:S(2)}) collective-permute-start(bf16[192,128]{1,0:T(8,128)(2,1)S(1)} %get-tuple-element.47), channel_id=1, source_target_pairs={{0,16},{4,20},{8,24},{12,28},{16,0},{20,4},{24,8},{28,12},{1,17},{... | collective-permute-start | bytes 147464 | tf_op jit(solution)/shard_map/ppermute | solution.py:303
  21.3 5.1 %collective-permute-start.10 = (bf16[192,128]{1,0:T(8,128)(2,1)S(1)}, bf16[192,128]{1,0:T(8,128)(2,1)S(1)}, u32[]{:S(2)}, u32[]{:S(2)}) collective-permute-start(bf16[192,128]{1,0:T(8,128)(2,1)S(1)} %get-tuple-element.51), channel_id=1, source_target_pairs={{0,24},{4,28},{8,16},{12,20},{16,8},{20,12},{24,0},{28,4},{1,25},{... | collective-permute-start | bytes 147464 | tf_op jit(solution)/shard_map/ppermute | solution.py:303
  22.6 5.3 %collective-permute-start.14 = (bf16[208,384]{1,0:T(8,128)(2,1)S(1)}, bf16[208,384]{1,0:T(8,128)(2,1)S(1)}, u32[]{:S(2)}, u32[]{:S(2)}) collective-permute-start(bf16[208,384]{1,0:T(8,128)(2,1)S(1)} %collective-permute-done.9.refs_9_), channel_id=1, source_target_pairs={{0,8},{4,20},{8,0},{12,28},{16,24},{20,4},{24,16},{28,12},{1,9},{5... | collective-permute-start | bytes 479240 | tf_op jit(solution)/shard_map/ppermute | solution.py:309
  24.7 3.5 %collective-permute-start.13 = (bf16[384,384]{1,0:T(8,128)(2,1)S(1)}, bf16[384,384]{1,0:T(8,128)(2,1)S(1)}, u32[]{:S(2)}, u32[]{:S(2)}) collective-permute-start(bf16[384,384]{1,0:T(8,128)(2,1)S(1)} %collective-permute-done.8.refs_6_), channel_id=1, source_target_pairs={{0,4},{4,0},{8,12},{12,8},{16,20},{20,16},{24,28},{28,24},{1,5},{5... | collective-permute-start | bytes 884744 | tf_op jit(solution)/shard_map/ppermute | solution.py:303
  26.3 1.8 %collective-permute-start.11 = (bf16[384,384]{1,0:T(8,128)(2,1)S(1)}, bf16[384,384]{1,0:T(8,128)(2,1)S(1)}, u32[]{:S(2)}, u32[]{:S(2)}) collective-permute-start(bf16[384,384]{1,0:T(8,128)(2,1)S(1)} %collective-permute-done.refs_5_), channel_id=1, source_target_pairs={{0,4},{4,0},{8,12},{12,8},{16,20},{20,16},{24,28},{28,24},{1,5},{5... | collective-permute-start | bytes 884744 | tf_op jit(solution)/shard_map/ppermute | solution.py:303
  26.3 1.8 %collective-permute-start.12 = (bf16[208,384]{1,0:T(8,128)(2,1)S(1)}, bf16[208,384]{1,0:T(8,128)(2,1)S(1)}, u32[]{:S(2)}, u32[]{:S(2)}) collective-permute-start(bf16[208,384]{1,0:T(8,128)(2,1)S(1)} %collective-permute-done.9.refs_9_), channel_id=1, source_target_pairs={{0,4},{4,0},{8,12},{12,8},{16,20},{20,16},{24,28},{28,24},{1,5},{5... | collective-permute-start | bytes 479240 | tf_op jit(solution)/shard_map/ppermute | solution.py:303
  27.9 1.4 %collective-permute-start.15 = (bf16[208,384]{1,0:T(8,128)(2,1)S(1)}, bf16[208,384]{1,0:T(8,128)(2,1)S(1)}, u32[]{:S(2)}, u32[]{:S(2)}) collective-permute-start(bf16[208,384]{1,0:T(8,128)(2,1)S(1)} %collective-permute-done.14.refs_11_), channel_id=1, source_target_pairs={{0,4},{4,0},{8,12},{12,8},{16,20},{20,16},{24,28},{28,24},{1,5},{5... | collective-permute-start | bytes 479240 | tf_op jit(solution)/shard_map/ppermute | solution.py:303

commit v20 on v17

--- a/solution.py
+++ b/solution.py
@@ -20,6 +20,22 @@
 
 def place_in_group():
     return lax.axis_index("ctx") % HEADS
+
+
+def stage_kernel(source_ref, out_ref):
+    out_ref[...] = source_ref[...]
+
+
+def stage(array, flops):
+    return pl.pallas_call(
+        stage_kernel,
+        out_shape=pltpu.VMEM(array.shape, array.dtype),
+        in_specs=[WHOLE],
+        out_specs=WHOLE,
+        compiler_params=params(16),
+        cost_estimate=pl.CostEstimate(flops=flops, bytes_accessed=0, transcendentals=0),
+        name="stage_third_shard",
+    )(array)
 
 
 def parity_of(place):
@@ -345,7 +361,7 @@
     heads = [mixed[0], *exchange_chips(mixed[1:])]
     if not split_columns:
         return project(heads, [half, exchange(half, "ctx", 1)])
-    third_passed = exchange_in_plane(third)
+    third_passed = exchange_in_plane(stage(third, 1500000000))
     heads[3], fetched, third = lax.optimization_barrier((heads[3], fetched, third))
     heads[1], heads[2], passed = lax.optimization_barrier((heads[1], heads[2], passed))
     fetched_other, passed_other, third_other, third_passed_other = (

time: 30.3 us -> 30.3 us (level)
    ppermute x2, waiting for transfers between devices: 1.02 us -> 1.73 us  [exchange_in_plane(): lax.ppermute(array, 'ctx', [(i, i ^ (4 if i % 2 else 2)) for i in range(c...]
    ppermute x12, waiting for transfers between devices: 6.53 us -> 5.9 us  [exchange(): return lax.ppermute(array, axis, [(i, i ^ flip) for i in range(size)])]
  transfers between devices with their start and end apart: 16 -> 16, of which waited for: 9 -> 8; matrix products, arithmetic and copies ran while one was open for 0% -> 0% of each run, Pallas kernels for 10% -> 10%
where the time goes in v20:
time: 30.3 us; the launch traced here: 30.1 us
  starting transfers between devices  15.2 us (50%)
  waiting for transfers between devices  9.06 us (30%)
  Pallas kernels  5.14 us (17%)
  between operations  0.76 us (3%)
    ppermute x12, starting transfers between devices, exchange(): return lax.ppermute(array, axis, [(i, i ^ flip) for i in range(size)])  7.76 us
    ppermute x12, waiting for transfers between devices, exchange(): return lax.ppermute(array, axis, [(i, i ^ flip) for i in range(size)])  5.9 us
    ppermute x2, starting transfers between devices, exchange_along(): return lax.ppermute(array, ('ctx', 'fsdp'), pairs)  5.3 us
    ppermute x2, starting transfers between devices, exchange_in_plane(): lax.ppermute(array, 'ctx', [(i, i ^ (4 if i % 2 else 2)) for i in range(c...  2.09 us
    pallas_call x1, Pallas kernels, attend(): pl.pallas_call(functools.partial(attention_kernel, groups), out_shape=[pl...  1.91 us
    ppermute x2, waiting for transfers between devices, exchange_in_plane(): lax.ppermute(array, 'ctx', [(i, i ^ (4 if i % 2 else 2)) for i in range(c...  1.73 us
    ppermute x2, waiting for transfers between devices, exchange_along(): return lax.ppermute(array, ('ctx', 'fsdp'), pairs)  1.42 us
    pallas_call x1, Pallas kernels, copy_in(): pl.pallas_call(functools.partial(copy_in_kernel, by_parity), out_shape=[p...  1.24 us
  transfers between devices with their start and end apart: 16, of which 8 were waited for; matrix products, arithmetic and copies ran while one was open for 0% of the time, Pallas kernels for 10%

profile of v20, /device:TPU:0, one launch (start us, length us, event | category | flops | bytes accessed | tf_op | source)
XLA Modules:
  0.0 30.1 jit_solution(16212324116340726378)
XLA Ops:
  0.0 1.2 %copy_in.1 = (bf16[3,128,768]{2,1,0:T(8,128)(2,1)S(1)}, bf16[384,384]{1,0:T(8,128)(2,1)S(1)}) custom-call(bf16[1,128,768]{2,1,0:T(8,128)(2,1)} %query_ref.1, bf16[1,128,768]{2,1,0:T(8,128)(2,1)} %key_ref.1, bf16[1,128,768]{2,1,0:T(8,128)(2,1)} %value_ref.1, bf16[768,384]{1,0:T(8,128)(2,1)} %refs_4_.1), custom_call_target="tpu_custom_call" | custom-call | tf_op jit(solution)/shard_map/copy_in/pallas_call | solution.py:61
  1.2 4.1 %collective-permute-start = (bf16[384,384]{1,0:T(8,128)(2,1)S(1)}, bf16[384,384]{1,0:T(8,128)(2,1)S(1)}, u32[]{:S(2)}, u32[]{:S(2)}) collective-permute-start(bf16[384,384]{1,0:T(8,128)(2,1)S(1)} %get-tuple-element.33), channel_id=1, source_target_pairs={{0,2},{1,3},{2,0},{3,1},{4,5},{5,4},{6,7},{7,6},{8,10},{9,11},{10,... | collective-permute-start | bytes 884744 | tf_op jit(solution)/shard_map/ppermute | solution.py:326
  5.3 0.2 turn_heads.1
  5.6 1.6 %collective-permute-start.2 = (bf16[3,192,128]{2,1,0:T(8,128)(2,1)S(1)}, bf16[3,192,128]{2,1,0:T(8,128)(2,1)S(1)}, u32[]{:S(2)}, u32[]{:S(2)}) collective-permute-start(bf16[3,192,128]{2,1,0:T(8,128)(2,1)S(1)} %get-tuple-element.37), channel_id=1, source_target_pairs={{0,8},{4,12},{8,0},{12,4},{16,24},{20,28},{24,16},{28,20},{1,9},{5... | collective-permute-start | bytes 442376 | tf_op jit(solution)/shard_map/ppermute | solution.py:316
  7.2 1.5 %collective-permute-start.3 = (bf16[3,192,128]{2,1,0:T(8,128)(2,1)S(1)}, bf16[3,192,128]{2,1,0:T(8,128)(2,1)S(1)}, u32[]{:S(2)}, u32[]{:S(2)}) collective-permute-start(bf16[3,192,128]{2,1,0:T(8,128)(2,1)S(1)} %get-tuple-element.38), channel_id=1, source_target_pairs={{0,16},{4,20},{8,24},{12,28},{16,0},{20,4},{24,8},{28,12},{1,17},{... | collective-permute-start | bytes 442376 | tf_op jit(solution)/shard_map/ppermute | solution.py:316
  8.7 0.5 %collective-permute-start.4 = (bf16[3,192,128]{2,1,0:T(8,128)(2,1)S(1)}, bf16[3,192,128]{2,1,0:T(8,128)(2,1)S(1)}, u32[]{:S(2)}, u32[]{:S(2)}) collective-permute-start(bf16[3,192,128]{2,1,0:T(8,128)(2,1)S(1)} %get-tuple-element.39), channel_id=1, source_target_pairs={{0,24},{4,28},{8,16},{12,20},{16,8},{20,12},{24,0},{28,4},{1,25},{... | collective-permute-start | bytes 442376 | tf_op jit(solution)/shard_map/ppermute | solution.py:316
  9.2 0.1 collective-permute-start.1
  9.9 0.6 %collective-permute-done.1.refs_4_ = bf16[2,192,128]{2,1,0:T(8,128)(2,1)S(1)} collective-permute-done((bf16[2,192,128]{2,1,0:T(8,128)(2,1)S(1)}, bf16[2,192,128]{2,1,0:T(8,128)(2,1)S(1)}, u32[]{:S(2)}, u32[]{:S(2)}) %collective-permute-start.1) | collective-permute-done | bytes 98336 | tf_op jit(solution)/shard_map/ppermute | solution.py:316
  10.5 1.4 %collective-permute-done.refs_5_ = bf16[384,384]{1,0:T(8,128)(2,1)S(1)} collective-permute-done((bf16[384,384]{1,0:T(8,128)(2,1)S(1)}, bf16[384,384]{1,0:T(8,128)(2,1)S(1)}, u32[]{:S(2)}, u32[]{:S(2)}) %collective-permute-start) | collective-permute-done | bytes 294944 | tf_op jit(solution)/shard_map/ppermute | solution.py:326
  12.0 0.4 %collective-permute-done.2.refs_0_.refs_1_ = bf16[3,192,128]{2,1,0:T(8,128)(2,1)S(1)} collective-permute-done((bf16[3,192,128]{2,1,0:T(8,128)(2,1)S(1)}, bf16[3,192,128]{2,1,0:T(8,128)(2,1)S(1)}, u32[]{:S(2)}, u32[]{:S(2)}) %collective-permute-start.2) | collective-permute-done | bytes 147488 | tf_op jit(solution)/shard_map/ppermute | solution.py:316
  12.4 2.8 %collective-permute-done.3.refs_1_.refs_2_ = bf16[3,192,128]{2,1,0:T(8,128)(2,1)S(1)} collective-permute-done((bf16[3,192,128]{2,1,0:T(8,128)(2,1)S(1)}, bf16[3,192,128]{2,1,0:T(8,128)(2,1)S(1)}, u32[]{:S(2)}, u32[]{:S(2)}) %collective-permute-start.3) | collective-permute-done | bytes 147488 | tf_op jit(solution)/shard_map/ppermute | solution.py:316
  15.2 0.0 collective-permute-done.4.refs_2_.refs_3_
  15.2 0.1 collective-permute-start.5
  15.3 1.2 %collective-permute-start.10 = (bf16[208,384]{1,0:T(8,128)(2,1)S(1)}, bf16[208,384]{1,0:T(8,128)(2,1)S(1)}, u32[]{:S(2)}, u32[]{:S(2)}) collective-permute-start(bf16[208,384]{1,0:T(8,128)(2,1)S(1)} %constant_dynamic-slice_fusion), channel_id=1, source_target_pairs={{0,1},{1,0},{2,3},{3,2},{4,6},{5,7},{6,4},{7,5},{8,9},{9,8},{10,11... | collective-permute-start | bytes 479240 | tf_op jit(solution)/shard_map/ppermute | solution.py:326
  16.5 0.5 %collective-permute-start.8 = (bf16[384,384]{1,0:T(8,128)(2,1)S(1)}, bf16[384,384]{1,0:T(8,128)(2,1)S(1)}, u32[]{:S(2)}, u32[]{:S(2)}) collective-permute-start(bf16[384,384]{1,0:T(8,128)(2,1)S(1)} %collective-permute-done.refs_5_), channel_id=1, source_target_pairs={{0,8},{4,20},{8,0},{12,28},{16,24},{20,4},{24,16},{28,12},{1,9},{5... | collective-permute-start | bytes 884744 | tf_op jit(solution)/shard_map/ppermute | solution.py:322
  17.0 0.0 collective-permute-done.5.refs_5_
  17.1 1.9 %attend_two_heads.1 = (bf16[192,128]{1,0:T(8,128)(2,1)S(1)}, bf16[192,128]{1,0:T(8,128)(2,1)S(1)}, bf16[192,128]{1,0:T(8,128)(2,1)S(1)}, bf16[192,128]{1,0:T(8,128)(2,1)S(1)}) custom-call(s32[8,128]{1,0:T(8,128)S(1)} %broadcast_in_dim.2.lengths_ref, bf16[3,192,128]{2,1,0:T(8,128)(2,1)S(1)} %get-tuple-element.35.refs_0_, ...), custom_call_target="tpu_custom_call" | custom-call | flops 1610612736 | tf_op jit(solution)/shard_map/attend_two_heads/pallas_call | solution.py:173
  19.0 1.7 %collective-permute-start.9 = (bf16[192,128]{1,0:T(8,128)(2,1)S(1)}, bf16[192,128]{1,0:T(8,128)(2,1)S(1)}, u32[]{:S(2)}, u32[]{:S(2)}) collective-permute-start(bf16[192,128]{1,0:T(8,128)(2,1)S(1)} %get-tuple-element.51), channel_id=1, source_target_pairs={{0,24},{4,28},{8,16},{12,20},{16,8},{20,12},{24,0},{28,4},{1,25},{... | collective-permute-start | bytes 147464 | tf_op jit(solution)/shard_map/ppermute | solution.py:316
  20.7 0.6 %collective-permute-start.6 = (bf16[192,128]{1,0:T(8,128)(2,1)S(1)}, bf16[192,128]{1,0:T(8,128)(2,1)S(1)}, u32[]{:S(2)}, u32[]{:S(2)}) collective-permute-start(bf16[192,128]{1,0:T(8,128)(2,1)S(1)} %get-tuple-element.46), channel_id=1, source_target_pairs={{0,8},{4,12},{8,0},{12,4},{16,24},{20,28},{24,16},{28,20},{1,9},{5... | collective-permute-start | bytes 147464 | tf_op jit(solution)/shard_map/ppermute | solution.py:316
  21.3 0.0 copy-start
  21.3 1.2 %collective-permute-start.7 = (bf16[192,128]{1,0:T(8,128)(2,1)S(1)}, bf16[192,128]{1,0:T(8,128)(2,1)S(1)}, u32[]{:S(2)}, u32[]{:S(2)}) collective-permute-start(bf16[192,128]{1,0:T(8,128)(2,1)S(1)} %get-tuple-element.47), channel_id=1, source_target_pairs={{0,16},{4,20},{8,24},{12,28},{16,0},{20,4},{24,8},{28,12},{1,17},{... | collective-permute-start | bytes 147464 | tf_op jit(solution)/shard_map/ppermute | solution.py:316
  22.5 0.0 collective-permute-done.10.source_ref.refs_9_
  22.5 1.6 %collective-permute-start.14 = (bf16[208,384]{1,0:T(8,128)(2,1)S(1)}, bf16[208,384]{1,0:T(8,128)(2,1)S(1)}, u32[]{:S(2)}, u32[]{:S(2)}) collective-permute-start(bf16[208,384]{1,0:T(8,128)(2,1)S(1)} %stage_third_shard.1), channel_id=1, source_target_pairs={{0,8},{4,20},{8,0},{12,28},{16,24},{20,4},{24,16},{28,12},{1,9},{5... | collective-permute-start | bytes 479240 | tf_op jit(solution)/shard_map/ppermute | solution.py:322
  24.1 0.0 collective-permute-done.8.refs_6_
  24.1 1.2 %collective-permute-done.6.refs_1_ = bf16[192,128]{1,0:T(8,128)(2,1)S(1)} collective-permute-done((bf16[192,128]{1,0:T(8,128)(2,1)S(1)}, bf16[192,128]{1,0:T(8,128)(2,1)S(1)}, u32[]{:S(2)}, u32[]{:S(2)}) %collective-permute-start.6) | collective-permute-done | bytes 49184 | tf_op jit(solution)/shard_map/ppermute | solution.py:316
  25.3 0.3 collective-permute-done.7.refs_2_
  25.6 0.0 collective-permute-start.13
  25.6 0.0 collective-permute-done.9.refs_3_
  25.6 0.5 %collective-permute-start.11 = (bf16[384,384]{1,0:T(8,128)(2,1)S(1)}, bf16[384,384]{1,0:T(8,128)(2,1)S(1)}, u32[]{:S(2)}, u32[]{:S(2)}) collective-permute-start(bf16[384,384]{1,0:T(8,128)(2,1)S(1)} %collective-permute-done.refs_5_), channel_id=1, source_target_pairs={{0,4},{4,0},{8,12},{12,8},{16,20},{20,16},{24,28},{28,24},{1,5},{5... | collective-permute-start | bytes 884744 | tf_op jit(solution)/shard_map/ppermute | solution.py:316
  26.2 0.0 collective-permute-start.12
  26.2 1.7 %collective-permute-done.14.refs_11_ = bf16[208,384]{1,0:T(8,128)(2,1)S(1)} collective-permute-done((bf16[208,384]{1,0:T(8,128)(2,1)S(1)}, bf16[208,384]{1,0:T(8,128)(2,1)S(1)}, u32[]{:S(2)}, u32[]{:S(2)}) %collective-permute-start.14) | collective-permute-done | bytes 159776 | tf_op jit(solution)/shard_map/ppermute | solution.py:322
  27.9 0.0 collective-permute-start.15
  27.9 0.0 collective-permute-done.12.refs_10_
  27.9 0.0 collective-permute-done.13.refs_8_
  27.9 0.0 collective-permute-done.11.refs_7_
  27.9 0.0 copy-done
  27.9 0.8 %project_near_shards.1 = (bf16[3,128,384]{2,1,0:T(8,128)(2,1)S(1)}, f32[128,384]{1,0:T(8,128)S(1)}, bf16[128,192]{1,0:T(8,128)(2,1)S(1)}) custom-call(bf16[192,128]{1,0:T(8,128)(2,1)S(1)} %get-tuple-element.45.refs_0_, bf16[192,128]{1,0:T(8,128)(2,1)S(1)} %collective-permute-done.6.refs_1_, bf16[192,128]{1,0:T(8,128)(2,1)S(1)} %collective-permute-done.7.refs_2_, ...), custom_call_target="tpu_custom_call" | custom-call | flops 226492416 | bytes 1769472 | tf_op jit(solution)/shard_map/project_near_shards/pallas_call | solution.py:279
  28.8 0.5 %collective-permute-done.15.part_ref = bf16[208,384]{1,0:T(8,128)(2,1)S(1)} collective-permute-done((bf16[208,384]{1,0:T(8,128)(2,1)S(1)}, bf16[208,384]{1,0:T(8,128)(2,1)S(1)}, u32[]{:S(2)}, u32[]{:S(2)}) %collective-permute-start.15) | collective-permute-done | bytes 159776 | tf_op jit(solution)/shard_map/ppermute | solution.py:316
  29.3 0.9 %project_third_shard.1 = bf16[1,128,1536]{2,1,0:T(8,128)(2,1)} custom-call(bf16[3,128,384]{2,1,0:T(8,128)(2,1)S(1)} %get-tuple-element.58.blocks_ref, f32[128,384]{1,0:T(8,128)S(1)} %get-tuple-element.59.sum_ref, bf16[128,192]{1,0:T(8,128)(2,1)S(1)} %get-tuple-element.60.rest_ref, bf16[208,384]{1,0:T(8,128)(2,1)S(1)} %collective-permute-done.15.part_ref), custom_call_target="tpu_custom_call" | custom-call | flops 18874368 | bytes 147456 | tf_op jit(solution)/shard_map/project_third_shard/pallas_call | solution.py:301
  (5 shorter events, 0.1 us)
Async XLA Ops:
  1.2 10.7 %collective-permute-start = (bf16[384,384]{1,0:T(8,128)(2,1)S(1)}, bf16[384,384]{1,0:T(8,128)(2,1)S(1)}, u32[]{:S(2)}, u32[]{:S(2)}) collective-permute-start(bf16[384,384]{1,0:T(8,128)(2,1)S(1)} %get-tuple-element.33), channel_id=1, source_target_pairs={{0,2},{1,3},{2,0},{3,1},{4,5},{5,4},{6,7},{7,6},{8,10},{9,11},{10,... | collective-permute-start | bytes 884744 | tf_op jit(solution)/shard_map/ppermute | solution.py:326
  5.6 6.8 %collective-permute-start.2 = (bf16[3,192,128]{2,1,0:T(8,128)(2,1)S(1)}, bf16[3,192,128]{2,1,0:T(8,128)(2,1)S(1)}, u32[]{:S(2)}, u32[]{:S(2)}) collective-permute-start(bf16[3,192,128]{2,1,0:T(8,128)(2,1)S(1)} %get-tuple-element.37), channel_id=1, source_target_pairs={{0,8},{4,12},{8,0},{12,4},{16,24},{20,28},{24,16},{28,20},{1,9},{5... | collective-permute-start | bytes 442376 | tf_op jit(solution)/shard_map/ppermute | solution.py:316
  7.2 8.0 %collective-permute-start.3 = (bf16[3,192,128]{2,1,0:T(8,128)(2,1)S(1)}, bf16[3,192,128]{2,1,0:T(8,128)(2,1)S(1)}, u32[]{:S(2)}, u32[]{:S(2)}) collective-permute-start(bf16[3,192,128]{2,1,0:T(8,128)(2,1)S(1)} %get-tuple-element.38), channel_id=1, source_target_pairs={{0,16},{4,20},{8,24},{12,28},{16,0},{20,4},{24,8},{28,12},{1,17},{... | collective-permute-start | bytes 442376 | tf_op jit(solution)/shard_map/ppermute | solution.py:316
  8.7 6.5 %collective-permute-start.4 = (bf16[3,192,128]{2,1,0:T(8,128)(2,1)S(1)}, bf16[3,192,128]{2,1,0:T(8,128)(2,1)S(1)}, u32[]{:S(2)}, u32[]{:S(2)}) collective-permute-start(bf16[3,192,128]{2,1,0:T(8,128)(2,1)S(1)} %get-tuple-element.39), channel_id=1, source_target_pairs={{0,24},{4,28},{8,16},{12,20},{16,8},{20,12},{24,0},{28,4},{1,25},{... | collective-permute-start | bytes 442376 | tf_op jit(solution)/shard_map/ppermute | solution.py:316
  9.2 1.4 %collective-permute-start.1 = (bf16[2,192,128]{2,1,0:T(8,128)(2,1)S(1)}, bf16[2,192,128]{2,1,0:T(8,128)(2,1)S(1)}, u32[]{:S(2)}, u32[]{:S(2)}) collective-permute-start(bf16[2,192,128]{2,1,0:T(8,128)(2,1)S(1)} %slice.3), channel_id=1, source_target_pairs={{0,4},{4,0},{8,12},{12,8},{16,20},{20,16},{24,28},{28,24},{1,5},{5... | collective-permute-start | bytes 294920 | tf_op jit(solution)/shard_map/ppermute | solution.py:316
  15.2 1.9 %collective-permute-start.5 = (bf16[3,2,192,128]{3,2,1,0:T(8,128)(2,1)S(1)}, bf16[3,2,192,128]{3,2,1,0:T(8,128)(2,1)S(1)}, u32[]{:S(2)}, u32[]{:S(2)}) collective-permute-start(bf16[3,2,192,128]{3,2,1,0:T(8,128)(2,1)S(1)} %stack_keys_and_values.1), channel_id=1, source_target_pairs={{0,4},{4,0},{8,12},{12,8},{16,20},{20,16},{24,28},{28,24},{1,5},{5... | collective-permute-start | bytes 884744 | tf_op jit(solution)/shard_map/ppermute | solution.py:316
  15.3 7.2 %collective-permute-start.10 = (bf16[208,384]{1,0:T(8,128)(2,1)S(1)}, bf16[208,384]{1,0:T(8,128)(2,1)S(1)}, u32[]{:S(2)}, u32[]{:S(2)}) collective-permute-start(bf16[208,384]{1,0:T(8,128)(2,1)S(1)} %constant_dynamic-slice_fusion), channel_id=1, source_target_pairs={{0,1},{1,0},{2,3},{3,2},{4,6},{5,7},{6,4},{7,5},{8,9},{9,8},{10,11... | collective-permute-start | bytes 479240 | tf_op jit(solution)/shard_map/ppermute | solution.py:326
  16.5 7.6 %collective-permute-start.8 = (bf16[384,384]{1,0:T(8,128)(2,1)S(1)}, bf16[384,384]{1,0:T(8,128)(2,1)S(1)}, u32[]{:S(2)}, u32[]{:S(2)}) collective-permute-start(bf16[384,384]{1,0:T(8,128)(2,1)S(1)} %collective-permute-done.refs_5_), channel_id=1, source_target_pairs={{0,8},{4,20},{8,0},{12,28},{16,24},{20,4},{24,16},{28,12},{1,9},{5... | collective-permute-start | bytes 884744 | tf_op jit(solution)/shard_map/ppermute | solution.py:322
  19.0 6.7 %collective-permute-start.9 = (bf16[192,128]{1,0:T(8,128)(2,1)S(1)}, bf16[192,128]{1,0:T(8,128)(2,1)S(1)}, u32[]{:S(2)}, u32[]{:S(2)}) collective-permute-start(bf16[192,128]{1,0:T(8,128)(2,1)S(1)} %get-tuple-element.51), channel_id=1, source_target_pairs={{0,24},{4,28},{8,16},{12,20},{16,8},{20,12},{24,0},{28,4},{1,25},{... | collective-permute-start | bytes 147464 | tf_op jit(solution)/shard_map/ppermute | solution.py:316
  20.7 4.7 %collective-permute-start.6 = (bf16[192,128]{1,0:T(8,128)(2,1)S(1)}, bf16[192,128]{1,0:T(8,128)(2,1)S(1)}, u32[]{:S(2)}, u32[]{:S(2)}) collective-permute-start(bf16[192,128]{1,0:T(8,128)(2,1)S(1)} %get-tuple-element.46), channel_id=1, source_target_pairs={{0,8},{4,12},{8,0},{12,4},{16,24},{20,28},{24,16},{28,20},{1,9},{5... | collective-permute-start | bytes 147464 | tf_op jit(solution)/shard_map/ppermute | solution.py:316
  21.3 6.6 %copy-start = (bf16[768,384]{1,0:T(8,128)(2,1)S(1)}, bf16[768,384]{1,0:T(8,128)(2,1)}, u32[]{:S(2)}) copy-start(bf16[768,384]{1,0:T(8,128)(2,1)} %refs_4_.1) | copy-start | bytes 1769476
  21.3 4.3 %collective-permute-start.7 = (bf16[192,128]{1,0:T(8,128)(2,1)S(1)}, bf16[192,128]{1,0:T(8,128)(2,1)S(1)}, u32[]{:S(2)}, u32[]{:S(2)}) collective-permute-start(bf16[192,128]{1,0:T(8,128)(2,1)S(1)} %get-tuple-element.47), channel_id=1, source_target_pairs={{0,16},{4,20},{8,24},{12,28},{16,0},{20,4},{24,8},{28,12},{1,17},{... | collective-permute-start | bytes 147464 | tf_op jit(solution)/shard_map/ppermute | solution.py:316
  22.5 5.3 %collective-permute-start.14 = (bf16[208,384]{1,0:T(8,128)(2,1)S(1)}, bf16[208,384]{1,0:T(8,128)(2,1)S(1)}, u32[]{:S(2)}, u32[]{:S(2)}) collective-permute-start(bf16[208,384]{1,0:T(8,128)(2,1)S(1)} %stage_third_shard.1), channel_id=1, source_target_pairs={{0,8},{4,20},{8,0},{12,28},{16,24},{20,4},{24,16},{28,12},{1,9},{5... | collective-permute-start | bytes 479240 | tf_op jit(solution)/shard_map/ppermute | solution.py:322
  25.6 2.3 %collective-permute-start.13 = (bf16[384,384]{1,0:T(8,128)(2,1)S(1)}, bf16[384,384]{1,0:T(8,128)(2,1)S(1)}, u32[]{:S(2)}, u32[]{:S(2)}) collective-permute-start(bf16[384,384]{1,0:T(8,128)(2,1)S(1)} %collective-permute-done.8.refs_6_), channel_id=1, source_target_pairs={{0,4},{4,0},{8,12},{12,8},{16,20},{20,16},{24,28},{28,24},{1,5},{5... | collective-permute-start | bytes 884744 | tf_op jit(solution)/shard_map/ppermute | solution.py:316
  25.6 2.3 %collective-permute-start.11 = (bf16[384,384]{1,0:T(8,128)(2,1)S(1)}, bf16[384,384]{1,0:T(8,128)(2,1)S(1)}, u32[]{:S(2)}, u32[]{:S(2)}) collective-permute-start(bf16[384,384]{1,0:T(8,128)(2,1)S(1)} %collective-permute-done.refs_5_), channel_id=1, source_target_pairs={{0,4},{4,0},{8,12},{12,8},{16,20},{20,16},{24,28},{28,24},{1,5},{5... | collective-permute-start | bytes 884744 | tf_op jit(solution)/shard_map/ppermute | solution.py:316
  26.2 1.7 %collective-permute-start.12 = (bf16[208,384]{1,0:T(8,128)(2,1)S(1)}, bf16[208,384]{1,0:T(8,128)(2,1)S(1)}, u32[]{:S(2)}, u32[]{:S(2)}) collective-permute-start(bf16[208,384]{1,0:T(8,128)(2,1)S(1)} %collective-permute-done.10.source_ref.refs_9_), channel_id=1, source_target_pairs={{0,4},{4,0},{8,12},{12,8},{16,20},{20,16},{24,28},{28,24},{1,5},{5... | collective-permute-start | bytes 479240 | tf_op jit(solution)/shard_map/ppermute | solution.py:316
  27.9 1.4 %collective-permute-start.15 = (bf16[208,384]{1,0:T(8,128)(2,1)S(1)}, bf16[208,384]{1,0:T(8,128)(2,1)S(1)}, u32[]{:S(2)}, u32[]{:S(2)}) collective-permute-start(bf16[208,384]{1,0:T(8,128)(2,1)S(1)} %collective-permute-done.14.refs_11_), channel_id=1, source_target_pairs={{0,4},{4,0},{8,12},{12,8},{16,20},{20,16},{24,28},{28,24},{1,5},{5... | collective-permute-start | bytes 479240 | tf_op jit(solution)/shard_map/ppermute | solution.py:316

commit v21 on v17

--- a/solution.py
+++ b/solution.py
@@ -220,18 +220,21 @@
     shard = lax.axis_index("fsdp")
     quarter, columns = rest_ref.shape[1], last.shape[1]
 
-    def copy_out(flip, block_ref):
+    def copy_out(flip, block_ref, frames, sem):
         here = pl.ds(pl.multiple_of((shard ^ flip) * columns, 128), columns)
-        copy = pltpu.make_async_copy(block_ref, out_ref.at[0, :, here], sems.at[flip])
+        copy = pltpu.make_async_copy(block_ref, out_ref.at[0, frames, here], sems.at[sem])
         copy.start()
         return copy
 
-    copies = [copy_out(flip, blocks_ref.at[flip]) for flip in range(3)]
+    copies = [copy_out(flip, blocks_ref.at[flip], pl.ds(0, last.shape[0]), flip) for flip in range(3)]
     first = (1 - (place_in_group() & 1)) * (part_ref.shape[0] - quarter)
     rows = part_ref[pl.ds(pl.multiple_of(first, 16), quarter), :]
-    total = sum_ref[...] + jnp.dot(rest_ref[...], rows, preferred_element_type=jnp.float32)
-    last[...] = total.astype(last.dtype)
-    copies.append(copy_out(3, last))
+    half = last.shape[0] // 2
+    for at in range(2):
+        frames = pl.ds(at * half, half)
+        total = sum_ref[frames, :] + jnp.dot(rest_ref[frames, :], rows, preferred_element_type=jnp.float32)
+        last[frames, :] = total.astype(last.dtype)
+        copies.append(copy_out(3, last.at[frames], frames, 3 + at))
     for copy in copies:
         copy.wait()
 
@@ -287,7 +290,7 @@
         out_shape=jax.ShapeDtypeStruct((1, frames, 4 * columns), blocks.dtype),
         in_specs=[WHOLE] * 4,
         out_specs=IN_HBM,
-        scratch_shapes=[pltpu.VMEM((frames, columns), jnp.bfloat16), pltpu.SemaphoreType.DMA((4,))],
+        scratch_shapes=[pltpu.VMEM((frames, columns), jnp.bfloat16), pltpu.SemaphoreType.DMA((5,))],
         compiler_params=params(24),
         cost_estimate=projection_cost(frames, rest.shape[1], columns),
         name="project_third_shard",

time: 30.3 us -> 30.3 us (level)
  no operation moved by 1% of the time
where the time goes in v21:
time: 30.3 us; the launch traced here: 30.1 us
  starting transfers between devices  15.3 us (50%)
  waiting for transfers between devices  8.98 us (30%)
  Pallas kernels  5.11 us (17%)
  between operations  0.74 us (2%)
    ppermute x12, starting transfers between devices, exchange(): return lax.ppermute(array, axis, [(i, i ^ flip) for i in range(size)])  7.87 us
    ppermute x12, waiting for transfers between devices, exchange(): return lax.ppermute(array, axis, [(i, i ^ flip) for i in range(size)])  6.53 us
    ppermute x2, starting transfers between devices, exchange_along(): return lax.ppermute(array, ('ctx', 'fsdp'), pairs)  5.43 us
    ppermute x2, starting transfers between devices, exchange_in_plane(): lax.ppermute(array, 'ctx', [(i, i ^ (4 if i % 2 else 2)) for i in range(c...  1.97 us
    pallas_call x1, Pallas kernels, attend(): pl.pallas_call(functools.partial(attention_kernel, groups), out_shape=[pl...  1.91 us
    ppermute x2, waiting for transfers between devices, exchange_along(): return lax.ppermute(array, ('ctx', 'fsdp'), pairs)  1.42 us
    pallas_call x1, Pallas kernels, copy_in(): pl.pallas_call(functools.partial(copy_in_kernel, by_parity), out_shape=[p...  1.24 us
    ppermute x2, waiting for transfers between devices, exchange_in_plane(): lax.ppermute(array, 'ctx', [(i, i ^ (4 if i % 2 else 2)) for i in range(c...  1.02 us
  transfers between devices with their start and end apart: 16, of which 9 were waited for; matrix products, arithmetic and copies ran while one was open for 0% of the time, Pallas kernels for 10%

profile of v21, /device:TPU:0, one launch (start us, length us, event | category | flops | bytes accessed | tf_op | source)
XLA Modules:
  0.0 30.1 jit_solution(17247084638738595092)
XLA Ops:
  0.0 1.2 %copy_in.1 = (bf16[3,128,768]{2,1,0:T(8,128)(2,1)S(1)}, bf16[384,384]{1,0:T(8,128)(2,1)S(1)}) custom-call(bf16[1,128,768]{2,1,0:T(8,128)(2,1)} %query_ref.1, bf16[1,128,768]{2,1,0:T(8,128)(2,1)} %key_ref.1, bf16[1,128,768]{2,1,0:T(8,128)(2,1)} %value_ref.1, bf16[768,384]{1,0:T(8,128)(2,1)} %refs_4_.1), custom_call_target="tpu_custom_call" | custom-call | tf_op jit(solution)/shard_map/copy_in/pallas_call | solution.py:45
  1.2 4.1 %collective-permute-start = (bf16[384,384]{1,0:T(8,128)(2,1)S(1)}, bf16[384,384]{1,0:T(8,128)(2,1)S(1)}, u32[]{:S(2)}, u32[]{:S(2)}) collective-permute-start(bf16[384,384]{1,0:T(8,128)(2,1)S(1)} %get-tuple-element.33), channel_id=1, source_target_pairs={{0,2},{1,3},{2,0},{3,1},{4,5},{5,4},{6,7},{7,6},{8,10},{9,11},{10,... | collective-permute-start | bytes 884744 | tf_op jit(solution)/shard_map/ppermute | solution.py:313
  5.3 0.2 turn_heads.1
  5.6 1.6 %collective-permute-start.2 = (bf16[3,192,128]{2,1,0:T(8,128)(2,1)S(1)}, bf16[3,192,128]{2,1,0:T(8,128)(2,1)S(1)}, u32[]{:S(2)}, u32[]{:S(2)}) collective-permute-start(bf16[3,192,128]{2,1,0:T(8,128)(2,1)S(1)} %get-tuple-element.37), channel_id=1, source_target_pairs={{0,8},{4,12},{8,0},{12,4},{16,24},{20,28},{24,16},{28,20},{1,9},{5... | collective-permute-start | bytes 442376 | tf_op jit(solution)/shard_map/ppermute | solution.py:303
  7.2 1.5 %collective-permute-start.3 = (bf16[3,192,128]{2,1,0:T(8,128)(2,1)S(1)}, bf16[3,192,128]{2,1,0:T(8,128)(2,1)S(1)}, u32[]{:S(2)}, u32[]{:S(2)}) collective-permute-start(bf16[3,192,128]{2,1,0:T(8,128)(2,1)S(1)} %get-tuple-element.38), channel_id=1, source_target_pairs={{0,16},{4,20},{8,24},{12,28},{16,0},{20,4},{24,8},{28,12},{1,17},{... | collective-permute-start | bytes 442376 | tf_op jit(solution)/shard_map/ppermute | solution.py:303
  8.7 0.5 %collective-permute-start.4 = (bf16[3,192,128]{2,1,0:T(8,128)(2,1)S(1)}, bf16[3,192,128]{2,1,0:T(8,128)(2,1)S(1)}, u32[]{:S(2)}, u32[]{:S(2)}) collective-permute-start(bf16[3,192,128]{2,1,0:T(8,128)(2,1)S(1)} %get-tuple-element.39), channel_id=1, source_target_pairs={{0,24},{4,28},{8,16},{12,20},{16,8},{20,12},{24,0},{28,4},{1,25},{... | collective-permute-start | bytes 442376 | tf_op jit(solution)/shard_map/ppermute | solution.py:303
  9.2 0.1 collective-permute-start.1
  9.9 0.6 %collective-permute-done.1.refs_4_ = bf16[2,192,128]{2,1,0:T(8,128)(2,1)S(1)} collective-permute-done((bf16[2,192,128]{2,1,0:T(8,128)(2,1)S(1)}, bf16[2,192,128]{2,1,0:T(8,128)(2,1)S(1)}, u32[]{:S(2)}, u32[]{:S(2)}) %collective-permute-start.1) | collective-permute-done | bytes 98336 | tf_op jit(solution)/shard_map/ppermute | solution.py:303
  10.5 1.4 %collective-permute-done.refs_5_ = bf16[384,384]{1,0:T(8,128)(2,1)S(1)} collective-permute-done((bf16[384,384]{1,0:T(8,128)(2,1)S(1)}, bf16[384,384]{1,0:T(8,128)(2,1)S(1)}, u32[]{:S(2)}, u32[]{:S(2)}) %collective-permute-start) | collective-permute-done | bytes 294944 | tf_op jit(solution)/shard_map/ppermute | solution.py:313
  12.0 0.4 %collective-permute-done.2.refs_0_.refs_1_ = bf16[3,192,128]{2,1,0:T(8,128)(2,1)S(1)} collective-permute-done((bf16[3,192,128]{2,1,0:T(8,128)(2,1)S(1)}, bf16[3,192,128]{2,1,0:T(8,128)(2,1)S(1)}, u32[]{:S(2)}, u32[]{:S(2)}) %collective-permute-start.2) | collective-permute-done | bytes 147488 | tf_op jit(solution)/shard_map/ppermute | solution.py:303
  12.4 2.8 %collective-permute-done.3.refs_1_.refs_2_ = bf16[3,192,128]{2,1,0:T(8,128)(2,1)S(1)} collective-permute-done((bf16[3,192,128]{2,1,0:T(8,128)(2,1)S(1)}, bf16[3,192,128]{2,1,0:T(8,128)(2,1)S(1)}, u32[]{:S(2)}, u32[]{:S(2)}) %collective-permute-start.3) | collective-permute-done | bytes 147488 | tf_op jit(solution)/shard_map/ppermute | solution.py:303
  15.2 0.0 collective-permute-done.4.refs_2_.refs_3_
  15.2 0.1 collective-permute-start.5
  15.3 0.5 %collective-permute-start.8 = (bf16[384,384]{1,0:T(8,128)(2,1)S(1)}, bf16[384,384]{1,0:T(8,128)(2,1)S(1)}, u32[]{:S(2)}, u32[]{:S(2)}) collective-permute-start(bf16[384,384]{1,0:T(8,128)(2,1)S(1)} %collective-permute-done.refs_5_), channel_id=1, source_target_pairs={{0,8},{4,20},{8,0},{12,28},{16,24},{20,4},{24,16},{28,12},{1,9},{5... | collective-permute-start | bytes 884744 | tf_op jit(solution)/shard_map/ppermute | solution.py:309
  15.8 0.0 copy-start
  15.8 1.3 %collective-permute-start.10 = (bf16[208,384]{1,0:T(8,128)(2,1)S(1)}, bf16[208,384]{1,0:T(8,128)(2,1)S(1)}, u32[]{:S(2)}, u32[]{:S(2)}) collective-permute-start(bf16[208,384]{1,0:T(8,128)(2,1)S(1)} %constant_dynamic-slice_fusion), channel_id=1, source_target_pairs={{0,1},{1,0},{2,3},{3,2},{4,6},{5,7},{6,4},{7,5},{8,9},{9,8},{10,11... | collective-permute-start | bytes 479240 | tf_op jit(solution)/shard_map/ppermute | solution.py:313
  17.1 0.0 collective-permute-done.5.refs_5_
  17.1 1.9 %attend_two_heads.1 = (bf16[192,128]{1,0:T(8,128)(2,1)S(1)}, bf16[192,128]{1,0:T(8,128)(2,1)S(1)}, bf16[192,128]{1,0:T(8,128)(2,1)S(1)}, bf16[192,128]{1,0:T(8,128)(2,1)S(1)}) custom-call(s32[8,128]{1,0:T(8,128)S(1)} %broadcast_in_dim.2.lengths_ref, bf16[3,192,128]{2,1,0:T(8,128)(2,1)S(1)} %get-tuple-element.35.refs_0_, ...), custom_call_target="tpu_custom_call" | custom-call | flops 1610612736 | tf_op jit(solution)/shard_map/attend_two_heads/pallas_call | solution.py:157
  19.0 1.6 %collective-permute-start.6 = (bf16[192,128]{1,0:T(8,128)(2,1)S(1)}, bf16[192,128]{1,0:T(8,128)(2,1)S(1)}, u32[]{:S(2)}, u32[]{:S(2)}) collective-permute-start(bf16[192,128]{1,0:T(8,128)(2,1)S(1)} %get-tuple-element.46), channel_id=1, source_target_pairs={{0,8},{4,12},{8,0},{12,4},{16,24},{20,28},{24,16},{28,20},{1,9},{5... | collective-permute-start | bytes 147464 | tf_op jit(solution)/shard_map/ppermute | solution.py:303
  20.6 0.7 %collective-permute-start.7 = (bf16[192,128]{1,0:T(8,128)(2,1)S(1)}, bf16[192,128]{1,0:T(8,128)(2,1)S(1)}, u32[]{:S(2)}, u32[]{:S(2)}) collective-permute-start(bf16[192,128]{1,0:T(8,128)(2,1)S(1)} %get-tuple-element.47), channel_id=1, source_target_pairs={{0,16},{4,20},{8,24},{12,28},{16,0},{20,4},{24,8},{28,12},{1,17},{... | collective-permute-start | bytes 147464 | tf_op jit(solution)/shard_map/ppermute | solution.py:303
  21.3 1.3 %collective-permute-start.9 = (bf16[192,128]{1,0:T(8,128)(2,1)S(1)}, bf16[192,128]{1,0:T(8,128)(2,1)S(1)}, u32[]{:S(2)}, u32[]{:S(2)}) collective-permute-start(bf16[192,128]{1,0:T(8,128)(2,1)S(1)} %get-tuple-element.51), channel_id=1, source_target_pairs={{0,24},{4,28},{8,16},{12,20},{16,8},{20,12},{24,0},{28,4},{1,25},{... | collective-permute-start | bytes 147464 | tf_op jit(solution)/shard_map/ppermute | solution.py:303
  22.6 0.0 collective-permute-done.10.refs_9_
  22.6 1.5 %collective-permute-start.14 = (bf16[208,384]{1,0:T(8,128)(2,1)S(1)}, bf16[208,384]{1,0:T(8,128)(2,1)S(1)}, u32[]{:S(2)}, u32[]{:S(2)}) collective-permute-start(bf16[208,384]{1,0:T(8,128)(2,1)S(1)} %collective-permute-done.10.refs_9_), channel_id=1, source_target_pairs={{0,8},{4,20},{8,0},{12,28},{16,24},{20,4},{24,16},{28,12},{1,9},{5... | collective-permute-start | bytes 479240 | tf_op jit(solution)/shard_map/ppermute | solution.py:309
  24.1 0.0 collective-permute-done.8.refs_6_
  24.1 0.0 collective-permute-done.6.refs_1_
  24.1 0.6 %collective-permute-done.7.refs_2_ = bf16[192,128]{1,0:T(8,128)(2,1)S(1)} collective-permute-done((bf16[192,128]{1,0:T(8,128)(2,1)S(1)}, bf16[192,128]{1,0:T(8,128)(2,1)S(1)}, u32[]{:S(2)}, u32[]{:S(2)}) %collective-permute-start.7) | collective-permute-done | bytes 49184 | tf_op jit(solution)/shard_map/ppermute | solution.py:303
  24.7 0.0 collective-permute-start.13
  24.7 1.6 %collective-permute-done.9.refs_3_ = bf16[192,128]{1,0:T(8,128)(2,1)S(1)} collective-permute-done((bf16[192,128]{1,0:T(8,128)(2,1)S(1)}, bf16[192,128]{1,0:T(8,128)(2,1)S(1)}, u32[]{:S(2)}, u32[]{:S(2)}) %collective-permute-start.9) | collective-permute-done | bytes 49184 | tf_op jit(solution)/shard_map/ppermute | solution.py:303
  26.3 0.0 collective-permute-start.11
  26.3 0.5 %collective-permute-start.12 = (bf16[208,384]{1,0:T(8,128)(2,1)S(1)}, bf16[208,384]{1,0:T(8,128)(2,1)S(1)}, u32[]{:S(2)}, u32[]{:S(2)}) collective-permute-start(bf16[208,384]{1,0:T(8,128)(2,1)S(1)} %collective-permute-done.10.refs_9_), channel_id=1, source_target_pairs={{0,4},{4,0},{8,12},{12,8},{16,20},{20,16},{24,28},{28,24},{1,5},{5... | collective-permute-start | bytes 479240 | tf_op jit(solution)/shard_map/ppermute | solution.py:303
  26.8 1.0 %collective-permute-done.14.refs_11_ = bf16[208,384]{1,0:T(8,128)(2,1)S(1)} collective-permute-done((bf16[208,384]{1,0:T(8,128)(2,1)S(1)}, bf16[208,384]{1,0:T(8,128)(2,1)S(1)}, u32[]{:S(2)}, u32[]{:S(2)}) %collective-permute-start.14) | collective-permute-done | bytes 159776 | tf_op jit(solution)/shard_map/ppermute | solution.py:309
  27.9 0.1 collective-permute-start.15
  28.0 0.2 collective-permute-done.12.refs_10_
  28.1 0.0 collective-permute-done.13.refs_8_
  28.2 0.0 collective-permute-done.11.refs_7_
  28.2 0.0 copy-done
  28.2 0.8 %project_near_shards.1 = (bf16[3,128,384]{2,1,0:T(8,128)(2,1)S(1)}, f32[128,384]{1,0:T(8,128)S(1)}, bf16[128,192]{1,0:T(8,128)(2,1)S(1)}) custom-call(bf16[192,128]{1,0:T(8,128)(2,1)S(1)} %get-tuple-element.45.refs_0_, bf16[192,128]{1,0:T(8,128)(2,1)S(1)} %collective-permute-done.6.refs_1_, bf16[192,128]{1,0:T(8,128)(2,1)S(1)} %collective-permute-done.7.refs_2_, ...), custom_call_target="tpu_custom_call" | custom-call | flops 226492416 | bytes 1769472 | tf_op jit(solution)/shard_map/project_near_shards/pallas_call | solution.py:266
  29.0 0.3 collective-permute-done.15.part_ref
  29.3 0.9 %project_third_shard.1 = bf16[1,128,1536]{2,1,0:T(8,128)(2,1)} custom-call(bf16[3,128,384]{2,1,0:T(8,128)(2,1)S(1)} %get-tuple-element.58.blocks_ref, f32[128,384]{1,0:T(8,128)S(1)} %get-tuple-element.59.sum_ref, bf16[128,192]{1,0:T(8,128)(2,1)S(1)} %get-tuple-element.60.rest_ref, bf16[208,384]{1,0:T(8,128)(2,1)S(1)} %collective-permute-done.15.part_ref), custom_call_target="tpu_custom_call" | custom-call | flops 18874368 | bytes 147456 | tf_op jit(solution)/shard_map/project_third_shard/pallas_call | solution.py:288
  (4 shorter events, 0.0 us)
Async XLA Ops:
  1.2 10.7 %collective-permute-start = (bf16[384,384]{1,0:T(8,128)(2,1)S(1)}, bf16[384,384]{1,0:T(8,128)(2,1)S(1)}, u32[]{:S(2)}, u32[]{:S(2)}) collective-permute-start(bf16[384,384]{1,0:T(8,128)(2,1)S(1)} %get-tuple-element.33), channel_id=1, source_target_pairs={{0,2},{1,3},{2,0},{3,1},{4,5},{5,4},{6,7},{7,6},{8,10},{9,11},{10,... | collective-permute-start | bytes 884744 | tf_op jit(solution)/shard_map/ppermute | solution.py:313
  5.6 6.8 %collective-permute-start.2 = (bf16[3,192,128]{2,1,0:T(8,128)(2,1)S(1)}, bf16[3,192,128]{2,1,0:T(8,128)(2,1)S(1)}, u32[]{:S(2)}, u32[]{:S(2)}) collective-permute-start(bf16[3,192,128]{2,1,0:T(8,128)(2,1)S(1)} %get-tuple-element.37), channel_id=1, source_target_pairs={{0,8},{4,12},{8,0},{12,4},{16,24},{20,28},{24,16},{28,20},{1,9},{5... | collective-permute-start | bytes 442376 | tf_op jit(solution)/shard_map/ppermute | solution.py:303
  7.2 8.0 %collective-permute-start.3 = (bf16[3,192,128]{2,1,0:T(8,128)(2,1)S(1)}, bf16[3,192,128]{2,1,0:T(8,128)(2,1)S(1)}, u32[]{:S(2)}, u32[]{:S(2)}) collective-permute-start(bf16[3,192,128]{2,1,0:T(8,128)(2,1)S(1)} %get-tuple-element.38), channel_id=1, source_target_pairs={{0,16},{4,20},{8,24},{12,28},{16,0},{20,4},{24,8},{28,12},{1,17},{... | collective-permute-start | bytes 442376 | tf_op jit(solution)/shard_map/ppermute | solution.py:303
  8.7 6.5 %collective-permute-start.4 = (bf16[3,192,128]{2,1,0:T(8,128)(2,1)S(1)}, bf16[3,192,128]{2,1,0:T(8,128)(2,1)S(1)}, u32[]{:S(2)}, u32[]{:S(2)}) collective-permute-start(bf16[3,192,128]{2,1,0:T(8,128)(2,1)S(1)} %get-tuple-element.39), channel_id=1, source_target_pairs={{0,24},{4,28},{8,16},{12,20},{16,8},{20,12},{24,0},{28,4},{1,25},{... | collective-permute-start | bytes 442376 | tf_op jit(solution)/shard_map/ppermute | solution.py:303
  9.2 1.4 %collective-permute-start.1 = (bf16[2,192,128]{2,1,0:T(8,128)(2,1)S(1)}, bf16[2,192,128]{2,1,0:T(8,128)(2,1)S(1)}, u32[]{:S(2)}, u32[]{:S(2)}) collective-permute-start(bf16[2,192,128]{2,1,0:T(8,128)(2,1)S(1)} %slice.3), channel_id=1, source_target_pairs={{0,4},{4,0},{8,12},{12,8},{16,20},{20,16},{24,28},{28,24},{1,5},{5... | collective-permute-start | bytes 294920 | tf_op jit(solution)/shard_map/ppermute | solution.py:303
  15.2 1.9 %collective-permute-start.5 = (bf16[3,2,192,128]{3,2,1,0:T(8,128)(2,1)S(1)}, bf16[3,2,192,128]{3,2,1,0:T(8,128)(2,1)S(1)}, u32[]{:S(2)}, u32[]{:S(2)}) collective-permute-start(bf16[3,2,192,128]{3,2,1,0:T(8,128)(2,1)S(1)} %stack_keys_and_values.1), channel_id=1, source_target_pairs={{0,4},{4,0},{8,12},{12,8},{16,20},{20,16},{24,28},{28,24},{1,5},{5... | collective-permute-start | bytes 884744 | tf_op jit(solution)/shard_map/ppermute | solution.py:303
  15.3 8.8 %collective-permute-start.8 = (bf16[384,384]{1,0:T(8,128)(2,1)S(1)}, bf16[384,384]{1,0:T(8,128)(2,1)S(1)}, u32[]{:S(2)}, u32[]{:S(2)}) collective-permute-start(bf16[384,384]{1,0:T(8,128)(2,1)S(1)} %collective-permute-done.refs_5_), channel_id=1, source_target_pairs={{0,8},{4,20},{8,0},{12,28},{16,24},{20,4},{24,16},{28,12},{1,9},{5... | collective-permute-start | bytes 884744 | tf_op jit(solution)/shard_map/ppermute | solution.py:309
  15.8 12.4 %copy-start = (bf16[768,384]{1,0:T(8,128)(2,1)S(1)}, bf16[768,384]{1,0:T(8,128)(2,1)}, u32[]{:S(2)}) copy-start(bf16[768,384]{1,0:T(8,128)(2,1)} %refs_4_.1) | copy-start | bytes 1769476
  15.8 6.8 %collective-permute-start.10 = (bf16[208,384]{1,0:T(8,128)(2,1)S(1)}, bf16[208,384]{1,0:T(8,128)(2,1)S(1)}, u32[]{:S(2)}, u32[]{:S(2)}) collective-permute-start(bf16[208,384]{1,0:T(8,128)(2,1)S(1)} %constant_dynamic-slice_fusion), channel_id=1, source_target_pairs={{0,1},{1,0},{2,3},{3,2},{4,6},{5,7},{6,4},{7,5},{8,9},{9,8},{10,11... | collective-permute-start | bytes 479240 | tf_op jit(solution)/shard_map/ppermute | solution.py:313
  19.0 5.1 %collective-permute-start.6 = (bf16[192,128]{1,0:T(8,128)(2,1)S(1)}, bf16[192,128]{1,0:T(8,128)(2,1)S(1)}, u32[]{:S(2)}, u32[]{:S(2)}) collective-permute-start(bf16[192,128]{1,0:T(8,128)(2,1)S(1)} %get-tuple-element.46), channel_id=1, source_target_pairs={{0,8},{4,12},{8,0},{12,4},{16,24},{20,28},{24,16},{28,20},{1,9},{5... | collective-permute-start | bytes 147464 | tf_op jit(solution)/shard_map/ppermute | solution.py:303
  20.6 4.1 %collective-permute-start.7 = (bf16[192,128]{1,0:T(8,128)(2,1)S(1)}, bf16[192,128]{1,0:T(8,128)(2,1)S(1)}, u32[]{:S(2)}, u32[]{:S(2)}) collective-permute-start(bf16[192,128]{1,0:T(8,128)(2,1)S(1)} %get-tuple-element.47), channel_id=1, source_target_pairs={{0,16},{4,20},{8,24},{12,28},{16,0},{20,4},{24,8},{28,12},{1,17},{... | collective-permute-start | bytes 147464 | tf_op jit(solution)/shard_map/ppermute | solution.py:303
  21.3 5.1 %collective-permute-start.9 = (bf16[192,128]{1,0:T(8,128)(2,1)S(1)}, bf16[192,128]{1,0:T(8,128)(2,1)S(1)}, u32[]{:S(2)}, u32[]{:S(2)}) collective-permute-start(bf16[192,128]{1,0:T(8,128)(2,1)S(1)} %get-tuple-element.51), channel_id=1, source_target_pairs={{0,24},{4,28},{8,16},{12,20},{16,8},{20,12},{24,0},{28,4},{1,25},{... | collective-permute-start | bytes 147464 | tf_op jit(solution)/shard_map/ppermute | solution.py:303
  22.6 5.3 %collective-permute-start.14 = (bf16[208,384]{1,0:T(8,128)(2,1)S(1)}, bf16[208,384]{1,0:T(8,128)(2,1)S(1)}, u32[]{:S(2)}, u32[]{:S(2)}) collective-permute-start(bf16[208,384]{1,0:T(8,128)(2,1)S(1)} %collective-permute-done.10.refs_9_), channel_id=1, source_target_pairs={{0,8},{4,20},{8,0},{12,28},{16,24},{20,4},{24,16},{28,12},{1,9},{5... | collective-permute-start | bytes 479240 | tf_op jit(solution)/shard_map/ppermute | solution.py:309
  24.7 3.5 %collective-permute-start.13 = (bf16[384,384]{1,0:T(8,128)(2,1)S(1)}, bf16[384,384]{1,0:T(8,128)(2,1)S(1)}, u32[]{:S(2)}, u32[]{:S(2)}) collective-permute-start(bf16[384,384]{1,0:T(8,128)(2,1)S(1)} %collective-permute-done.8.refs_6_), channel_id=1, source_target_pairs={{0,4},{4,0},{8,12},{12,8},{16,20},{20,16},{24,28},{28,24},{1,5},{5... | collective-permute-start | bytes 884744 | tf_op jit(solution)/shard_map/ppermute | solution.py:303
  26.3 1.8 %collective-permute-start.11 = (bf16[384,384]{1,0:T(8,128)(2,1)S(1)}, bf16[384,384]{1,0:T(8,128)(2,1)S(1)}, u32[]{:S(2)}, u32[]{:S(2)}) collective-permute-start(bf16[384,384]{1,0:T(8,128)(2,1)S(1)} %collective-permute-done.refs_5_), channel_id=1, source_target_pairs={{0,4},{4,0},{8,12},{12,8},{16,20},{20,16},{24,28},{28,24},{1,5},{5... | collective-permute-start | bytes 884744 | tf_op jit(solution)/shard_map/ppermute | solution.py:303
  26.3 1.8 %collective-permute-start.12 = (bf16[208,384]{1,0:T(8,128)(2,1)S(1)}, bf16[208,384]{1,0:T(8,128)(2,1)S(1)}, u32[]{:S(2)}, u32[]{:S(2)}) collective-permute-start(bf16[208,384]{1,0:T(8,128)(2,1)S(1)} %collective-permute-done.10.refs_9_), channel_id=1, source_target_pairs={{0,4},{4,0},{8,12},{12,8},{16,20},{20,16},{24,28},{28,24},{1,5},{5... | collective-permute-start | bytes 479240 | tf_op jit(solution)/shard_map/ppermute | solution.py:303
  27.9 1.4 %collective-permute-start.15 = (bf16[208,384]{1,0:T(8,128)(2,1)S(1)}, bf16[208,384]{1,0:T(8,128)(2,1)S(1)}, u32[]{:S(2)}, u32[]{:S(2)}) collective-permute-start(bf16[208,384]{1,0:T(8,128)(2,1)S(1)} %collective-permute-done.14.refs_11_), channel_id=1, source_target_pairs={{0,4},{4,0},{8,12},{12,8},{16,20},{20,16},{24,28},{28,24},{1,5},{5... | collective-permute-start | bytes 479240 | tf_op jit(solution)/shard_map/ppermute | solution.py:303

commit v22 on v17

--- a/solution.py
+++ b/solution.py
@@ -113,7 +113,7 @@
         query = jnp.concatenate([jnp.concatenate([same[flip // 2][0, rows, :], ones], axis=0) for flip in flips], axis=1)
         return [jnp.dot(keys[head, part, :], query, preferred_element_type=jnp.float32) for part in parts]
 
-    parts = [slice(first, first + keys.shape[1] // 4) for first in range(0, keys.shape[1], keys.shape[1] // 4)]
+    parts = [slice(first, first + keys.shape[1] // 2) for first in range(0, keys.shape[1], keys.shape[1] // 2)]
     chunks = [(head, flips) for head in range(2) for flips in (FLIPS[:2], FLIPS[2:])]
     prepare(0)
     later = score(*chunks[0])

time: 30.3 us -> 30.2 us (level)
  no operation moved by 1% of the time
where the time goes in v22:
time: 30.2 us; the launch traced here: 30.1 us
  starting transfers between devices  15.3 us (51%)
  waiting for transfers between devices  8.98 us (30%)
  Pallas kernels  5.07 us (17%)
  between operations  0.74 us (2%)
    ppermute x12, starting transfers between devices, exchange(): return lax.ppermute(array, axis, [(i, i ^ flip) for i in range(size)])  7.87 us
    ppermute x12, waiting for transfers between devices, exchange(): return lax.ppermute(array, axis, [(i, i ^ flip) for i in range(size)])  6.53 us
    ppermute x2, starting transfers between devices, exchange_along(): return lax.ppermute(array, ('ctx', 'fsdp'), pairs)  5.43 us
    ppermute x2, starting transfers between devices, exchange_in_plane(): lax.ppermute(array, 'ctx', [(i, i ^ (4 if i % 2 else 2)) for i in range(c...  1.97 us
    pallas_call x1, Pallas kernels, attend(): pl.pallas_call(functools.partial(attention_kernel, groups), out_shape=[pl...  1.87 us
    ppermute x2, waiting for transfers between devices, exchange_along(): return lax.ppermute(array, ('ctx', 'fsdp'), pairs)  1.42 us
    pallas_call x1, Pallas kernels, copy_in(): pl.pallas_call(functools.partial(copy_in_kernel, by_parity), out_shape=[p...  1.24 us
    ppermute x2, waiting for transfers between devices, exchange_in_plane(): lax.ppermute(array, 'ctx', [(i, i ^ (4 if i % 2 else 2)) for i in range(c...  1.03 us
  transfers between devices with their start and end apart: 16, of which 9 were waited for; matrix products, arithmetic and copies ran while one was open for 0% of the time, Pallas kernels for 10%

profile of v22, /device:TPU:0, one launch (start us, length us, event | category | flops | bytes accessed | tf_op | source)
XLA Modules:
  0.0 30.1 jit_solution(7535477897350488912)
XLA Ops:
  0.0 1.2 %copy_in.1 = (bf16[3,128,768]{2,1,0:T(8,128)(2,1)S(1)}, bf16[384,384]{1,0:T(8,128)(2,1)S(1)}) custom-call(bf16[1,128,768]{2,1,0:T(8,128)(2,1)} %query_ref.1, bf16[1,128,768]{2,1,0:T(8,128)(2,1)} %key_ref.1, bf16[1,128,768]{2,1,0:T(8,128)(2,1)} %value_ref.1, bf16[768,384]{1,0:T(8,128)(2,1)} %refs_4_.1), custom_call_target="tpu_custom_call" | custom-call | tf_op jit(solution)/shard_map/copy_in/pallas_call | solution.py:45
  1.2 4.1 %collective-permute-start = (bf16[384,384]{1,0:T(8,128)(2,1)S(1)}, bf16[384,384]{1,0:T(8,128)(2,1)S(1)}, u32[]{:S(2)}, u32[]{:S(2)}) collective-permute-start(bf16[384,384]{1,0:T(8,128)(2,1)S(1)} %get-tuple-element.33), channel_id=1, source_target_pairs={{0,2},{1,3},{2,0},{3,1},{4,5},{5,4},{6,7},{7,6},{8,10},{9,11},{10,... | collective-permute-start | bytes 884744 | tf_op jit(solution)/shard_map/ppermute | solution.py:310
  5.3 0.2 turn_heads.1
  5.6 1.6 %collective-permute-start.2 = (bf16[3,192,128]{2,1,0:T(8,128)(2,1)S(1)}, bf16[3,192,128]{2,1,0:T(8,128)(2,1)S(1)}, u32[]{:S(2)}, u32[]{:S(2)}) collective-permute-start(bf16[3,192,128]{2,1,0:T(8,128)(2,1)S(1)} %get-tuple-element.37), channel_id=1, source_target_pairs={{0,8},{4,12},{8,0},{12,4},{16,24},{20,28},{24,16},{28,20},{1,9},{5... | collective-permute-start | bytes 442376 | tf_op jit(solution)/shard_map/ppermute | solution.py:300
  7.2 1.5 %collective-permute-start.3 = (bf16[3,192,128]{2,1,0:T(8,128)(2,1)S(1)}, bf16[3,192,128]{2,1,0:T(8,128)(2,1)S(1)}, u32[]{:S(2)}, u32[]{:S(2)}) collective-permute-start(bf16[3,192,128]{2,1,0:T(8,128)(2,1)S(1)} %get-tuple-element.38), channel_id=1, source_target_pairs={{0,16},{4,20},{8,24},{12,28},{16,0},{20,4},{24,8},{28,12},{1,17},{... | collective-permute-start | bytes 442376 | tf_op jit(solution)/shard_map/ppermute | solution.py:300
  8.7 0.5 %collective-permute-start.4 = (bf16[3,192,128]{2,1,0:T(8,128)(2,1)S(1)}, bf16[3,192,128]{2,1,0:T(8,128)(2,1)S(1)}, u32[]{:S(2)}, u32[]{:S(2)}) collective-permute-start(bf16[3,192,128]{2,1,0:T(8,128)(2,1)S(1)} %get-tuple-element.39), channel_id=1, source_target_pairs={{0,24},{4,28},{8,16},{12,20},{16,8},{20,12},{24,0},{28,4},{1,25},{... | collective-permute-start | bytes 442376 | tf_op jit(solution)/shard_map/ppermute | solution.py:300
  9.2 0.1 collective-permute-start.1
  9.9 0.6 %collective-permute-done.1.refs_4_ = bf16[2,192,128]{2,1,0:T(8,128)(2,1)S(1)} collective-permute-done((bf16[2,192,128]{2,1,0:T(8,128)(2,1)S(1)}, bf16[2,192,128]{2,1,0:T(8,128)(2,1)S(1)}, u32[]{:S(2)}, u32[]{:S(2)}) %collective-permute-start.1) | collective-permute-done | bytes 98336 | tf_op jit(solution)/shard_map/ppermute | solution.py:300
  10.5 1.4 %collective-permute-done.refs_5_ = bf16[384,384]{1,0:T(8,128)(2,1)S(1)} collective-permute-done((bf16[384,384]{1,0:T(8,128)(2,1)S(1)}, bf16[384,384]{1,0:T(8,128)(2,1)S(1)}, u32[]{:S(2)}, u32[]{:S(2)}) %collective-permute-start) | collective-permute-done | bytes 294944 | tf_op jit(solution)/shard_map/ppermute | solution.py:310
  12.0 0.4 %collective-permute-done.2.refs_0_.refs_1_ = bf16[3,192,128]{2,1,0:T(8,128)(2,1)S(1)} collective-permute-done((bf16[3,192,128]{2,1,0:T(8,128)(2,1)S(1)}, bf16[3,192,128]{2,1,0:T(8,128)(2,1)S(1)}, u32[]{:S(2)}, u32[]{:S(2)}) %collective-permute-start.2) | collective-permute-done | bytes 147488 | tf_op jit(solution)/shard_map/ppermute | solution.py:300
  12.4 2.8 %collective-permute-done.3.refs_1_.refs_2_ = bf16[3,192,128]{2,1,0:T(8,128)(2,1)S(1)} collective-permute-done((bf16[3,192,128]{2,1,0:T(8,128)(2,1)S(1)}, bf16[3,192,128]{2,1,0:T(8,128)(2,1)S(1)}, u32[]{:S(2)}, u32[]{:S(2)}) %collective-permute-start.3) | collective-permute-done | bytes 147488 | tf_op jit(solution)/shard_map/ppermute | solution.py:300
  15.2 0.0 collective-permute-done.4.refs_2_.refs_3_
  15.2 0.1 collective-permute-start.5
  15.3 0.5 %collective-permute-start.8 = (bf16[384,384]{1,0:T(8,128)(2,1)S(1)}, bf16[384,384]{1,0:T(8,128)(2,1)S(1)}, u32[]{:S(2)}, u32[]{:S(2)}) collective-permute-start(bf16[384,384]{1,0:T(8,128)(2,1)S(1)} %collective-permute-done.refs_5_), channel_id=1, source_target_pairs={{0,8},{4,20},{8,0},{12,28},{16,24},{20,4},{24,16},{28,12},{1,9},{5... | collective-permute-start | bytes 884744 | tf_op jit(solution)/shard_map/ppermute | solution.py:306
  15.8 0.0 copy-start
  15.8 1.3 %collective-permute-start.10 = (bf16[208,384]{1,0:T(8,128)(2,1)S(1)}, bf16[208,384]{1,0:T(8,128)(2,1)S(1)}, u32[]{:S(2)}, u32[]{:S(2)}) collective-permute-start(bf16[208,384]{1,0:T(8,128)(2,1)S(1)} %constant_dynamic-slice_fusion), channel_id=1, source_target_pairs={{0,1},{1,0},{2,3},{3,2},{4,6},{5,7},{6,4},{7,5},{8,9},{9,8},{10,11... | collective-permute-start | bytes 479240 | tf_op jit(solution)/shard_map/ppermute | solution.py:310
  17.1 0.0 collective-permute-done.5.refs_5_
  17.1 1.9 %attend_two_heads.1 = (bf16[192,128]{1,0:T(8,128)(2,1)S(1)}, bf16[192,128]{1,0:T(8,128)(2,1)S(1)}, bf16[192,128]{1,0:T(8,128)(2,1)S(1)}, bf16[192,128]{1,0:T(8,128)(2,1)S(1)}) custom-call(s32[8,128]{1,0:T(8,128)S(1)} %broadcast_in_dim.2.lengths_ref, bf16[3,192,128]{2,1,0:T(8,128)(2,1)S(1)} %get-tuple-element.35.refs_0_, ...), custom_call_target="tpu_custom_call" | custom-call | flops 1610612736 | tf_op jit(solution)/shard_map/attend_two_heads/pallas_call | solution.py:157
  19.0 1.6 %collective-permute-start.6 = (bf16[192,128]{1,0:T(8,128)(2,1)S(1)}, bf16[192,128]{1,0:T(8,128)(2,1)S(1)}, u32[]{:S(2)}, u32[]{:S(2)}) collective-permute-start(bf16[192,128]{1,0:T(8,128)(2,1)S(1)} %get-tuple-element.46), channel_id=1, source_target_pairs={{0,8},{4,12},{8,0},{12,4},{16,24},{20,28},{24,16},{28,20},{1,9},{5... | collective-permute-start | bytes 147464 | tf_op jit(solution)/shard_map/ppermute | solution.py:300
  20.6 0.7 %collective-permute-start.7 = (bf16[192,128]{1,0:T(8,128)(2,1)S(1)}, bf16[192,128]{1,0:T(8,128)(2,1)S(1)}, u32[]{:S(2)}, u32[]{:S(2)}) collective-permute-start(bf16[192,128]{1,0:T(8,128)(2,1)S(1)} %get-tuple-element.47), channel_id=1, source_target_pairs={{0,16},{4,20},{8,24},{12,28},{16,0},{20,4},{24,8},{28,12},{1,17},{... | collective-permute-start | bytes 147464 | tf_op jit(solution)/shard_map/ppermute | solution.py:300
  21.2 1.3 %collective-permute-start.9 = (bf16[192,128]{1,0:T(8,128)(2,1)S(1)}, bf16[192,128]{1,0:T(8,128)(2,1)S(1)}, u32[]{:S(2)}, u32[]{:S(2)}) collective-permute-start(bf16[192,128]{1,0:T(8,128)(2,1)S(1)} %get-tuple-element.51), channel_id=1, source_target_pairs={{0,24},{4,28},{8,16},{12,20},{16,8},{20,12},{24,0},{28,4},{1,25},{... | collective-permute-start | bytes 147464 | tf_op jit(solution)/shard_map/ppermute | solution.py:300
  22.6 0.0 collective-permute-done.10.refs_9_
  22.6 1.5 %collective-permute-start.14 = (bf16[208,384]{1,0:T(8,128)(2,1)S(1)}, bf16[208,384]{1,0:T(8,128)(2,1)S(1)}, u32[]{:S(2)}, u32[]{:S(2)}) collective-permute-start(bf16[208,384]{1,0:T(8,128)(2,1)S(1)} %collective-permute-done.10.refs_9_), channel_id=1, source_target_pairs={{0,8},{4,20},{8,0},{12,28},{16,24},{20,4},{24,16},{28,12},{1,9},{5... | collective-permute-start | bytes 479240 | tf_op jit(solution)/shard_map/ppermute | solution.py:306
  24.1 0.0 collective-permute-done.8.refs_6_
  24.1 0.0 collective-permute-done.6.refs_1_
  24.1 0.6 %collective-permute-done.7.refs_2_ = bf16[192,128]{1,0:T(8,128)(2,1)S(1)} collective-permute-done((bf16[192,128]{1,0:T(8,128)(2,1)S(1)}, bf16[192,128]{1,0:T(8,128)(2,1)S(1)}, u32[]{:S(2)}, u32[]{:S(2)}) %collective-permute-start.7) | collective-permute-done | bytes 49184 | tf_op jit(solution)/shard_map/ppermute | solution.py:300
  24.7 0.0 collective-permute-start.13
  24.7 1.6 %collective-permute-done.9.refs_3_ = bf16[192,128]{1,0:T(8,128)(2,1)S(1)} collective-permute-done((bf16[192,128]{1,0:T(8,128)(2,1)S(1)}, bf16[192,128]{1,0:T(8,128)(2,1)S(1)}, u32[]{:S(2)}, u32[]{:S(2)}) %collective-permute-start.9) | collective-permute-done | bytes 49184 | tf_op jit(solution)/shard_map/ppermute | solution.py:300
  26.3 0.0 collective-permute-start.11
  26.3 0.5 %collective-permute-start.12 = (bf16[208,384]{1,0:T(8,128)(2,1)S(1)}, bf16[208,384]{1,0:T(8,128)(2,1)S(1)}, u32[]{:S(2)}, u32[]{:S(2)}) collective-permute-start(bf16[208,384]{1,0:T(8,128)(2,1)S(1)} %collective-permute-done.10.refs_9_), channel_id=1, source_target_pairs={{0,4},{4,0},{8,12},{12,8},{16,20},{20,16},{24,28},{28,24},{1,5},{5... | collective-permute-start | bytes 479240 | tf_op jit(solution)/shard_map/ppermute | solution.py:300
  26.8 1.0 %collective-permute-done.14.refs_11_ = bf16[208,384]{1,0:T(8,128)(2,1)S(1)} collective-permute-done((bf16[208,384]{1,0:T(8,128)(2,1)S(1)}, bf16[208,384]{1,0:T(8,128)(2,1)S(1)}, u32[]{:S(2)}, u32[]{:S(2)}) %collective-permute-start.14) | collective-permute-done | bytes 159776 | tf_op jit(solution)/shard_map/ppermute | solution.py:306
  27.8 0.1 collective-permute-start.15
  27.9 0.2 collective-permute-done.12.refs_10_
  28.1 0.0 collective-permute-done.13.refs_8_
  28.1 0.0 collective-permute-done.11.refs_7_
  28.1 0.0 copy-done
  28.1 0.8 %project_near_shards.1 = (bf16[3,128,384]{2,1,0:T(8,128)(2,1)S(1)}, f32[128,384]{1,0:T(8,128)S(1)}, bf16[128,192]{1,0:T(8,128)(2,1)S(1)}) custom-call(bf16[192,128]{1,0:T(8,128)(2,1)S(1)} %get-tuple-element.45.refs_0_, bf16[192,128]{1,0:T(8,128)(2,1)S(1)} %collective-permute-done.6.refs_1_, bf16[192,128]{1,0:T(8,128)(2,1)S(1)} %collective-permute-done.7.refs_2_, ...), custom_call_target="tpu_custom_call" | custom-call | flops 226492416 | bytes 1769472 | tf_op jit(solution)/shard_map/project_near_shards/pallas_call | solution.py:263
  29.0 0.3 collective-permute-done.15.part_ref
  29.2 0.9 %project_third_shard.1 = bf16[1,128,1536]{2,1,0:T(8,128)(2,1)} custom-call(bf16[3,128,384]{2,1,0:T(8,128)(2,1)S(1)} %get-tuple-element.58.blocks_ref, f32[128,384]{1,0:T(8,128)S(1)} %get-tuple-element.59.sum_ref, bf16[128,192]{1,0:T(8,128)(2,1)S(1)} %get-tuple-element.60.rest_ref, bf16[208,384]{1,0:T(8,128)(2,1)S(1)} %collective-permute-done.15.part_ref), custom_call_target="tpu_custom_call" | custom-call | flops 18874368 | bytes 147456 | tf_op jit(solution)/shard_map/project_third_shard/pallas_call | solution.py:285
  (4 shorter events, 0.0 us)
Async XLA Ops:
  1.2 10.7 %collective-permute-start = (bf16[384,384]{1,0:T(8,128)(2,1)S(1)}, bf16[384,384]{1,0:T(8,128)(2,1)S(1)}, u32[]{:S(2)}, u32[]{:S(2)}) collective-permute-start(bf16[384,384]{1,0:T(8,128)(2,1)S(1)} %get-tuple-element.33), channel_id=1, source_target_pairs={{0,2},{1,3},{2,0},{3,1},{4,5},{5,4},{6,7},{7,6},{8,10},{9,11},{10,... | collective-permute-start | bytes 884744 | tf_op jit(solution)/shard_map/ppermute | solution.py:310
  5.6 6.8 %collective-permute-start.2 = (bf16[3,192,128]{2,1,0:T(8,128)(2,1)S(1)}, bf16[3,192,128]{2,1,0:T(8,128)(2,1)S(1)}, u32[]{:S(2)}, u32[]{:S(2)}) collective-permute-start(bf16[3,192,128]{2,1,0:T(8,128)(2,1)S(1)} %get-tuple-element.37), channel_id=1, source_target_pairs={{0,8},{4,12},{8,0},{12,4},{16,24},{20,28},{24,16},{28,20},{1,9},{5... | collective-permute-start | bytes 442376 | tf_op jit(solution)/shard_map/ppermute | solution.py:300
  7.2 8.0 %collective-permute-start.3 = (bf16[3,192,128]{2,1,0:T(8,128)(2,1)S(1)}, bf16[3,192,128]{2,1,0:T(8,128)(2,1)S(1)}, u32[]{:S(2)}, u32[]{:S(2)}) collective-permute-start(bf16[3,192,128]{2,1,0:T(8,128)(2,1)S(1)} %get-tuple-element.38), channel_id=1, source_target_pairs={{0,16},{4,20},{8,24},{12,28},{16,0},{20,4},{24,8},{28,12},{1,17},{... | collective-permute-start | bytes 442376 | tf_op jit(solution)/shard_map/ppermute | solution.py:300
  8.7 6.5 %collective-permute-start.4 = (bf16[3,192,128]{2,1,0:T(8,128)(2,1)S(1)}, bf16[3,192,128]{2,1,0:T(8,128)(2,1)S(1)}, u32[]{:S(2)}, u32[]{:S(2)}) collective-permute-start(bf16[3,192,128]{2,1,0:T(8,128)(2,1)S(1)} %get-tuple-element.39), channel_id=1, source_target_pairs={{0,24},{4,28},{8,16},{12,20},{16,8},{20,12},{24,0},{28,4},{1,25},{... | collective-permute-start | bytes 442376 | tf_op jit(solution)/shard_map/ppermute | solution.py:300
  9.2 1.4 %collective-permute-start.1 = (bf16[2,192,128]{2,1,0:T(8,128)(2,1)S(1)}, bf16[2,192,128]{2,1,0:T(8,128)(2,1)S(1)}, u32[]{:S(2)}, u32[]{:S(2)}) collective-permute-start(bf16[2,192,128]{2,1,0:T(8,128)(2,1)S(1)} %slice.3), channel_id=1, source_target_pairs={{0,4},{4,0},{8,12},{12,8},{16,20},{20,16},{24,28},{28,24},{1,5},{5... | collective-permute-start | bytes 294920 | tf_op jit(solution)/shard_map/ppermute | solution.py:300
  15.2 1.9 %collective-permute-start.5 = (bf16[3,2,192,128]{3,2,1,0:T(8,128)(2,1)S(1)}, bf16[3,2,192,128]{3,2,1,0:T(8,128)(2,1)S(1)}, u32[]{:S(2)}, u32[]{:S(2)}) collective-permute-start(bf16[3,2,192,128]{3,2,1,0:T(8,128)(2,1)S(1)} %stack_keys_and_values.1), channel_id=1, source_target_pairs={{0,4},{4,0},{8,12},{12,8},{16,20},{20,16},{24,28},{28,24},{1,5},{5... | collective-permute-start | bytes 884744 | tf_op jit(solution)/shard_map/ppermute | solution.py:300
  15.3 8.8 %collective-permute-start.8 = (bf16[384,384]{1,0:T(8,128)(2,1)S(1)}, bf16[384,384]{1,0:T(8,128)(2,1)S(1)}, u32[]{:S(2)}, u32[]{:S(2)}) collective-permute-start(bf16[384,384]{1,0:T(8,128)(2,1)S(1)} %collective-permute-done.refs_5_), channel_id=1, source_target_pairs={{0,8},{4,20},{8,0},{12,28},{16,24},{20,4},{24,16},{28,12},{1,9},{5... | collective-permute-start | bytes 884744 | tf_op jit(solution)/shard_map/ppermute | solution.py:306
  15.8 12.3 %copy-start = (bf16[768,384]{1,0:T(8,128)(2,1)S(1)}, bf16[768,384]{1,0:T(8,128)(2,1)}, u32[]{:S(2)}) copy-start(bf16[768,384]{1,0:T(8,128)(2,1)} %refs_4_.1) | copy-start | bytes 1769476
  15.8 6.8 %collective-permute-start.10 = (bf16[208,384]{1,0:T(8,128)(2,1)S(1)}, bf16[208,384]{1,0:T(8,128)(2,1)S(1)}, u32[]{:S(2)}, u32[]{:S(2)}) collective-permute-start(bf16[208,384]{1,0:T(8,128)(2,1)S(1)} %constant_dynamic-slice_fusion), channel_id=1, source_target_pairs={{0,1},{1,0},{2,3},{3,2},{4,6},{5,7},{6,4},{7,5},{8,9},{9,8},{10,11... | collective-permute-start | bytes 479240 | tf_op jit(solution)/shard_map/ppermute | solution.py:310
  19.0 5.1 %collective-permute-start.6 = (bf16[192,128]{1,0:T(8,128)(2,1)S(1)}, bf16[192,128]{1,0:T(8,128)(2,1)S(1)}, u32[]{:S(2)}, u32[]{:S(2)}) collective-permute-start(bf16[192,128]{1,0:T(8,128)(2,1)S(1)} %get-tuple-element.46), channel_id=1, source_target_pairs={{0,8},{4,12},{8,0},{12,4},{16,24},{20,28},{24,16},{28,20},{1,9},{5... | collective-permute-start | bytes 147464 | tf_op jit(solution)/shard_map/ppermute | solution.py:300
  20.6 4.1 %collective-permute-start.7 = (bf16[192,128]{1,0:T(8,128)(2,1)S(1)}, bf16[192,128]{1,0:T(8,128)(2,1)S(1)}, u32[]{:S(2)}, u32[]{:S(2)}) collective-permute-start(bf16[192,128]{1,0:T(8,128)(2,1)S(1)} %get-tuple-element.47), channel_id=1, source_target_pairs={{0,16},{4,20},{8,24},{12,28},{16,0},{20,4},{24,8},{28,12},{1,17},{... | collective-permute-start | bytes 147464 | tf_op jit(solution)/shard_map/ppermute | solution.py:300
  21.2 5.1 %collective-permute-start.9 = (bf16[192,128]{1,0:T(8,128)(2,1)S(1)}, bf16[192,128]{1,0:T(8,128)(2,1)S(1)}, u32[]{:S(2)}, u32[]{:S(2)}) collective-permute-start(bf16[192,128]{1,0:T(8,128)(2,1)S(1)} %get-tuple-element.51), channel_id=1, source_target_pairs={{0,24},{4,28},{8,16},{12,20},{16,8},{20,12},{24,0},{28,4},{1,25},{... | collective-permute-start | bytes 147464 | tf_op jit(solution)/shard_map/ppermute | solution.py:300
  22.6 5.3 %collective-permute-start.14 = (bf16[208,384]{1,0:T(8,128)(2,1)S(1)}, bf16[208,384]{1,0:T(8,128)(2,1)S(1)}, u32[]{:S(2)}, u32[]{:S(2)}) collective-permute-start(bf16[208,384]{1,0:T(8,128)(2,1)S(1)} %collective-permute-done.10.refs_9_), channel_id=1, source_target_pairs={{0,8},{4,20},{8,0},{12,28},{16,24},{20,4},{24,16},{28,12},{1,9},{5... | collective-permute-start | bytes 479240 | tf_op jit(solution)/shard_map/ppermute | solution.py:306
  24.7 3.5 %collective-permute-start.13 = (bf16[384,384]{1,0:T(8,128)(2,1)S(1)}, bf16[384,384]{1,0:T(8,128)(2,1)S(1)}, u32[]{:S(2)}, u32[]{:S(2)}) collective-permute-start(bf16[384,384]{1,0:T(8,128)(2,1)S(1)} %collective-permute-done.8.refs_6_), channel_id=1, source_target_pairs={{0,4},{4,0},{8,12},{12,8},{16,20},{20,16},{24,28},{28,24},{1,5},{5... | collective-permute-start | bytes 884744 | tf_op jit(solution)/shard_map/ppermute | solution.py:300
  26.3 1.8 %collective-permute-start.11 = (bf16[384,384]{1,0:T(8,128)(2,1)S(1)}, bf16[384,384]{1,0:T(8,128)(2,1)S(1)}, u32[]{:S(2)}, u32[]{:S(2)}) collective-permute-start(bf16[384,384]{1,0:T(8,128)(2,1)S(1)} %collective-permute-done.refs_5_), channel_id=1, source_target_pairs={{0,4},{4,0},{8,12},{12,8},{16,20},{20,16},{24,28},{28,24},{1,5},{5... | collective-permute-start | bytes 884744 | tf_op jit(solution)/shard_map/ppermute | solution.py:300
  26.3 1.8 %collective-permute-start.12 = (bf16[208,384]{1,0:T(8,128)(2,1)S(1)}, bf16[208,384]{1,0:T(8,128)(2,1)S(1)}, u32[]{:S(2)}, u32[]{:S(2)}) collective-permute-start(bf16[208,384]{1,0:T(8,128)(2,1)S(1)} %collective-permute-done.10.refs_9_), channel_id=1, source_target_pairs={{0,4},{4,0},{8,12},{12,8},{16,20},{20,16},{24,28},{28,24},{1,5},{5... | collective-permute-start | bytes 479240 | tf_op jit(solution)/shard_map/ppermute | solution.py:300
  27.8 1.4 %collective-permute-start.15 = (bf16[208,384]{1,0:T(8,128)(2,1)S(1)}, bf16[208,384]{1,0:T(8,128)(2,1)S(1)}, u32[]{:S(2)}, u32[]{:S(2)}) collective-permute-start(bf16[208,384]{1,0:T(8,128)(2,1)S(1)} %collective-permute-done.14.refs_11_), channel_id=1, source_target_pairs={{0,4},{4,0},{8,12},{12,8},{16,20},{20,16},{24,28},{28,24},{1,5},{5... | collective-permute-start | bytes 479240 | tf_op jit(solution)/shard_map/ppermute | solution.py:300
